TPU v7x, 32 devices: a whole 2x2x4 slice. The times are simulated.
32 devices in a mesh: section: 2 (over x), expert: 8 (over z, y), dp: 2 (over core).
Axes of the slice: x: 2, y: 2, z: 4, core: 2. Of those that a mesh axis runs over, the one named last changes fastest.
Arguments:
- blocks: bfloat16 [2, 2048, 3072], P('section', ('dp', 'expert')), parts along dimension 1, may hold values from -6 to 6
- norm_gain: bfloat16 [2, 3072], P('section'), may hold values from 0.25 to 1.75
- w_gate: bfloat16 [2, 3072, 1536], P('section', None, 'expert'), may hold values from -0.109375 to 0.109375
- w_up: bfloat16 [2, 3072, 1536], P('section', None, 'expert'), may hold values from -0.109375 to 0.109375
- w_down: bfloat16 [2, 1536, 3072], P('section', 'expert'), may hold values from -0.15625 to 0.15625
- route_ids: int32 [2, 2048, 2], P('section', ('dp', 'expert')), parts along dimension 1, may hold values from 0 to 8, as said below
- route_weights: float32 [2, 2048, 2], P('section', ('dp', 'expert')), parts along dimension 1, may hold values from 0.05 to 1
Outputs:
- mixed: bfloat16 [2, 2048, 3072], P('section', ('dp', 'expert')), parts along dimension 1
There are 2 independent parts, one for each index of `dp`. A program takes and returns all parts, laid end to end along the dimension named above; an argument that names none is the same for every part. Nothing has to cross between parts.
Inputs may be any that keep to these rules, and one draw needn't show every extreme that they name: `route_ids`: each token names 2 different ids. Within each aligned block of 128 tokens of a section (the tokens of one device), every computing expert (ids below 1) is named exactly 32 times and every zero-computation id at most 32 times.
All inputs are finite; a program needn't handle non-finite values.
Results may differ from a plain program's by a relative error of at most 0.0085.
Values may be sent and summed in bfloat16 or wider, within the bound.
No kernel may reach another device: no remote copies, remote signals or barrier semaphores. Data moves between devices by JAX's collectives and lax.ppermute only.
A program may use at most 64 MiB of HBM per device.

v0:
```python
import jax
import jax.numpy as jnp
from jax import lax
from jax.sharding import PartitionSpec as P

HID = 1536
CAP = 32


def passed_along(value, axis, steps):
    count = lax.axis_size(axis)
    pairs = [(source, (source + steps) % count) for source in range(count)]
    return lax.ppermute(value, axis, pairs)


def local(blocks, norm_gain, w_gate, w_up, w_down, route_ids, route_weights):
    arrived = passed_along(blocks, "section", 1)[0]
    residual = arrived.astype(jnp.float32)
    inverse = lax.rsqrt(jnp.mean(residual * residual, axis=-1, keepdims=True) + 1e-06)
    normed = (residual * inverse * norm_gain[0].astype(jnp.float32)).astype(jnp.bfloat16)
    slice_width = w_gate.shape[2]
    slice_count = HID // slice_width
    experts = lax.axis_size("expert") // slice_count
    token_count = arrived.shape[0]
    pick_count = route_ids.shape[2]
    pick_ids = route_ids[0].reshape(-1)
    member = (pick_ids[:, None] == jnp.arange(experts, dtype=jnp.int32)[None, :]).astype(jnp.int32)
    slot_rank = jnp.cumsum(member, axis=0) - 1
    slot_range = jnp.arange(CAP, dtype=jnp.int32)
    slot_table = (member[:, :, None] == 1) & (slot_rank[:, :, None] == slot_range[None, None, :])
    slot_table = slot_table.astype(jnp.float32).reshape(token_count, pick_count, experts, CAP)
    dispatch_table = jnp.sum(slot_table, axis=1)
    weighted_table = jnp.einsum(
        "tjec,tj->tec", slot_table, route_weights[0], precision=lax.Precision.HIGHEST
    )
    buffer = jnp.einsum(
        "tec,td->ecd",
        dispatch_table.astype(jnp.bfloat16),
        normed,
        preferred_element_type=jnp.float32,
    ).astype(jnp.bfloat16)
    outgoing = jnp.repeat(buffer, slice_count, axis=0)
    received = lax.all_to_all(outgoing, "expert", split_axis=0, concat_axis=0, tiled=True)
    flat_rows = received.reshape(-1, received.shape[-1])
    gate_act = jnp.dot(flat_rows, w_gate[0], preferred_element_type=jnp.float32)
    up_act = jnp.dot(flat_rows, w_up[0], preferred_element_type=jnp.float32)
    hidden = (jax.nn.silu(gate_act) * up_act).astype(jnp.bfloat16)
    partial_value = jnp.dot(hidden, w_down[0], preferred_element_type=jnp.float32).astype(
        jnp.bfloat16
    )
    returned = lax.all_to_all(
        partial_value.reshape(received.shape), "expert", split_axis=0, concat_axis=0, tiled=True
    )
    expert_out = jnp.sum(
        returned.reshape(experts, slice_count, CAP, returned.shape[-1]).astype(jnp.float32), axis=1
    )
    zero_weight = jnp.sum(jnp.where(route_ids[0] >= experts, route_weights[0], 0.0), axis=1)
    mixed = residual + zero_weight[:, None] * normed.astype(jnp.float32)
    mixed = mixed + jnp.einsum(
        "tec,ecd->td", weighted_table, expert_out, precision=lax.Precision.HIGHEST
    )
    return mixed.astype(jnp.bfloat16)[None]


def solution(mesh):
    placed = (
        P("section", ("dp", "expert"), None),
        P("section", None),
        P("section", None, "expert"),
        P("section", None, "expert"),
        P("section", "expert", None),
        P("section", ("dp", "expert"), None),
        P("section", ("dp", "expert"), None),
    )
    return jax.shard_map(
        local,
        mesh=mesh,
        in_specs=placed,
        out_specs=P("section", ("dp", "expert"), None),
        check_vma=False,
    )
```

profile of v0, /device:TPU:0, one launch (start us, length us, event | category | flops | bytes accessed | tf_op | source)
XLA Modules:
  0.0 113.2 jit_solution(18012069598603254807)
XLA Ops:
  0.0 0.0 copy-start
  0.0 2.9 %collective-permute-start = (bf16[1,128,3072]{2,1,0:T(8,128)(2,1)}, bf16[1,128,3072]{2,1,0:T(8,128)(2,1)S(1)}, u32[]{:S(2)}, u32[]{:S(2)}) collective-permute-start(bf16[1,128,3072]{2,1,0:T(8,128)(2,1)} %param.7), channel_id=1, source_target_pairs={{0,16},{16,0},{1,17},{17,1},{2,18},{18,2},{3,19},{19,3},{4,20},{20... | collective-permute-start | bytes 2359304 | tf_op jit(solution)/shard_map/ppermute | solution.py:13
  2.9 0.7 compare_convert_fusion
  3.6 0.7 mul.64
  4.3 0.0 copy-start.5
  4.4 0.1 copy.14
  4.5 0.1 reshape.206
  4.6 0.3 reduce-window.6
  4.9 0.1 reshape.197
  5.1 0.2 slice_reduce_fusion
  5.3 0.2 reduce-window.9
  5.4 0.1 broadcast.101
  5.5 0.1 reshape.200
  5.7 0.0 copy-start.4
  5.7 0.1 copy.15
  5.8 14.9 %collective-permute-done = bf16[1,128,3072]{2,1,0:T(8,128)(2,1)S(1)} collective-permute-done((bf16[1,128,3072]{2,1,0:T(8,128)(2,1)}, bf16[1,128,3072]{2,1,0:T(8,128)(2,1)S(1)}, u32[]{:S(2)}, u32[]{:S(2)}) %collective-permute-start) | collective-permute-done | bytes 786464 | tf_op jit(solution)/shard_map/ppermute | solution.py:13
  20.7 0.0 copy-start.2
  20.7 0.2 fusion.3
  20.9 0.0 copy-start.11
  20.9 0.4 convolution_convert_fusion.1
  21.4 0.0 copy-done.5
  21.4 0.0 copy-done.4
  21.4 0.2 copy-done.2
  21.6 0.0 copy-done.11
  21.6 0.2 reshape.201
  21.7 0.0 copy-start.1
  21.8 42.2 %all_to_all.10 = bf16[8,32,3072]{2,1,0:T(8,128)(2,1)S(1)} all-to-all(bf16[8,32,3072]{2,1,0:T(8,128)(2,1)S(1)} %reshape.201), channel_id=1, replica_groups=mesh['section'=2,'expert'=8,'dp'=2] {'expert'}, dimensions={0} | all-to-all | bytes 3145728 | tf_op jit(solution)/shard_map/all_to_all | solution.py:43
  64.0 0.0 copy-done.1
  64.0 0.7 fusion.13
  64.6 0.0 copy-done
  64.7 4.4 %convolution_convert_fusion = bf16[256,3072]{1,0:T(8,128)(2,1)} fusion(bf16[1,192,3072]{2,1,0:T(8,128)(2,1)S(1)} %copy-done, bf16[256,3072]{1,0:T(8,128)(2,1)S(1)} %bitcast.68, bf16[1,3072,192]{1,2,0:T(8,128)(2,1)} %param.10, f32[256,192]{0,1:T(8,128)S(1)} %fusion.13), kind=kOutput, calls=%fused_computation | convolution fusion | flops 605061120 | bytes 5701632 | tf_op jit(solution)/shard_map/dot_general | solution.py:48
  69.1 0.0 copy-start.7
  69.1 0.0 copy-start.8
  69.1 3.7 %all-to-all-start.1 = ((bf16[8,32,3072]{2,1,0:T(8,128)(2,1)}), bf16[8,32,3072]{2,1,0:T(8,128)(2,1)S(1)}, u32[]{:S(2)}, u32[]{:S(2)}) async-start(bf16[8,32,3072]{2,1,0:T(8,128)(2,1)} %bitcast.69), calls=%async_computation.1 | async-start | bytes 3145728 | tf_op jit(solution)/shard_map/all_to_all | solution.py:51
  72.8 0.1 copy.13
  72.9 0.0 copy-done.7
  72.9 0.7 copy.16
  73.7 0.0 copy-done.8
  73.7 0.6 fusion.40
  74.3 0.0 copy-start.3
  74.3 2.3 %fusion.28 = f32[128,1,32]{2,1,0:T(1,128)} fusion(f32[128,2,1]{1,2,0:T(1,128)} %copy.16, pred[128,2]{1,0:T(8,128)(4,1)S(1)} %copy.13, s32[128,2]{1,0:T(8,128)} %copy-done.4), kind=kOutput, calls=%fused_computation.27 | convolution fusion | flops 114688 | bytes 18688 | tf_op jit(solution)/shard_map/tjec,tj->tec/dot_general | solution.py:33
  76.6 32.7 %all-to-all-done.1 = bf16[8,32,3072]{2,1,0:T(8,128)(2,1)S(1)} async-done(((bf16[8,32,3072]{2,1,0:T(8,128)(2,1)}), bf16[8,32,3072]{2,1,0:T(8,128)(2,1)S(1)}, u32[]{:S(2)}, u32[]{:S(2)}) %all-to-all-start.1) | async-done | bytes 1572896 | tf_op jit(solution)/shard_map/all_to_all | solution.py:51
  109.3 0.2 convert_reduce_fusion
  109.5 0.0 copy-done.3
  109.5 0.0 copy-done.6
  109.5 0.0 copy-done.9
  109.5 0.6 copy-done.10
  110.1 3.1 %fusion.25 = bf16[1,128,3072]{2,1,0:T(8,128)(2,1)} fusion(bf16[1,128,3072]{2,1,0:T(8,128)(2,1)S(1)} %copy-done.3, f32[3072]{0:T(1024)S(1)} %bitcast.71, f32[128]{0:T(128)} %copy-done.11, f32[128]{0:T(128)S(1)} %copy-done.9, f32[128,32]{1,0:T(8,128)S(1)} %bitcast.73, f32[32,3072]{1,0:T(8,128)S(1)} %convert_reduce_fusion), kind=kOutput, calls=%fused_computation.23 | convolution fusion | flops 154533888 | bytes 1995776 | tf_op jit(solution)/shard_map/tec,ecd->td/dot_general | solution.py:59
  (7 shorter events, 0.1 us)
Async XLA Ops:
  0.0 64.6 %copy-start = (bf16[1,192,3072]{2,1,0:T(8,128)(2,1)S(1)}, bf16[1,192,3072]{2,1,0:T(8,128)(2,1)}, u32[]{:S(2)}) copy-start(bf16[1,192,3072]{2,1,0:T(8,128)(2,1)} %param.11) | copy-start | bytes 3538948
  0.0 20.7 %collective-permute-start = (bf16[1,128,3072]{2,1,0:T(8,128)(2,1)}, bf16[1,128,3072]{2,1,0:T(8,128)(2,1)S(1)}, u32[]{:S(2)}, u32[]{:S(2)}) collective-permute-start(bf16[1,128,3072]{2,1,0:T(8,128)(2,1)} %param.7), channel_id=1, source_target_pairs={{0,16},{16,0},{1,17},{17,1},{2,18},{18,2},{3,19},{19,3},{4,20},{20... | collective-permute-start | bytes 2359304 | tf_op jit(solution)/shard_map/ppermute | solution.py:13
  4.3 17.0 %copy-start.5 = (f32[1,3072]{1,0:T(1,128)}, f32[1,3072]{1,0:T(1,128)S(1)}, u32[]{:S(2)}) copy-start(f32[1,3072]{1,0:T(1,128)S(1)} %mul.64) | copy-start | bytes 36868
  5.7 15.7 %copy-start.4 = (s32[128,2]{1,0:T(8,128)}, s32[128,2]{1,0:T(8,128)S(1)}, u32[]{:S(2)}) copy-start(s32[128,2]{1,0:T(8,128)S(1)} %add_add_fusion) | copy-start | bytes 3076
  20.7 0.9 copy-start.2
  20.9 0.6 copy-start.11
  21.7 42.2 %copy-start.1 = (bf16[1,3072,192]{1,2,0:T(8,128)(2,1)S(1)}, bf16[1,3072,192]{1,2,0:T(8,128)(2,1)}, u32[]{:S(2)}) copy-start(bf16[1,3072,192]{1,2,0:T(8,128)(2,1)} %param.9) | copy-start | bytes 3538948
  69.1 3.9 %copy-start.7 = (f32[1,128,2]{1,2,0:T(2,128)S(1)}, f32[1,128,2]{1,2,0:T(2,128)}, u32[]{:S(2)}) copy-start(f32[1,128,2]{1,2,0:T(2,128)} %param.13) | copy-start | bytes 3076
  69.1 4.6 %copy-start.8 = (s32[1,128,2]{1,2,0:T(2,128)S(1)}, s32[1,128,2]{1,2,0:T(2,128)}, u32[]{:S(2)}) copy-start(s32[1,128,2]{1,2,0:T(2,128)} %param.12) | copy-start | bytes 3076
  69.1 40.2 %all-to-all-start.1 = ((bf16[8,32,3072]{2,1,0:T(8,128)(2,1)}), bf16[8,32,3072]{2,1,0:T(8,128)(2,1)S(1)}, u32[]{:S(2)}, u32[]{:S(2)}) async-start(bf16[8,32,3072]{2,1,0:T(8,128)(2,1)} %bitcast.69), calls=%async_computation.1 | async-start | bytes 3145728 | tf_op jit(solution)/shard_map/all_to_all | solution.py:51
  74.3 35.2 %copy-start.3 = (bf16[1,128,3072]{2,1,0:T(8,128)(2,1)S(1)}, bf16[1,128,3072]{2,1,0:T(8,128)(2,1)}, u32[]{:S(2)}) copy-start(bf16[1,128,3072]{2,1,0:T(8,128)(2,1)} %copy-done.2) | copy-start | bytes 2359300
  76.6 32.9 %copy-start.6 = (f32[1,3072]{1,0:T(1,128)S(1)}, f32[1,3072]{1,0:T(1,128)}, u32[]{:S(2)}) copy-start(f32[1,3072]{1,0:T(1,128)} %copy-done.5) | copy-start | bytes 36868
  76.6 32.9 %copy-start.9 = (f32[128]{0:T(128)S(1)}, f32[128]{0:T(128)}, u32[]{:S(2)}) copy-start(f32[128]{0:T(128)} %fusion.40) | copy-start | bytes 1540
  109.3 0.8 copy-start.10
where the time goes:
time: 114 us; the launch traced here: 113 us
  waiting for transfers between devices  47.6 us (42%)
  blocking collectives  42.2 us (37%)
  matrix products  10.9 us (10%)
  starting transfers between devices  6.65 us (6%)
  other arithmetic  3 us (3%)
  local copies, waits for them, and re-layouts  2.71 us (2%)
    all_to_all x1, blocking collectives, local(): lax.all_to_all(outgoing, 'expert', split_axis=0, concat_axis=0, tiled=True)  42.2 us
    all_to_all x1, waiting for transfers between devices, local(): lax.all_to_all(partial_value.reshape(received.shape), 'expert', split_axi...  32.7 us
    ppermute x1, waiting for transfers between devices, passed_along(): return lax.ppermute(value, axis, pairs)  14.9 us
    dot_general x1, matrix products, local(): jnp.dot(hidden, w_down[0], preferred_element_type=jnp.float32)  4.42 us
    all_to_all x1, starting transfers between devices, local(): lax.all_to_all(partial_value.reshape(received.shape), 'expert', split_axi...  3.71 us
    dot_general x1, matrix products, local(): jnp.einsum('tec,ecd->td', weighted_table, expert_out, precision=lax.Preci...  3.09 us
    ppermute x1, starting transfers between devices, passed_along(): return lax.ppermute(value, axis, pairs)  2.94 us
    dot_general x1, matrix products, local(): jnp.einsum('tjec,tj->tec', slot_table, route_weights[0], precision=lax.Pr...  2.3 us
  transfers between devices with their start and end apart: 2, of which 2 were waited for; matrix products, arithmetic and copies ran while one was open for 6% of the time, Pallas kernels for 0%

commit v1 on v0

v1 whole, which is shorter than its diff:
```python
import functools

import jax
import jax.numpy as jnp
from jax import lax
from jax.experimental import pallas as pl
from jax.experimental.pallas import tpu as pltpu
from jax.sharding import PartitionSpec as P

HID = 1536
CAP = 32
VMEM = pl.BlockSpec(memory_space=pltpu.VMEM)
HBM = pl.BlockSpec(memory_space=pltpu.HBM)
PARAMS = pltpu.CompilerParams(vmem_limit_bytes=24 * 1024 * 1024)


def after(value, *others):
    return lax.optimization_barrier((value, *others))[0]


def load_kernel(count, *refs):
    sources, targets, sems = refs[:count], refs[count:2 * count], refs[2 * count]
    copies = [
        pltpu.make_async_copy(a, b, sems.at[i]) for i, (a, b) in enumerate(zip(sources, targets))
    ]
    for copy in copies:
        copy.start()
    for copy in copies:
        copy.wait()


def loaded(*arrays):
    return pl.pallas_call(
        functools.partial(load_kernel, len(arrays)),
        out_shape=tuple(jax.ShapeDtypeStruct(a.shape, a.dtype) for a in arrays),
        in_specs=[HBM] * len(arrays),
        out_specs=(VMEM,) * len(arrays),
        scratch_shapes=[pltpu.SemaphoreType.DMA((len(arrays),))],
        compiler_params=PARAMS,
        cost_estimate=pl.CostEstimate(flops=0, bytes_accessed=6 * 1024 * 1024, transcendentals=0),
    )(*(pltpu.with_memory_space_constraint(a, pltpu.HBM) for a in arrays))


def slot_rows(ids, e):
    count = ids.shape[1]
    earlier = lax.broadcasted_iota(jnp.int32, (count, count), 0)
    later = lax.broadcasted_iota(jnp.int32, (count, count), 1)
    before = jnp.where(earlier < later, 1.0, 0.0).astype(jnp.bfloat16)
    slot = lax.broadcasted_iota(jnp.int32, (CAP, count), 0).astype(jnp.float32)
    hit = jnp.max(jnp.where(ids == e, 1.0, 0.0), axis=0, keepdims=True)
    hit = jnp.broadcast_to(hit, (CAP, count))
    rank = jnp.dot(hit.astype(jnp.bfloat16), before, preferred_element_type=jnp.float32)
    return jnp.where(rank == slot, hit, 0.0)


def pick_kernel(experts, ids_ref, block_ref, out_ref):
    for e in range(experts):
        table = slot_rows(ids_ref[...], e).astype(jnp.bfloat16)
        rows = jnp.dot(table, block_ref[...], preferred_element_type=jnp.float32)
        out_ref[e * CAP:(e + 1) * CAP, :] = rows.astype(jnp.bfloat16)


def picked_rows(experts, ids_t, block):
    return pl.pallas_call(
        functools.partial(pick_kernel, experts),
        out_shape=jax.ShapeDtypeStruct((experts * CAP, block.shape[1]), jnp.bfloat16),
        in_specs=[VMEM, VMEM],
        out_specs=VMEM,
        compiler_params=PARAMS,
        cost_estimate=pl.CostEstimate(
            flops=2 * experts * CAP * block.size, bytes_accessed=block.size, transcendentals=0
        ),
    )(ids_t, block)


def mlp_kernel(near_ref, far_ref, gain_ref, gate_ref, up_ref, down_ref, near_out, far_out):
    count = near_ref.shape[0]
    rows = jnp.concatenate([near_ref[...], far_ref[...]], axis=0).astype(jnp.float32)
    inverse = lax.rsqrt(jnp.mean(rows * rows, axis=-1, keepdims=True) + 1e-06)
    normed = (rows * inverse * gain_ref[...].astype(jnp.float32)).astype(jnp.bfloat16)
    across = (((1,), (1,)), ((), ()))
    gate = lax.dot_general(normed, gate_ref[...], across, preferred_element_type=jnp.float32)
    up = lax.dot_general(normed, up_ref[...], across, preferred_element_type=jnp.float32)
    hidden = (gate / (1.0 + jnp.exp(-gate)) * up).astype(jnp.bfloat16)
    partial = jnp.dot(hidden, down_ref[...], preferred_element_type=jnp.float32)
    partial = partial.astype(jnp.bfloat16)
    near_out[...] = partial[:count]
    far_out[...] = partial[count:]


def mlp(near, far, gain, gate_t, up_t, down):
    rows = 2 * near.shape[0]
    width, hidden = down.shape[1], down.shape[0]
    out = jax.ShapeDtypeStruct(near.shape, jnp.bfloat16)
    return pl.pallas_call(
        mlp_kernel,
        out_shape=(out, out),
        in_specs=[VMEM] * 6,
        out_specs=(VMEM, VMEM),
        compiler_params=PARAMS,
        cost_estimate=pl.CostEstimate(
            flops=6 * rows * width * hidden, bytes_accessed=6 * width * hidden, transcendentals=0
        ),
    )(near, far, gain, gate_t, up_t, down)


def parts_of(value):
    terms = []
    for _ in range(3):
        terms.append(value.astype(jnp.bfloat16))
        value = value - terms[-1].astype(jnp.float32)
    return terms


def base_kernel(experts, gain_ref, ids_ref, weights_ref, *refs):
    block_refs, out_ref, table_ref = refs[:-2], refs[-2], refs[-1]
    ids, weights = ids_ref[...], weights_ref[...]
    count = ids.shape[1]
    zero = jnp.sum(jnp.where(ids >= experts, weights, 0.0), axis=0, keepdims=True)
    same = lax.broadcasted_iota(jnp.int32, (count, count), 0) == lax.broadcasted_iota(
        jnp.int32, (count, count), 1
    )
    zero = jnp.sum(jnp.where(same, zero, 0.0), axis=1, keepdims=True)
    start = 0
    for ref in block_refs:
        end = start + ref.shape[0]
        rows = ref[...].astype(jnp.float32)
        inverse = lax.rsqrt(jnp.mean(rows * rows, axis=-1, keepdims=True) + 1e-06)
        normed = (rows * inverse * gain_ref[...].astype(jnp.float32)).astype(jnp.bfloat16)
        out_ref[start:end] = rows + zero[start:end] * normed.astype(jnp.float32)
        start = end
    tables = []
    for e in range(experts):
        weight = jnp.sum(jnp.where(ids == e, weights, 0.0), axis=0, keepdims=True)
        tables.append(slot_rows(ids, e) * weight)
    terms = parts_of(jnp.concatenate(tables, axis=0).T)
    table_ref[...] = jnp.concatenate(terms + terms[:2], axis=1)


def based(experts, blocks, gain, ids_t, weights_t):
    count, width = ids_t.shape[1], blocks[0].shape[1]
    return pl.pallas_call(
        functools.partial(base_kernel, experts),
        out_shape=(
            jax.ShapeDtypeStruct((count, width), jnp.float32),
            jax.ShapeDtypeStruct((count, 5 * experts * CAP), jnp.bfloat16),
        ),
        in_specs=[VMEM] * (3 + len(blocks)),
        out_specs=(VMEM, VMEM),
        compiler_params=PARAMS,
        cost_estimate=pl.CostEstimate(
            flops=8 * count * width, bytes_accessed=6 * count * width, transcendentals=0
        ),
    )(gain, ids_t, weights_t, *blocks)


def end_kernel(columns, base_ref, table_ref, *refs):
    back_refs, out_ref = refs[:-1], refs[-1]
    here = pl.ds(pl.multiple_of(pl.program_id(0) * columns, columns), columns)
    total = back_refs[0][:, here].astype(jnp.float32)
    for ref in back_refs[1:]:
        total = total + ref[:, here].astype(jnp.float32)
    high, low, _ = parts_of(total)
    rows = jnp.concatenate([high, high, high, low, low], axis=0)
    added = jnp.dot(table_ref[...], rows, preferred_element_type=jnp.float32)
    out_ref[...] = (base_ref[:, here] + added).astype(jnp.bfloat16)


def ended(base, table, backs):
    count, width = base.shape
    steps = 3
    columns = width // steps
    return pl.pallas_call(
        functools.partial(end_kernel, columns),
        out_shape=jax.ShapeDtypeStruct((count, width), jnp.bfloat16),
        grid=(steps,),
        in_specs=[VMEM] * (2 + len(backs)),
        out_specs=pl.BlockSpec((count, columns), lambda i: (0, i)),
        compiler_params=PARAMS,
        cost_estimate=pl.CostEstimate(
            flops=2 * count * width * table.shape[0], bytes_accessed=6 * count * width,
            transcendentals=0,
        ),
    )(base, table, *backs)


def early_kernel(left_ref, right_ref, out_ref):
    out_ref[...] = left_ref[...].astype(jnp.float32) + right_ref[...].astype(jnp.float32)


def summed_early(left, right):
    return pl.pallas_call(
        early_kernel,
        out_shape=jax.ShapeDtypeStruct(left.shape, jnp.float32),
        in_specs=[VMEM, VMEM],
        out_specs=VMEM,
        compiler_params=PARAMS,
        cost_estimate=pl.CostEstimate(
            flops=left.size, bytes_accessed=128 * left.size, transcendentals=0
        ),
    )(left, right)


def local(blocks, norm_gain, w_gate, w_up, w_down, route_ids, route_weights):
    slice_width = w_gate.shape[2]
    slice_count = HID // slice_width
    sections = lax.axis_size("section")
    devices = lax.axis_size("expert")
    experts = devices // slice_count
    same_slice = [[e * slice_count + k for e in range(experts)] for k in range(slice_count)]
    places = slice_count // 2
    token_count, width = blocks.shape[1:]

    def moved(value, sections_on, flip, side=0):
        pairs = []
        for s in range(sections):
            for d in range(devices):
                target = d ^ (2 * flip + side)
                pairs.append((s * devices + d, (s + sections_on) % sections * devices + target))
        return lax.ppermute(value, ("section", "expert"), pairs)

    next_ids = moved(route_ids, -1, 0)[0]
    block, = loaded(blocks[0])
    picked = picked_rows(experts, jnp.swapaxes(next_ids, 0, 1), block)
    if experts > 1:
        picked = lax.all_to_all(
            picked.reshape(experts, CAP, width), "expert", split_axis=0, concat_axis=0,
            tiled=True, axis_index_groups=same_slice,
        ).reshape(experts * CAP, width)
    gate_t, up_t, down, gain = loaded(
        after(jnp.swapaxes(w_gate[0], 0, 1), picked), jnp.swapaxes(w_up[0], 0, 1), w_down[0], norm_gain
    )

    near, far = {}, {}
    near[2] = moved(picked, 1, 2)
    near[0] = moved(picked, 1, 0)
    far[0] = moved(picked, 1, 0, 1)
    far[2] = moved(after(near[2], near[0], gain), 0, 0, 1)
    near[3] = moved(after(near[2], far[0]), 0, 1)
    near[1] = moved(after(near[0], near[2]), 0, 1)
    far[3] = moved(far[2], 0, 1)
    far[1] = moved(near[1], 0, 0, 1)
    pieces = 2
    size = token_count // pieces
    arrived = [
        moved(after(blocks[0, i * size:(i + 1) * size], near[0], far[0], near[2]), 1, 0)
        for i in range(pieces)
    ]
    base, table = based(
        experts, arrived, gain, jnp.swapaxes(route_ids[0], 0, 1),
        jnp.swapaxes(route_weights[0], 0, 1),
    )

    own, other = {}, {}
    for k in (2, 3, 1, 0):
        first = {2: (gain,), 3: (other.get(2),), 1: (own.get(3),), 0: (other.get(3), base)}[k]
        own[k], sent = mlp(after(near[k], *first), far[k], gain, gate_t, up_t, down)
        other[k] = moved(sent, 0, 0, 1)
    both = {
        k: (own[k].astype(jnp.float32) + other[k].astype(jnp.float32)).astype(jnp.bfloat16)
        for k in (2, 3, 1)
    }
    early = summed_early(own[0], moved(both[2], 0, 2))
    backs = [
        early, moved(both[3], 0, 3), moved(after(both[1], early), 0, 1), other[0],
    ]
    if experts > 1:
        summed = sum(back.astype(jnp.float32) for back in backs).reshape(experts, CAP, width)
        summed = lax.all_to_all(
            summed.astype(jnp.bfloat16), "expert", split_axis=0, concat_axis=0, tiled=True,
            axis_index_groups=same_slice,
        )
        backs = [summed.reshape(experts * CAP, width)]
    return ended(base, table, backs)[None]


def solution(mesh):
    placed = (
        P("section", ("dp", "expert"), None),
        P("section", None),
        P("section", None, "expert"),
        P("section", None, "expert"),
        P("section", "expert", None),
        P("section", ("dp", "expert"), None),
        P("section", ("dp", "expert"), None),
    )
    return jax.shard_map(
        local,
        mesh=mesh,
        in_specs=placed,
        out_specs=P("section", ("dp", "expert"), None),
        check_vma=False,
    )
```

time: 114 us -> 61.3 us (0.54)
  blocking collectives: 42.2 us -> 0 us
  waiting for transfers between devices: 47.6 us -> 23.7 us
  starting transfers between devices: 6.65 us -> 25.9 us
  Pallas kernels: 0 us -> 11.2 us
  matrix products: 10.9 us -> 0 us
  other arithmetic: 3 us -> 0.15 us
  local copies, waits for them, and re-layouts: 2.71 us -> 0.06 us
    all_to_all x1 -> x0, blocking collectives: 42.2 us -> none  [local(): lax.all_to_all(outgoing, 'expert', split_axis=0, concat_axis=0, tiled=True)]
    all_to_all x1 -> x0, waiting for transfers between devices: 32.7 us -> none  [local(): lax.all_to_all(partial_value.reshape(received.shape), 'expert', split_axi...]
    ppermute x1 -> x18, starting transfers between devices: 2.94 us -> 25.9 us  [moved(): return lax.ppermute(value, ('section', 'expert'), pairs)]
    pallas_call x0 -> x10, Pallas kernels: none -> 11.2 us  [the longest x4 5.03 us: mlp(): pl.pallas_call(mlp_kernel, out_shape=(out, out), in_specs=[VMEM] * 6, out...]
    dot_general x5 -> x0, matrix products: 10.9 us -> none  [the longest x1 4.42 us: local(): jnp.dot(hidden, w_down[0], preferred_element_type=jnp.float32)]
    ppermute x1 -> x18, waiting for transfers between devices: 14.9 us -> 23.7 us  [moved(): return lax.ppermute(value, ('section', 'expert'), pairs)]
    all_to_all x1 -> x0, starting transfers between devices: 3.71 us -> none  [local(): lax.all_to_all(partial_value.reshape(received.shape), 'expert', split_axi...]
  transfers between devices with their start and end apart: 2 -> 18, of which waited for: 2 -> 10; matrix products, arithmetic and copies ran while one was open for 6% -> 0% of each run, Pallas kernels for 0% -> 15%
where the time goes in v1:
time: 61.3 us; the launch traced here: 61.1 us
  starting transfers between devices  25.9 us (42%)
  waiting for transfers between devices  23.7 us (39%)
  Pallas kernels  11.2 us (18%)
    ppermute x18, starting transfers between devices, moved(): return lax.ppermute(value, ('section', 'expert'), pairs)  25.9 us
    ppermute x18, waiting for transfers between devices, moved(): return lax.ppermute(value, ('section', 'expert'), pairs)  23.7 us
    pallas_call x4, Pallas kernels, mlp(): pl.pallas_call(mlp_kernel, out_shape=(out, out), in_specs=[VMEM] * 6, out...  5.03 us
    pallas_call x2, Pallas kernels, loaded(): pl.pallas_call(functools.partial(load_kernel, len(arrays)), out_shape=tup...  3.16 us
    pallas_call x1, Pallas kernels, ended(): pl.pallas_call(functools.partial(end_kernel, columns), out_shape=jax.Shap...  1.88 us
  transfers between devices with their start and end apart: 18, of which 10 were waited for; matrix products, arithmetic and copies ran while one was open for 0% of the time, Pallas kernels for 15%

profile of v1, /device:TPU:0, one launch (start us, length us, event | category | flops | bytes accessed | tf_op | source)
XLA Modules:
  0.0 61.1 jit_solution(2547390540101292036)
XLA Ops:
  0.0 2.9 %collective-permute-start = (s32[1,128,2]{1,2,0:T(2,128)}, s32[1,128,2]{1,2,0:T(2,128)S(1)}, u32[]{:S(2)}, u32[]{:S(2)}) collective-permute-start(s32[1,128,2]{1,2,0:T(2,128)} %param.12), channel_id=1, source_target_pairs={{0,16},{2,18},{4,20},{6,22},{8,24},{10,26},{12,28},{14,30},{16,0},... | collective-permute-start | bytes 3080 | tf_op jit(solution)/shard_map/ppermute | solution.py:220
  2.9 1.1 %shard_map.73.block_ref = bf16[128,3072]{1,0:T(8,128)(2,1)S(1)} custom-call(bf16[128,3072]{1,0:T(8,128)(2,1)} %bitcast.25), custom_call_target="tpu_custom_call" | custom-call | bytes 6291456 | tf_op jit(solution)/shard_map/pallas_call | solution.py:33
  4.1 0.6 collective-permute-done
  4.7 0.4 shard_map.74
  5.1 2.1 %collective-permute-start.1 = (bf16[32,3072]{1,0:T(8,128)(2,1)S(1)}, bf16[32,3072]{1,0:T(8,128)(2,1)S(1)}, u32[]{:S(2)}, u32[]{:S(2)}) collective-permute-start(bf16[32,3072]{1,0:T(8,128)(2,1)S(1)} %shard_map.74), channel_id=1, source_target_pairs={{0,16},{2,18},{4,20},{6,22},{8,24},{10,26},{12,28},{14,30},{16,0},... | collective-permute-start | bytes 589832 | tf_op jit(solution)/shard_map/ppermute | solution.py:220
  7.1 2.6 %collective-permute-start.3 = (bf16[32,3072]{1,0:T(8,128)(2,1)S(1)}, bf16[32,3072]{1,0:T(8,128)(2,1)S(1)}, u32[]{:S(2)}, u32[]{:S(2)}) collective-permute-start(bf16[32,3072]{1,0:T(8,128)(2,1)S(1)} %shard_map.74), channel_id=1, source_target_pairs={{0,24},{2,26},{4,28},{6,30},{8,16},{10,18},{12,20},{14,22},{16,8},... | collective-permute-start | bytes 589832 | tf_op jit(solution)/shard_map/ppermute | solution.py:220
  9.7 2.4 %collective-permute-start.2 = (bf16[32,3072]{1,0:T(8,128)(2,1)S(1)}, bf16[32,3072]{1,0:T(8,128)(2,1)S(1)}, u32[]{:S(2)}, u32[]{:S(2)}) collective-permute-start(bf16[32,3072]{1,0:T(8,128)(2,1)S(1)} %shard_map.74), channel_id=1, source_target_pairs={{0,18},{2,16},{4,22},{6,20},{8,26},{10,24},{12,30},{14,28},{16,2},... | collective-permute-start | bytes 589832 | tf_op jit(solution)/shard_map/ppermute | solution.py:220
  12.2 2.0 %shard_map.75 = (bf16[192,3072]{1,0:T(8,128)(2,1)S(1)}, bf16[192,3072]{1,0:T(8,128)(2,1)S(1)}, bf16[192,3072]{1,0:T(8,128)(2,1)S(1)}, bf16[1,3072]{1,0:T(2,128)(2,1)S(1)}) custom-call(bf16[192,3072]{1,0:T(8,128)(2,1)} %bitcast.26, bf16[192,3072]{1,0:T(8,128)(2,1)} %bitcast.27, bf16[192,3072]{1,0:T(8,128)(2,1)} %bitcast.28, bf16[1,3072]{1,0:T(2,128)(2,1)} %refs_3_.1), custom_call_target="tpu_custom_call" | custom-call | bytes 6291456 | tf_op jit(solution)/shard_map/pallas_call | solution.py:33
  14.2 0.0 collective-permute-done.1.near_ref
  14.2 4.3 %collective-permute-done.3.near_ref = bf16[32,3072]{1,0:T(8,128)(2,1)S(1)} collective-permute-done((bf16[32,3072]{1,0:T(8,128)(2,1)S(1)}, bf16[32,3072]{1,0:T(8,128)(2,1)S(1)}, u32[]{:S(2)}, u32[]{:S(2)}) %collective-permute-start.3) | collective-permute-done | bytes 196640 | tf_op jit(solution)/shard_map/ppermute | solution.py:220
  18.5 1.5 %collective-permute-start.7 = (bf16[32,3072]{1,0:T(8,128)(2,1)S(1)}, bf16[32,3072]{1,0:T(8,128)(2,1)S(1)}, u32[]{:S(2)}, u32[]{:S(2)}) collective-permute-start(bf16[32,3072]{1,0:T(8,128)(2,1)S(1)} %collective-permute-done.3.near_ref), channel_id=1, source_target_pairs={{0,2},{2,0},{4,6},{6,4},{8,10},{10,8},{12,14},{14,12},{16,18},{18,... | collective-permute-start | bytes 589832 | tf_op jit(solution)/shard_map/ppermute | solution.py:220
  20.0 0.8 %collective-permute-done.2.far_ref = bf16[32,3072]{1,0:T(8,128)(2,1)S(1)} collective-permute-done((bf16[32,3072]{1,0:T(8,128)(2,1)S(1)}, bf16[32,3072]{1,0:T(8,128)(2,1)S(1)}, u32[]{:S(2)}, u32[]{:S(2)}) %collective-permute-start.2) | collective-permute-done | bytes 196640 | tf_op jit(solution)/shard_map/ppermute | solution.py:220
  20.8 1.6 %collective-permute-start.6 = (bf16[32,3072]{1,0:T(8,128)(2,1)S(1)}, bf16[32,3072]{1,0:T(8,128)(2,1)S(1)}, u32[]{:S(2)}, u32[]{:S(2)}) collective-permute-start(bf16[32,3072]{1,0:T(8,128)(2,1)S(1)} %collective-permute-done.3.near_ref), channel_id=1, source_target_pairs={{0,4},{2,6},{4,0},{6,2},{8,12},{10,14},{12,8},{14,10},{16,20},{18,... | collective-permute-start | bytes 589832 | tf_op jit(solution)/shard_map/ppermute | solution.py:220
  22.4 0.4 collective-permute-start.13
  22.8 2.1 %collective-permute-done.7.far_ref = bf16[32,3072]{1,0:T(8,128)(2,1)S(1)} collective-permute-done((bf16[32,3072]{1,0:T(8,128)(2,1)S(1)}, bf16[32,3072]{1,0:T(8,128)(2,1)S(1)}, u32[]{:S(2)}, u32[]{:S(2)}) %collective-permute-start.7) | collective-permute-done | bytes 196640 | tf_op jit(solution)/shard_map/ppermute | solution.py:220
  24.9 1.3 %shard_map.77 = (bf16[32,3072]{1,0:T(8,128)(2,1)S(1)}, bf16[32,3072]{1,0:T(8,128)(2,1)S(1)}) custom-call(bf16[32,3072]{1,0:T(8,128)(2,1)S(1)} %collective-permute-done.3.near_ref, bf16[32,3072]{1,0:T(8,128)(2,1)S(1)} %collective-permute-done.7.far_ref, bf16[1,3072]{1,0:T(2,128)(2,1)S(1)} %get-tuple-element.31.gain_ref, ...), custom_call_target="tpu_custom_call" | custom-call | flops 226492416 | bytes 3538944 | tf_op jit(solution)/shard_map/pallas_call | solution.py:95
  26.2 0.8 %collective-permute-start.8 = (bf16[32,3072]{1,0:T(8,128)(2,1)S(1)}, bf16[32,3072]{1,0:T(8,128)(2,1)S(1)}, u32[]{:S(2)}, u32[]{:S(2)}) collective-permute-start(bf16[32,3072]{1,0:T(8,128)(2,1)S(1)} %get-tuple-element.42), channel_id=1, source_target_pairs={{0,2},{2,0},{4,6},{6,4},{8,10},{10,8},{12,14},{14,12},{16,18},{18,... | collective-permute-start | bytes 589832 | tf_op jit(solution)/shard_map/ppermute | solution.py:220
  27.0 1.3 %collective-permute-start.9 = (bf16[32,3072]{1,0:T(8,128)(2,1)S(1)}, bf16[32,3072]{1,0:T(8,128)(2,1)S(1)}, u32[]{:S(2)}, u32[]{:S(2)}) collective-permute-start(bf16[32,3072]{1,0:T(8,128)(2,1)S(1)} %collective-permute-done.7.far_ref), channel_id=1, source_target_pairs={{0,4},{2,6},{4,0},{6,2},{8,12},{10,14},{12,8},{14,10},{16,20},{18,... | collective-permute-start | bytes 589832 | tf_op jit(solution)/shard_map/ppermute | solution.py:220
  28.3 0.0 copy-done.2
  28.3 0.1 slice_bitcast_fusion
  28.4 1.4 %collective-permute-start.4 = (bf16[64,3072]{1,0:T(8,128)(2,1)S(1)}, bf16[64,3072]{1,0:T(8,128)(2,1)S(1)}, u32[]{:S(2)}, u32[]{:S(2)}) collective-permute-start(bf16[64,3072]{1,0:T(8,128)(2,1)S(1)} %get-tuple-element.32), channel_id=1, source_target_pairs={{0,16},{2,18},{4,20},{6,22},{8,24},{10,26},{12,28},{14,30},{16,0},... | collective-permute-start | bytes 1179656 | tf_op jit(solution)/shard_map/ppermute | solution.py:220
  29.8 0.0 collective-permute-done.6.near_ref
  29.8 0.7 %collective-permute-start.5 = (bf16[64,3072]{1,0:T(8,128)(2,1)S(1)}, bf16[64,3072]{1,0:T(8,128)(2,1)S(1)}, u32[]{:S(2)}, u32[]{:S(2)}) collective-permute-start(bf16[64,3072]{1,0:T(8,128)(2,1)S(1)} %get-tuple-element.33), channel_id=1, source_target_pairs={{0,16},{2,18},{4,20},{6,22},{8,24},{10,26},{12,28},{14,30},{16,0},... | collective-permute-start | bytes 1179656 | tf_op jit(solution)/shard_map/ppermute | solution.py:220
  30.5 1.8 %collective-permute-done.13.near_ref = bf16[32,3072]{1,0:T(8,128)(2,1)S(1)} collective-permute-done((bf16[32,3072]{1,0:T(8,128)(2,1)S(1)}, bf16[32,3072]{1,0:T(8,128)(2,1)S(1)}, u32[]{:S(2)}, u32[]{:S(2)}) %collective-permute-start.13) | collective-permute-done | bytes 196640 | tf_op jit(solution)/shard_map/ppermute | solution.py:220
  32.3 0.0 collective-permute-start.14
  32.3 0.0 collective-permute-done.8
  32.3 2.5 %collective-permute-done.9.far_ref = bf16[32,3072]{1,0:T(8,128)(2,1)S(1)} collective-permute-done((bf16[32,3072]{1,0:T(8,128)(2,1)S(1)}, bf16[32,3072]{1,0:T(8,128)(2,1)S(1)}, u32[]{:S(2)}, u32[]{:S(2)}) %collective-permute-start.9) | collective-permute-done | bytes 196640 | tf_op jit(solution)/shard_map/ppermute | solution.py:220
  34.8 1.3 %shard_map.78 = (bf16[32,3072]{1,0:T(8,128)(2,1)S(1)}, bf16[32,3072]{1,0:T(8,128)(2,1)S(1)}) custom-call(bf16[32,3072]{1,0:T(8,128)(2,1)S(1)} %collective-permute-done.6.near_ref, bf16[32,3072]{1,0:T(8,128)(2,1)S(1)} %collective-permute-done.9.far_ref, bf16[1,3072]{1,0:T(2,128)(2,1)S(1)} %get-tuple-element.31.gain_ref, ...), custom_call_target="tpu_custom_call" | custom-call | flops 226492416 | bytes 3538944 | tf_op jit(solution)/shard_map/pallas_call | solution.py:95
  36.1 0.5 collective-permute-start.10
  36.6 2.1 %collective-permute-start.11 = (bf16[32,3072]{1,0:T(8,128)(2,1)S(1)}, bf16[32,3072]{1,0:T(8,128)(2,1)S(1)}, u32[]{:S(2)}, u32[]{:S(2)}) collective-permute-start(bf16[32,3072]{1,0:T(8,128)(2,1)S(1)} %add_convert_fusion.2), channel_id=1, source_target_pairs={{0,8},{2,10},{4,12},{6,14},{8,0},{10,2},{12,4},{14,6},{16,24},{18,... | collective-permute-start | bytes 589832 | tf_op jit(solution)/shard_map/ppermute | solution.py:220
  38.7 0.1 collective-permute-done.14.far_ref
  38.8 1.3 %shard_map.81 = (bf16[32,3072]{1,0:T(8,128)(2,1)S(1)}, bf16[32,3072]{1,0:T(8,128)(2,1)S(1)}) custom-call(bf16[32,3072]{1,0:T(8,128)(2,1)S(1)} %collective-permute-done.13.near_ref, bf16[32,3072]{1,0:T(8,128)(2,1)S(1)} %collective-permute-done.14.far_ref, bf16[1,3072]{1,0:T(2,128)(2,1)S(1)} %get-tuple-element.31.gain_ref, ...), custom_call_target="tpu_custom_call" | custom-call | flops 226492416 | bytes 3538944 | tf_op jit(solution)/shard_map/pallas_call | solution.py:95
  40.1 1.5 %collective-permute-start.15 = (bf16[32,3072]{1,0:T(8,128)(2,1)S(1)}, bf16[32,3072]{1,0:T(8,128)(2,1)S(1)}, u32[]{:S(2)}, u32[]{:S(2)}) collective-permute-start(bf16[32,3072]{1,0:T(8,128)(2,1)S(1)} %get-tuple-element.52), channel_id=1, source_target_pairs={{0,2},{2,0},{4,6},{6,4},{8,10},{10,8},{12,14},{14,12},{16,18},{18,... | collective-permute-start | bytes 589832 | tf_op jit(solution)/shard_map/ppermute | solution.py:220
  41.6 0.0 collective-permute-done.4.refs_0_
  41.6 5.7 %collective-permute-done.5.refs_1_ = bf16[64,3072]{1,0:T(8,128)(2,1)S(1)} collective-permute-done((bf16[64,3072]{1,0:T(8,128)(2,1)S(1)}, bf16[64,3072]{1,0:T(8,128)(2,1)S(1)}, u32[]{:S(2)}, u32[]{:S(2)}) %collective-permute-start.5) | collective-permute-done | bytes 393248 | tf_op jit(solution)/shard_map/ppermute | solution.py:220
  47.2 0.7 %shard_map.76 = (f32[128,3072]{1,0:T(8,128)S(1)}, bf16[128,160]{1,0:T(8,128)(2,1)S(1)}) custom-call(bf16[1,3072]{1,0:T(2,128)(2,1)S(1)} %get-tuple-element.31.gain_ref, s32[2,128]{1,0:T(2,128)S(1)} %bitcast.22, f32[2,128]{1,0:T(2,128)S(1)} %bitcast.23, bf16[64,3072]{1,0:T(8,128)(2,1)S(1)} %collective-permute-done.4.refs_0_, ...), custom_call_target="tpu_custom_call" | custom-call | flops 3145728 | bytes 2359296 | tf_op jit(solution)/shard_map/pallas_call | solution.py:142
  47.9 0.0 collective-permute-done.10
  48.0 1.8 %collective-permute-start.12 = (bf16[32,3072]{1,0:T(8,128)(2,1)S(1)}, bf16[32,3072]{1,0:T(8,128)(2,1)S(1)}, u32[]{:S(2)}, u32[]{:S(2)}) collective-permute-start(bf16[32,3072]{1,0:T(8,128)(2,1)S(1)} %add_convert_fusion.1), channel_id=1, source_target_pairs={{0,12},{2,14},{4,8},{6,10},{8,4},{10,6},{12,0},{14,2},{16,28},{18,... | collective-permute-start | bytes 589832 | tf_op jit(solution)/shard_map/ppermute | solution.py:220
  49.8 1.3 %shard_map.79 = (bf16[32,3072]{1,0:T(8,128)(2,1)S(1)}, bf16[32,3072]{1,0:T(8,128)(2,1)S(1)}) custom-call(bf16[32,3072]{1,0:T(8,128)(2,1)S(1)} %collective-permute-done.1.near_ref, bf16[32,3072]{1,0:T(8,128)(2,1)S(1)} %collective-permute-done.2.far_ref, bf16[1,3072]{1,0:T(2,128)(2,1)S(1)} %get-tuple-element.31.gain_ref, ...), custom_call_target="tpu_custom_call" | custom-call | flops 226492416 | bytes 3538944 | tf_op jit(solution)/shard_map/pallas_call | solution.py:95
  51.0 0.0 collective-permute-done.11.right_ref
  51.1 0.1 shard_map.80.refs_0_
  51.1 0.0 collective-permute-done.15
  51.2 0.9 %collective-permute-start.16 = (bf16[32,3072]{1,0:T(8,128)(2,1)S(1)}, bf16[32,3072]{1,0:T(8,128)(2,1)S(1)}, u32[]{:S(2)}, u32[]{:S(2)}) collective-permute-start(bf16[32,3072]{1,0:T(8,128)(2,1)S(1)} %add_convert_fusion), channel_id=1, source_target_pairs={{0,4},{2,6},{4,0},{6,2},{8,12},{10,14},{12,8},{14,10},{16,20},{18,... | collective-permute-start | bytes 589832 | tf_op jit(solution)/shard_map/ppermute | solution.py:220
  52.1 1.2 %collective-permute-start.17 = (bf16[32,3072]{1,0:T(8,128)(2,1)S(1)}, bf16[32,3072]{1,0:T(8,128)(2,1)S(1)}, u32[]{:S(2)}, u32[]{:S(2)}) collective-permute-start(bf16[32,3072]{1,0:T(8,128)(2,1)S(1)} %get-tuple-element.54), channel_id=1, source_target_pairs={{0,2},{2,0},{4,6},{6,4},{8,10},{10,8},{12,14},{14,12},{16,18},{18,... | collective-permute-start | bytes 589832 | tf_op jit(solution)/shard_map/ppermute | solution.py:220
  53.3 3.9 %collective-permute-done.12.refs_1_ = bf16[32,3072]{1,0:T(8,128)(2,1)S(1)} collective-permute-done((bf16[32,3072]{1,0:T(8,128)(2,1)S(1)}, bf16[32,3072]{1,0:T(8,128)(2,1)S(1)}, u32[]{:S(2)}, u32[]{:S(2)}) %collective-permute-start.12) | collective-permute-done | bytes 196640 | tf_op jit(solution)/shard_map/ppermute | solution.py:220
  57.2 2.0 %collective-permute-done.16.refs_2_ = bf16[32,3072]{1,0:T(8,128)(2,1)S(1)} collective-permute-done((bf16[32,3072]{1,0:T(8,128)(2,1)S(1)}, bf16[32,3072]{1,0:T(8,128)(2,1)S(1)}, u32[]{:S(2)}, u32[]{:S(2)}) %collective-permute-start.16) | collective-permute-done | bytes 196640 | tf_op jit(solution)/shard_map/ppermute | solution.py:220
  59.2 0.0 collective-permute-done.17.refs_3_
  59.2 1.9 %shard_map.82 = bf16[128,3072]{1,0:T(8,128)(2,1)} custom-call(f32[128,3072]{1,0:T(8,128)S(1)} %get-tuple-element.34.base_ref, bf16[128,160]{1,0:T(8,128)(2,1)S(1)} %get-tuple-element.35.table_ref, f32[32,3072]{1,0:T(8,128)S(1)} %shard_map.80.refs_0_, bf16[32,3072]{1,0:T(8,128)(2,1)S(1)} %collective-permute-done.12.refs_1_, ...), custom_call_target="tpu_custom_call" | custom-call | flops 100663296 | bytes 2359296 | tf_op jit(solution)/shard_map/pallas_call | solution.py:173
  (8 shorter events, 0.2 us)
Async XLA Ops:
  0.0 4.7 %collective-permute-start = (s32[1,128,2]{1,2,0:T(2,128)}, s32[1,128,2]{1,2,0:T(2,128)S(1)}, u32[]{:S(2)}, u32[]{:S(2)}) collective-permute-start(s32[1,128,2]{1,2,0:T(2,128)} %param.12), channel_id=1, source_target_pairs={{0,16},{2,18},{4,20},{6,22},{8,24},{10,26},{12,28},{14,30},{16,0},... | collective-permute-start | bytes 3080 | tf_op jit(solution)/shard_map/ppermute | solution.py:220
  5.1 9.1 %collective-permute-start.1 = (bf16[32,3072]{1,0:T(8,128)(2,1)S(1)}, bf16[32,3072]{1,0:T(8,128)(2,1)S(1)}, u32[]{:S(2)}, u32[]{:S(2)}) collective-permute-start(bf16[32,3072]{1,0:T(8,128)(2,1)S(1)} %shard_map.74), channel_id=1, source_target_pairs={{0,16},{2,18},{4,20},{6,22},{8,24},{10,26},{12,28},{14,30},{16,0},... | collective-permute-start | bytes 589832 | tf_op jit(solution)/shard_map/ppermute | solution.py:220
  7.1 11.3 %collective-permute-start.3 = (bf16[32,3072]{1,0:T(8,128)(2,1)S(1)}, bf16[32,3072]{1,0:T(8,128)(2,1)S(1)}, u32[]{:S(2)}, u32[]{:S(2)}) collective-permute-start(bf16[32,3072]{1,0:T(8,128)(2,1)S(1)} %shard_map.74), channel_id=1, source_target_pairs={{0,24},{2,26},{4,28},{6,30},{8,16},{10,18},{12,20},{14,22},{16,8},... | collective-permute-start | bytes 589832 | tf_op jit(solution)/shard_map/ppermute | solution.py:220
  9.7 11.1 %collective-permute-start.2 = (bf16[32,3072]{1,0:T(8,128)(2,1)S(1)}, bf16[32,3072]{1,0:T(8,128)(2,1)S(1)}, u32[]{:S(2)}, u32[]{:S(2)}) collective-permute-start(bf16[32,3072]{1,0:T(8,128)(2,1)S(1)} %shard_map.74), channel_id=1, source_target_pairs={{0,18},{2,16},{4,22},{6,20},{8,26},{10,24},{12,30},{14,28},{16,2},... | collective-permute-start | bytes 589832 | tf_op jit(solution)/shard_map/ppermute | solution.py:220
  18.5 6.5 %collective-permute-start.7 = (bf16[32,3072]{1,0:T(8,128)(2,1)S(1)}, bf16[32,3072]{1,0:T(8,128)(2,1)S(1)}, u32[]{:S(2)}, u32[]{:S(2)}) collective-permute-start(bf16[32,3072]{1,0:T(8,128)(2,1)S(1)} %collective-permute-done.3.near_ref), channel_id=1, source_target_pairs={{0,2},{2,0},{4,6},{6,4},{8,10},{10,8},{12,14},{14,12},{16,18},{18,... | collective-permute-start | bytes 589832 | tf_op jit(solution)/shard_map/ppermute | solution.py:220
  20.8 9.0 %collective-permute-start.6 = (bf16[32,3072]{1,0:T(8,128)(2,1)S(1)}, bf16[32,3072]{1,0:T(8,128)(2,1)S(1)}, u32[]{:S(2)}, u32[]{:S(2)}) collective-permute-start(bf16[32,3072]{1,0:T(8,128)(2,1)S(1)} %collective-permute-done.3.near_ref), channel_id=1, source_target_pairs={{0,4},{2,6},{4,0},{6,2},{8,12},{10,14},{12,8},{14,10},{16,20},{18,... | collective-permute-start | bytes 589832 | tf_op jit(solution)/shard_map/ppermute | solution.py:220
  22.4 9.9 %collective-permute-start.13 = (bf16[32,3072]{1,0:T(8,128)(2,1)S(1)}, bf16[32,3072]{1,0:T(8,128)(2,1)S(1)}, u32[]{:S(2)}, u32[]{:S(2)}) collective-permute-start(bf16[32,3072]{1,0:T(8,128)(2,1)S(1)} %collective-permute-done.1.near_ref), channel_id=1, source_target_pairs={{0,4},{2,6},{4,0},{6,2},{8,12},{10,14},{12,8},{14,10},{16,20},{18,... | collective-permute-start | bytes 589832 | tf_op jit(solution)/shard_map/ppermute | solution.py:220
  24.9 3.4 %copy-start.2 = (bf16[1,128,3072]{2,1,0:T(8,128)(2,1)S(1)}, bf16[1,128,3072]{2,1,0:T(8,128)(2,1)}, u32[]{:S(2)}) copy-start(bf16[1,128,3072]{2,1,0:T(8,128)(2,1)} %param.7) | copy-start | bytes 2359300
  26.2 6.1 %collective-permute-start.8 = (bf16[32,3072]{1,0:T(8,128)(2,1)S(1)}, bf16[32,3072]{1,0:T(8,128)(2,1)S(1)}, u32[]{:S(2)}, u32[]{:S(2)}) collective-permute-start(bf16[32,3072]{1,0:T(8,128)(2,1)S(1)} %get-tuple-element.42), channel_id=1, source_target_pairs={{0,2},{2,0},{4,6},{6,4},{8,10},{10,8},{12,14},{14,12},{16,18},{18,... | collective-permute-start | bytes 589832 | tf_op jit(solution)/shard_map/ppermute | solution.py:220
  27.0 7.8 %collective-permute-start.9 = (bf16[32,3072]{1,0:T(8,128)(2,1)S(1)}, bf16[32,3072]{1,0:T(8,128)(2,1)S(1)}, u32[]{:S(2)}, u32[]{:S(2)}) collective-permute-start(bf16[32,3072]{1,0:T(8,128)(2,1)S(1)} %collective-permute-done.7.far_ref), channel_id=1, source_target_pairs={{0,4},{2,6},{4,0},{6,2},{8,12},{10,14},{12,8},{14,10},{16,20},{18,... | collective-permute-start | bytes 589832 | tf_op jit(solution)/shard_map/ppermute | solution.py:220
  28.4 13.2 %collective-permute-start.4 = (bf16[64,3072]{1,0:T(8,128)(2,1)S(1)}, bf16[64,3072]{1,0:T(8,128)(2,1)S(1)}, u32[]{:S(2)}, u32[]{:S(2)}) collective-permute-start(bf16[64,3072]{1,0:T(8,128)(2,1)S(1)} %get-tuple-element.32), channel_id=1, source_target_pairs={{0,16},{2,18},{4,20},{6,22},{8,24},{10,26},{12,28},{14,30},{16,0},... | collective-permute-start | bytes 1179656 | tf_op jit(solution)/shard_map/ppermute | solution.py:220
  29.8 17.4 %collective-permute-start.5 = (bf16[64,3072]{1,0:T(8,128)(2,1)S(1)}, bf16[64,3072]{1,0:T(8,128)(2,1)S(1)}, u32[]{:S(2)}, u32[]{:S(2)}) collective-permute-start(bf16[64,3072]{1,0:T(8,128)(2,1)S(1)} %get-tuple-element.33), channel_id=1, source_target_pairs={{0,16},{2,18},{4,20},{6,22},{8,24},{10,26},{12,28},{14,30},{16,0},... | collective-permute-start | bytes 1179656 | tf_op jit(solution)/shard_map/ppermute | solution.py:220
  32.3 6.5 %collective-permute-start.14 = (bf16[32,3072]{1,0:T(8,128)(2,1)S(1)}, bf16[32,3072]{1,0:T(8,128)(2,1)S(1)}, u32[]{:S(2)}, u32[]{:S(2)}) collective-permute-start(bf16[32,3072]{1,0:T(8,128)(2,1)S(1)} %collective-permute-done.13.near_ref), channel_id=1, source_target_pairs={{0,2},{2,0},{4,6},{6,4},{8,10},{10,8},{12,14},{14,12},{16,18},{18,... | collective-permute-start | bytes 589832 | tf_op jit(solution)/shard_map/ppermute | solution.py:220
  36.1 11.9 %collective-permute-start.10 = (bf16[32,3072]{1,0:T(8,128)(2,1)S(1)}, bf16[32,3072]{1,0:T(8,128)(2,1)S(1)}, u32[]{:S(2)}, u32[]{:S(2)}) collective-permute-start(bf16[32,3072]{1,0:T(8,128)(2,1)S(1)} %get-tuple-element.44), channel_id=1, source_target_pairs={{0,2},{2,0},{4,6},{6,4},{8,10},{10,8},{12,14},{14,12},{16,18},{18,... | collective-permute-start | bytes 589832 | tf_op jit(solution)/shard_map/ppermute | solution.py:220
  36.6 14.4 %collective-permute-start.11 = (bf16[32,3072]{1,0:T(8,128)(2,1)S(1)}, bf16[32,3072]{1,0:T(8,128)(2,1)S(1)}, u32[]{:S(2)}, u32[]{:S(2)}) collective-permute-start(bf16[32,3072]{1,0:T(8,128)(2,1)S(1)} %add_convert_fusion.2), channel_id=1, source_target_pairs={{0,8},{2,10},{4,12},{6,14},{8,0},{10,2},{12,4},{14,6},{16,24},{18,... | collective-permute-start | bytes 589832 | tf_op jit(solution)/shard_map/ppermute | solution.py:220
  38.7 8.5 %copy-start = (s32[1,128,2]{1,2,0:T(2,128)S(1)}, s32[1,128,2]{1,2,0:T(2,128)}, u32[]{:S(2)}) copy-start(s32[1,128,2]{1,2,0:T(2,128)} %param.12) | copy-start | bytes 3076
  38.7 8.5 %copy-start.1 = (f32[1,128,2]{1,2,0:T(2,128)S(1)}, f32[1,128,2]{1,2,0:T(2,128)}, u32[]{:S(2)}) copy-start(f32[1,128,2]{1,2,0:T(2,128)} %param.13) | copy-start | bytes 3076
  40.1 11.0 %collective-permute-start.15 = (bf16[32,3072]{1,0:T(8,128)(2,1)S(1)}, bf16[32,3072]{1,0:T(8,128)(2,1)S(1)}, u32[]{:S(2)}, u32[]{:S(2)}) collective-permute-start(bf16[32,3072]{1,0:T(8,128)(2,1)S(1)} %get-tuple-element.52), channel_id=1, source_target_pairs={{0,2},{2,0},{4,6},{6,4},{8,10},{10,8},{12,14},{14,12},{16,18},{18,... | collective-permute-start | bytes 589832 | tf_op jit(solution)/shard_map/ppermute | solution.py:220
  48.0 9.2 %collective-permute-start.12 = (bf16[32,3072]{1,0:T(8,128)(2,1)S(1)}, bf16[32,3072]{1,0:T(8,128)(2,1)S(1)}, u32[]{:S(2)}, u32[]{:S(2)}) collective-permute-start(bf16[32,3072]{1,0:T(8,128)(2,1)S(1)} %add_convert_fusion.1), channel_id=1, source_target_pairs={{0,12},{2,14},{4,8},{6,10},{8,4},{10,6},{12,0},{14,2},{16,28},{18,... | collective-permute-start | bytes 589832 | tf_op jit(solution)/shard_map/ppermute | solution.py:220
  51.2 8.1 %collective-permute-start.16 = (bf16[32,3072]{1,0:T(8,128)(2,1)S(1)}, bf16[32,3072]{1,0:T(8,128)(2,1)S(1)}, u32[]{:S(2)}, u32[]{:S(2)}) collective-permute-start(bf16[32,3072]{1,0:T(8,128)(2,1)S(1)} %add_convert_fusion), channel_id=1, source_target_pairs={{0,4},{2,6},{4,0},{6,2},{8,12},{10,14},{12,8},{14,10},{16,20},{18,... | collective-permute-start | bytes 589832 | tf_op jit(solution)/shard_map/ppermute | solution.py:220
  52.1 7.1 %collective-permute-start.17 = (bf16[32,3072]{1,0:T(8,128)(2,1)S(1)}, bf16[32,3072]{1,0:T(8,128)(2,1)S(1)}, u32[]{:S(2)}, u32[]{:S(2)}) collective-permute-start(bf16[32,3072]{1,0:T(8,128)(2,1)S(1)} %get-tuple-element.54), channel_id=1, source_target_pairs={{0,2},{2,0},{4,6},{6,4},{8,10},{10,8},{12,14},{14,12},{16,18},{18,... | collective-permute-start | bytes 589832 | tf_op jit(solution)/shard_map/ppermute | solution.py:220

commit v2 on v1

--- a/solution.py
+++ b/solution.py
@@ -236,8 +236,8 @@
     near[0] = moved(picked, 1, 0)
     far[0] = moved(picked, 1, 0, 1)
     far[2] = moved(after(near[2], near[0], gain), 0, 0, 1)
+    near[1] = moved(near[0], 0, 1)
     near[3] = moved(after(near[2], far[0]), 0, 1)
-    near[1] = moved(after(near[0], near[2]), 0, 1)
     far[3] = moved(far[2], 0, 1)
     far[1] = moved(near[1], 0, 0, 1)
     pieces = 2
@@ -253,7 +253,7 @@
 
     own, other = {}, {}
     for k in (2, 3, 1, 0):
-        first = {2: (gain,), 3: (other.get(2),), 1: (own.get(3),), 0: (other.get(3), base)}[k]
+        first = {2: (gain,), 3: (other.get(2), arrived[0]), 1: (own.get(3),), 0: (other.get(3), base)}[k]
         own[k], sent = mlp(after(near[k], *first), far[k], gain, gate_t, up_t, down)
         other[k] = moved(sent, 0, 0, 1)
     both = {

time: 61.3 us -> 60.7 us (level)
  transfers between devices with their start and end apart: 18 -> 18, of which waited for: 10 -> 13; matrix products, arithmetic and copies ran while one was open for 0% -> 0% of each run, Pallas kernels for 15% -> 15%
where the time goes in v2:
time: 60.7 us; the launch traced here: 60.6 us
  starting transfers between devices  25.7 us (42%)
  waiting for transfers between devices  23.3 us (38%)
  Pallas kernels  11.2 us (18%)
    ppermute x18, starting transfers between devices, moved(): return lax.ppermute(value, ('section', 'expert'), pairs)  25.7 us
    ppermute x18, waiting for transfers between devices, moved(): return lax.ppermute(value, ('section', 'expert'), pairs)  23.3 us
    pallas_call x4, Pallas kernels, mlp(): pl.pallas_call(mlp_kernel, out_shape=(out, out), in_specs=[VMEM] * 6, out...  5.03 us
    pallas_call x2, Pallas kernels, loaded(): pl.pallas_call(functools.partial(load_kernel, len(arrays)), out_shape=tup...  3.23 us
    pallas_call x1, Pallas kernels, ended(): pl.pallas_call(functools.partial(end_kernel, columns), out_shape=jax.Shap...  1.88 us
  transfers between devices with their start and end apart: 18, of which 13 were waited for; matrix products, arithmetic and copies ran while one was open for 0% of the time, Pallas kernels for 15%

profile of v2, /device:TPU:0, one launch (start us, length us, event | category | flops | bytes accessed | tf_op | source)
XLA Modules:
  0.0 60.6 jit_solution(9250365631408946080)
XLA Ops:
  0.0 2.9 %collective-permute-start = (s32[1,128,2]{1,2,0:T(2,128)}, s32[1,128,2]{1,2,0:T(2,128)S(1)}, u32[]{:S(2)}, u32[]{:S(2)}) collective-permute-start(s32[1,128,2]{1,2,0:T(2,128)} %param.12), channel_id=1, source_target_pairs={{0,16},{2,18},{4,20},{6,22},{8,24},{10,26},{12,28},{14,30},{16,0},... | collective-permute-start | bytes 3080 | tf_op jit(solution)/shard_map/ppermute | solution.py:220
  2.9 1.1 %shard_map.73.block_ref = bf16[128,3072]{1,0:T(8,128)(2,1)S(1)} custom-call(bf16[128,3072]{1,0:T(8,128)(2,1)} %bitcast.25), custom_call_target="tpu_custom_call" | custom-call | bytes 6291456 | tf_op jit(solution)/shard_map/pallas_call | solution.py:33
  4.1 0.6 %collective-permute-done = s32[1,128,2]{1,2,0:T(2,128)S(1)} collective-permute-done((s32[1,128,2]{1,2,0:T(2,128)}, s32[1,128,2]{1,2,0:T(2,128)S(1)}, u32[]{:S(2)}, u32[]{:S(2)}) %collective-permute-start) | collective-permute-done | bytes 1056 | tf_op jit(solution)/shard_map/ppermute | solution.py:220
  4.7 0.4 shard_map.74
  5.1 2.1 %collective-permute-start.1 = (bf16[32,3072]{1,0:T(8,128)(2,1)S(1)}, bf16[32,3072]{1,0:T(8,128)(2,1)S(1)}, u32[]{:S(2)}, u32[]{:S(2)}) collective-permute-start(bf16[32,3072]{1,0:T(8,128)(2,1)S(1)} %shard_map.74), channel_id=1, source_target_pairs={{0,16},{2,18},{4,20},{6,22},{8,24},{10,26},{12,28},{14,30},{16,0},... | collective-permute-start | bytes 589832 | tf_op jit(solution)/shard_map/ppermute | solution.py:220
  7.1 2.6 %collective-permute-start.3 = (bf16[32,3072]{1,0:T(8,128)(2,1)S(1)}, bf16[32,3072]{1,0:T(8,128)(2,1)S(1)}, u32[]{:S(2)}, u32[]{:S(2)}) collective-permute-start(bf16[32,3072]{1,0:T(8,128)(2,1)S(1)} %shard_map.74), channel_id=1, source_target_pairs={{0,24},{2,26},{4,28},{6,30},{8,16},{10,18},{12,20},{14,22},{16,8},... | collective-permute-start | bytes 589832 | tf_op jit(solution)/shard_map/ppermute | solution.py:220
  9.7 2.4 %collective-permute-start.2 = (bf16[32,3072]{1,0:T(8,128)(2,1)S(1)}, bf16[32,3072]{1,0:T(8,128)(2,1)S(1)}, u32[]{:S(2)}, u32[]{:S(2)}) collective-permute-start(bf16[32,3072]{1,0:T(8,128)(2,1)S(1)} %shard_map.74), channel_id=1, source_target_pairs={{0,18},{2,16},{4,22},{6,20},{8,26},{10,24},{12,30},{14,28},{16,2},... | collective-permute-start | bytes 589832 | tf_op jit(solution)/shard_map/ppermute | solution.py:220
  12.2 2.1 %shard_map.75 = (bf16[192,3072]{1,0:T(8,128)(2,1)S(1)}, bf16[192,3072]{1,0:T(8,128)(2,1)S(1)}, bf16[192,3072]{1,0:T(8,128)(2,1)S(1)}, bf16[1,3072]{1,0:T(2,128)(2,1)S(1)}) custom-call(bf16[192,3072]{1,0:T(8,128)(2,1)} %bitcast.26, bf16[192,3072]{1,0:T(8,128)(2,1)} %bitcast.27, bf16[192,3072]{1,0:T(8,128)(2,1)} %bitcast.28, bf16[1,3072]{1,0:T(2,128)(2,1)} %refs_3_.1), custom_call_target="tpu_custom_call" | custom-call | bytes 6291456 | tf_op jit(solution)/shard_map/pallas_call | solution.py:33
  14.3 0.0 collective-permute-done.1.near_ref
  14.3 4.2 %collective-permute-done.3.near_ref = bf16[32,3072]{1,0:T(8,128)(2,1)S(1)} collective-permute-done((bf16[32,3072]{1,0:T(8,128)(2,1)S(1)}, bf16[32,3072]{1,0:T(8,128)(2,1)S(1)}, u32[]{:S(2)}, u32[]{:S(2)}) %collective-permute-start.3) | collective-permute-done | bytes 196640 | tf_op jit(solution)/shard_map/ppermute | solution.py:220
  18.5 1.5 %collective-permute-start.7 = (bf16[32,3072]{1,0:T(8,128)(2,1)S(1)}, bf16[32,3072]{1,0:T(8,128)(2,1)S(1)}, u32[]{:S(2)}, u32[]{:S(2)}) collective-permute-start(bf16[32,3072]{1,0:T(8,128)(2,1)S(1)} %collective-permute-done.3.near_ref), channel_id=1, source_target_pairs={{0,2},{2,0},{4,6},{6,4},{8,10},{10,8},{12,14},{14,12},{16,18},{18,... | collective-permute-start | bytes 589832 | tf_op jit(solution)/shard_map/ppermute | solution.py:220
  20.0 0.0 copy-done.2
  20.0 0.1 slice_bitcast_fusion
  20.0 0.7 %collective-permute-done.2.far_ref = bf16[32,3072]{1,0:T(8,128)(2,1)S(1)} collective-permute-done((bf16[32,3072]{1,0:T(8,128)(2,1)S(1)}, bf16[32,3072]{1,0:T(8,128)(2,1)S(1)}, u32[]{:S(2)}, u32[]{:S(2)}) %collective-permute-start.2) | collective-permute-done | bytes 196640 | tf_op jit(solution)/shard_map/ppermute | solution.py:220
  20.8 1.3 %collective-permute-start.4 = (bf16[64,3072]{1,0:T(8,128)(2,1)S(1)}, bf16[64,3072]{1,0:T(8,128)(2,1)S(1)}, u32[]{:S(2)}, u32[]{:S(2)}) collective-permute-start(bf16[64,3072]{1,0:T(8,128)(2,1)S(1)} %get-tuple-element.31), channel_id=1, source_target_pairs={{0,16},{2,18},{4,20},{6,22},{8,24},{10,26},{12,28},{14,30},{16,0},... | collective-permute-start | bytes 1179656 | tf_op jit(solution)/shard_map/ppermute | solution.py:220
  22.1 1.6 %collective-permute-start.6 = (bf16[32,3072]{1,0:T(8,128)(2,1)S(1)}, bf16[32,3072]{1,0:T(8,128)(2,1)S(1)}, u32[]{:S(2)}, u32[]{:S(2)}) collective-permute-start(bf16[32,3072]{1,0:T(8,128)(2,1)S(1)} %collective-permute-done.3.near_ref), channel_id=1, source_target_pairs={{0,4},{2,6},{4,0},{6,2},{8,12},{10,14},{12,8},{14,10},{16,20},{18,... | collective-permute-start | bytes 589832 | tf_op jit(solution)/shard_map/ppermute | solution.py:220
  23.7 0.4 collective-permute-start.13
  24.2 0.8 %collective-permute-done.7.far_ref = bf16[32,3072]{1,0:T(8,128)(2,1)S(1)} collective-permute-done((bf16[32,3072]{1,0:T(8,128)(2,1)S(1)}, bf16[32,3072]{1,0:T(8,128)(2,1)S(1)}, u32[]{:S(2)}, u32[]{:S(2)}) %collective-permute-start.7) | collective-permute-done | bytes 196640 | tf_op jit(solution)/shard_map/ppermute | solution.py:220
  24.9 1.3 %shard_map.77 = (bf16[32,3072]{1,0:T(8,128)(2,1)S(1)}, bf16[32,3072]{1,0:T(8,128)(2,1)S(1)}) custom-call(bf16[32,3072]{1,0:T(8,128)(2,1)S(1)} %collective-permute-done.3.near_ref, bf16[32,3072]{1,0:T(8,128)(2,1)S(1)} %collective-permute-done.7.far_ref, bf16[1,3072]{1,0:T(2,128)(2,1)S(1)} %get-tuple-element.30.gain_ref, ...), custom_call_target="tpu_custom_call" | custom-call | flops 226492416 | bytes 3538944 | tf_op jit(solution)/shard_map/pallas_call | solution.py:95
  26.2 0.8 %collective-permute-start.8 = (bf16[32,3072]{1,0:T(8,128)(2,1)S(1)}, bf16[32,3072]{1,0:T(8,128)(2,1)S(1)}, u32[]{:S(2)}, u32[]{:S(2)}) collective-permute-start(bf16[32,3072]{1,0:T(8,128)(2,1)S(1)} %get-tuple-element.41), channel_id=1, source_target_pairs={{0,2},{2,0},{4,6},{6,4},{8,10},{10,8},{12,14},{14,12},{16,18},{18,... | collective-permute-start | bytes 589832 | tf_op jit(solution)/shard_map/ppermute | solution.py:220
  27.0 1.3 %collective-permute-start.9 = (bf16[32,3072]{1,0:T(8,128)(2,1)S(1)}, bf16[32,3072]{1,0:T(8,128)(2,1)S(1)}, u32[]{:S(2)}, u32[]{:S(2)}) collective-permute-start(bf16[32,3072]{1,0:T(8,128)(2,1)S(1)} %collective-permute-done.7.far_ref), channel_id=1, source_target_pairs={{0,4},{2,6},{4,0},{6,2},{8,12},{10,14},{12,8},{14,10},{16,20},{18,... | collective-permute-start | bytes 589832 | tf_op jit(solution)/shard_map/ppermute | solution.py:220
  28.3 0.6 collective-permute-done.6.near_ref
  28.9 1.5 %collective-permute-start.5 = (bf16[64,3072]{1,0:T(8,128)(2,1)S(1)}, bf16[64,3072]{1,0:T(8,128)(2,1)S(1)}, u32[]{:S(2)}, u32[]{:S(2)}) collective-permute-start(bf16[64,3072]{1,0:T(8,128)(2,1)S(1)} %get-tuple-element.32), channel_id=1, source_target_pairs={{0,16},{2,18},{4,20},{6,22},{8,24},{10,26},{12,28},{14,30},{16,0},... | collective-permute-start | bytes 1179656 | tf_op jit(solution)/shard_map/ppermute | solution.py:220
  30.4 2.7 %collective-permute-done.13.near_ref = bf16[32,3072]{1,0:T(8,128)(2,1)S(1)} collective-permute-done((bf16[32,3072]{1,0:T(8,128)(2,1)S(1)}, bf16[32,3072]{1,0:T(8,128)(2,1)S(1)}, u32[]{:S(2)}, u32[]{:S(2)}) %collective-permute-start.13) | collective-permute-done | bytes 196640 | tf_op jit(solution)/shard_map/ppermute | solution.py:220
  33.1 0.0 collective-permute-start.14
  33.1 0.0 collective-permute-done.4.refs_0_
  33.1 0.0 collective-permute-done.8
  33.1 2.1 %collective-permute-done.9.far_ref = bf16[32,3072]{1,0:T(8,128)(2,1)S(1)} collective-permute-done((bf16[32,3072]{1,0:T(8,128)(2,1)S(1)}, bf16[32,3072]{1,0:T(8,128)(2,1)S(1)}, u32[]{:S(2)}, u32[]{:S(2)}) %collective-permute-start.9) | collective-permute-done | bytes 196640 | tf_op jit(solution)/shard_map/ppermute | solution.py:220
  35.2 1.3 %shard_map.78 = (bf16[32,3072]{1,0:T(8,128)(2,1)S(1)}, bf16[32,3072]{1,0:T(8,128)(2,1)S(1)}) custom-call(bf16[32,3072]{1,0:T(8,128)(2,1)S(1)} %collective-permute-done.6.near_ref, bf16[32,3072]{1,0:T(8,128)(2,1)S(1)} %collective-permute-done.9.far_ref, bf16[1,3072]{1,0:T(2,128)(2,1)S(1)} %get-tuple-element.30.gain_ref, ...), custom_call_target="tpu_custom_call" | custom-call | flops 226492416 | bytes 3538944 | tf_op jit(solution)/shard_map/pallas_call | solution.py:95
  36.5 0.8 %collective-permute-start.10 = (bf16[32,3072]{1,0:T(8,128)(2,1)S(1)}, bf16[32,3072]{1,0:T(8,128)(2,1)S(1)}, u32[]{:S(2)}, u32[]{:S(2)}) collective-permute-start(bf16[32,3072]{1,0:T(8,128)(2,1)S(1)} %get-tuple-element.43), channel_id=1, source_target_pairs={{0,2},{2,0},{4,6},{6,4},{8,10},{10,8},{12,14},{14,12},{16,18},{18,... | collective-permute-start | bytes 589832 | tf_op jit(solution)/shard_map/ppermute | solution.py:220
  37.3 1.9 %collective-permute-start.11 = (bf16[32,3072]{1,0:T(8,128)(2,1)S(1)}, bf16[32,3072]{1,0:T(8,128)(2,1)S(1)}, u32[]{:S(2)}, u32[]{:S(2)}) collective-permute-start(bf16[32,3072]{1,0:T(8,128)(2,1)S(1)} %add_convert_fusion.2), channel_id=1, source_target_pairs={{0,8},{2,10},{4,12},{6,14},{8,0},{10,2},{12,4},{14,6},{16,24},{18,... | collective-permute-start | bytes 589832 | tf_op jit(solution)/shard_map/ppermute | solution.py:220
  39.3 1.3 %collective-permute-done.14.far_ref = bf16[32,3072]{1,0:T(8,128)(2,1)S(1)} collective-permute-done((bf16[32,3072]{1,0:T(8,128)(2,1)S(1)}, bf16[32,3072]{1,0:T(8,128)(2,1)S(1)}, u32[]{:S(2)}, u32[]{:S(2)}) %collective-permute-start.14) | collective-permute-done | bytes 196640 | tf_op jit(solution)/shard_map/ppermute | solution.py:220
  40.5 1.3 %shard_map.81 = (bf16[32,3072]{1,0:T(8,128)(2,1)S(1)}, bf16[32,3072]{1,0:T(8,128)(2,1)S(1)}) custom-call(bf16[32,3072]{1,0:T(8,128)(2,1)S(1)} %collective-permute-done.13.near_ref, bf16[32,3072]{1,0:T(8,128)(2,1)S(1)} %collective-permute-done.14.far_ref, bf16[1,3072]{1,0:T(2,128)(2,1)S(1)} %get-tuple-element.30.gain_ref, ...), custom_call_target="tpu_custom_call" | custom-call | flops 226492416 | bytes 3538944 | tf_op jit(solution)/shard_map/pallas_call | solution.py:95
  41.8 0.2 collective-permute-start.15
  42.0 0.0 collective-permute-done.5.refs_1_
  42.0 0.0 copy-done
  42.0 0.7 %shard_map.76 = (f32[128,3072]{1,0:T(8,128)S(1)}, bf16[128,160]{1,0:T(8,128)(2,1)S(1)}) custom-call(bf16[1,3072]{1,0:T(2,128)(2,1)S(1)} %get-tuple-element.30.gain_ref, s32[2,128]{1,0:T(2,128)S(1)} %bitcast.22, f32[2,128]{1,0:T(2,128)S(1)} %bitcast.23, bf16[64,3072]{1,0:T(8,128)(2,1)S(1)} %collective-permute-done.4.refs_0_, ...), custom_call_target="tpu_custom_call" | custom-call | flops 3145728 | bytes 2359296 | tf_op jit(solution)/shard_map/pallas_call | solution.py:142
  42.7 2.0 %collective-permute-done.10 = bf16[32,3072]{1,0:T(8,128)(2,1)S(1)} collective-permute-done((bf16[32,3072]{1,0:T(8,128)(2,1)S(1)}, bf16[32,3072]{1,0:T(8,128)(2,1)S(1)}, u32[]{:S(2)}, u32[]{:S(2)}) %collective-permute-start.10) | collective-permute-done | bytes 196640 | tf_op jit(solution)/shard_map/ppermute | solution.py:220
  44.8 2.9 %collective-permute-start.12 = (bf16[32,3072]{1,0:T(8,128)(2,1)S(1)}, bf16[32,3072]{1,0:T(8,128)(2,1)S(1)}, u32[]{:S(2)}, u32[]{:S(2)}) collective-permute-start(bf16[32,3072]{1,0:T(8,128)(2,1)S(1)} %add_convert_fusion.1), channel_id=1, source_target_pairs={{0,12},{2,14},{4,8},{6,10},{8,4},{10,6},{12,0},{14,2},{16,28},{18,... | collective-permute-start | bytes 589832 | tf_op jit(solution)/shard_map/ppermute | solution.py:220
  47.7 1.3 %shard_map.79 = (bf16[32,3072]{1,0:T(8,128)(2,1)S(1)}, bf16[32,3072]{1,0:T(8,128)(2,1)S(1)}) custom-call(bf16[32,3072]{1,0:T(8,128)(2,1)S(1)} %collective-permute-done.1.near_ref, bf16[32,3072]{1,0:T(8,128)(2,1)S(1)} %collective-permute-done.2.far_ref, bf16[1,3072]{1,0:T(2,128)(2,1)S(1)} %get-tuple-element.30.gain_ref, ...), custom_call_target="tpu_custom_call" | custom-call | flops 226492416 | bytes 3538944 | tf_op jit(solution)/shard_map/pallas_call | solution.py:95
  49.0 3.8 %collective-permute-done.11.right_ref = bf16[32,3072]{1,0:T(8,128)(2,1)S(1)} collective-permute-done((bf16[32,3072]{1,0:T(8,128)(2,1)S(1)}, bf16[32,3072]{1,0:T(8,128)(2,1)S(1)}, u32[]{:S(2)}, u32[]{:S(2)}) %collective-permute-start.11) | collective-permute-done | bytes 196640 | tf_op jit(solution)/shard_map/ppermute | solution.py:220
  52.8 0.0 collective-permute-done.15
  52.9 0.1 collective-permute-start.16
  52.9 1.1 %collective-permute-start.17 = (bf16[32,3072]{1,0:T(8,128)(2,1)S(1)}, bf16[32,3072]{1,0:T(8,128)(2,1)S(1)}, u32[]{:S(2)}, u32[]{:S(2)}) collective-permute-start(bf16[32,3072]{1,0:T(8,128)(2,1)S(1)} %get-tuple-element.52), channel_id=1, source_target_pairs={{0,2},{2,0},{4,6},{6,4},{8,10},{10,8},{12,14},{14,12},{16,18},{18,... | collective-permute-start | bytes 589832 | tf_op jit(solution)/shard_map/ppermute | solution.py:220
  54.1 0.1 collective-permute-done.12.refs_1_
  54.2 4.4 %collective-permute-done.16.refs_2_ = bf16[32,3072]{1,0:T(8,128)(2,1)S(1)} collective-permute-done((bf16[32,3072]{1,0:T(8,128)(2,1)S(1)}, bf16[32,3072]{1,0:T(8,128)(2,1)S(1)}, u32[]{:S(2)}, u32[]{:S(2)}) %collective-permute-start.16) | collective-permute-done | bytes 196640 | tf_op jit(solution)/shard_map/ppermute | solution.py:220
  58.6 0.1 collective-permute-done.17.refs_3_
  58.7 1.9 %shard_map.82 = bf16[128,3072]{1,0:T(8,128)(2,1)} custom-call(f32[128,3072]{1,0:T(8,128)S(1)} %get-tuple-element.33.base_ref, bf16[128,160]{1,0:T(8,128)(2,1)S(1)} %get-tuple-element.34.table_ref, f32[32,3072]{1,0:T(8,128)S(1)} %shard_map.80.refs_0_, bf16[32,3072]{1,0:T(8,128)(2,1)S(1)} %collective-permute-done.12.refs_1_, ...), custom_call_target="tpu_custom_call" | custom-call | flops 100663296 | bytes 2359296 | tf_op jit(solution)/shard_map/pallas_call | solution.py:173
  (8 shorter events, 0.2 us)
Async XLA Ops:
  0.0 4.7 %collective-permute-start = (s32[1,128,2]{1,2,0:T(2,128)}, s32[1,128,2]{1,2,0:T(2,128)S(1)}, u32[]{:S(2)}, u32[]{:S(2)}) collective-permute-start(s32[1,128,2]{1,2,0:T(2,128)} %param.12), channel_id=1, source_target_pairs={{0,16},{2,18},{4,20},{6,22},{8,24},{10,26},{12,28},{14,30},{16,0},... | collective-permute-start | bytes 3080 | tf_op jit(solution)/shard_map/ppermute | solution.py:220
  5.1 9.2 %collective-permute-start.1 = (bf16[32,3072]{1,0:T(8,128)(2,1)S(1)}, bf16[32,3072]{1,0:T(8,128)(2,1)S(1)}, u32[]{:S(2)}, u32[]{:S(2)}) collective-permute-start(bf16[32,3072]{1,0:T(8,128)(2,1)S(1)} %shard_map.74), channel_id=1, source_target_pairs={{0,16},{2,18},{4,20},{6,22},{8,24},{10,26},{12,28},{14,30},{16,0},... | collective-permute-start | bytes 589832 | tf_op jit(solution)/shard_map/ppermute | solution.py:220
  7.1 11.3 %collective-permute-start.3 = (bf16[32,3072]{1,0:T(8,128)(2,1)S(1)}, bf16[32,3072]{1,0:T(8,128)(2,1)S(1)}, u32[]{:S(2)}, u32[]{:S(2)}) collective-permute-start(bf16[32,3072]{1,0:T(8,128)(2,1)S(1)} %shard_map.74), channel_id=1, source_target_pairs={{0,24},{2,26},{4,28},{6,30},{8,16},{10,18},{12,20},{14,22},{16,8},... | collective-permute-start | bytes 589832 | tf_op jit(solution)/shard_map/ppermute | solution.py:220
  9.7 11.1 %collective-permute-start.2 = (bf16[32,3072]{1,0:T(8,128)(2,1)S(1)}, bf16[32,3072]{1,0:T(8,128)(2,1)S(1)}, u32[]{:S(2)}, u32[]{:S(2)}) collective-permute-start(bf16[32,3072]{1,0:T(8,128)(2,1)S(1)} %shard_map.74), channel_id=1, source_target_pairs={{0,18},{2,16},{4,22},{6,20},{8,26},{10,24},{12,30},{14,28},{16,2},... | collective-permute-start | bytes 589832 | tf_op jit(solution)/shard_map/ppermute | solution.py:220
  12.2 7.8 %copy-start.2 = (bf16[1,128,3072]{2,1,0:T(8,128)(2,1)S(1)}, bf16[1,128,3072]{2,1,0:T(8,128)(2,1)}, u32[]{:S(2)}) copy-start(bf16[1,128,3072]{2,1,0:T(8,128)(2,1)} %param.7) | copy-start | bytes 2359300
  18.5 6.5 %collective-permute-start.7 = (bf16[32,3072]{1,0:T(8,128)(2,1)S(1)}, bf16[32,3072]{1,0:T(8,128)(2,1)S(1)}, u32[]{:S(2)}, u32[]{:S(2)}) collective-permute-start(bf16[32,3072]{1,0:T(8,128)(2,1)S(1)} %collective-permute-done.3.near_ref), channel_id=1, source_target_pairs={{0,2},{2,0},{4,6},{6,4},{8,10},{10,8},{12,14},{14,12},{16,18},{18,... | collective-permute-start | bytes 589832 | tf_op jit(solution)/shard_map/ppermute | solution.py:220
  20.8 12.3 %collective-permute-start.4 = (bf16[64,3072]{1,0:T(8,128)(2,1)S(1)}, bf16[64,3072]{1,0:T(8,128)(2,1)S(1)}, u32[]{:S(2)}, u32[]{:S(2)}) collective-permute-start(bf16[64,3072]{1,0:T(8,128)(2,1)S(1)} %get-tuple-element.31), channel_id=1, source_target_pairs={{0,16},{2,18},{4,20},{6,22},{8,24},{10,26},{12,28},{14,30},{16,0},... | collective-permute-start | bytes 1179656 | tf_op jit(solution)/shard_map/ppermute | solution.py:220
  22.1 6.8 %collective-permute-start.6 = (bf16[32,3072]{1,0:T(8,128)(2,1)S(1)}, bf16[32,3072]{1,0:T(8,128)(2,1)S(1)}, u32[]{:S(2)}, u32[]{:S(2)}) collective-permute-start(bf16[32,3072]{1,0:T(8,128)(2,1)S(1)} %collective-permute-done.3.near_ref), channel_id=1, source_target_pairs={{0,4},{2,6},{4,0},{6,2},{8,12},{10,14},{12,8},{14,10},{16,20},{18,... | collective-permute-start | bytes 589832 | tf_op jit(solution)/shard_map/ppermute | solution.py:220
  23.7 9.3 %collective-permute-start.13 = (bf16[32,3072]{1,0:T(8,128)(2,1)S(1)}, bf16[32,3072]{1,0:T(8,128)(2,1)S(1)}, u32[]{:S(2)}, u32[]{:S(2)}) collective-permute-start(bf16[32,3072]{1,0:T(8,128)(2,1)S(1)} %collective-permute-done.1.near_ref), channel_id=1, source_target_pairs={{0,4},{2,6},{4,0},{6,2},{8,12},{10,14},{12,8},{14,10},{16,20},{18,... | collective-permute-start | bytes 589832 | tf_op jit(solution)/shard_map/ppermute | solution.py:220
  26.2 6.9 %collective-permute-start.8 = (bf16[32,3072]{1,0:T(8,128)(2,1)S(1)}, bf16[32,3072]{1,0:T(8,128)(2,1)S(1)}, u32[]{:S(2)}, u32[]{:S(2)}) collective-permute-start(bf16[32,3072]{1,0:T(8,128)(2,1)S(1)} %get-tuple-element.41), channel_id=1, source_target_pairs={{0,2},{2,0},{4,6},{6,4},{8,10},{10,8},{12,14},{14,12},{16,18},{18,... | collective-permute-start | bytes 589832 | tf_op jit(solution)/shard_map/ppermute | solution.py:220
  27.0 8.2 %collective-permute-start.9 = (bf16[32,3072]{1,0:T(8,128)(2,1)S(1)}, bf16[32,3072]{1,0:T(8,128)(2,1)S(1)}, u32[]{:S(2)}, u32[]{:S(2)}) collective-permute-start(bf16[32,3072]{1,0:T(8,128)(2,1)S(1)} %collective-permute-done.7.far_ref), channel_id=1, source_target_pairs={{0,4},{2,6},{4,0},{6,2},{8,12},{10,14},{12,8},{14,10},{16,20},{18,... | collective-permute-start | bytes 589832 | tf_op jit(solution)/shard_map/ppermute | solution.py:220
  28.9 13.1 %collective-permute-start.5 = (bf16[64,3072]{1,0:T(8,128)(2,1)S(1)}, bf16[64,3072]{1,0:T(8,128)(2,1)S(1)}, u32[]{:S(2)}, u32[]{:S(2)}) collective-permute-start(bf16[64,3072]{1,0:T(8,128)(2,1)S(1)} %get-tuple-element.32), channel_id=1, source_target_pairs={{0,16},{2,18},{4,20},{6,22},{8,24},{10,26},{12,28},{14,30},{16,0},... | collective-permute-start | bytes 1179656 | tf_op jit(solution)/shard_map/ppermute | solution.py:220
  33.1 7.4 %collective-permute-start.14 = (bf16[32,3072]{1,0:T(8,128)(2,1)S(1)}, bf16[32,3072]{1,0:T(8,128)(2,1)S(1)}, u32[]{:S(2)}, u32[]{:S(2)}) collective-permute-start(bf16[32,3072]{1,0:T(8,128)(2,1)S(1)} %collective-permute-done.13.near_ref), channel_id=1, source_target_pairs={{0,2},{2,0},{4,6},{6,4},{8,10},{10,8},{12,14},{14,12},{16,18},{18,... | collective-permute-start | bytes 589832 | tf_op jit(solution)/shard_map/ppermute | solution.py:220
  36.5 8.3 %collective-permute-start.10 = (bf16[32,3072]{1,0:T(8,128)(2,1)S(1)}, bf16[32,3072]{1,0:T(8,128)(2,1)S(1)}, u32[]{:S(2)}, u32[]{:S(2)}) collective-permute-start(bf16[32,3072]{1,0:T(8,128)(2,1)S(1)} %get-tuple-element.43), channel_id=1, source_target_pairs={{0,2},{2,0},{4,6},{6,4},{8,10},{10,8},{12,14},{14,12},{16,18},{18,... | collective-permute-start | bytes 589832 | tf_op jit(solution)/shard_map/ppermute | solution.py:220
  37.3 15.4 %collective-permute-start.11 = (bf16[32,3072]{1,0:T(8,128)(2,1)S(1)}, bf16[32,3072]{1,0:T(8,128)(2,1)S(1)}, u32[]{:S(2)}, u32[]{:S(2)}) collective-permute-start(bf16[32,3072]{1,0:T(8,128)(2,1)S(1)} %add_convert_fusion.2), channel_id=1, source_target_pairs={{0,8},{2,10},{4,12},{6,14},{8,0},{10,2},{12,4},{14,6},{16,24},{18,... | collective-permute-start | bytes 589832 | tf_op jit(solution)/shard_map/ppermute | solution.py:220
  39.2 2.7 %copy-start = (s32[1,128,2]{1,2,0:T(2,128)S(1)}, s32[1,128,2]{1,2,0:T(2,128)}, u32[]{:S(2)}) copy-start(s32[1,128,2]{1,2,0:T(2,128)} %param.12) | copy-start | bytes 3076
  39.3 2.7 %copy-start.1 = (f32[1,128,2]{1,2,0:T(2,128)S(1)}, f32[1,128,2]{1,2,0:T(2,128)}, u32[]{:S(2)}) copy-start(f32[1,128,2]{1,2,0:T(2,128)} %param.13) | copy-start | bytes 3076
  41.8 11.0 %collective-permute-start.15 = (bf16[32,3072]{1,0:T(8,128)(2,1)S(1)}, bf16[32,3072]{1,0:T(8,128)(2,1)S(1)}, u32[]{:S(2)}, u32[]{:S(2)}) collective-permute-start(bf16[32,3072]{1,0:T(8,128)(2,1)S(1)} %get-tuple-element.50), channel_id=1, source_target_pairs={{0,2},{2,0},{4,6},{6,4},{8,10},{10,8},{12,14},{14,12},{16,18},{18,... | collective-permute-start | bytes 589832 | tf_op jit(solution)/shard_map/ppermute | solution.py:220
  44.8 9.4 %collective-permute-start.12 = (bf16[32,3072]{1,0:T(8,128)(2,1)S(1)}, bf16[32,3072]{1,0:T(8,128)(2,1)S(1)}, u32[]{:S(2)}, u32[]{:S(2)}) collective-permute-start(bf16[32,3072]{1,0:T(8,128)(2,1)S(1)} %add_convert_fusion.1), channel_id=1, source_target_pairs={{0,12},{2,14},{4,8},{6,10},{8,4},{10,6},{12,0},{14,2},{16,28},{18,... | collective-permute-start | bytes 589832 | tf_op jit(solution)/shard_map/ppermute | solution.py:220
  52.9 5.7 %collective-permute-start.16 = (bf16[32,3072]{1,0:T(8,128)(2,1)S(1)}, bf16[32,3072]{1,0:T(8,128)(2,1)S(1)}, u32[]{:S(2)}, u32[]{:S(2)}) collective-permute-start(bf16[32,3072]{1,0:T(8,128)(2,1)S(1)} %add_convert_fusion), channel_id=1, source_target_pairs={{0,4},{2,6},{4,0},{6,2},{8,12},{10,14},{12,8},{14,10},{16,20},{18,... | collective-permute-start | bytes 589832 | tf_op jit(solution)/shard_map/ppermute | solution.py:220
  52.9 5.7 %collective-permute-start.17 = (bf16[32,3072]{1,0:T(8,128)(2,1)S(1)}, bf16[32,3072]{1,0:T(8,128)(2,1)S(1)}, u32[]{:S(2)}, u32[]{:S(2)}) collective-permute-start(bf16[32,3072]{1,0:T(8,128)(2,1)S(1)} %get-tuple-element.52), channel_id=1, source_target_pairs={{0,2},{2,0},{4,6},{6,4},{8,10},{10,8},{12,14},{14,12},{16,18},{18,... | collective-permute-start | bytes 589832 | tf_op jit(solution)/shard_map/ppermute | solution.py:220

commit v3 on v2

--- a/solution.py
+++ b/solution.py
@@ -253,7 +253,7 @@
 
     own, other = {}, {}
     for k in (2, 3, 1, 0):
-        first = {2: (gain,), 3: (other.get(2), arrived[0]), 1: (own.get(3),), 0: (other.get(3), base)}[k]
+        first = {2: (gain,), 3: (other.get(2), arrived[0]), 1: (own.get(3),), 0: (own.get(3),)}[k]
         own[k], sent = mlp(after(near[k], *first), far[k], gain, gate_t, up_t, down)
         other[k] = moved(sent, 0, 0, 1)
     both = {
@@ -262,7 +262,7 @@
     }
     early = summed_early(own[0], moved(both[2], 0, 2))
     backs = [
-        early, moved(both[3], 0, 3), moved(after(both[1], early), 0, 1), other[0],
+        early, moved(both[3], 0, 3), moved(after(both[1], base), 0, 1), other[0],
     ]
     if experts > 1:
         summed = sum(back.astype(jnp.float32) for back in backs).reshape(experts, CAP, width)

time: 60.7 us -> 62.4 us (1.028)
  waiting for transfers between devices: 23.3 us -> 24.8 us
    ppermute x18, waiting for transfers between devices: 23.3 us -> 24.8 us  [moved(): return lax.ppermute(value, ('section', 'expert'), pairs)]
  transfers between devices with their start and end apart: 18 -> 18, of which waited for: 13 -> 11; matrix products, arithmetic and copies ran while one was open for 0% -> 0% of each run, Pallas kernels for 15% -> 14%
where the time goes in v3:
time: 62.4 us; the launch traced here: 62.2 us
  starting transfers between devices  25.8 us (41%)
  waiting for transfers between devices  24.8 us (40%)
  Pallas kernels  11.2 us (18%)
    ppermute x18, starting transfers between devices, moved(): return lax.ppermute(value, ('section', 'expert'), pairs)  25.8 us
    ppermute x18, waiting for transfers between devices, moved(): return lax.ppermute(value, ('section', 'expert'), pairs)  24.8 us
    pallas_call x4, Pallas kernels, mlp(): pl.pallas_call(mlp_kernel, out_shape=(out, out), in_specs=[VMEM] * 6, out...  5.05 us
    pallas_call x2, Pallas kernels, loaded(): pl.pallas_call(functools.partial(load_kernel, len(arrays)), out_shape=tup...  3.23 us
    pallas_call x1, Pallas kernels, ended(): pl.pallas_call(functools.partial(end_kernel, columns), out_shape=jax.Shap...  1.89 us
  transfers between devices with their start and end apart: 18, of which 11 were waited for; matrix products, arithmetic and copies ran while one was open for 0% of the time, Pallas kernels for 14%

profile of v3, /device:TPU:0, one launch (start us, length us, event | category | flops | bytes accessed | tf_op | source)
XLA Modules:
  0.0 62.2 jit_solution(6322062677075590297)
XLA Ops:
  0.0 2.9 %collective-permute-start = (s32[1,128,2]{1,2,0:T(2,128)}, s32[1,128,2]{1,2,0:T(2,128)S(1)}, u32[]{:S(2)}, u32[]{:S(2)}) collective-permute-start(s32[1,128,2]{1,2,0:T(2,128)} %param.12), channel_id=1, source_target_pairs={{0,16},{2,18},{4,20},{6,22},{8,24},{10,26},{12,28},{14,30},{16,0},... | collective-permute-start | bytes 3080 | tf_op jit(solution)/shard_map/ppermute | solution.py:220
  2.9 1.1 %shard_map.73.block_ref = bf16[128,3072]{1,0:T(8,128)(2,1)S(1)} custom-call(bf16[128,3072]{1,0:T(8,128)(2,1)} %bitcast.25), custom_call_target="tpu_custom_call" | custom-call | bytes 6291456 | tf_op jit(solution)/shard_map/pallas_call | solution.py:33
  4.1 0.6 collective-permute-done
  4.7 0.4 shard_map.74
  5.1 4.1 %collective-permute-start.3 = (bf16[32,3072]{1,0:T(8,128)(2,1)S(1)}, bf16[32,3072]{1,0:T(8,128)(2,1)S(1)}, u32[]{:S(2)}, u32[]{:S(2)}) collective-permute-start(bf16[32,3072]{1,0:T(8,128)(2,1)S(1)} %shard_map.74), channel_id=1, source_target_pairs={{0,24},{2,26},{4,28},{6,30},{8,16},{10,18},{12,20},{14,22},{16,8},... | collective-permute-start | bytes 589832 | tf_op jit(solution)/shard_map/ppermute | solution.py:220
  9.2 0.5 collective-permute-start.1
  9.7 2.4 %collective-permute-start.2 = (bf16[32,3072]{1,0:T(8,128)(2,1)S(1)}, bf16[32,3072]{1,0:T(8,128)(2,1)S(1)}, u32[]{:S(2)}, u32[]{:S(2)}) collective-permute-start(bf16[32,3072]{1,0:T(8,128)(2,1)S(1)} %shard_map.74), channel_id=1, source_target_pairs={{0,18},{2,16},{4,22},{6,20},{8,26},{10,24},{12,30},{14,28},{16,2},... | collective-permute-start | bytes 589832 | tf_op jit(solution)/shard_map/ppermute | solution.py:220
  12.2 2.1 %shard_map.75 = (bf16[192,3072]{1,0:T(8,128)(2,1)S(1)}, bf16[192,3072]{1,0:T(8,128)(2,1)S(1)}, bf16[192,3072]{1,0:T(8,128)(2,1)S(1)}, bf16[1,3072]{1,0:T(2,128)(2,1)S(1)}) custom-call(bf16[192,3072]{1,0:T(8,128)(2,1)} %bitcast.26, bf16[192,3072]{1,0:T(8,128)(2,1)} %bitcast.27, bf16[192,3072]{1,0:T(8,128)(2,1)} %bitcast.28, bf16[1,3072]{1,0:T(2,128)(2,1)} %refs_3_.1), custom_call_target="tpu_custom_call" | custom-call | bytes 6291456 | tf_op jit(solution)/shard_map/pallas_call | solution.py:33
  14.3 3.0 %collective-permute-done.3.near_ref = bf16[32,3072]{1,0:T(8,128)(2,1)S(1)} collective-permute-done((bf16[32,3072]{1,0:T(8,128)(2,1)S(1)}, bf16[32,3072]{1,0:T(8,128)(2,1)S(1)}, u32[]{:S(2)}, u32[]{:S(2)}) %collective-permute-start.3) | collective-permute-done | bytes 196640 | tf_op jit(solution)/shard_map/ppermute | solution.py:220
  17.2 2.3 %collective-permute-done.1.near_ref = bf16[32,3072]{1,0:T(8,128)(2,1)S(1)} collective-permute-done((bf16[32,3072]{1,0:T(8,128)(2,1)S(1)}, bf16[32,3072]{1,0:T(8,128)(2,1)S(1)}, u32[]{:S(2)}, u32[]{:S(2)}) %collective-permute-start.1) | collective-permute-done | bytes 196640 | tf_op jit(solution)/shard_map/ppermute | solution.py:220
  19.6 1.5 %collective-permute-start.7 = (bf16[32,3072]{1,0:T(8,128)(2,1)S(1)}, bf16[32,3072]{1,0:T(8,128)(2,1)S(1)}, u32[]{:S(2)}, u32[]{:S(2)}) collective-permute-start(bf16[32,3072]{1,0:T(8,128)(2,1)S(1)} %collective-permute-done.3.near_ref), channel_id=1, source_target_pairs={{0,2},{2,0},{4,6},{6,4},{8,10},{10,8},{12,14},{14,12},{16,18},{18,... | collective-permute-start | bytes 589832 | tf_op jit(solution)/shard_map/ppermute | solution.py:220
  21.1 0.1 slice_bitcast_fusion
  21.2 1.6 %collective-permute-done.2.far_ref = bf16[32,3072]{1,0:T(8,128)(2,1)S(1)} collective-permute-done((bf16[32,3072]{1,0:T(8,128)(2,1)S(1)}, bf16[32,3072]{1,0:T(8,128)(2,1)S(1)}, u32[]{:S(2)}, u32[]{:S(2)}) %collective-permute-start.2) | collective-permute-done | bytes 196640 | tf_op jit(solution)/shard_map/ppermute | solution.py:220
  22.8 1.2 %collective-permute-start.4 = (bf16[64,3072]{1,0:T(8,128)(2,1)S(1)}, bf16[64,3072]{1,0:T(8,128)(2,1)S(1)}, u32[]{:S(2)}, u32[]{:S(2)}) collective-permute-start(bf16[64,3072]{1,0:T(8,128)(2,1)S(1)} %get-tuple-element.31), channel_id=1, source_target_pairs={{0,16},{2,18},{4,20},{6,22},{8,24},{10,26},{12,28},{14,30},{16,0},... | collective-permute-start | bytes 1179656 | tf_op jit(solution)/shard_map/ppermute | solution.py:220
  23.9 1.7 %collective-permute-start.6 = (bf16[32,3072]{1,0:T(8,128)(2,1)S(1)}, bf16[32,3072]{1,0:T(8,128)(2,1)S(1)}, u32[]{:S(2)}, u32[]{:S(2)}) collective-permute-start(bf16[32,3072]{1,0:T(8,128)(2,1)S(1)} %collective-permute-done.3.near_ref), channel_id=1, source_target_pairs={{0,4},{2,6},{4,0},{6,2},{8,12},{10,14},{12,8},{14,10},{16,20},{18,... | collective-permute-start | bytes 589832 | tf_op jit(solution)/shard_map/ppermute | solution.py:220
  25.6 0.3 collective-permute-start.13
  25.9 0.0 collective-permute-done.7.far_ref
  26.0 1.3 %shard_map.77 = (bf16[32,3072]{1,0:T(8,128)(2,1)S(1)}, bf16[32,3072]{1,0:T(8,128)(2,1)S(1)}) custom-call(bf16[32,3072]{1,0:T(8,128)(2,1)S(1)} %collective-permute-done.3.near_ref, bf16[32,3072]{1,0:T(8,128)(2,1)S(1)} %collective-permute-done.7.far_ref, bf16[1,3072]{1,0:T(2,128)(2,1)S(1)} %get-tuple-element.30.gain_ref, ...), custom_call_target="tpu_custom_call" | custom-call | flops 226492416 | bytes 3538944 | tf_op jit(solution)/shard_map/pallas_call | solution.py:95
  27.2 0.9 %collective-permute-start.8 = (bf16[32,3072]{1,0:T(8,128)(2,1)S(1)}, bf16[32,3072]{1,0:T(8,128)(2,1)S(1)}, u32[]{:S(2)}, u32[]{:S(2)}) collective-permute-start(bf16[32,3072]{1,0:T(8,128)(2,1)S(1)} %get-tuple-element.41), channel_id=1, source_target_pairs={{0,2},{2,0},{4,6},{6,4},{8,10},{10,8},{12,14},{14,12},{16,18},{18,... | collective-permute-start | bytes 589832 | tf_op jit(solution)/shard_map/ppermute | solution.py:220
  28.1 1.9 %collective-permute-start.9 = (bf16[32,3072]{1,0:T(8,128)(2,1)S(1)}, bf16[32,3072]{1,0:T(8,128)(2,1)S(1)}, u32[]{:S(2)}, u32[]{:S(2)}) collective-permute-start(bf16[32,3072]{1,0:T(8,128)(2,1)S(1)} %collective-permute-done.7.far_ref), channel_id=1, source_target_pairs={{0,4},{2,6},{4,0},{6,2},{8,12},{10,14},{12,8},{14,10},{16,20},{18,... | collective-permute-start | bytes 589832 | tf_op jit(solution)/shard_map/ppermute | solution.py:220
  30.1 1.7 %collective-permute-done.6.near_ref = bf16[32,3072]{1,0:T(8,128)(2,1)S(1)} collective-permute-done((bf16[32,3072]{1,0:T(8,128)(2,1)S(1)}, bf16[32,3072]{1,0:T(8,128)(2,1)S(1)}, u32[]{:S(2)}, u32[]{:S(2)}) %collective-permute-start.6) | collective-permute-done | bytes 196640 | tf_op jit(solution)/shard_map/ppermute | solution.py:220
  31.8 0.9 %collective-permute-start.5 = (bf16[64,3072]{1,0:T(8,128)(2,1)S(1)}, bf16[64,3072]{1,0:T(8,128)(2,1)S(1)}, u32[]{:S(2)}, u32[]{:S(2)}) collective-permute-start(bf16[64,3072]{1,0:T(8,128)(2,1)S(1)} %get-tuple-element.32), channel_id=1, source_target_pairs={{0,16},{2,18},{4,20},{6,22},{8,24},{10,26},{12,28},{14,30},{16,0},... | collective-permute-start | bytes 1179656 | tf_op jit(solution)/shard_map/ppermute | solution.py:220
  32.6 3.3 %collective-permute-done.13.near_ref = bf16[32,3072]{1,0:T(8,128)(2,1)S(1)} collective-permute-done((bf16[32,3072]{1,0:T(8,128)(2,1)S(1)}, bf16[32,3072]{1,0:T(8,128)(2,1)S(1)}, u32[]{:S(2)}, u32[]{:S(2)}) %collective-permute-start.13) | collective-permute-done | bytes 196640 | tf_op jit(solution)/shard_map/ppermute | solution.py:220
  36.0 0.5 collective-permute-start.14
  36.5 0.0 collective-permute-done.4.refs_0_
  36.5 0.0 collective-permute-done.8
  36.5 2.2 %collective-permute-done.9.far_ref = bf16[32,3072]{1,0:T(8,128)(2,1)S(1)} collective-permute-done((bf16[32,3072]{1,0:T(8,128)(2,1)S(1)}, bf16[32,3072]{1,0:T(8,128)(2,1)S(1)}, u32[]{:S(2)}, u32[]{:S(2)}) %collective-permute-start.9) | collective-permute-done | bytes 196640 | tf_op jit(solution)/shard_map/ppermute | solution.py:220
  38.7 1.3 %shard_map.78 = (bf16[32,3072]{1,0:T(8,128)(2,1)S(1)}, bf16[32,3072]{1,0:T(8,128)(2,1)S(1)}) custom-call(bf16[32,3072]{1,0:T(8,128)(2,1)S(1)} %collective-permute-done.6.near_ref, bf16[32,3072]{1,0:T(8,128)(2,1)S(1)} %collective-permute-done.9.far_ref, bf16[1,3072]{1,0:T(2,128)(2,1)S(1)} %get-tuple-element.30.gain_ref, ...), custom_call_target="tpu_custom_call" | custom-call | flops 226492416 | bytes 3538944 | tf_op jit(solution)/shard_map/pallas_call | solution.py:95
  40.0 0.5 collective-permute-start.11
  40.6 0.1 collective-permute-start.10
  40.7 1.3 %shard_map.79 = (bf16[32,3072]{1,0:T(8,128)(2,1)S(1)}, bf16[32,3072]{1,0:T(8,128)(2,1)S(1)}) custom-call(bf16[32,3072]{1,0:T(8,128)(2,1)S(1)} %collective-permute-done.1.near_ref, bf16[32,3072]{1,0:T(8,128)(2,1)S(1)} %collective-permute-done.2.far_ref, bf16[1,3072]{1,0:T(2,128)(2,1)S(1)} %get-tuple-element.30.gain_ref, ...), custom_call_target="tpu_custom_call" | custom-call | flops 226492416 | bytes 3538944 | tf_op jit(solution)/shard_map/pallas_call | solution.py:95
  41.9 0.0 copy-start
  41.9 0.0 copy-start.1
  41.9 1.6 %collective-permute-start.17 = (bf16[32,3072]{1,0:T(8,128)(2,1)S(1)}, bf16[32,3072]{1,0:T(8,128)(2,1)S(1)}, u32[]{:S(2)}, u32[]{:S(2)}) collective-permute-start(bf16[32,3072]{1,0:T(8,128)(2,1)S(1)} %get-tuple-element.52), channel_id=1, source_target_pairs={{0,2},{2,0},{4,6},{6,4},{8,10},{10,8},{12,14},{14,12},{16,18},{18,... | collective-permute-start | bytes 589832 | tf_op jit(solution)/shard_map/ppermute | solution.py:220
  43.6 0.0 collective-permute-done.14.far_ref
  43.6 1.3 %shard_map.81 = (bf16[32,3072]{1,0:T(8,128)(2,1)S(1)}, bf16[32,3072]{1,0:T(8,128)(2,1)S(1)}) custom-call(bf16[32,3072]{1,0:T(8,128)(2,1)S(1)} %collective-permute-done.13.near_ref, bf16[32,3072]{1,0:T(8,128)(2,1)S(1)} %collective-permute-done.14.far_ref, bf16[1,3072]{1,0:T(2,128)(2,1)S(1)} %get-tuple-element.30.gain_ref, ...), custom_call_target="tpu_custom_call" | custom-call | flops 226492416 | bytes 3538944 | tf_op jit(solution)/shard_map/pallas_call | solution.py:95
  44.8 0.5 collective-permute-start.15
  45.4 0.0 collective-permute-done.5.refs_1_
  45.4 0.7 %shard_map.76 = (f32[128,3072]{1,0:T(8,128)S(1)}, bf16[128,160]{1,0:T(8,128)(2,1)S(1)}) custom-call(bf16[1,3072]{1,0:T(2,128)(2,1)S(1)} %get-tuple-element.30.gain_ref, s32[2,128]{1,0:T(2,128)S(1)} %bitcast.22, f32[2,128]{1,0:T(2,128)S(1)} %bitcast.23, bf16[64,3072]{1,0:T(8,128)(2,1)S(1)} %collective-permute-done.4.refs_0_, ...), custom_call_target="tpu_custom_call" | custom-call | flops 3145728 | bytes 2359296 | tf_op jit(solution)/shard_map/pallas_call | solution.py:142
  46.1 1.8 %collective-permute-done.11 = bf16[32,3072]{1,0:T(8,128)(2,1)S(1)} collective-permute-done((bf16[32,3072]{1,0:T(8,128)(2,1)S(1)}, bf16[32,3072]{1,0:T(8,128)(2,1)S(1)}, u32[]{:S(2)}, u32[]{:S(2)}) %collective-permute-start.11) | collective-permute-done | bytes 196640 | tf_op jit(solution)/shard_map/ppermute | solution.py:220
  47.9 2.3 %collective-permute-start.12 = (bf16[32,3072]{1,0:T(8,128)(2,1)S(1)}, bf16[32,3072]{1,0:T(8,128)(2,1)S(1)}, u32[]{:S(2)}, u32[]{:S(2)}) collective-permute-start(bf16[32,3072]{1,0:T(8,128)(2,1)S(1)} %add_convert_fusion.1), channel_id=1, source_target_pairs={{0,12},{2,14},{4,8},{6,10},{8,4},{10,6},{12,0},{14,2},{16,28},{18,... | collective-permute-start | bytes 589832 | tf_op jit(solution)/shard_map/ppermute | solution.py:220
  50.3 4.0 %collective-permute-done.15 = bf16[32,3072]{1,0:T(8,128)(2,1)S(1)} collective-permute-done((bf16[32,3072]{1,0:T(8,128)(2,1)S(1)}, bf16[32,3072]{1,0:T(8,128)(2,1)S(1)}, u32[]{:S(2)}, u32[]{:S(2)}) %collective-permute-start.15) | collective-permute-done | bytes 196640 | tf_op jit(solution)/shard_map/ppermute | solution.py:220
  54.3 1.7 %collective-permute-start.16 = (bf16[32,3072]{1,0:T(8,128)(2,1)S(1)}, bf16[32,3072]{1,0:T(8,128)(2,1)S(1)}, u32[]{:S(2)}, u32[]{:S(2)}) collective-permute-start(bf16[32,3072]{1,0:T(8,128)(2,1)S(1)} %add_convert_fusion), channel_id=1, source_target_pairs={{0,4},{2,6},{4,0},{6,2},{8,12},{10,14},{12,8},{14,10},{16,20},{18,... | collective-permute-start | bytes 589832 | tf_op jit(solution)/shard_map/ppermute | solution.py:220
  56.1 0.5 collective-permute-done.10.right_ref
  56.6 0.0 collective-permute-done.17.refs_3_
  56.6 0.0 collective-permute-done.12.refs_1_
  56.6 3.7 %collective-permute-done.16.refs_2_ = bf16[32,3072]{1,0:T(8,128)(2,1)S(1)} collective-permute-done((bf16[32,3072]{1,0:T(8,128)(2,1)S(1)}, bf16[32,3072]{1,0:T(8,128)(2,1)S(1)}, u32[]{:S(2)}, u32[]{:S(2)}) %collective-permute-start.16) | collective-permute-done | bytes 196640 | tf_op jit(solution)/shard_map/ppermute | solution.py:220
  60.3 1.9 %shard_map.82 = bf16[128,3072]{1,0:T(8,128)(2,1)} custom-call(f32[128,3072]{1,0:T(8,128)S(1)} %get-tuple-element.33.base_ref, bf16[128,160]{1,0:T(8,128)(2,1)S(1)} %get-tuple-element.34.table_ref, f32[32,3072]{1,0:T(8,128)S(1)} %shard_map.80.refs_0_, bf16[32,3072]{1,0:T(8,128)(2,1)S(1)} %collective-permute-done.12.refs_1_, ...), custom_call_target="tpu_custom_call" | custom-call | flops 100663296 | bytes 2359296 | tf_op jit(solution)/shard_map/pallas_call | solution.py:173
  (8 shorter events, 0.2 us)
Async XLA Ops:
  0.0 4.7 %collective-permute-start = (s32[1,128,2]{1,2,0:T(2,128)}, s32[1,128,2]{1,2,0:T(2,128)S(1)}, u32[]{:S(2)}, u32[]{:S(2)}) collective-permute-start(s32[1,128,2]{1,2,0:T(2,128)} %param.12), channel_id=1, source_target_pairs={{0,16},{2,18},{4,20},{6,22},{8,24},{10,26},{12,28},{14,30},{16,0},... | collective-permute-start | bytes 3080 | tf_op jit(solution)/shard_map/ppermute | solution.py:220
  5.1 12.2 %collective-permute-start.3 = (bf16[32,3072]{1,0:T(8,128)(2,1)S(1)}, bf16[32,3072]{1,0:T(8,128)(2,1)S(1)}, u32[]{:S(2)}, u32[]{:S(2)}) collective-permute-start(bf16[32,3072]{1,0:T(8,128)(2,1)S(1)} %shard_map.74), channel_id=1, source_target_pairs={{0,24},{2,26},{4,28},{6,30},{8,16},{10,18},{12,20},{14,22},{16,8},... | collective-permute-start | bytes 589832 | tf_op jit(solution)/shard_map/ppermute | solution.py:220
  9.2 10.4 %collective-permute-start.1 = (bf16[32,3072]{1,0:T(8,128)(2,1)S(1)}, bf16[32,3072]{1,0:T(8,128)(2,1)S(1)}, u32[]{:S(2)}, u32[]{:S(2)}) collective-permute-start(bf16[32,3072]{1,0:T(8,128)(2,1)S(1)} %shard_map.74), channel_id=1, source_target_pairs={{0,16},{2,18},{4,20},{6,22},{8,24},{10,26},{12,28},{14,30},{16,0},... | collective-permute-start | bytes 589832 | tf_op jit(solution)/shard_map/ppermute | solution.py:220
  9.7 13.0 %collective-permute-start.2 = (bf16[32,3072]{1,0:T(8,128)(2,1)S(1)}, bf16[32,3072]{1,0:T(8,128)(2,1)S(1)}, u32[]{:S(2)}, u32[]{:S(2)}) collective-permute-start(bf16[32,3072]{1,0:T(8,128)(2,1)S(1)} %shard_map.74), channel_id=1, source_target_pairs={{0,18},{2,16},{4,22},{6,20},{8,26},{10,24},{12,30},{14,28},{16,2},... | collective-permute-start | bytes 589832 | tf_op jit(solution)/shard_map/ppermute | solution.py:220
  12.2 9.0 %copy-start.2 = (bf16[1,128,3072]{2,1,0:T(8,128)(2,1)S(1)}, bf16[1,128,3072]{2,1,0:T(8,128)(2,1)}, u32[]{:S(2)}) copy-start(bf16[1,128,3072]{2,1,0:T(8,128)(2,1)} %param.7) | copy-start | bytes 2359300
  19.6 6.4 %collective-permute-start.7 = (bf16[32,3072]{1,0:T(8,128)(2,1)S(1)}, bf16[32,3072]{1,0:T(8,128)(2,1)S(1)}, u32[]{:S(2)}, u32[]{:S(2)}) collective-permute-start(bf16[32,3072]{1,0:T(8,128)(2,1)S(1)} %collective-permute-done.3.near_ref), channel_id=1, source_target_pairs={{0,2},{2,0},{4,6},{6,4},{8,10},{10,8},{12,14},{14,12},{16,18},{18,... | collective-permute-start | bytes 589832 | tf_op jit(solution)/shard_map/ppermute | solution.py:220
  22.8 13.7 %collective-permute-start.4 = (bf16[64,3072]{1,0:T(8,128)(2,1)S(1)}, bf16[64,3072]{1,0:T(8,128)(2,1)S(1)}, u32[]{:S(2)}, u32[]{:S(2)}) collective-permute-start(bf16[64,3072]{1,0:T(8,128)(2,1)S(1)} %get-tuple-element.31), channel_id=1, source_target_pairs={{0,16},{2,18},{4,20},{6,22},{8,24},{10,26},{12,28},{14,30},{16,0},... | collective-permute-start | bytes 1179656 | tf_op jit(solution)/shard_map/ppermute | solution.py:220
  23.9 7.8 %collective-permute-start.6 = (bf16[32,3072]{1,0:T(8,128)(2,1)S(1)}, bf16[32,3072]{1,0:T(8,128)(2,1)S(1)}, u32[]{:S(2)}, u32[]{:S(2)}) collective-permute-start(bf16[32,3072]{1,0:T(8,128)(2,1)S(1)} %collective-permute-done.3.near_ref), channel_id=1, source_target_pairs={{0,4},{2,6},{4,0},{6,2},{8,12},{10,14},{12,8},{14,10},{16,20},{18,... | collective-permute-start | bytes 589832 | tf_op jit(solution)/shard_map/ppermute | solution.py:220
  25.6 10.4 %collective-permute-start.13 = (bf16[32,3072]{1,0:T(8,128)(2,1)S(1)}, bf16[32,3072]{1,0:T(8,128)(2,1)S(1)}, u32[]{:S(2)}, u32[]{:S(2)}) collective-permute-start(bf16[32,3072]{1,0:T(8,128)(2,1)S(1)} %collective-permute-done.1.near_ref), channel_id=1, source_target_pairs={{0,4},{2,6},{4,0},{6,2},{8,12},{10,14},{12,8},{14,10},{16,20},{18,... | collective-permute-start | bytes 589832 | tf_op jit(solution)/shard_map/ppermute | solution.py:220
  27.2 9.3 %collective-permute-start.8 = (bf16[32,3072]{1,0:T(8,128)(2,1)S(1)}, bf16[32,3072]{1,0:T(8,128)(2,1)S(1)}, u32[]{:S(2)}, u32[]{:S(2)}) collective-permute-start(bf16[32,3072]{1,0:T(8,128)(2,1)S(1)} %get-tuple-element.41), channel_id=1, source_target_pairs={{0,2},{2,0},{4,6},{6,4},{8,10},{10,8},{12,14},{14,12},{16,18},{18,... | collective-permute-start | bytes 589832 | tf_op jit(solution)/shard_map/ppermute | solution.py:220
  28.1 10.6 %collective-permute-start.9 = (bf16[32,3072]{1,0:T(8,128)(2,1)S(1)}, bf16[32,3072]{1,0:T(8,128)(2,1)S(1)}, u32[]{:S(2)}, u32[]{:S(2)}) collective-permute-start(bf16[32,3072]{1,0:T(8,128)(2,1)S(1)} %collective-permute-done.7.far_ref), channel_id=1, source_target_pairs={{0,4},{2,6},{4,0},{6,2},{8,12},{10,14},{12,8},{14,10},{16,20},{18,... | collective-permute-start | bytes 589832 | tf_op jit(solution)/shard_map/ppermute | solution.py:220
  31.8 13.6 %collective-permute-start.5 = (bf16[64,3072]{1,0:T(8,128)(2,1)S(1)}, bf16[64,3072]{1,0:T(8,128)(2,1)S(1)}, u32[]{:S(2)}, u32[]{:S(2)}) collective-permute-start(bf16[64,3072]{1,0:T(8,128)(2,1)S(1)} %get-tuple-element.32), channel_id=1, source_target_pairs={{0,16},{2,18},{4,20},{6,22},{8,24},{10,26},{12,28},{14,30},{16,0},... | collective-permute-start | bytes 1179656 | tf_op jit(solution)/shard_map/ppermute | solution.py:220
  36.0 7.6 %collective-permute-start.14 = (bf16[32,3072]{1,0:T(8,128)(2,1)S(1)}, bf16[32,3072]{1,0:T(8,128)(2,1)S(1)}, u32[]{:S(2)}, u32[]{:S(2)}) collective-permute-start(bf16[32,3072]{1,0:T(8,128)(2,1)S(1)} %collective-permute-done.13.near_ref), channel_id=1, source_target_pairs={{0,2},{2,0},{4,6},{6,4},{8,10},{10,8},{12,14},{14,12},{16,18},{18,... | collective-permute-start | bytes 589832 | tf_op jit(solution)/shard_map/ppermute | solution.py:220
  40.0 7.9 %collective-permute-start.11 = (bf16[32,3072]{1,0:T(8,128)(2,1)S(1)}, bf16[32,3072]{1,0:T(8,128)(2,1)S(1)}, u32[]{:S(2)}, u32[]{:S(2)}) collective-permute-start(bf16[32,3072]{1,0:T(8,128)(2,1)S(1)} %get-tuple-element.47), channel_id=1, source_target_pairs={{0,2},{2,0},{4,6},{6,4},{8,10},{10,8},{12,14},{14,12},{16,18},{18,... | collective-permute-start | bytes 589832 | tf_op jit(solution)/shard_map/ppermute | solution.py:220
  40.6 16.0 %collective-permute-start.10 = (bf16[32,3072]{1,0:T(8,128)(2,1)S(1)}, bf16[32,3072]{1,0:T(8,128)(2,1)S(1)}, u32[]{:S(2)}, u32[]{:S(2)}) collective-permute-start(bf16[32,3072]{1,0:T(8,128)(2,1)S(1)} %add_convert_fusion.2), channel_id=1, source_target_pairs={{0,8},{2,10},{4,12},{6,14},{8,0},{10,2},{12,4},{14,6},{16,24},{18,... | collective-permute-start | bytes 589832 | tf_op jit(solution)/shard_map/ppermute | solution.py:220
  41.9 3.5 %copy-start = (s32[1,128,2]{1,2,0:T(2,128)S(1)}, s32[1,128,2]{1,2,0:T(2,128)}, u32[]{:S(2)}) copy-start(s32[1,128,2]{1,2,0:T(2,128)} %param.12) | copy-start | bytes 3076
  41.9 3.4 %copy-start.1 = (f32[1,128,2]{1,2,0:T(2,128)S(1)}, f32[1,128,2]{1,2,0:T(2,128)}, u32[]{:S(2)}) copy-start(f32[1,128,2]{1,2,0:T(2,128)} %param.13) | copy-start | bytes 3076
  41.9 14.6 %collective-permute-start.17 = (bf16[32,3072]{1,0:T(8,128)(2,1)S(1)}, bf16[32,3072]{1,0:T(8,128)(2,1)S(1)}, u32[]{:S(2)}, u32[]{:S(2)}) collective-permute-start(bf16[32,3072]{1,0:T(8,128)(2,1)S(1)} %get-tuple-element.52), channel_id=1, source_target_pairs={{0,2},{2,0},{4,6},{6,4},{8,10},{10,8},{12,14},{14,12},{16,18},{18,... | collective-permute-start | bytes 589832 | tf_op jit(solution)/shard_map/ppermute | solution.py:220
  44.8 9.4 %collective-permute-start.15 = (bf16[32,3072]{1,0:T(8,128)(2,1)S(1)}, bf16[32,3072]{1,0:T(8,128)(2,1)S(1)}, u32[]{:S(2)}, u32[]{:S(2)}) collective-permute-start(bf16[32,3072]{1,0:T(8,128)(2,1)S(1)} %get-tuple-element.50), channel_id=1, source_target_pairs={{0,2},{2,0},{4,6},{6,4},{8,10},{10,8},{12,14},{14,12},{16,18},{18,... | collective-permute-start | bytes 589832 | tf_op jit(solution)/shard_map/ppermute | solution.py:220
  47.9 8.6 %collective-permute-start.12 = (bf16[32,3072]{1,0:T(8,128)(2,1)S(1)}, bf16[32,3072]{1,0:T(8,128)(2,1)S(1)}, u32[]{:S(2)}, u32[]{:S(2)}) collective-permute-start(bf16[32,3072]{1,0:T(8,128)(2,1)S(1)} %add_convert_fusion.1), channel_id=1, source_target_pairs={{0,12},{2,14},{4,8},{6,10},{8,4},{10,6},{12,0},{14,2},{16,28},{18,... | collective-permute-start | bytes 589832 | tf_op jit(solution)/shard_map/ppermute | solution.py:220
  54.3 6.0 %collective-permute-start.16 = (bf16[32,3072]{1,0:T(8,128)(2,1)S(1)}, bf16[32,3072]{1,0:T(8,128)(2,1)S(1)}, u32[]{:S(2)}, u32[]{:S(2)}) collective-permute-start(bf16[32,3072]{1,0:T(8,128)(2,1)S(1)} %add_convert_fusion), channel_id=1, source_target_pairs={{0,4},{2,6},{4,0},{6,2},{8,12},{10,14},{12,8},{14,10},{16,20},{18,... | collective-permute-start | bytes 589832 | tf_op jit(solution)/shard_map/ppermute | solution.py:220

commit v4 on v2

--- a/solution.py
+++ b/solution.py
@@ -113,7 +113,7 @@
 
 
 def base_kernel(experts, gain_ref, ids_ref, weights_ref, *refs):
-    block_refs, out_ref, table_ref = refs[:-2], refs[-2], refs[-1]
+    block_refs, (out_ref, table_ref, pick_ref) = refs[:-3], refs[-3:]
     ids, weights = ids_ref[...], weights_ref[...]
     count = ids.shape[1]
     zero = jnp.sum(jnp.where(ids >= experts, weights, 0.0), axis=0, keepdims=True)
@@ -132,7 +132,15 @@
     tables = []
     for e in range(experts):
         weight = jnp.sum(jnp.where(ids == e, weights, 0.0), axis=0, keepdims=True)
-        tables.append(slot_rows(ids, e) * weight)
+        slots = slot_rows(ids, e)
+        tables.append(slots * weight)
+        start, total = 0, 0.0
+        for ref in block_refs:
+            end = start + ref.shape[0]
+            part = slots[:, start:end].astype(jnp.bfloat16)
+            total += jnp.dot(part, ref[...], preferred_element_type=jnp.float32)
+            start = end
+        pick_ref[e * CAP:(e + 1) * CAP, :] = total.astype(jnp.bfloat16)
     terms = parts_of(jnp.concatenate(tables, axis=0).T)
     table_ref[...] = jnp.concatenate(terms + terms[:2], axis=1)
 
@@ -144,9 +152,10 @@
         out_shape=(
             jax.ShapeDtypeStruct((count, width), jnp.float32),
             jax.ShapeDtypeStruct((count, 5 * experts * CAP), jnp.bfloat16),
+            jax.ShapeDtypeStruct((experts * CAP, width), jnp.bfloat16),
         ),
         in_specs=[VMEM] * (3 + len(blocks)),
-        out_specs=(VMEM, VMEM),
+        out_specs=(VMEM, VMEM, VMEM),
         compiler_params=PARAMS,
         cost_estimate=pl.CostEstimate(
             flops=8 * count * width, bytes_accessed=6 * count * width, transcendentals=0
@@ -219,41 +228,45 @@
                 pairs.append((s * devices + d, (s + sections_on) % sections * devices + target))
         return lax.ppermute(value, ("section", "expert"), pairs)
 
+    def exchanged(rows):
+        rows = rows.reshape(experts, CAP, width)
+        return lax.all_to_all(
+            rows, "expert", split_axis=0, concat_axis=0, tiled=True, axis_index_groups=same_slice
+        ).reshape(experts * CAP, width)
+
     next_ids = moved(route_ids, -1, 0)[0]
     block, = loaded(blocks[0])
     picked = picked_rows(experts, jnp.swapaxes(next_ids, 0, 1), block)
     if experts > 1:
-        picked = lax.all_to_all(
-            picked.reshape(experts, CAP, width), "expert", split_axis=0, concat_axis=0,
-            tiled=True, axis_index_groups=same_slice,
-        ).reshape(experts * CAP, width)
+        picked = exchanged(picked)
     gate_t, up_t, down, gain = loaded(
         after(jnp.swapaxes(w_gate[0], 0, 1), picked), jnp.swapaxes(w_up[0], 0, 1), w_down[0], norm_gain
     )
 
     near, far = {}, {}
     near[2] = moved(picked, 1, 2)
-    near[0] = moved(picked, 1, 0)
+    near[1] = moved(picked, 1, 1)
     far[0] = moved(picked, 1, 0, 1)
-    far[2] = moved(after(near[2], near[0], gain), 0, 0, 1)
-    near[1] = moved(near[0], 0, 1)
-    near[3] = moved(after(near[2], far[0]), 0, 1)
+    far[2] = moved(after(near[2], gain), 0, 0, 1)
+    far[1] = moved(near[1], 0, 0, 1)
+    near[3] = moved(after(near[2], far[0], near[1]), 0, 1)
     far[3] = moved(far[2], 0, 1)
-    far[1] = moved(near[1], 0, 0, 1)
     pieces = 2
     size = token_count // pieces
     arrived = [
-        moved(after(blocks[0, i * size:(i + 1) * size], near[0], far[0], near[2]), 1, 0)
+        moved(after(blocks[0, i * size:(i + 1) * size], near[1], far[0], near[2]), 1, 0)
         for i in range(pieces)
     ]
-    base, table = based(
+    base, table, near[0] = based(
         experts, arrived, gain, jnp.swapaxes(route_ids[0], 0, 1),
         jnp.swapaxes(route_weights[0], 0, 1),
     )
 
+    if experts > 1:
+        near[0] = exchanged(near[0])
     own, other = {}, {}
     for k in (2, 3, 1, 0):
-        first = {2: (gain,), 3: (other.get(2), arrived[0]), 1: (own.get(3),), 0: (other.get(3), base)}[k]
+        first = {2: (gain,), 3: (other.get(2), arrived[0], far[1]), 1: (own.get(3),), 0: (own.get(1),)}[k]
         own[k], sent = mlp(after(near[k], *first), far[k], gain, gate_t, up_t, down)
         other[k] = moved(sent, 0, 0, 1)
     both = {
@@ -265,12 +278,7 @@
         early, moved(both[3], 0, 3), moved(after(both[1], early), 0, 1), other[0],
     ]
     if experts > 1:
-        summed = sum(back.astype(jnp.float32) for back in backs).reshape(experts, CAP, width)
-        summed = lax.all_to_all(
-            summed.astype(jnp.bfloat16), "expert", split_axis=0, concat_axis=0, tiled=True,
-            axis_index_groups=same_slice,
-        )
-        backs = [summed.reshape(experts * CAP, width)]
+        backs = [exchanged(sum(back.astype(jnp.float32) for back in backs).astype(jnp.bfloat16))]
     return ended(base, table, backs)[None]
 
 

time: 60.7 us -> 61.6 us (1.015)
  starting transfers between devices: 25.7 us -> 27.2 us
  waiting for transfers between devices: 23.3 us -> 22.3 us
    ppermute x18 -> x17, starting transfers between devices: 25.7 us -> 27.2 us  [moved(): return lax.ppermute(value, ('section', 'expert'), pairs)]
    ppermute x18 -> x17, waiting for transfers between devices: 23.3 us -> 22.3 us  [moved(): return lax.ppermute(value, ('section', 'expert'), pairs)]
  transfers between devices with their start and end apart: 18 -> 17, of which waited for: 13 -> 8; matrix products, arithmetic and copies ran while one was open for 0% -> 0% of each run, Pallas kernels for 15% -> 15%
where the time goes in v4:
time: 61.6 us; the launch traced here: 61.4 us
  starting transfers between devices  27.2 us (44%)
  waiting for transfers between devices  22.3 us (36%)
  Pallas kernels  11.5 us (19%)
    ppermute x17, starting transfers between devices, moved(): return lax.ppermute(value, ('section', 'expert'), pairs)  27.2 us
    ppermute x17, waiting for transfers between devices, moved(): return lax.ppermute(value, ('section', 'expert'), pairs)  22.3 us
    pallas_call x4, Pallas kernels, mlp(): pl.pallas_call(mlp_kernel, out_shape=(out, out), in_specs=[VMEM] * 6, out...  5.05 us
    pallas_call x2, Pallas kernels, loaded(): pl.pallas_call(functools.partial(load_kernel, len(arrays)), out_shape=tup...  3.23 us
    pallas_call x1, Pallas kernels, ended(): pl.pallas_call(functools.partial(end_kernel, columns), out_shape=jax.Shap...  1.88 us
  transfers between devices with their start and end apart: 17, of which 8 were waited for; matrix products, arithmetic and copies ran while one was open for 0% of the time, Pallas kernels for 15%

profile of v4, /device:TPU:0, one launch (start us, length us, event | category | flops | bytes accessed | tf_op | source)
XLA Modules:
  0.0 61.4 jit_solution(10016263349115435029)
XLA Ops:
  0.0 2.9 %collective-permute-start = (s32[1,128,2]{1,2,0:T(2,128)}, s32[1,128,2]{1,2,0:T(2,128)S(1)}, u32[]{:S(2)}, u32[]{:S(2)}) collective-permute-start(s32[1,128,2]{1,2,0:T(2,128)} %param.12), channel_id=1, source_target_pairs={{0,16},{2,18},{4,20},{6,22},{8,24},{10,26},{12,28},{14,30},{16,0},... | collective-permute-start | bytes 3080 | tf_op jit(solution)/shard_map/ppermute | solution.py:229
  2.9 1.1 %shard_map.73.block_ref = bf16[128,3072]{1,0:T(8,128)(2,1)S(1)} custom-call(bf16[128,3072]{1,0:T(8,128)(2,1)} %bitcast.25), custom_call_target="tpu_custom_call" | custom-call | bytes 6291456 | tf_op jit(solution)/shard_map/pallas_call | solution.py:33
  4.1 0.6 collective-permute-done
  4.7 0.4 shard_map.74
  5.1 4.1 %collective-permute-start.3 = (bf16[32,3072]{1,0:T(8,128)(2,1)S(1)}, bf16[32,3072]{1,0:T(8,128)(2,1)S(1)}, u32[]{:S(2)}, u32[]{:S(2)}) collective-permute-start(bf16[32,3072]{1,0:T(8,128)(2,1)S(1)} %shard_map.74), channel_id=1, source_target_pairs={{0,24},{2,26},{4,28},{6,30},{8,16},{10,18},{12,20},{14,22},{16,8},... | collective-permute-start | bytes 589832 | tf_op jit(solution)/shard_map/ppermute | solution.py:229
  9.2 1.5 %collective-permute-start.2 = (bf16[32,3072]{1,0:T(8,128)(2,1)S(1)}, bf16[32,3072]{1,0:T(8,128)(2,1)S(1)}, u32[]{:S(2)}, u32[]{:S(2)}) collective-permute-start(bf16[32,3072]{1,0:T(8,128)(2,1)S(1)} %shard_map.74), channel_id=1, source_target_pairs={{0,18},{2,16},{4,22},{6,20},{8,26},{10,24},{12,30},{14,28},{16,2},... | collective-permute-start | bytes 589832 | tf_op jit(solution)/shard_map/ppermute | solution.py:229
  10.7 2.5 %collective-permute-start.1 = (bf16[32,3072]{1,0:T(8,128)(2,1)S(1)}, bf16[32,3072]{1,0:T(8,128)(2,1)S(1)}, u32[]{:S(2)}, u32[]{:S(2)}) collective-permute-start(bf16[32,3072]{1,0:T(8,128)(2,1)S(1)} %shard_map.74), channel_id=1, source_target_pairs={{0,20},{2,22},{4,16},{6,18},{8,28},{10,30},{12,24},{14,26},{16,4},... | collective-permute-start | bytes 589832 | tf_op jit(solution)/shard_map/ppermute | solution.py:229
  13.2 0.0 copy-start.2
  13.2 2.1 %shard_map.75 = (bf16[192,3072]{1,0:T(8,128)(2,1)S(1)}, bf16[192,3072]{1,0:T(8,128)(2,1)S(1)}, bf16[192,3072]{1,0:T(8,128)(2,1)S(1)}, bf16[1,3072]{1,0:T(2,128)(2,1)S(1)}) custom-call(bf16[192,3072]{1,0:T(8,128)(2,1)} %bitcast.26, bf16[192,3072]{1,0:T(8,128)(2,1)} %bitcast.27, bf16[192,3072]{1,0:T(8,128)(2,1)} %bitcast.28, bf16[1,3072]{1,0:T(2,128)(2,1)} %refs_3_.1), custom_call_target="tpu_custom_call" | custom-call | bytes 6291456 | tf_op jit(solution)/shard_map/pallas_call | solution.py:33
  15.3 2.0 %collective-permute-done.3.near_ref = bf16[32,3072]{1,0:T(8,128)(2,1)S(1)} collective-permute-done((bf16[32,3072]{1,0:T(8,128)(2,1)S(1)}, bf16[32,3072]{1,0:T(8,128)(2,1)S(1)}, u32[]{:S(2)}, u32[]{:S(2)}) %collective-permute-start.3) | collective-permute-done | bytes 196640 | tf_op jit(solution)/shard_map/ppermute | solution.py:229
  17.2 1.5 %collective-permute-start.7 = (bf16[32,3072]{1,0:T(8,128)(2,1)S(1)}, bf16[32,3072]{1,0:T(8,128)(2,1)S(1)}, u32[]{:S(2)}, u32[]{:S(2)}) collective-permute-start(bf16[32,3072]{1,0:T(8,128)(2,1)S(1)} %collective-permute-done.3.near_ref), channel_id=1, source_target_pairs={{0,2},{2,0},{4,6},{6,4},{8,10},{10,8},{12,14},{14,12},{16,18},{18,... | collective-permute-start | bytes 589832 | tf_op jit(solution)/shard_map/ppermute | solution.py:229
  18.7 0.0 copy-done.2
  18.7 0.1 slice_bitcast_fusion
  18.8 3.9 %collective-permute-done.2.far_ref = bf16[32,3072]{1,0:T(8,128)(2,1)S(1)} collective-permute-done((bf16[32,3072]{1,0:T(8,128)(2,1)S(1)}, bf16[32,3072]{1,0:T(8,128)(2,1)S(1)}, u32[]{:S(2)}, u32[]{:S(2)}) %collective-permute-start.2) | collective-permute-done | bytes 196640 | tf_op jit(solution)/shard_map/ppermute | solution.py:229
  22.7 0.0 collective-permute-done.1.near_ref
  22.7 1.2 %collective-permute-start.4 = (bf16[64,3072]{1,0:T(8,128)(2,1)S(1)}, bf16[64,3072]{1,0:T(8,128)(2,1)S(1)}, u32[]{:S(2)}, u32[]{:S(2)}) collective-permute-start(bf16[64,3072]{1,0:T(8,128)(2,1)S(1)} %get-tuple-element.31), channel_id=1, source_target_pairs={{0,16},{2,18},{4,20},{6,22},{8,24},{10,26},{12,28},{14,30},{16,0},... | collective-permute-start | bytes 1179656 | tf_op jit(solution)/shard_map/ppermute | solution.py:229
  23.9 1.7 %collective-permute-start.6 = (bf16[32,3072]{1,0:T(8,128)(2,1)S(1)}, bf16[32,3072]{1,0:T(8,128)(2,1)S(1)}, u32[]{:S(2)}, u32[]{:S(2)}) collective-permute-start(bf16[32,3072]{1,0:T(8,128)(2,1)S(1)} %collective-permute-done.3.near_ref), channel_id=1, source_target_pairs={{0,4},{2,6},{4,0},{6,2},{8,12},{10,14},{12,8},{14,10},{16,20},{18,... | collective-permute-start | bytes 589832 | tf_op jit(solution)/shard_map/ppermute | solution.py:229
  25.6 0.5 collective-permute-start.9
  26.1 0.0 collective-permute-done.7.far_ref
  26.1 1.3 %shard_map.77 = (bf16[32,3072]{1,0:T(8,128)(2,1)S(1)}, bf16[32,3072]{1,0:T(8,128)(2,1)S(1)}) custom-call(bf16[32,3072]{1,0:T(8,128)(2,1)S(1)} %collective-permute-done.3.near_ref, bf16[32,3072]{1,0:T(8,128)(2,1)S(1)} %collective-permute-done.7.far_ref, bf16[1,3072]{1,0:T(2,128)(2,1)S(1)} %get-tuple-element.30.gain_ref, ...), custom_call_target="tpu_custom_call" | custom-call | flops 226492416 | bytes 3538944 | tf_op jit(solution)/shard_map/pallas_call | solution.py:95
  27.4 1.6 %collective-permute-start.8 = (bf16[32,3072]{1,0:T(8,128)(2,1)S(1)}, bf16[32,3072]{1,0:T(8,128)(2,1)S(1)}, u32[]{:S(2)}, u32[]{:S(2)}) collective-permute-start(bf16[32,3072]{1,0:T(8,128)(2,1)S(1)} %get-tuple-element.41), channel_id=1, source_target_pairs={{0,2},{2,0},{4,6},{6,4},{8,10},{10,8},{12,14},{14,12},{16,18},{18,... | collective-permute-start | bytes 589832 | tf_op jit(solution)/shard_map/ppermute | solution.py:229
  29.0 1.3 %collective-permute-start.10 = (bf16[32,3072]{1,0:T(8,128)(2,1)S(1)}, bf16[32,3072]{1,0:T(8,128)(2,1)S(1)}, u32[]{:S(2)}, u32[]{:S(2)}) collective-permute-start(bf16[32,3072]{1,0:T(8,128)(2,1)S(1)} %collective-permute-done.7.far_ref), channel_id=1, source_target_pairs={{0,4},{2,6},{4,0},{6,2},{8,12},{10,14},{12,8},{14,10},{16,20},{18,... | collective-permute-start | bytes 589832 | tf_op jit(solution)/shard_map/ppermute | solution.py:229
  30.2 0.0 collective-permute-done.6.near_ref
  30.3 1.4 %collective-permute-start.5 = (bf16[64,3072]{1,0:T(8,128)(2,1)S(1)}, bf16[64,3072]{1,0:T(8,128)(2,1)S(1)}, u32[]{:S(2)}, u32[]{:S(2)}) collective-permute-start(bf16[64,3072]{1,0:T(8,128)(2,1)S(1)} %get-tuple-element.32), channel_id=1, source_target_pairs={{0,16},{2,18},{4,20},{6,22},{8,24},{10,26},{12,28},{14,30},{16,0},... | collective-permute-start | bytes 1179656 | tf_op jit(solution)/shard_map/ppermute | solution.py:229
  31.6 1.8 %collective-permute-done.9.far_ref = bf16[32,3072]{1,0:T(8,128)(2,1)S(1)} collective-permute-done((bf16[32,3072]{1,0:T(8,128)(2,1)S(1)}, bf16[32,3072]{1,0:T(8,128)(2,1)S(1)}, u32[]{:S(2)}, u32[]{:S(2)}) %collective-permute-start.9) | collective-permute-done | bytes 196640 | tf_op jit(solution)/shard_map/ppermute | solution.py:229
  33.5 0.0 collective-permute-done.4.refs_0_
  33.5 2.4 %collective-permute-done.8 = bf16[32,3072]{1,0:T(8,128)(2,1)S(1)} collective-permute-done((bf16[32,3072]{1,0:T(8,128)(2,1)S(1)}, bf16[32,3072]{1,0:T(8,128)(2,1)S(1)}, u32[]{:S(2)}, u32[]{:S(2)}) %collective-permute-start.8) | collective-permute-done | bytes 196640 | tf_op jit(solution)/shard_map/ppermute | solution.py:229
  35.9 0.0 collective-permute-done.10.far_ref
  35.9 1.3 %shard_map.78 = (bf16[32,3072]{1,0:T(8,128)(2,1)S(1)}, bf16[32,3072]{1,0:T(8,128)(2,1)S(1)}) custom-call(bf16[32,3072]{1,0:T(8,128)(2,1)S(1)} %collective-permute-done.6.near_ref, bf16[32,3072]{1,0:T(8,128)(2,1)S(1)} %collective-permute-done.10.far_ref, bf16[1,3072]{1,0:T(2,128)(2,1)S(1)} %get-tuple-element.30.gain_ref, ...), custom_call_target="tpu_custom_call" | custom-call | flops 226492416 | bytes 3538944 | tf_op jit(solution)/shard_map/pallas_call | solution.py:95
  37.2 0.6 collective-permute-start.12
  37.8 1.7 %collective-permute-start.11 = (bf16[32,3072]{1,0:T(8,128)(2,1)S(1)}, bf16[32,3072]{1,0:T(8,128)(2,1)S(1)}, u32[]{:S(2)}, u32[]{:S(2)}) collective-permute-start(bf16[32,3072]{1,0:T(8,128)(2,1)S(1)} %add_convert_fusion.2), channel_id=1, source_target_pairs={{0,8},{2,10},{4,12},{6,14},{8,0},{10,2},{12,4},{14,6},{16,24},{18,... | collective-permute-start | bytes 589832 | tf_op jit(solution)/shard_map/ppermute | solution.py:229
  39.4 1.3 %shard_map.79 = (bf16[32,3072]{1,0:T(8,128)(2,1)S(1)}, bf16[32,3072]{1,0:T(8,128)(2,1)S(1)}) custom-call(bf16[32,3072]{1,0:T(8,128)(2,1)S(1)} %collective-permute-done.1.near_ref, bf16[32,3072]{1,0:T(8,128)(2,1)S(1)} %collective-permute-done.9.far_ref, bf16[1,3072]{1,0:T(2,128)(2,1)S(1)} %get-tuple-element.30.gain_ref, ...), custom_call_target="tpu_custom_call" | custom-call | flops 226492416 | bytes 3538944 | tf_op jit(solution)/shard_map/pallas_call | solution.py:95
  40.7 1.6 %collective-permute-start.14 = (bf16[32,3072]{1,0:T(8,128)(2,1)S(1)}, bf16[32,3072]{1,0:T(8,128)(2,1)S(1)}, u32[]{:S(2)}, u32[]{:S(2)}) collective-permute-start(bf16[32,3072]{1,0:T(8,128)(2,1)S(1)} %get-tuple-element.50), channel_id=1, source_target_pairs={{0,2},{2,0},{4,6},{6,4},{8,10},{10,8},{12,14},{14,12},{16,18},{18,... | collective-permute-start | bytes 589832 | tf_op jit(solution)/shard_map/ppermute | solution.py:229
  42.3 0.0 collective-permute-done.5.refs_1_
  42.3 0.0 copy-done
  42.3 0.0 copy-done.1
  42.3 1.0 %shard_map.76 = (f32[128,3072]{1,0:T(8,128)S(1)}, bf16[128,160]{1,0:T(8,128)(2,1)S(1)}, bf16[32,3072]{1,0:T(8,128)(2,1)S(1)}) custom-call(bf16[1,3072]{1,0:T(2,128)(2,1)S(1)} %get-tuple-element.30.gain_ref, s32[2,128]{1,0:T(2,128)S(1)} %bitcast.22, f32[2,128]{1,0:T(2,128)S(1)} %bitcast.23, bf16[64,3072]{1,0:T(8,128)(2,1)S(1)} %collective-permute-done.4.refs_0_, ...), custom_call_target="tpu_custom_call" | custom-call | flops 3145728 | bytes 2359296 | tf_op jit(solution)/shard_map/pallas_call | solution.py:150
  43.3 1.3 %shard_map.80 = (bf16[32,3072]{1,0:T(8,128)(2,1)S(1)}, bf16[32,3072]{1,0:T(8,128)(2,1)S(1)}) custom-call(bf16[32,3072]{1,0:T(8,128)(2,1)S(1)} %get-tuple-element.46.near_ref, bf16[32,3072]{1,0:T(8,128)(2,1)S(1)} %collective-permute-done.2.far_ref, bf16[1,3072]{1,0:T(2,128)(2,1)S(1)} %get-tuple-element.30.gain_ref, ...), custom_call_target="tpu_custom_call" | custom-call | flops 226492416 | bytes 3538944 | tf_op jit(solution)/shard_map/pallas_call | solution.py:95
  44.6 0.6 collective-permute-start.16
  45.1 0.0 collective-permute-done.12
  45.2 2.6 %collective-permute-start.13 = (bf16[32,3072]{1,0:T(8,128)(2,1)S(1)}, bf16[32,3072]{1,0:T(8,128)(2,1)S(1)}, u32[]{:S(2)}, u32[]{:S(2)}) collective-permute-start(bf16[32,3072]{1,0:T(8,128)(2,1)S(1)} %add_convert_fusion.1), channel_id=1, source_target_pairs={{0,12},{2,14},{4,8},{6,10},{8,4},{10,6},{12,0},{14,2},{16,28},{18,... | collective-permute-start | bytes 589832 | tf_op jit(solution)/shard_map/ppermute | solution.py:229
  47.8 0.9 %collective-permute-done.14 = bf16[32,3072]{1,0:T(8,128)(2,1)S(1)} collective-permute-done((bf16[32,3072]{1,0:T(8,128)(2,1)S(1)}, bf16[32,3072]{1,0:T(8,128)(2,1)S(1)}, u32[]{:S(2)}, u32[]{:S(2)}) %collective-permute-start.14) | collective-permute-done | bytes 196640 | tf_op jit(solution)/shard_map/ppermute | solution.py:229
  48.7 5.1 %collective-permute-done.11.right_ref = bf16[32,3072]{1,0:T(8,128)(2,1)S(1)} collective-permute-done((bf16[32,3072]{1,0:T(8,128)(2,1)S(1)}, bf16[32,3072]{1,0:T(8,128)(2,1)S(1)}, u32[]{:S(2)}, u32[]{:S(2)}) %collective-permute-start.11) | collective-permute-done | bytes 196640 | tf_op jit(solution)/shard_map/ppermute | solution.py:229
  53.8 0.1 collective-permute-start.15
  53.9 0.0 collective-permute-done.16.refs_3_
  53.9 0.0 collective-permute-done.13.refs_1_
  53.9 5.6 %collective-permute-done.15.refs_2_ = bf16[32,3072]{1,0:T(8,128)(2,1)S(1)} collective-permute-done((bf16[32,3072]{1,0:T(8,128)(2,1)S(1)}, bf16[32,3072]{1,0:T(8,128)(2,1)S(1)}, u32[]{:S(2)}, u32[]{:S(2)}) %collective-permute-start.15) | collective-permute-done | bytes 196640 | tf_op jit(solution)/shard_map/ppermute | solution.py:229
  59.5 1.9 %shard_map.82 = bf16[128,3072]{1,0:T(8,128)(2,1)} custom-call(f32[128,3072]{1,0:T(8,128)S(1)} %get-tuple-element.33.base_ref, bf16[128,160]{1,0:T(8,128)(2,1)S(1)} %get-tuple-element.34.table_ref, f32[32,3072]{1,0:T(8,128)S(1)} %shard_map.81.refs_0_, bf16[32,3072]{1,0:T(8,128)(2,1)S(1)} %collective-permute-done.13.refs_1_, ...), custom_call_target="tpu_custom_call" | custom-call | flops 100663296 | bytes 2359296 | tf_op jit(solution)/shard_map/pallas_call | solution.py:182
  (6 shorter events, 0.2 us)
Async XLA Ops:
  0.0 4.7 %collective-permute-start = (s32[1,128,2]{1,2,0:T(2,128)}, s32[1,128,2]{1,2,0:T(2,128)S(1)}, u32[]{:S(2)}, u32[]{:S(2)}) collective-permute-start(s32[1,128,2]{1,2,0:T(2,128)} %param.12), channel_id=1, source_target_pairs={{0,16},{2,18},{4,20},{6,22},{8,24},{10,26},{12,28},{14,30},{16,0},... | collective-permute-start | bytes 3080 | tf_op jit(solution)/shard_map/ppermute | solution.py:229
  5.1 12.2 %collective-permute-start.3 = (bf16[32,3072]{1,0:T(8,128)(2,1)S(1)}, bf16[32,3072]{1,0:T(8,128)(2,1)S(1)}, u32[]{:S(2)}, u32[]{:S(2)}) collective-permute-start(bf16[32,3072]{1,0:T(8,128)(2,1)S(1)} %shard_map.74), channel_id=1, source_target_pairs={{0,24},{2,26},{4,28},{6,30},{8,16},{10,18},{12,20},{14,22},{16,8},... | collective-permute-start | bytes 589832 | tf_op jit(solution)/shard_map/ppermute | solution.py:229
  9.2 13.5 %collective-permute-start.2 = (bf16[32,3072]{1,0:T(8,128)(2,1)S(1)}, bf16[32,3072]{1,0:T(8,128)(2,1)S(1)}, u32[]{:S(2)}, u32[]{:S(2)}) collective-permute-start(bf16[32,3072]{1,0:T(8,128)(2,1)S(1)} %shard_map.74), channel_id=1, source_target_pairs={{0,18},{2,16},{4,22},{6,20},{8,26},{10,24},{12,30},{14,28},{16,2},... | collective-permute-start | bytes 589832 | tf_op jit(solution)/shard_map/ppermute | solution.py:229
  10.7 12.0 %collective-permute-start.1 = (bf16[32,3072]{1,0:T(8,128)(2,1)S(1)}, bf16[32,3072]{1,0:T(8,128)(2,1)S(1)}, u32[]{:S(2)}, u32[]{:S(2)}) collective-permute-start(bf16[32,3072]{1,0:T(8,128)(2,1)S(1)} %shard_map.74), channel_id=1, source_target_pairs={{0,20},{2,22},{4,16},{6,18},{8,28},{10,30},{12,24},{14,26},{16,4},... | collective-permute-start | bytes 589832 | tf_op jit(solution)/shard_map/ppermute | solution.py:229
  13.2 5.6 %copy-start.2 = (bf16[1,128,3072]{2,1,0:T(8,128)(2,1)S(1)}, bf16[1,128,3072]{2,1,0:T(8,128)(2,1)}, u32[]{:S(2)}) copy-start(bf16[1,128,3072]{2,1,0:T(8,128)(2,1)} %param.7) | copy-start | bytes 2359300
  17.2 8.9 %collective-permute-start.7 = (bf16[32,3072]{1,0:T(8,128)(2,1)S(1)}, bf16[32,3072]{1,0:T(8,128)(2,1)S(1)}, u32[]{:S(2)}, u32[]{:S(2)}) collective-permute-start(bf16[32,3072]{1,0:T(8,128)(2,1)S(1)} %collective-permute-done.3.near_ref), channel_id=1, source_target_pairs={{0,2},{2,0},{4,6},{6,4},{8,10},{10,8},{12,14},{14,12},{16,18},{18,... | collective-permute-start | bytes 589832 | tf_op jit(solution)/shard_map/ppermute | solution.py:229
  22.7 10.7 %collective-permute-start.4 = (bf16[64,3072]{1,0:T(8,128)(2,1)S(1)}, bf16[64,3072]{1,0:T(8,128)(2,1)S(1)}, u32[]{:S(2)}, u32[]{:S(2)}) collective-permute-start(bf16[64,3072]{1,0:T(8,128)(2,1)S(1)} %get-tuple-element.31), channel_id=1, source_target_pairs={{0,16},{2,18},{4,20},{6,22},{8,24},{10,26},{12,28},{14,30},{16,0},... | collective-permute-start | bytes 1179656 | tf_op jit(solution)/shard_map/ppermute | solution.py:229
  23.9 6.3 %collective-permute-start.6 = (bf16[32,3072]{1,0:T(8,128)(2,1)S(1)}, bf16[32,3072]{1,0:T(8,128)(2,1)S(1)}, u32[]{:S(2)}, u32[]{:S(2)}) collective-permute-start(bf16[32,3072]{1,0:T(8,128)(2,1)S(1)} %collective-permute-done.3.near_ref), channel_id=1, source_target_pairs={{0,4},{2,6},{4,0},{6,2},{8,12},{10,14},{12,8},{14,10},{16,20},{18,... | collective-permute-start | bytes 589832 | tf_op jit(solution)/shard_map/ppermute | solution.py:229
  25.6 7.8 %collective-permute-start.9 = (bf16[32,3072]{1,0:T(8,128)(2,1)S(1)}, bf16[32,3072]{1,0:T(8,128)(2,1)S(1)}, u32[]{:S(2)}, u32[]{:S(2)}) collective-permute-start(bf16[32,3072]{1,0:T(8,128)(2,1)S(1)} %collective-permute-done.1.near_ref), channel_id=1, source_target_pairs={{0,2},{2,0},{4,6},{6,4},{8,10},{10,8},{12,14},{14,12},{16,18},{18,... | collective-permute-start | bytes 589832 | tf_op jit(solution)/shard_map/ppermute | solution.py:229
  27.4 8.5 %collective-permute-start.8 = (bf16[32,3072]{1,0:T(8,128)(2,1)S(1)}, bf16[32,3072]{1,0:T(8,128)(2,1)S(1)}, u32[]{:S(2)}, u32[]{:S(2)}) collective-permute-start(bf16[32,3072]{1,0:T(8,128)(2,1)S(1)} %get-tuple-element.41), channel_id=1, source_target_pairs={{0,2},{2,0},{4,6},{6,4},{8,10},{10,8},{12,14},{14,12},{16,18},{18,... | collective-permute-start | bytes 589832 | tf_op jit(solution)/shard_map/ppermute | solution.py:229
  29.0 6.9 %collective-permute-start.10 = (bf16[32,3072]{1,0:T(8,128)(2,1)S(1)}, bf16[32,3072]{1,0:T(8,128)(2,1)S(1)}, u32[]{:S(2)}, u32[]{:S(2)}) collective-permute-start(bf16[32,3072]{1,0:T(8,128)(2,1)S(1)} %collective-permute-done.7.far_ref), channel_id=1, source_target_pairs={{0,4},{2,6},{4,0},{6,2},{8,12},{10,14},{12,8},{14,10},{16,20},{18,... | collective-permute-start | bytes 589832 | tf_op jit(solution)/shard_map/ppermute | solution.py:229
  30.3 12.0 %collective-permute-start.5 = (bf16[64,3072]{1,0:T(8,128)(2,1)S(1)}, bf16[64,3072]{1,0:T(8,128)(2,1)S(1)}, u32[]{:S(2)}, u32[]{:S(2)}) collective-permute-start(bf16[64,3072]{1,0:T(8,128)(2,1)S(1)} %get-tuple-element.32), channel_id=1, source_target_pairs={{0,16},{2,18},{4,20},{6,22},{8,24},{10,26},{12,28},{14,30},{16,0},... | collective-permute-start | bytes 1179656 | tf_op jit(solution)/shard_map/ppermute | solution.py:229
  37.2 8.0 %collective-permute-start.12 = (bf16[32,3072]{1,0:T(8,128)(2,1)S(1)}, bf16[32,3072]{1,0:T(8,128)(2,1)S(1)}, u32[]{:S(2)}, u32[]{:S(2)}) collective-permute-start(bf16[32,3072]{1,0:T(8,128)(2,1)S(1)} %get-tuple-element.49), channel_id=1, source_target_pairs={{0,2},{2,0},{4,6},{6,4},{8,10},{10,8},{12,14},{14,12},{16,18},{18,... | collective-permute-start | bytes 589832 | tf_op jit(solution)/shard_map/ppermute | solution.py:229
  37.8 16.0 %collective-permute-start.11 = (bf16[32,3072]{1,0:T(8,128)(2,1)S(1)}, bf16[32,3072]{1,0:T(8,128)(2,1)S(1)}, u32[]{:S(2)}, u32[]{:S(2)}) collective-permute-start(bf16[32,3072]{1,0:T(8,128)(2,1)S(1)} %add_convert_fusion.2), channel_id=1, source_target_pairs={{0,8},{2,10},{4,12},{6,14},{8,0},{10,2},{12,4},{14,6},{16,24},{18,... | collective-permute-start | bytes 589832 | tf_op jit(solution)/shard_map/ppermute | solution.py:229
  39.4 2.8 %copy-start = (s32[1,128,2]{1,2,0:T(2,128)S(1)}, s32[1,128,2]{1,2,0:T(2,128)}, u32[]{:S(2)}) copy-start(s32[1,128,2]{1,2,0:T(2,128)} %param.12) | copy-start | bytes 3076
  39.4 2.8 %copy-start.1 = (f32[1,128,2]{1,2,0:T(2,128)S(1)}, f32[1,128,2]{1,2,0:T(2,128)}, u32[]{:S(2)}) copy-start(f32[1,128,2]{1,2,0:T(2,128)} %param.13) | copy-start | bytes 3076
  40.7 7.9 %collective-permute-start.14 = (bf16[32,3072]{1,0:T(8,128)(2,1)S(1)}, bf16[32,3072]{1,0:T(8,128)(2,1)S(1)}, u32[]{:S(2)}, u32[]{:S(2)}) collective-permute-start(bf16[32,3072]{1,0:T(8,128)(2,1)S(1)} %get-tuple-element.50), channel_id=1, source_target_pairs={{0,2},{2,0},{4,6},{6,4},{8,10},{10,8},{12,14},{14,12},{16,18},{18,... | collective-permute-start | bytes 589832 | tf_op jit(solution)/shard_map/ppermute | solution.py:229
  44.6 9.3 %collective-permute-start.16 = (bf16[32,3072]{1,0:T(8,128)(2,1)S(1)}, bf16[32,3072]{1,0:T(8,128)(2,1)S(1)}, u32[]{:S(2)}, u32[]{:S(2)}) collective-permute-start(bf16[32,3072]{1,0:T(8,128)(2,1)S(1)} %get-tuple-element.52), channel_id=1, source_target_pairs={{0,2},{2,0},{4,6},{6,4},{8,10},{10,8},{12,14},{14,12},{16,18},{18,... | collective-permute-start | bytes 589832 | tf_op jit(solution)/shard_map/ppermute | solution.py:229
  45.2 8.7 %collective-permute-start.13 = (bf16[32,3072]{1,0:T(8,128)(2,1)S(1)}, bf16[32,3072]{1,0:T(8,128)(2,1)S(1)}, u32[]{:S(2)}, u32[]{:S(2)}) collective-permute-start(bf16[32,3072]{1,0:T(8,128)(2,1)S(1)} %add_convert_fusion.1), channel_id=1, source_target_pairs={{0,12},{2,14},{4,8},{6,10},{8,4},{10,6},{12,0},{14,2},{16,28},{18,... | collective-permute-start | bytes 589832 | tf_op jit(solution)/shard_map/ppermute | solution.py:229
  53.8 5.7 %collective-permute-start.15 = (bf16[32,3072]{1,0:T(8,128)(2,1)S(1)}, bf16[32,3072]{1,0:T(8,128)(2,1)S(1)}, u32[]{:S(2)}, u32[]{:S(2)}) collective-permute-start(bf16[32,3072]{1,0:T(8,128)(2,1)S(1)} %add_convert_fusion), channel_id=1, source_target_pairs={{0,4},{2,6},{4,0},{6,2},{8,12},{10,14},{12,8},{14,10},{16,20},{18,... | collective-permute-start | bytes 589832 | tf_op jit(solution)/shard_map/ppermute | solution.py:229

commit v5 on v4

--- a/solution.py
+++ b/solution.py
@@ -244,17 +244,16 @@
     )
 
     near, far = {}, {}
+    far[0] = moved(picked, 1, 0, 1)
     near[2] = moved(picked, 1, 2)
+    far[2] = moved(after(near[2], far[0], gain), 0, 0, 1)
+    near[3] = moved(near[2], 0, 1)
+    far[3] = moved(far[2], 0, 1)
     near[1] = moved(picked, 1, 1)
-    far[0] = moved(picked, 1, 0, 1)
-    far[2] = moved(after(near[2], gain), 0, 0, 1)
-    far[1] = moved(near[1], 0, 0, 1)
-    near[3] = moved(after(near[2], far[0], near[1]), 0, 1)
-    far[3] = moved(far[2], 0, 1)
     pieces = 2
     size = token_count // pieces
     arrived = [
-        moved(after(blocks[0, i * size:(i + 1) * size], near[1], far[0], near[2]), 1, 0)
+        moved(after(blocks[0, i * size:(i + 1) * size], near[1], near[2]), 1, 0)
         for i in range(pieces)
     ]
     base, table, near[0] = based(
@@ -266,7 +265,9 @@
         near[0] = exchanged(near[0])
     own, other = {}, {}
     for k in (2, 3, 1, 0):
-        first = {2: (gain,), 3: (other.get(2), arrived[0], far[1]), 1: (own.get(3),), 0: (own.get(1),)}[k]
+        first = {2: (near[3],), 3: (other.get(2), arrived[0]), 1: (own.get(3),), 0: (own.get(1),)}[k]
+        if k == 3:
+            far[1] = moved(after(near[1], own[2]), 0, 0, 1)
         own[k], sent = mlp(after(near[k], *first), far[k], gain, gate_t, up_t, down)
         other[k] = moved(sent, 0, 0, 1)
     both = {

time: 61.6 us -> 59.9 us (0.972)
  waiting for transfers between devices: 22.3 us -> 17.4 us
  starting transfers between devices: 27.2 us -> 30.5 us
    ppermute x17, waiting for transfers between devices: 22.3 us -> 17.4 us  [moved(): return lax.ppermute(value, ('section', 'expert'), pairs)]
    ppermute x17, starting transfers between devices: 27.2 us -> 30.5 us  [moved(): return lax.ppermute(value, ('section', 'expert'), pairs)]
  transfers between devices with their start and end apart: 17 -> 17, of which waited for: 8 -> 7; matrix products, arithmetic and copies ran while one was open for 0% -> 0% of each run, Pallas kernels for 15% -> 16%
where the time goes in v5:
time: 59.9 us; the launch traced here: 59.8 us
  starting transfers between devices  30.5 us (51%)
  waiting for transfers between devices  17.4 us (29%)
  Pallas kernels  11.5 us (19%)
    ppermute x17, starting transfers between devices, moved(): return lax.ppermute(value, ('section', 'expert'), pairs)  30.5 us
    ppermute x17, waiting for transfers between devices, moved(): return lax.ppermute(value, ('section', 'expert'), pairs)  17.4 us
    pallas_call x4, Pallas kernels, mlp(): pl.pallas_call(mlp_kernel, out_shape=(out, out), in_specs=[VMEM] * 6, out...  5.05 us
    pallas_call x2, Pallas kernels, loaded(): pl.pallas_call(functools.partial(load_kernel, len(arrays)), out_shape=tup...  3.23 us
    pallas_call x1, Pallas kernels, ended(): pl.pallas_call(functools.partial(end_kernel, columns), out_shape=jax.Shap...  1.88 us
  transfers between devices with their start and end apart: 17, of which 7 were waited for; matrix products, arithmetic and copies ran while one was open for 0% of the time, Pallas kernels for 16%

profile of v5, /device:TPU:0, one launch (start us, length us, event | category | flops | bytes accessed | tf_op | source)
XLA Modules:
  0.0 59.8 jit_solution(13725893351603948612)
XLA Ops:
  0.0 2.9 %collective-permute-start = (s32[1,128,2]{1,2,0:T(2,128)}, s32[1,128,2]{1,2,0:T(2,128)S(1)}, u32[]{:S(2)}, u32[]{:S(2)}) collective-permute-start(s32[1,128,2]{1,2,0:T(2,128)} %param.12), channel_id=1, source_target_pairs={{0,16},{2,18},{4,20},{6,22},{8,24},{10,26},{12,28},{14,30},{16,0},... | collective-permute-start | bytes 3080 | tf_op jit(solution)/shard_map/ppermute | solution.py:229
  2.9 1.1 %shard_map.73.block_ref = bf16[128,3072]{1,0:T(8,128)(2,1)S(1)} custom-call(bf16[128,3072]{1,0:T(8,128)(2,1)} %bitcast.25), custom_call_target="tpu_custom_call" | custom-call | bytes 6291456 | tf_op jit(solution)/shard_map/pallas_call | solution.py:33
  4.1 0.6 %collective-permute-done = s32[1,128,2]{1,2,0:T(2,128)S(1)} collective-permute-done((s32[1,128,2]{1,2,0:T(2,128)}, s32[1,128,2]{1,2,0:T(2,128)S(1)}, u32[]{:S(2)}, u32[]{:S(2)}) %collective-permute-start) | collective-permute-done | bytes 1056 | tf_op jit(solution)/shard_map/ppermute | solution.py:229
  4.7 0.4 shard_map.74
  5.1 3.0 %collective-permute-start.6 = (bf16[32,3072]{1,0:T(8,128)(2,1)S(1)}, bf16[32,3072]{1,0:T(8,128)(2,1)S(1)}, u32[]{:S(2)}, u32[]{:S(2)}) collective-permute-start(bf16[32,3072]{1,0:T(8,128)(2,1)S(1)} %shard_map.74), channel_id=1, source_target_pairs={{0,18},{2,16},{4,22},{6,20},{8,26},{10,24},{12,30},{14,28},{16,2},... | collective-permute-start | bytes 589832 | tf_op jit(solution)/shard_map/ppermute | solution.py:229
  8.1 2.6 %collective-permute-start.2 = (bf16[32,3072]{1,0:T(8,128)(2,1)S(1)}, bf16[32,3072]{1,0:T(8,128)(2,1)S(1)}, u32[]{:S(2)}, u32[]{:S(2)}) collective-permute-start(bf16[32,3072]{1,0:T(8,128)(2,1)S(1)} %shard_map.74), channel_id=1, source_target_pairs={{0,24},{2,26},{4,28},{6,30},{8,16},{10,18},{12,20},{14,22},{16,8},... | collective-permute-start | bytes 589832 | tf_op jit(solution)/shard_map/ppermute | solution.py:229
  10.7 2.5 %collective-permute-start.1 = (bf16[32,3072]{1,0:T(8,128)(2,1)S(1)}, bf16[32,3072]{1,0:T(8,128)(2,1)S(1)}, u32[]{:S(2)}, u32[]{:S(2)}) collective-permute-start(bf16[32,3072]{1,0:T(8,128)(2,1)S(1)} %shard_map.74), channel_id=1, source_target_pairs={{0,20},{2,22},{4,16},{6,18},{8,28},{10,30},{12,24},{14,26},{16,4},... | collective-permute-start | bytes 589832 | tf_op jit(solution)/shard_map/ppermute | solution.py:229
  13.2 0.0 copy-start.2
  13.2 2.1 %shard_map.75 = (bf16[192,3072]{1,0:T(8,128)(2,1)S(1)}, bf16[192,3072]{1,0:T(8,128)(2,1)S(1)}, bf16[192,3072]{1,0:T(8,128)(2,1)S(1)}, bf16[1,3072]{1,0:T(2,128)(2,1)S(1)}) custom-call(bf16[192,3072]{1,0:T(8,128)(2,1)} %bitcast.26, bf16[192,3072]{1,0:T(8,128)(2,1)} %bitcast.27, bf16[192,3072]{1,0:T(8,128)(2,1)} %bitcast.28, bf16[1,3072]{1,0:T(2,128)(2,1)} %refs_3_.1), custom_call_target="tpu_custom_call" | custom-call | bytes 6291456 | tf_op jit(solution)/shard_map/pallas_call | solution.py:33
  15.3 5.0 %collective-permute-done.6.far_ref = bf16[32,3072]{1,0:T(8,128)(2,1)S(1)} collective-permute-done((bf16[32,3072]{1,0:T(8,128)(2,1)S(1)}, bf16[32,3072]{1,0:T(8,128)(2,1)S(1)}, u32[]{:S(2)}, u32[]{:S(2)}) %collective-permute-start.6) | collective-permute-done | bytes 196640 | tf_op jit(solution)/shard_map/ppermute | solution.py:229
  20.3 0.0 collective-permute-done.2.near_ref
  20.3 2.0 %collective-permute-start.7 = (bf16[32,3072]{1,0:T(8,128)(2,1)S(1)}, bf16[32,3072]{1,0:T(8,128)(2,1)S(1)}, u32[]{:S(2)}, u32[]{:S(2)}) collective-permute-start(bf16[32,3072]{1,0:T(8,128)(2,1)S(1)} %collective-permute-done.2.near_ref), channel_id=1, source_target_pairs={{0,2},{2,0},{4,6},{6,4},{8,10},{10,8},{12,14},{14,12},{16,18},{18,... | collective-permute-start | bytes 589832 | tf_op jit(solution)/shard_map/ppermute | solution.py:229
  22.3 1.6 %collective-permute-start.5 = (bf16[32,3072]{1,0:T(8,128)(2,1)S(1)}, bf16[32,3072]{1,0:T(8,128)(2,1)S(1)}, u32[]{:S(2)}, u32[]{:S(2)}) collective-permute-start(bf16[32,3072]{1,0:T(8,128)(2,1)S(1)} %collective-permute-done.2.near_ref), channel_id=1, source_target_pairs={{0,4},{2,6},{4,0},{6,2},{8,12},{10,14},{12,8},{14,10},{16,20},{18,... | collective-permute-start | bytes 589832 | tf_op jit(solution)/shard_map/ppermute | solution.py:229
  23.9 0.0 copy-done.2
  23.9 0.1 slice_bitcast_fusion
  23.9 0.0 collective-permute-done.1.near_ref
  23.9 1.9 %collective-permute-start.3 = (bf16[64,3072]{1,0:T(8,128)(2,1)S(1)}, bf16[64,3072]{1,0:T(8,128)(2,1)S(1)}, u32[]{:S(2)}, u32[]{:S(2)}) collective-permute-start(bf16[64,3072]{1,0:T(8,128)(2,1)S(1)} %get-tuple-element.32), channel_id=1, source_target_pairs={{0,16},{2,18},{4,20},{6,22},{8,24},{10,26},{12,28},{14,30},{16,0},... | collective-permute-start | bytes 1179656 | tf_op jit(solution)/shard_map/ppermute | solution.py:229
  25.8 2.5 %collective-permute-done.5.near_ref = bf16[32,3072]{1,0:T(8,128)(2,1)S(1)} collective-permute-done((bf16[32,3072]{1,0:T(8,128)(2,1)S(1)}, bf16[32,3072]{1,0:T(8,128)(2,1)S(1)}, u32[]{:S(2)}, u32[]{:S(2)}) %collective-permute-start.5) | collective-permute-done | bytes 196640 | tf_op jit(solution)/shard_map/ppermute | solution.py:229
  28.3 0.0 collective-permute-done.7.far_ref
  28.3 1.3 %shard_map.77 = (bf16[32,3072]{1,0:T(8,128)(2,1)S(1)}, bf16[32,3072]{1,0:T(8,128)(2,1)S(1)}) custom-call(bf16[32,3072]{1,0:T(8,128)(2,1)S(1)} %collective-permute-done.2.near_ref, bf16[32,3072]{1,0:T(8,128)(2,1)S(1)} %collective-permute-done.7.far_ref, bf16[1,3072]{1,0:T(2,128)(2,1)S(1)} %get-tuple-element.31.gain_ref, ...), custom_call_target="tpu_custom_call" | custom-call | flops 226492416 | bytes 3538944 | tf_op jit(solution)/shard_map/pallas_call | solution.py:95
  29.5 0.1 collective-permute-start.8
  29.6 2.3 %collective-permute-start.9 = (bf16[32,3072]{1,0:T(8,128)(2,1)S(1)}, bf16[32,3072]{1,0:T(8,128)(2,1)S(1)}, u32[]{:S(2)}, u32[]{:S(2)}) collective-permute-start(bf16[32,3072]{1,0:T(8,128)(2,1)S(1)} %collective-permute-done.7.far_ref), channel_id=1, source_target_pairs={{0,4},{2,6},{4,0},{6,2},{8,12},{10,14},{12,8},{14,10},{16,20},{18,... | collective-permute-start | bytes 589832 | tf_op jit(solution)/shard_map/ppermute | solution.py:229
  31.9 1.4 %collective-permute-start.4 = (bf16[64,3072]{1,0:T(8,128)(2,1)S(1)}, bf16[64,3072]{1,0:T(8,128)(2,1)S(1)}, u32[]{:S(2)}, u32[]{:S(2)}) collective-permute-start(bf16[64,3072]{1,0:T(8,128)(2,1)S(1)} %get-tuple-element.33), channel_id=1, source_target_pairs={{0,16},{2,18},{4,20},{6,22},{8,24},{10,26},{12,28},{14,30},{16,0},... | collective-permute-start | bytes 1179656 | tf_op jit(solution)/shard_map/ppermute | solution.py:229
  33.3 1.9 %collective-permute-start.10 = (bf16[32,3072]{1,0:T(8,128)(2,1)S(1)}, bf16[32,3072]{1,0:T(8,128)(2,1)S(1)}, u32[]{:S(2)}, u32[]{:S(2)}) collective-permute-start(bf16[32,3072]{1,0:T(8,128)(2,1)S(1)} %collective-permute-done.1.near_ref), channel_id=1, source_target_pairs={{0,2},{2,0},{4,6},{6,4},{8,10},{10,8},{12,14},{14,12},{16,18},{18,... | collective-permute-start | bytes 589832 | tf_op jit(solution)/shard_map/ppermute | solution.py:229
  35.3 0.0 collective-permute-done.3.refs_0_
  35.3 1.2 %collective-permute-done.8 = bf16[32,3072]{1,0:T(8,128)(2,1)S(1)} collective-permute-done((bf16[32,3072]{1,0:T(8,128)(2,1)S(1)}, bf16[32,3072]{1,0:T(8,128)(2,1)S(1)}, u32[]{:S(2)}, u32[]{:S(2)}) %collective-permute-start.8) | collective-permute-done | bytes 196640 | tf_op jit(solution)/shard_map/ppermute | solution.py:229
  36.5 0.0 collective-permute-done.9.far_ref
  36.5 1.3 %shard_map.78 = (bf16[32,3072]{1,0:T(8,128)(2,1)S(1)}, bf16[32,3072]{1,0:T(8,128)(2,1)S(1)}) custom-call(bf16[32,3072]{1,0:T(8,128)(2,1)S(1)} %collective-permute-done.5.near_ref, bf16[32,3072]{1,0:T(8,128)(2,1)S(1)} %collective-permute-done.9.far_ref, bf16[1,3072]{1,0:T(2,128)(2,1)S(1)} %get-tuple-element.31.gain_ref, ...), custom_call_target="tpu_custom_call" | custom-call | flops 226492416 | bytes 3538944 | tf_op jit(solution)/shard_map/pallas_call | solution.py:95
  37.7 2.5 %collective-permute-start.12 = (bf16[32,3072]{1,0:T(8,128)(2,1)S(1)}, bf16[32,3072]{1,0:T(8,128)(2,1)S(1)}, u32[]{:S(2)}, u32[]{:S(2)}) collective-permute-start(bf16[32,3072]{1,0:T(8,128)(2,1)S(1)} %get-tuple-element.51), channel_id=1, source_target_pairs={{0,2},{2,0},{4,6},{6,4},{8,10},{10,8},{12,14},{14,12},{16,18},{18,... | collective-permute-start | bytes 589832 | tf_op jit(solution)/shard_map/ppermute | solution.py:229
  40.3 1.0 %collective-permute-start.11 = (bf16[32,3072]{1,0:T(8,128)(2,1)S(1)}, bf16[32,3072]{1,0:T(8,128)(2,1)S(1)}, u32[]{:S(2)}, u32[]{:S(2)}) collective-permute-start(bf16[32,3072]{1,0:T(8,128)(2,1)S(1)} %add_convert_fusion.2), channel_id=1, source_target_pairs={{0,8},{2,10},{4,12},{6,14},{8,0},{10,2},{12,4},{14,6},{16,24},{18,... | collective-permute-start | bytes 589832 | tf_op jit(solution)/shard_map/ppermute | solution.py:229
  41.3 0.0 collective-permute-done.10.far_ref
  41.3 1.3 %shard_map.79 = (bf16[32,3072]{1,0:T(8,128)(2,1)S(1)}, bf16[32,3072]{1,0:T(8,128)(2,1)S(1)}) custom-call(bf16[32,3072]{1,0:T(8,128)(2,1)S(1)} %collective-permute-done.1.near_ref, bf16[32,3072]{1,0:T(8,128)(2,1)S(1)} %collective-permute-done.10.far_ref, bf16[1,3072]{1,0:T(2,128)(2,1)S(1)} %get-tuple-element.31.gain_ref, ...), custom_call_target="tpu_custom_call" | custom-call | flops 226492416 | bytes 3538944 | tf_op jit(solution)/shard_map/pallas_call | solution.py:95
  42.5 0.6 collective-permute-start.14
  43.1 0.0 collective-permute-done.4.refs_1_
  43.1 0.0 copy-done
  43.1 0.0 copy-done.1
  43.1 1.0 %shard_map.76 = (f32[128,3072]{1,0:T(8,128)S(1)}, bf16[128,160]{1,0:T(8,128)(2,1)S(1)}, bf16[32,3072]{1,0:T(8,128)(2,1)S(1)}) custom-call(bf16[1,3072]{1,0:T(2,128)(2,1)S(1)} %get-tuple-element.31.gain_ref, s32[2,128]{1,0:T(2,128)S(1)} %bitcast.22, f32[2,128]{1,0:T(2,128)S(1)} %bitcast.23, bf16[64,3072]{1,0:T(8,128)(2,1)S(1)} %collective-permute-done.3.refs_0_, ...), custom_call_target="tpu_custom_call" | custom-call | flops 3145728 | bytes 2359296 | tf_op jit(solution)/shard_map/pallas_call | solution.py:150
  44.1 1.3 %shard_map.80 = (bf16[32,3072]{1,0:T(8,128)(2,1)S(1)}, bf16[32,3072]{1,0:T(8,128)(2,1)S(1)}) custom-call(bf16[32,3072]{1,0:T(8,128)(2,1)S(1)} %get-tuple-element.49.near_ref, bf16[32,3072]{1,0:T(8,128)(2,1)S(1)} %collective-permute-done.6.far_ref, bf16[1,3072]{1,0:T(2,128)(2,1)S(1)} %get-tuple-element.31.gain_ref, ...), custom_call_target="tpu_custom_call" | custom-call | flops 226492416 | bytes 3538944 | tf_op jit(solution)/shard_map/pallas_call | solution.py:95
  45.4 1.6 %collective-permute-start.16 = (bf16[32,3072]{1,0:T(8,128)(2,1)S(1)}, bf16[32,3072]{1,0:T(8,128)(2,1)S(1)}, u32[]{:S(2)}, u32[]{:S(2)}) collective-permute-start(bf16[32,3072]{1,0:T(8,128)(2,1)S(1)} %get-tuple-element.54), channel_id=1, source_target_pairs={{0,2},{2,0},{4,6},{6,4},{8,10},{10,8},{12,14},{14,12},{16,18},{18,... | collective-permute-start | bytes 589832 | tf_op jit(solution)/shard_map/ppermute | solution.py:229
  47.0 0.0 collective-permute-done.12
  47.0 2.6 %collective-permute-start.13 = (bf16[32,3072]{1,0:T(8,128)(2,1)S(1)}, bf16[32,3072]{1,0:T(8,128)(2,1)S(1)}, u32[]{:S(2)}, u32[]{:S(2)}) collective-permute-start(bf16[32,3072]{1,0:T(8,128)(2,1)S(1)} %add_convert_fusion.1), channel_id=1, source_target_pairs={{0,12},{2,14},{4,8},{6,10},{8,4},{10,6},{12,0},{14,2},{16,28},{18,... | collective-permute-start | bytes 589832 | tf_op jit(solution)/shard_map/ppermute | solution.py:229
  49.6 0.0 collective-permute-done.14
  49.7 2.5 %collective-permute-done.11.right_ref = bf16[32,3072]{1,0:T(8,128)(2,1)S(1)} collective-permute-done((bf16[32,3072]{1,0:T(8,128)(2,1)S(1)}, bf16[32,3072]{1,0:T(8,128)(2,1)S(1)}, u32[]{:S(2)}, u32[]{:S(2)}) %collective-permute-start.11) | collective-permute-done | bytes 196640 | tf_op jit(solution)/shard_map/ppermute | solution.py:229
  52.2 0.1 collective-permute-start.15
  52.3 0.0 collective-permute-done.16.refs_3_
  52.3 2.4 %collective-permute-done.13.refs_1_ = bf16[32,3072]{1,0:T(8,128)(2,1)S(1)} collective-permute-done((bf16[32,3072]{1,0:T(8,128)(2,1)S(1)}, bf16[32,3072]{1,0:T(8,128)(2,1)S(1)}, u32[]{:S(2)}, u32[]{:S(2)}) %collective-permute-start.13) | collective-permute-done | bytes 196640 | tf_op jit(solution)/shard_map/ppermute | solution.py:229
  54.7 3.3 %collective-permute-done.15.refs_2_ = bf16[32,3072]{1,0:T(8,128)(2,1)S(1)} collective-permute-done((bf16[32,3072]{1,0:T(8,128)(2,1)S(1)}, bf16[32,3072]{1,0:T(8,128)(2,1)S(1)}, u32[]{:S(2)}, u32[]{:S(2)}) %collective-permute-start.15) | collective-permute-done | bytes 196640 | tf_op jit(solution)/shard_map/ppermute | solution.py:229
  57.9 1.9 %shard_map.82 = bf16[128,3072]{1,0:T(8,128)(2,1)} custom-call(f32[128,3072]{1,0:T(8,128)S(1)} %get-tuple-element.34.base_ref, bf16[128,160]{1,0:T(8,128)(2,1)S(1)} %get-tuple-element.35.table_ref, f32[32,3072]{1,0:T(8,128)S(1)} %shard_map.81.refs_0_, bf16[32,3072]{1,0:T(8,128)(2,1)S(1)} %collective-permute-done.13.refs_1_, ...), custom_call_target="tpu_custom_call" | custom-call | flops 100663296 | bytes 2359296 | tf_op jit(solution)/shard_map/pallas_call | solution.py:182
  (6 shorter events, 0.2 us)
Async XLA Ops:
  0.0 4.7 %collective-permute-start = (s32[1,128,2]{1,2,0:T(2,128)}, s32[1,128,2]{1,2,0:T(2,128)S(1)}, u32[]{:S(2)}, u32[]{:S(2)}) collective-permute-start(s32[1,128,2]{1,2,0:T(2,128)} %param.12), channel_id=1, source_target_pairs={{0,16},{2,18},{4,20},{6,22},{8,24},{10,26},{12,28},{14,30},{16,0},... | collective-permute-start | bytes 3080 | tf_op jit(solution)/shard_map/ppermute | solution.py:229
  5.1 15.2 %collective-permute-start.6 = (bf16[32,3072]{1,0:T(8,128)(2,1)S(1)}, bf16[32,3072]{1,0:T(8,128)(2,1)S(1)}, u32[]{:S(2)}, u32[]{:S(2)}) collective-permute-start(bf16[32,3072]{1,0:T(8,128)(2,1)S(1)} %shard_map.74), channel_id=1, source_target_pairs={{0,18},{2,16},{4,22},{6,20},{8,26},{10,24},{12,30},{14,28},{16,2},... | collective-permute-start | bytes 589832 | tf_op jit(solution)/shard_map/ppermute | solution.py:229
  8.1 12.2 %collective-permute-start.2 = (bf16[32,3072]{1,0:T(8,128)(2,1)S(1)}, bf16[32,3072]{1,0:T(8,128)(2,1)S(1)}, u32[]{:S(2)}, u32[]{:S(2)}) collective-permute-start(bf16[32,3072]{1,0:T(8,128)(2,1)S(1)} %shard_map.74), channel_id=1, source_target_pairs={{0,24},{2,26},{4,28},{6,30},{8,16},{10,18},{12,20},{14,22},{16,8},... | collective-permute-start | bytes 589832 | tf_op jit(solution)/shard_map/ppermute | solution.py:229
  10.7 13.3 %collective-permute-start.1 = (bf16[32,3072]{1,0:T(8,128)(2,1)S(1)}, bf16[32,3072]{1,0:T(8,128)(2,1)S(1)}, u32[]{:S(2)}, u32[]{:S(2)}) collective-permute-start(bf16[32,3072]{1,0:T(8,128)(2,1)S(1)} %shard_map.74), channel_id=1, source_target_pairs={{0,20},{2,22},{4,16},{6,18},{8,28},{10,30},{12,24},{14,26},{16,4},... | collective-permute-start | bytes 589832 | tf_op jit(solution)/shard_map/ppermute | solution.py:229
  13.2 10.7 %copy-start.2 = (bf16[1,128,3072]{2,1,0:T(8,128)(2,1)S(1)}, bf16[1,128,3072]{2,1,0:T(8,128)(2,1)}, u32[]{:S(2)}) copy-start(bf16[1,128,3072]{2,1,0:T(8,128)(2,1)} %param.7) | copy-start | bytes 2359300
  20.3 8.0 %collective-permute-start.7 = (bf16[32,3072]{1,0:T(8,128)(2,1)S(1)}, bf16[32,3072]{1,0:T(8,128)(2,1)S(1)}, u32[]{:S(2)}, u32[]{:S(2)}) collective-permute-start(bf16[32,3072]{1,0:T(8,128)(2,1)S(1)} %collective-permute-done.2.near_ref), channel_id=1, source_target_pairs={{0,2},{2,0},{4,6},{6,4},{8,10},{10,8},{12,14},{14,12},{16,18},{18,... | collective-permute-start | bytes 589832 | tf_op jit(solution)/shard_map/ppermute | solution.py:229
  22.3 6.0 %collective-permute-start.5 = (bf16[32,3072]{1,0:T(8,128)(2,1)S(1)}, bf16[32,3072]{1,0:T(8,128)(2,1)S(1)}, u32[]{:S(2)}, u32[]{:S(2)}) collective-permute-start(bf16[32,3072]{1,0:T(8,128)(2,1)S(1)} %collective-permute-done.2.near_ref), channel_id=1, source_target_pairs={{0,4},{2,6},{4,0},{6,2},{8,12},{10,14},{12,8},{14,10},{16,20},{18,... | collective-permute-start | bytes 589832 | tf_op jit(solution)/shard_map/ppermute | solution.py:229
  23.9 11.4 %collective-permute-start.3 = (bf16[64,3072]{1,0:T(8,128)(2,1)S(1)}, bf16[64,3072]{1,0:T(8,128)(2,1)S(1)}, u32[]{:S(2)}, u32[]{:S(2)}) collective-permute-start(bf16[64,3072]{1,0:T(8,128)(2,1)S(1)} %get-tuple-element.32), channel_id=1, source_target_pairs={{0,16},{2,18},{4,20},{6,22},{8,24},{10,26},{12,28},{14,30},{16,0},... | collective-permute-start | bytes 1179656 | tf_op jit(solution)/shard_map/ppermute | solution.py:229
  29.5 6.9 %collective-permute-start.8 = (bf16[32,3072]{1,0:T(8,128)(2,1)S(1)}, bf16[32,3072]{1,0:T(8,128)(2,1)S(1)}, u32[]{:S(2)}, u32[]{:S(2)}) collective-permute-start(bf16[32,3072]{1,0:T(8,128)(2,1)S(1)} %get-tuple-element.42), channel_id=1, source_target_pairs={{0,2},{2,0},{4,6},{6,4},{8,10},{10,8},{12,14},{14,12},{16,18},{18,... | collective-permute-start | bytes 589832 | tf_op jit(solution)/shard_map/ppermute | solution.py:229
  29.6 6.8 %collective-permute-start.9 = (bf16[32,3072]{1,0:T(8,128)(2,1)S(1)}, bf16[32,3072]{1,0:T(8,128)(2,1)S(1)}, u32[]{:S(2)}, u32[]{:S(2)}) collective-permute-start(bf16[32,3072]{1,0:T(8,128)(2,1)S(1)} %collective-permute-done.7.far_ref), channel_id=1, source_target_pairs={{0,4},{2,6},{4,0},{6,2},{8,12},{10,14},{12,8},{14,10},{16,20},{18,... | collective-permute-start | bytes 589832 | tf_op jit(solution)/shard_map/ppermute | solution.py:229
  31.9 11.2 %collective-permute-start.4 = (bf16[64,3072]{1,0:T(8,128)(2,1)S(1)}, bf16[64,3072]{1,0:T(8,128)(2,1)S(1)}, u32[]{:S(2)}, u32[]{:S(2)}) collective-permute-start(bf16[64,3072]{1,0:T(8,128)(2,1)S(1)} %get-tuple-element.33), channel_id=1, source_target_pairs={{0,16},{2,18},{4,20},{6,22},{8,24},{10,26},{12,28},{14,30},{16,0},... | collective-permute-start | bytes 1179656 | tf_op jit(solution)/shard_map/ppermute | solution.py:229
  33.3 7.9 %collective-permute-start.10 = (bf16[32,3072]{1,0:T(8,128)(2,1)S(1)}, bf16[32,3072]{1,0:T(8,128)(2,1)S(1)}, u32[]{:S(2)}, u32[]{:S(2)}) collective-permute-start(bf16[32,3072]{1,0:T(8,128)(2,1)S(1)} %collective-permute-done.1.near_ref), channel_id=1, source_target_pairs={{0,2},{2,0},{4,6},{6,4},{8,10},{10,8},{12,14},{14,12},{16,18},{18,... | collective-permute-start | bytes 589832 | tf_op jit(solution)/shard_map/ppermute | solution.py:229
  37.7 9.2 %collective-permute-start.12 = (bf16[32,3072]{1,0:T(8,128)(2,1)S(1)}, bf16[32,3072]{1,0:T(8,128)(2,1)S(1)}, u32[]{:S(2)}, u32[]{:S(2)}) collective-permute-start(bf16[32,3072]{1,0:T(8,128)(2,1)S(1)} %get-tuple-element.51), channel_id=1, source_target_pairs={{0,2},{2,0},{4,6},{6,4},{8,10},{10,8},{12,14},{14,12},{16,18},{18,... | collective-permute-start | bytes 589832 | tf_op jit(solution)/shard_map/ppermute | solution.py:229
  40.3 11.8 %collective-permute-start.11 = (bf16[32,3072]{1,0:T(8,128)(2,1)S(1)}, bf16[32,3072]{1,0:T(8,128)(2,1)S(1)}, u32[]{:S(2)}, u32[]{:S(2)}) collective-permute-start(bf16[32,3072]{1,0:T(8,128)(2,1)S(1)} %add_convert_fusion.2), channel_id=1, source_target_pairs={{0,8},{2,10},{4,12},{6,14},{8,0},{10,2},{12,4},{14,6},{16,24},{18,... | collective-permute-start | bytes 589832 | tf_op jit(solution)/shard_map/ppermute | solution.py:229
  41.3 1.8 %copy-start = (s32[1,128,2]{1,2,0:T(2,128)S(1)}, s32[1,128,2]{1,2,0:T(2,128)}, u32[]{:S(2)}) copy-start(s32[1,128,2]{1,2,0:T(2,128)} %param.12) | copy-start | bytes 3076
  41.3 1.8 %copy-start.1 = (f32[1,128,2]{1,2,0:T(2,128)S(1)}, f32[1,128,2]{1,2,0:T(2,128)}, u32[]{:S(2)}) copy-start(f32[1,128,2]{1,2,0:T(2,128)} %param.13) | copy-start | bytes 3076
  42.5 7.1 %collective-permute-start.14 = (bf16[32,3072]{1,0:T(8,128)(2,1)S(1)}, bf16[32,3072]{1,0:T(8,128)(2,1)S(1)}, u32[]{:S(2)}, u32[]{:S(2)}) collective-permute-start(bf16[32,3072]{1,0:T(8,128)(2,1)S(1)} %get-tuple-element.52), channel_id=1, source_target_pairs={{0,2},{2,0},{4,6},{6,4},{8,10},{10,8},{12,14},{14,12},{16,18},{18,... | collective-permute-start | bytes 589832 | tf_op jit(solution)/shard_map/ppermute | solution.py:229
  45.4 6.9 %collective-permute-start.16 = (bf16[32,3072]{1,0:T(8,128)(2,1)S(1)}, bf16[32,3072]{1,0:T(8,128)(2,1)S(1)}, u32[]{:S(2)}, u32[]{:S(2)}) collective-permute-start(bf16[32,3072]{1,0:T(8,128)(2,1)S(1)} %get-tuple-element.54), channel_id=1, source_target_pairs={{0,2},{2,0},{4,6},{6,4},{8,10},{10,8},{12,14},{14,12},{16,18},{18,... | collective-permute-start | bytes 589832 | tf_op jit(solution)/shard_map/ppermute | solution.py:229
  47.0 7.6 %collective-permute-start.13 = (bf16[32,3072]{1,0:T(8,128)(2,1)S(1)}, bf16[32,3072]{1,0:T(8,128)(2,1)S(1)}, u32[]{:S(2)}, u32[]{:S(2)}) collective-permute-start(bf16[32,3072]{1,0:T(8,128)(2,1)S(1)} %add_convert_fusion.1), channel_id=1, source_target_pairs={{0,12},{2,14},{4,8},{6,10},{8,4},{10,6},{12,0},{14,2},{16,28},{18,... | collective-permute-start | bytes 589832 | tf_op jit(solution)/shard_map/ppermute | solution.py:229
  52.2 5.7 %collective-permute-start.15 = (bf16[32,3072]{1,0:T(8,128)(2,1)S(1)}, bf16[32,3072]{1,0:T(8,128)(2,1)S(1)}, u32[]{:S(2)}, u32[]{:S(2)}) collective-permute-start(bf16[32,3072]{1,0:T(8,128)(2,1)S(1)} %add_convert_fusion), channel_id=1, source_target_pairs={{0,4},{2,6},{4,0},{6,2},{8,12},{10,14},{12,8},{14,10},{16,20},{18,... | collective-permute-start | bytes 589832 | tf_op jit(solution)/shard_map/ppermute | solution.py:229

commit v6 on v5

--- a/solution.py
+++ b/solution.py
@@ -244,16 +244,16 @@
     )
 
     near, far = {}, {}
+    near[2] = moved(picked, 1, 2)
     far[0] = moved(picked, 1, 0, 1)
-    near[2] = moved(picked, 1, 2)
     far[2] = moved(after(near[2], far[0], gain), 0, 0, 1)
     near[3] = moved(near[2], 0, 1)
     far[3] = moved(far[2], 0, 1)
-    near[1] = moved(picked, 1, 1)
+    near[1] = moved(after(picked, near[2]), 1, 1)
     pieces = 2
     size = token_count // pieces
     arrived = [
-        moved(after(blocks[0, i * size:(i + 1) * size], near[1], near[2]), 1, 0)
+        moved(after(blocks[0, i * size:(i + 1) * size], far[0], near[2]), 1, 0)
         for i in range(pieces)
     ]
     base, table, near[0] = based(

time: 59.9 us -> 59.7 us (level)
  starting transfers between devices: 30.5 us -> 25.8 us
  waiting for transfers between devices: 17.4 us -> 21.9 us
    ppermute x17, starting transfers between devices: 30.5 us -> 25.8 us  [moved(): return lax.ppermute(value, ('section', 'expert'), pairs)]
    ppermute x17, waiting for transfers between devices: 17.4 us -> 21.9 us  [moved(): return lax.ppermute(value, ('section', 'expert'), pairs)]
  transfers between devices with their start and end apart: 17 -> 17, of which waited for: 7 -> 9; matrix products, arithmetic and copies ran while one was open for 0% -> 0% of each run, Pallas kernels for 16% -> 16%
where the time goes in v6:
time: 59.7 us; the launch traced here: 59.6 us
  starting transfers between devices  25.8 us (43%)
  waiting for transfers between devices  21.9 us (37%)
  Pallas kernels  11.5 us (19%)
    ppermute x17, starting transfers between devices, moved(): return lax.ppermute(value, ('section', 'expert'), pairs)  25.8 us
    ppermute x17, waiting for transfers between devices, moved(): return lax.ppermute(value, ('section', 'expert'), pairs)  21.9 us
    pallas_call x4, Pallas kernels, mlp(): pl.pallas_call(mlp_kernel, out_shape=(out, out), in_specs=[VMEM] * 6, out...  5.05 us
    pallas_call x2, Pallas kernels, loaded(): pl.pallas_call(functools.partial(load_kernel, len(arrays)), out_shape=tup...  3.23 us
    pallas_call x1, Pallas kernels, ended(): pl.pallas_call(functools.partial(end_kernel, columns), out_shape=jax.Shap...  1.88 us
  transfers between devices with their start and end apart: 17, of which 9 were waited for; matrix products, arithmetic and copies ran while one was open for 0% of the time, Pallas kernels for 16%

profile of v6, /device:TPU:0, one launch (start us, length us, event | category | flops | bytes accessed | tf_op | source)
XLA Modules:
  0.0 59.6 jit_solution(11820341729484877184)
XLA Ops:
  0.0 2.9 %collective-permute-start = (s32[1,128,2]{1,2,0:T(2,128)}, s32[1,128,2]{1,2,0:T(2,128)S(1)}, u32[]{:S(2)}, u32[]{:S(2)}) collective-permute-start(s32[1,128,2]{1,2,0:T(2,128)} %param.12), channel_id=1, source_target_pairs={{0,16},{2,18},{4,20},{6,22},{8,24},{10,26},{12,28},{14,30},{16,0},... | collective-permute-start | bytes 3080 | tf_op jit(solution)/shard_map/ppermute | solution.py:229
  2.9 1.1 %shard_map.73.block_ref = bf16[128,3072]{1,0:T(8,128)(2,1)S(1)} custom-call(bf16[128,3072]{1,0:T(8,128)(2,1)} %bitcast.25), custom_call_target="tpu_custom_call" | custom-call | bytes 6291456 | tf_op jit(solution)/shard_map/pallas_call | solution.py:33
  4.1 0.6 %collective-permute-done = s32[1,128,2]{1,2,0:T(2,128)S(1)} collective-permute-done((s32[1,128,2]{1,2,0:T(2,128)}, s32[1,128,2]{1,2,0:T(2,128)S(1)}, u32[]{:S(2)}, u32[]{:S(2)}) %collective-permute-start) | collective-permute-done | bytes 1056 | tf_op jit(solution)/shard_map/ppermute | solution.py:229
  4.7 0.4 shard_map.74
  5.1 4.1 %collective-permute-start.2 = (bf16[32,3072]{1,0:T(8,128)(2,1)S(1)}, bf16[32,3072]{1,0:T(8,128)(2,1)S(1)}, u32[]{:S(2)}, u32[]{:S(2)}) collective-permute-start(bf16[32,3072]{1,0:T(8,128)(2,1)S(1)} %shard_map.74), channel_id=1, source_target_pairs={{0,24},{2,26},{4,28},{6,30},{8,16},{10,18},{12,20},{14,22},{16,8},... | collective-permute-start | bytes 589832 | tf_op jit(solution)/shard_map/ppermute | solution.py:229
  9.2 1.5 %collective-permute-start.1 = (bf16[32,3072]{1,0:T(8,128)(2,1)S(1)}, bf16[32,3072]{1,0:T(8,128)(2,1)S(1)}, u32[]{:S(2)}, u32[]{:S(2)}) collective-permute-start(bf16[32,3072]{1,0:T(8,128)(2,1)S(1)} %shard_map.74), channel_id=1, source_target_pairs={{0,18},{2,16},{4,22},{6,20},{8,26},{10,24},{12,30},{14,28},{16,2},... | collective-permute-start | bytes 589832 | tf_op jit(solution)/shard_map/ppermute | solution.py:229
  10.7 0.0 copy-start.2
  10.7 2.1 %shard_map.75 = (bf16[192,3072]{1,0:T(8,128)(2,1)S(1)}, bf16[192,3072]{1,0:T(8,128)(2,1)S(1)}, bf16[192,3072]{1,0:T(8,128)(2,1)S(1)}, bf16[1,3072]{1,0:T(2,128)(2,1)S(1)}) custom-call(bf16[192,3072]{1,0:T(8,128)(2,1)} %bitcast.26, bf16[192,3072]{1,0:T(8,128)(2,1)} %bitcast.27, bf16[192,3072]{1,0:T(8,128)(2,1)} %bitcast.28, bf16[1,3072]{1,0:T(2,128)(2,1)} %refs_3_.1), custom_call_target="tpu_custom_call" | custom-call | bytes 6291456 | tf_op jit(solution)/shard_map/pallas_call | solution.py:33
  12.8 4.5 %collective-permute-done.2.near_ref = bf16[32,3072]{1,0:T(8,128)(2,1)S(1)} collective-permute-done((bf16[32,3072]{1,0:T(8,128)(2,1)S(1)}, bf16[32,3072]{1,0:T(8,128)(2,1)S(1)}, u32[]{:S(2)}, u32[]{:S(2)}) %collective-permute-start.2) | collective-permute-done | bytes 196640 | tf_op jit(solution)/shard_map/ppermute | solution.py:229
  17.2 1.5 %collective-permute-done.1.far_ref = bf16[32,3072]{1,0:T(8,128)(2,1)S(1)} collective-permute-done((bf16[32,3072]{1,0:T(8,128)(2,1)S(1)}, bf16[32,3072]{1,0:T(8,128)(2,1)S(1)}, u32[]{:S(2)}, u32[]{:S(2)}) %collective-permute-start.1) | collective-permute-done | bytes 196640 | tf_op jit(solution)/shard_map/ppermute | solution.py:229
  18.8 1.5 %collective-permute-start.7 = (bf16[32,3072]{1,0:T(8,128)(2,1)S(1)}, bf16[32,3072]{1,0:T(8,128)(2,1)S(1)}, u32[]{:S(2)}, u32[]{:S(2)}) collective-permute-start(bf16[32,3072]{1,0:T(8,128)(2,1)S(1)} %collective-permute-done.2.near_ref), channel_id=1, source_target_pairs={{0,2},{2,0},{4,6},{6,4},{8,10},{10,8},{12,14},{14,12},{16,18},{18,... | collective-permute-start | bytes 589832 | tf_op jit(solution)/shard_map/ppermute | solution.py:229
  20.3 0.1 collective-permute-start.6
  20.4 0.0 copy-done.2
  20.4 0.1 slice_bitcast_fusion
  20.4 1.5 %collective-permute-start.3 = (bf16[64,3072]{1,0:T(8,128)(2,1)S(1)}, bf16[64,3072]{1,0:T(8,128)(2,1)S(1)}, u32[]{:S(2)}, u32[]{:S(2)}) collective-permute-start(bf16[64,3072]{1,0:T(8,128)(2,1)S(1)} %get-tuple-element.33), channel_id=1, source_target_pairs={{0,16},{2,18},{4,20},{6,22},{8,24},{10,26},{12,28},{14,30},{16,0},... | collective-permute-start | bytes 1179656 | tf_op jit(solution)/shard_map/ppermute | solution.py:229
  21.9 2.0 %collective-permute-start.5 = (bf16[32,3072]{1,0:T(8,128)(2,1)S(1)}, bf16[32,3072]{1,0:T(8,128)(2,1)S(1)}, u32[]{:S(2)}, u32[]{:S(2)}) collective-permute-start(bf16[32,3072]{1,0:T(8,128)(2,1)S(1)} %shard_map.74), channel_id=1, source_target_pairs={{0,20},{2,22},{4,16},{6,18},{8,28},{10,30},{12,24},{14,26},{16,4},... | collective-permute-start | bytes 589832 | tf_op jit(solution)/shard_map/ppermute | solution.py:229
  23.9 3.8 %collective-permute-done.6.near_ref = bf16[32,3072]{1,0:T(8,128)(2,1)S(1)} collective-permute-done((bf16[32,3072]{1,0:T(8,128)(2,1)S(1)}, bf16[32,3072]{1,0:T(8,128)(2,1)S(1)}, u32[]{:S(2)}, u32[]{:S(2)}) %collective-permute-start.6) | collective-permute-done | bytes 196640 | tf_op jit(solution)/shard_map/ppermute | solution.py:229
  27.7 0.0 collective-permute-done.7.far_ref
  27.7 1.3 %shard_map.77 = (bf16[32,3072]{1,0:T(8,128)(2,1)S(1)}, bf16[32,3072]{1,0:T(8,128)(2,1)S(1)}) custom-call(bf16[32,3072]{1,0:T(8,128)(2,1)S(1)} %collective-permute-done.2.near_ref, bf16[32,3072]{1,0:T(8,128)(2,1)S(1)} %collective-permute-done.7.far_ref, bf16[1,3072]{1,0:T(2,128)(2,1)S(1)} %get-tuple-element.32.gain_ref, ...), custom_call_target="tpu_custom_call" | custom-call | flops 226492416 | bytes 3538944 | tf_op jit(solution)/shard_map/pallas_call | solution.py:95
  29.0 0.5 collective-permute-start.8
  29.4 1.5 %collective-permute-start.9 = (bf16[32,3072]{1,0:T(8,128)(2,1)S(1)}, bf16[32,3072]{1,0:T(8,128)(2,1)S(1)}, u32[]{:S(2)}, u32[]{:S(2)}) collective-permute-start(bf16[32,3072]{1,0:T(8,128)(2,1)S(1)} %collective-permute-done.7.far_ref), channel_id=1, source_target_pairs={{0,4},{2,6},{4,0},{6,2},{8,12},{10,14},{12,8},{14,10},{16,20},{18,... | collective-permute-start | bytes 589832 | tf_op jit(solution)/shard_map/ppermute | solution.py:229
  31.0 1.5 %collective-permute-start.4 = (bf16[64,3072]{1,0:T(8,128)(2,1)S(1)}, bf16[64,3072]{1,0:T(8,128)(2,1)S(1)}, u32[]{:S(2)}, u32[]{:S(2)}) collective-permute-start(bf16[64,3072]{1,0:T(8,128)(2,1)S(1)} %get-tuple-element.34), channel_id=1, source_target_pairs={{0,16},{2,18},{4,20},{6,22},{8,24},{10,26},{12,28},{14,30},{16,0},... | collective-permute-start | bytes 1179656 | tf_op jit(solution)/shard_map/ppermute | solution.py:229
  32.5 0.0 collective-permute-done.5.near_ref
  32.5 0.5 collective-permute-start.10
  33.0 3.8 %collective-permute-done.3.refs_0_ = bf16[64,3072]{1,0:T(8,128)(2,1)S(1)} collective-permute-done((bf16[64,3072]{1,0:T(8,128)(2,1)S(1)}, bf16[64,3072]{1,0:T(8,128)(2,1)S(1)}, u32[]{:S(2)}, u32[]{:S(2)}) %collective-permute-start.3) | collective-permute-done | bytes 393248 | tf_op jit(solution)/shard_map/ppermute | solution.py:229
  36.8 0.0 collective-permute-done.8
  36.8 0.0 collective-permute-done.9.far_ref
  36.8 1.3 %shard_map.78 = (bf16[32,3072]{1,0:T(8,128)(2,1)S(1)}, bf16[32,3072]{1,0:T(8,128)(2,1)S(1)}) custom-call(bf16[32,3072]{1,0:T(8,128)(2,1)S(1)} %collective-permute-done.6.near_ref, bf16[32,3072]{1,0:T(8,128)(2,1)S(1)} %collective-permute-done.9.far_ref, bf16[1,3072]{1,0:T(2,128)(2,1)S(1)} %get-tuple-element.32.gain_ref, ...), custom_call_target="tpu_custom_call" | custom-call | flops 226492416 | bytes 3538944 | tf_op jit(solution)/shard_map/pallas_call | solution.py:95
  38.0 1.5 %collective-permute-start.12 = (bf16[32,3072]{1,0:T(8,128)(2,1)S(1)}, bf16[32,3072]{1,0:T(8,128)(2,1)S(1)}, u32[]{:S(2)}, u32[]{:S(2)}) collective-permute-start(bf16[32,3072]{1,0:T(8,128)(2,1)S(1)} %get-tuple-element.53), channel_id=1, source_target_pairs={{0,2},{2,0},{4,6},{6,4},{8,10},{10,8},{12,14},{14,12},{16,18},{18,... | collective-permute-start | bytes 589832 | tf_op jit(solution)/shard_map/ppermute | solution.py:229
  39.6 1.6 %collective-permute-start.11 = (bf16[32,3072]{1,0:T(8,128)(2,1)S(1)}, bf16[32,3072]{1,0:T(8,128)(2,1)S(1)}, u32[]{:S(2)}, u32[]{:S(2)}) collective-permute-start(bf16[32,3072]{1,0:T(8,128)(2,1)S(1)} %add_convert_fusion.2), channel_id=1, source_target_pairs={{0,8},{2,10},{4,12},{6,14},{8,0},{10,2},{12,4},{14,6},{16,24},{18,... | collective-permute-start | bytes 589832 | tf_op jit(solution)/shard_map/ppermute | solution.py:229
  41.2 0.0 collective-permute-done.10.far_ref
  41.2 1.3 %shard_map.79 = (bf16[32,3072]{1,0:T(8,128)(2,1)S(1)}, bf16[32,3072]{1,0:T(8,128)(2,1)S(1)}) custom-call(bf16[32,3072]{1,0:T(8,128)(2,1)S(1)} %collective-permute-done.5.near_ref, bf16[32,3072]{1,0:T(8,128)(2,1)S(1)} %collective-permute-done.10.far_ref, bf16[1,3072]{1,0:T(2,128)(2,1)S(1)} %get-tuple-element.32.gain_ref, ...), custom_call_target="tpu_custom_call" | custom-call | flops 226492416 | bytes 3538944 | tf_op jit(solution)/shard_map/pallas_call | solution.py:95
  42.5 2.0 %collective-permute-start.14 = (bf16[32,3072]{1,0:T(8,128)(2,1)S(1)}, bf16[32,3072]{1,0:T(8,128)(2,1)S(1)}, u32[]{:S(2)}, u32[]{:S(2)}) collective-permute-start(bf16[32,3072]{1,0:T(8,128)(2,1)S(1)} %get-tuple-element.54), channel_id=1, source_target_pairs={{0,2},{2,0},{4,6},{6,4},{8,10},{10,8},{12,14},{14,12},{16,18},{18,... | collective-permute-start | bytes 589832 | tf_op jit(solution)/shard_map/ppermute | solution.py:229
  44.4 0.0 collective-permute-done.4.refs_1_
  44.4 0.0 copy-done
  44.4 0.0 copy-done.1
  44.4 1.0 %shard_map.76 = (f32[128,3072]{1,0:T(8,128)S(1)}, bf16[128,160]{1,0:T(8,128)(2,1)S(1)}, bf16[32,3072]{1,0:T(8,128)(2,1)S(1)}) custom-call(bf16[1,3072]{1,0:T(2,128)(2,1)S(1)} %get-tuple-element.32.gain_ref, s32[2,128]{1,0:T(2,128)S(1)} %bitcast.22, f32[2,128]{1,0:T(2,128)S(1)} %bitcast.23, bf16[64,3072]{1,0:T(8,128)(2,1)S(1)} %collective-permute-done.3.refs_0_, ...), custom_call_target="tpu_custom_call" | custom-call | flops 3145728 | bytes 2359296 | tf_op jit(solution)/shard_map/pallas_call | solution.py:150
  45.4 1.3 %shard_map.80 = (bf16[32,3072]{1,0:T(8,128)(2,1)S(1)}, bf16[32,3072]{1,0:T(8,128)(2,1)S(1)}) custom-call(bf16[32,3072]{1,0:T(8,128)(2,1)S(1)} %get-tuple-element.51.near_ref, bf16[32,3072]{1,0:T(8,128)(2,1)S(1)} %collective-permute-done.1.far_ref, bf16[1,3072]{1,0:T(2,128)(2,1)S(1)} %get-tuple-element.32.gain_ref, ...), custom_call_target="tpu_custom_call" | custom-call | flops 226492416 | bytes 3538944 | tf_op jit(solution)/shard_map/pallas_call | solution.py:95
  46.7 0.7 %collective-permute-start.16 = (bf16[32,3072]{1,0:T(8,128)(2,1)S(1)}, bf16[32,3072]{1,0:T(8,128)(2,1)S(1)}, u32[]{:S(2)}, u32[]{:S(2)}) collective-permute-start(bf16[32,3072]{1,0:T(8,128)(2,1)S(1)} %get-tuple-element.56), channel_id=1, source_target_pairs={{0,2},{2,0},{4,6},{6,4},{8,10},{10,8},{12,14},{14,12},{16,18},{18,... | collective-permute-start | bytes 589832 | tf_op jit(solution)/shard_map/ppermute | solution.py:229
  47.4 0.0 collective-permute-done.12
  47.5 1.5 %collective-permute-start.13 = (bf16[32,3072]{1,0:T(8,128)(2,1)S(1)}, bf16[32,3072]{1,0:T(8,128)(2,1)S(1)}, u32[]{:S(2)}, u32[]{:S(2)}) collective-permute-start(bf16[32,3072]{1,0:T(8,128)(2,1)S(1)} %add_convert_fusion.1), channel_id=1, source_target_pairs={{0,12},{2,14},{4,8},{6,10},{8,4},{10,6},{12,0},{14,2},{16,28},{18,... | collective-permute-start | bytes 589832 | tf_op jit(solution)/shard_map/ppermute | solution.py:229
  48.9 0.7 %collective-permute-done.14 = bf16[32,3072]{1,0:T(8,128)(2,1)S(1)} collective-permute-done((bf16[32,3072]{1,0:T(8,128)(2,1)S(1)}, bf16[32,3072]{1,0:T(8,128)(2,1)S(1)}, u32[]{:S(2)}, u32[]{:S(2)}) %collective-permute-start.14) | collective-permute-done | bytes 196640 | tf_op jit(solution)/shard_map/ppermute | solution.py:229
  49.7 0.0 collective-permute-done.11.right_ref
  49.8 1.0 %collective-permute-start.15 = (bf16[32,3072]{1,0:T(8,128)(2,1)S(1)}, bf16[32,3072]{1,0:T(8,128)(2,1)S(1)}, u32[]{:S(2)}, u32[]{:S(2)}) collective-permute-start(bf16[32,3072]{1,0:T(8,128)(2,1)S(1)} %add_convert_fusion), channel_id=1, source_target_pairs={{0,4},{2,6},{4,0},{6,2},{8,12},{10,14},{12,8},{14,10},{16,20},{18,... | collective-permute-start | bytes 589832 | tf_op jit(solution)/shard_map/ppermute | solution.py:229
  50.8 1.6 %collective-permute-done.16.refs_3_ = bf16[32,3072]{1,0:T(8,128)(2,1)S(1)} collective-permute-done((bf16[32,3072]{1,0:T(8,128)(2,1)S(1)}, bf16[32,3072]{1,0:T(8,128)(2,1)S(1)}, u32[]{:S(2)}, u32[]{:S(2)}) %collective-permute-start.16) | collective-permute-done | bytes 196640 | tf_op jit(solution)/shard_map/ppermute | solution.py:229
  52.4 4.3 %collective-permute-done.13.refs_1_ = bf16[32,3072]{1,0:T(8,128)(2,1)S(1)} collective-permute-done((bf16[32,3072]{1,0:T(8,128)(2,1)S(1)}, bf16[32,3072]{1,0:T(8,128)(2,1)S(1)}, u32[]{:S(2)}, u32[]{:S(2)}) %collective-permute-start.13) | collective-permute-done | bytes 196640 | tf_op jit(solution)/shard_map/ppermute | solution.py:229
  56.7 1.0 %collective-permute-done.15.refs_2_ = bf16[32,3072]{1,0:T(8,128)(2,1)S(1)} collective-permute-done((bf16[32,3072]{1,0:T(8,128)(2,1)S(1)}, bf16[32,3072]{1,0:T(8,128)(2,1)S(1)}, u32[]{:S(2)}, u32[]{:S(2)}) %collective-permute-start.15) | collective-permute-done | bytes 196640 | tf_op jit(solution)/shard_map/ppermute | solution.py:229
  57.7 1.9 %shard_map.82 = bf16[128,3072]{1,0:T(8,128)(2,1)} custom-call(f32[128,3072]{1,0:T(8,128)S(1)} %get-tuple-element.35.base_ref, bf16[128,160]{1,0:T(8,128)(2,1)S(1)} %get-tuple-element.36.table_ref, f32[32,3072]{1,0:T(8,128)S(1)} %shard_map.81.refs_0_, bf16[32,3072]{1,0:T(8,128)(2,1)S(1)} %collective-permute-done.13.refs_1_, ...), custom_call_target="tpu_custom_call" | custom-call | flops 100663296 | bytes 2359296 | tf_op jit(solution)/shard_map/pallas_call | solution.py:182
  (6 shorter events, 0.2 us)
Async XLA Ops:
  0.0 4.7 %collective-permute-start = (s32[1,128,2]{1,2,0:T(2,128)}, s32[1,128,2]{1,2,0:T(2,128)S(1)}, u32[]{:S(2)}, u32[]{:S(2)}) collective-permute-start(s32[1,128,2]{1,2,0:T(2,128)} %param.12), channel_id=1, source_target_pairs={{0,16},{2,18},{4,20},{6,22},{8,24},{10,26},{12,28},{14,30},{16,0},... | collective-permute-start | bytes 3080 | tf_op jit(solution)/shard_map/ppermute | solution.py:229
  5.1 12.2 %collective-permute-start.2 = (bf16[32,3072]{1,0:T(8,128)(2,1)S(1)}, bf16[32,3072]{1,0:T(8,128)(2,1)S(1)}, u32[]{:S(2)}, u32[]{:S(2)}) collective-permute-start(bf16[32,3072]{1,0:T(8,128)(2,1)S(1)} %shard_map.74), channel_id=1, source_target_pairs={{0,24},{2,26},{4,28},{6,30},{8,16},{10,18},{12,20},{14,22},{16,8},... | collective-permute-start | bytes 589832 | tf_op jit(solution)/shard_map/ppermute | solution.py:229
  9.2 9.6 %collective-permute-start.1 = (bf16[32,3072]{1,0:T(8,128)(2,1)S(1)}, bf16[32,3072]{1,0:T(8,128)(2,1)S(1)}, u32[]{:S(2)}, u32[]{:S(2)}) collective-permute-start(bf16[32,3072]{1,0:T(8,128)(2,1)S(1)} %shard_map.74), channel_id=1, source_target_pairs={{0,18},{2,16},{4,22},{6,20},{8,26},{10,24},{12,30},{14,28},{16,2},... | collective-permute-start | bytes 589832 | tf_op jit(solution)/shard_map/ppermute | solution.py:229
  10.7 9.7 %copy-start.2 = (bf16[1,128,3072]{2,1,0:T(8,128)(2,1)S(1)}, bf16[1,128,3072]{2,1,0:T(8,128)(2,1)}, u32[]{:S(2)}) copy-start(bf16[1,128,3072]{2,1,0:T(8,128)(2,1)} %param.7) | copy-start | bytes 2359300
  18.8 8.9 %collective-permute-start.7 = (bf16[32,3072]{1,0:T(8,128)(2,1)S(1)}, bf16[32,3072]{1,0:T(8,128)(2,1)S(1)}, u32[]{:S(2)}, u32[]{:S(2)}) collective-permute-start(bf16[32,3072]{1,0:T(8,128)(2,1)S(1)} %collective-permute-done.2.near_ref), channel_id=1, source_target_pairs={{0,2},{2,0},{4,6},{6,4},{8,10},{10,8},{12,14},{14,12},{16,18},{18,... | collective-permute-start | bytes 589832 | tf_op jit(solution)/shard_map/ppermute | solution.py:229
  20.3 7.4 %collective-permute-start.6 = (bf16[32,3072]{1,0:T(8,128)(2,1)S(1)}, bf16[32,3072]{1,0:T(8,128)(2,1)S(1)}, u32[]{:S(2)}, u32[]{:S(2)}) collective-permute-start(bf16[32,3072]{1,0:T(8,128)(2,1)S(1)} %collective-permute-done.2.near_ref), channel_id=1, source_target_pairs={{0,4},{2,6},{4,0},{6,2},{8,12},{10,14},{12,8},{14,10},{16,20},{18,... | collective-permute-start | bytes 589832 | tf_op jit(solution)/shard_map/ppermute | solution.py:229
  20.4 16.3 %collective-permute-start.3 = (bf16[64,3072]{1,0:T(8,128)(2,1)S(1)}, bf16[64,3072]{1,0:T(8,128)(2,1)S(1)}, u32[]{:S(2)}, u32[]{:S(2)}) collective-permute-start(bf16[64,3072]{1,0:T(8,128)(2,1)S(1)} %get-tuple-element.33), channel_id=1, source_target_pairs={{0,16},{2,18},{4,20},{6,22},{8,24},{10,26},{12,28},{14,30},{16,0},... | collective-permute-start | bytes 1179656 | tf_op jit(solution)/shard_map/ppermute | solution.py:229
  21.9 10.5 %collective-permute-start.5 = (bf16[32,3072]{1,0:T(8,128)(2,1)S(1)}, bf16[32,3072]{1,0:T(8,128)(2,1)S(1)}, u32[]{:S(2)}, u32[]{:S(2)}) collective-permute-start(bf16[32,3072]{1,0:T(8,128)(2,1)S(1)} %shard_map.74), channel_id=1, source_target_pairs={{0,20},{2,22},{4,16},{6,18},{8,28},{10,30},{12,24},{14,26},{16,4},... | collective-permute-start | bytes 589832 | tf_op jit(solution)/shard_map/ppermute | solution.py:229
  29.0 7.8 %collective-permute-start.8 = (bf16[32,3072]{1,0:T(8,128)(2,1)S(1)}, bf16[32,3072]{1,0:T(8,128)(2,1)S(1)}, u32[]{:S(2)}, u32[]{:S(2)}) collective-permute-start(bf16[32,3072]{1,0:T(8,128)(2,1)S(1)} %get-tuple-element.44), channel_id=1, source_target_pairs={{0,2},{2,0},{4,6},{6,4},{8,10},{10,8},{12,14},{14,12},{16,18},{18,... | collective-permute-start | bytes 589832 | tf_op jit(solution)/shard_map/ppermute | solution.py:229
  29.4 7.4 %collective-permute-start.9 = (bf16[32,3072]{1,0:T(8,128)(2,1)S(1)}, bf16[32,3072]{1,0:T(8,128)(2,1)S(1)}, u32[]{:S(2)}, u32[]{:S(2)}) collective-permute-start(bf16[32,3072]{1,0:T(8,128)(2,1)S(1)} %collective-permute-done.7.far_ref), channel_id=1, source_target_pairs={{0,4},{2,6},{4,0},{6,2},{8,12},{10,14},{12,8},{14,10},{16,20},{18,... | collective-permute-start | bytes 589832 | tf_op jit(solution)/shard_map/ppermute | solution.py:229
  31.0 13.5 %collective-permute-start.4 = (bf16[64,3072]{1,0:T(8,128)(2,1)S(1)}, bf16[64,3072]{1,0:T(8,128)(2,1)S(1)}, u32[]{:S(2)}, u32[]{:S(2)}) collective-permute-start(bf16[64,3072]{1,0:T(8,128)(2,1)S(1)} %get-tuple-element.34), channel_id=1, source_target_pairs={{0,16},{2,18},{4,20},{6,22},{8,24},{10,26},{12,28},{14,30},{16,0},... | collective-permute-start | bytes 1179656 | tf_op jit(solution)/shard_map/ppermute | solution.py:229
  32.5 8.7 %collective-permute-start.10 = (bf16[32,3072]{1,0:T(8,128)(2,1)S(1)}, bf16[32,3072]{1,0:T(8,128)(2,1)S(1)}, u32[]{:S(2)}, u32[]{:S(2)}) collective-permute-start(bf16[32,3072]{1,0:T(8,128)(2,1)S(1)} %collective-permute-done.5.near_ref), channel_id=1, source_target_pairs={{0,2},{2,0},{4,6},{6,4},{8,10},{10,8},{12,14},{14,12},{16,18},{18,... | collective-permute-start | bytes 589832 | tf_op jit(solution)/shard_map/ppermute | solution.py:229
  38.0 9.4 %collective-permute-start.12 = (bf16[32,3072]{1,0:T(8,128)(2,1)S(1)}, bf16[32,3072]{1,0:T(8,128)(2,1)S(1)}, u32[]{:S(2)}, u32[]{:S(2)}) collective-permute-start(bf16[32,3072]{1,0:T(8,128)(2,1)S(1)} %get-tuple-element.53), channel_id=1, source_target_pairs={{0,2},{2,0},{4,6},{6,4},{8,10},{10,8},{12,14},{14,12},{16,18},{18,... | collective-permute-start | bytes 589832 | tf_op jit(solution)/shard_map/ppermute | solution.py:229
  39.6 10.1 %collective-permute-start.11 = (bf16[32,3072]{1,0:T(8,128)(2,1)S(1)}, bf16[32,3072]{1,0:T(8,128)(2,1)S(1)}, u32[]{:S(2)}, u32[]{:S(2)}) collective-permute-start(bf16[32,3072]{1,0:T(8,128)(2,1)S(1)} %add_convert_fusion.2), channel_id=1, source_target_pairs={{0,8},{2,10},{4,12},{6,14},{8,0},{10,2},{12,4},{14,6},{16,24},{18,... | collective-permute-start | bytes 589832 | tf_op jit(solution)/shard_map/ppermute | solution.py:229
  41.2 3.2 %copy-start = (s32[1,128,2]{1,2,0:T(2,128)S(1)}, s32[1,128,2]{1,2,0:T(2,128)}, u32[]{:S(2)}) copy-start(s32[1,128,2]{1,2,0:T(2,128)} %param.12) | copy-start | bytes 3076
  41.2 3.2 %copy-start.1 = (f32[1,128,2]{1,2,0:T(2,128)S(1)}, f32[1,128,2]{1,2,0:T(2,128)}, u32[]{:S(2)}) copy-start(f32[1,128,2]{1,2,0:T(2,128)} %param.13) | copy-start | bytes 3076
  42.5 7.2 %collective-permute-start.14 = (bf16[32,3072]{1,0:T(8,128)(2,1)S(1)}, bf16[32,3072]{1,0:T(8,128)(2,1)S(1)}, u32[]{:S(2)}, u32[]{:S(2)}) collective-permute-start(bf16[32,3072]{1,0:T(8,128)(2,1)S(1)} %get-tuple-element.54), channel_id=1, source_target_pairs={{0,2},{2,0},{4,6},{6,4},{8,10},{10,8},{12,14},{14,12},{16,18},{18,... | collective-permute-start | bytes 589832 | tf_op jit(solution)/shard_map/ppermute | solution.py:229
  46.7 5.7 %collective-permute-start.16 = (bf16[32,3072]{1,0:T(8,128)(2,1)S(1)}, bf16[32,3072]{1,0:T(8,128)(2,1)S(1)}, u32[]{:S(2)}, u32[]{:S(2)}) collective-permute-start(bf16[32,3072]{1,0:T(8,128)(2,1)S(1)} %get-tuple-element.56), channel_id=1, source_target_pairs={{0,2},{2,0},{4,6},{6,4},{8,10},{10,8},{12,14},{14,12},{16,18},{18,... | collective-permute-start | bytes 589832 | tf_op jit(solution)/shard_map/ppermute | solution.py:229
  47.5 9.2 %collective-permute-start.13 = (bf16[32,3072]{1,0:T(8,128)(2,1)S(1)}, bf16[32,3072]{1,0:T(8,128)(2,1)S(1)}, u32[]{:S(2)}, u32[]{:S(2)}) collective-permute-start(bf16[32,3072]{1,0:T(8,128)(2,1)S(1)} %add_convert_fusion.1), channel_id=1, source_target_pairs={{0,12},{2,14},{4,8},{6,10},{8,4},{10,6},{12,0},{14,2},{16,28},{18,... | collective-permute-start | bytes 589832 | tf_op jit(solution)/shard_map/ppermute | solution.py:229
  49.8 7.9 %collective-permute-start.15 = (bf16[32,3072]{1,0:T(8,128)(2,1)S(1)}, bf16[32,3072]{1,0:T(8,128)(2,1)S(1)}, u32[]{:S(2)}, u32[]{:S(2)}) collective-permute-start(bf16[32,3072]{1,0:T(8,128)(2,1)S(1)} %add_convert_fusion), channel_id=1, source_target_pairs={{0,4},{2,6},{4,0},{6,2},{8,12},{10,14},{12,8},{14,10},{16,20},{18,... | collective-permute-start | bytes 589832 | tf_op jit(solution)/shard_map/ppermute | solution.py:229

commit v7 on v6

--- a/solution.py
+++ b/solution.py
@@ -246,15 +246,14 @@
     near, far = {}, {}
     near[2] = moved(picked, 1, 2)
     far[0] = moved(picked, 1, 0, 1)
-    far[2] = moved(after(near[2], far[0], gain), 0, 0, 1)
+    far[2] = moved(after(near[2], gain), 0, 0, 1)
     near[3] = moved(near[2], 0, 1)
     far[3] = moved(far[2], 0, 1)
     near[1] = moved(after(picked, near[2]), 1, 1)
-    pieces = 2
-    size = token_count // pieces
+    cuts = [CAP * 3 // 2]
     arrived = [
-        moved(after(blocks[0, i * size:(i + 1) * size], far[0], near[2]), 1, 0)
-        for i in range(pieces)
+        moved(after(piece, far[0], near[2]), 1, 0)
+        for piece in jnp.split(blocks[0], cuts)
     ]
     base, table, near[0] = based(
         experts, arrived, gain, jnp.swapaxes(route_ids[0], 0, 1),

time: 59.7 us -> 60.5 us (1.013)
  starting transfers between devices: 25.8 us -> 27.1 us
    ppermute x17, starting transfers between devices: 25.8 us -> 27.1 us  [moved(): return lax.ppermute(value, ('section', 'expert'), pairs)]
  transfers between devices with their start and end apart: 17 -> 17, of which waited for: 9 -> 9; matrix products, arithmetic and copies ran while one was open for 0% -> 0% of each run, Pallas kernels for 16% -> 15%
where the time goes in v7:
time: 60.5 us; the launch traced here: 60.4 us
  starting transfers between devices  27.1 us (45%)
  waiting for transfers between devices  21.4 us (35%)
  Pallas kernels  11.6 us (19%)
    ppermute x17, starting transfers between devices, moved(): return lax.ppermute(value, ('section', 'expert'), pairs)  27.1 us
    ppermute x17, waiting for transfers between devices, moved(): return lax.ppermute(value, ('section', 'expert'), pairs)  21.4 us
    pallas_call x4, Pallas kernels, mlp(): pl.pallas_call(mlp_kernel, out_shape=(out, out), in_specs=[VMEM] * 6, out...  5.04 us
    pallas_call x2, Pallas kernels, loaded(): pl.pallas_call(functools.partial(load_kernel, len(arrays)), out_shape=tup...  3.23 us
    pallas_call x1, Pallas kernels, ended(): pl.pallas_call(functools.partial(end_kernel, columns), out_shape=jax.Shap...  1.89 us
  transfers between devices with their start and end apart: 17, of which 9 were waited for; matrix products, arithmetic and copies ran while one was open for 0% of the time, Pallas kernels for 15%

profile of v7, /device:TPU:0, one launch (start us, length us, event | category | flops | bytes accessed | tf_op | source)
XLA Modules:
  0.0 60.4 jit_solution(13926639241894698701)
XLA Ops:
  0.0 2.9 %collective-permute-start = (s32[1,128,2]{1,2,0:T(2,128)}, s32[1,128,2]{1,2,0:T(2,128)S(1)}, u32[]{:S(2)}, u32[]{:S(2)}) collective-permute-start(s32[1,128,2]{1,2,0:T(2,128)} %param.12), channel_id=1, source_target_pairs={{0,16},{2,18},{4,20},{6,22},{8,24},{10,26},{12,28},{14,30},{16,0},... | collective-permute-start | bytes 3080 | tf_op jit(solution)/shard_map/ppermute | solution.py:229
  2.9 1.1 %shard_map.73.block_ref = bf16[128,3072]{1,0:T(8,128)(2,1)S(1)} custom-call(bf16[128,3072]{1,0:T(8,128)(2,1)} %bitcast.25), custom_call_target="tpu_custom_call" | custom-call | bytes 6291456 | tf_op jit(solution)/shard_map/pallas_call | solution.py:33
  4.1 0.6 %collective-permute-done = s32[1,128,2]{1,2,0:T(2,128)S(1)} collective-permute-done((s32[1,128,2]{1,2,0:T(2,128)}, s32[1,128,2]{1,2,0:T(2,128)S(1)}, u32[]{:S(2)}, u32[]{:S(2)}) %collective-permute-start) | collective-permute-done | bytes 1056 | tf_op jit(solution)/shard_map/ppermute | solution.py:229
  4.7 0.4 shard_map.74
  5.1 4.1 %collective-permute-start.2 = (bf16[32,3072]{1,0:T(8,128)(2,1)S(1)}, bf16[32,3072]{1,0:T(8,128)(2,1)S(1)}, u32[]{:S(2)}, u32[]{:S(2)}) collective-permute-start(bf16[32,3072]{1,0:T(8,128)(2,1)S(1)} %shard_map.74), channel_id=1, source_target_pairs={{0,24},{2,26},{4,28},{6,30},{8,16},{10,18},{12,20},{14,22},{16,8},... | collective-permute-start | bytes 589832 | tf_op jit(solution)/shard_map/ppermute | solution.py:229
  9.2 1.5 %collective-permute-start.1 = (bf16[32,3072]{1,0:T(8,128)(2,1)S(1)}, bf16[32,3072]{1,0:T(8,128)(2,1)S(1)}, u32[]{:S(2)}, u32[]{:S(2)}) collective-permute-start(bf16[32,3072]{1,0:T(8,128)(2,1)S(1)} %shard_map.74), channel_id=1, source_target_pairs={{0,18},{2,16},{4,22},{6,20},{8,26},{10,24},{12,30},{14,28},{16,2},... | collective-permute-start | bytes 589832 | tf_op jit(solution)/shard_map/ppermute | solution.py:229
  10.7 0.0 copy-start.2
  10.7 2.1 %shard_map.75 = (bf16[192,3072]{1,0:T(8,128)(2,1)S(1)}, bf16[192,3072]{1,0:T(8,128)(2,1)S(1)}, bf16[192,3072]{1,0:T(8,128)(2,1)S(1)}, bf16[1,3072]{1,0:T(2,128)(2,1)S(1)}) custom-call(bf16[192,3072]{1,0:T(8,128)(2,1)} %bitcast.26, bf16[192,3072]{1,0:T(8,128)(2,1)} %bitcast.27, bf16[192,3072]{1,0:T(8,128)(2,1)} %bitcast.28, bf16[1,3072]{1,0:T(2,128)(2,1)} %refs_3_.1), custom_call_target="tpu_custom_call" | custom-call | bytes 6291456 | tf_op jit(solution)/shard_map/pallas_call | solution.py:33
  12.8 4.5 %collective-permute-done.2.near_ref = bf16[32,3072]{1,0:T(8,128)(2,1)S(1)} collective-permute-done((bf16[32,3072]{1,0:T(8,128)(2,1)S(1)}, bf16[32,3072]{1,0:T(8,128)(2,1)S(1)}, u32[]{:S(2)}, u32[]{:S(2)}) %collective-permute-start.2) | collective-permute-done | bytes 196640 | tf_op jit(solution)/shard_map/ppermute | solution.py:229
  17.2 1.5 %collective-permute-start.7 = (bf16[32,3072]{1,0:T(8,128)(2,1)S(1)}, bf16[32,3072]{1,0:T(8,128)(2,1)S(1)}, u32[]{:S(2)}, u32[]{:S(2)}) collective-permute-start(bf16[32,3072]{1,0:T(8,128)(2,1)S(1)} %collective-permute-done.2.near_ref), channel_id=1, source_target_pairs={{0,2},{2,0},{4,6},{6,4},{8,10},{10,8},{12,14},{14,12},{16,18},{18,... | collective-permute-start | bytes 589832 | tf_op jit(solution)/shard_map/ppermute | solution.py:229
  18.8 0.6 collective-permute-start.6
  19.4 0.0 copy-done.2
  19.4 2.3 %collective-permute-start.5 = (bf16[32,3072]{1,0:T(8,128)(2,1)S(1)}, bf16[32,3072]{1,0:T(8,128)(2,1)S(1)}, u32[]{:S(2)}, u32[]{:S(2)}) collective-permute-start(bf16[32,3072]{1,0:T(8,128)(2,1)S(1)} %shard_map.74), channel_id=1, source_target_pairs={{0,20},{2,22},{4,16},{6,18},{8,28},{10,30},{12,24},{14,26},{16,4},... | collective-permute-start | bytes 589832 | tf_op jit(solution)/shard_map/ppermute | solution.py:229
  21.7 0.0 collective-permute-done.1.far_ref
  21.7 0.6 %collective-permute-start.3 = (bf16[48,3072]{1,0:T(8,128)(2,1)S(1)}, bf16[48,3072]{1,0:T(8,128)(2,1)S(1)}, u32[]{:S(2)}, u32[]{:S(2)}) collective-permute-start(bf16[48,3072]{1,0:T(8,128)(2,1)S(1)} %slice_bitcast_fusion.1), channel_id=1, source_target_pairs={{0,16},{2,18},{4,20},{6,22},{8,24},{10,26},{12,28},{14,30},{16,0},... | collective-permute-start | bytes 884744 | tf_op jit(solution)/shard_map/ppermute | solution.py:229
  22.4 3.9 %collective-permute-done.6.near_ref = bf16[32,3072]{1,0:T(8,128)(2,1)S(1)} collective-permute-done((bf16[32,3072]{1,0:T(8,128)(2,1)S(1)}, bf16[32,3072]{1,0:T(8,128)(2,1)S(1)}, u32[]{:S(2)}, u32[]{:S(2)}) %collective-permute-start.6) | collective-permute-done | bytes 196640 | tf_op jit(solution)/shard_map/ppermute | solution.py:229
  26.2 0.0 collective-permute-done.7.far_ref
  26.3 1.3 %shard_map.77 = (bf16[32,3072]{1,0:T(8,128)(2,1)S(1)}, bf16[32,3072]{1,0:T(8,128)(2,1)S(1)}) custom-call(bf16[32,3072]{1,0:T(8,128)(2,1)S(1)} %collective-permute-done.2.near_ref, bf16[32,3072]{1,0:T(8,128)(2,1)S(1)} %collective-permute-done.7.far_ref, bf16[1,3072]{1,0:T(2,128)(2,1)S(1)} %get-tuple-element.32.gain_ref, ...), custom_call_target="tpu_custom_call" | custom-call | flops 226492416 | bytes 3538944 | tf_op jit(solution)/shard_map/pallas_call | solution.py:95
  27.5 0.5 collective-permute-start.8
  28.1 1.0 %collective-permute-start.9 = (bf16[32,3072]{1,0:T(8,128)(2,1)S(1)}, bf16[32,3072]{1,0:T(8,128)(2,1)S(1)}, u32[]{:S(2)}, u32[]{:S(2)}) collective-permute-start(bf16[32,3072]{1,0:T(8,128)(2,1)S(1)} %collective-permute-done.7.far_ref), channel_id=1, source_target_pairs={{0,4},{2,6},{4,0},{6,2},{8,12},{10,14},{12,8},{14,10},{16,20},{18,... | collective-permute-start | bytes 589832 | tf_op jit(solution)/shard_map/ppermute | solution.py:229
  29.1 1.0 %collective-permute-start.4 = (bf16[80,3072]{1,0:T(8,128)(2,1)S(1)}, bf16[80,3072]{1,0:T(8,128)(2,1)S(1)}, u32[]{:S(2)}, u32[]{:S(2)}) collective-permute-start(bf16[80,3072]{1,0:T(8,128)(2,1)S(1)} %slice_bitcast_fusion), channel_id=1, source_target_pairs={{0,16},{2,18},{4,20},{6,22},{8,24},{10,26},{12,28},{14,30},{16,0},... | collective-permute-start | bytes 1474568 | tf_op jit(solution)/shard_map/ppermute | solution.py:229
  30.1 1.2 %collective-permute-done.5.near_ref = bf16[32,3072]{1,0:T(8,128)(2,1)S(1)} collective-permute-done((bf16[32,3072]{1,0:T(8,128)(2,1)S(1)}, bf16[32,3072]{1,0:T(8,128)(2,1)S(1)}, u32[]{:S(2)}, u32[]{:S(2)}) %collective-permute-start.5) | collective-permute-done | bytes 196640 | tf_op jit(solution)/shard_map/ppermute | solution.py:229
  31.3 0.2 collective-permute-start.10
  31.5 3.1 %collective-permute-done.3.refs_0_ = bf16[48,3072]{1,0:T(8,128)(2,1)S(1)} collective-permute-done((bf16[48,3072]{1,0:T(8,128)(2,1)S(1)}, bf16[48,3072]{1,0:T(8,128)(2,1)S(1)}, u32[]{:S(2)}, u32[]{:S(2)}) %collective-permute-start.3) | collective-permute-done | bytes 294944 | tf_op jit(solution)/shard_map/ppermute | solution.py:229
  34.6 0.0 collective-permute-done.8
  34.6 0.0 collective-permute-done.9.far_ref
  34.6 1.3 %shard_map.78 = (bf16[32,3072]{1,0:T(8,128)(2,1)S(1)}, bf16[32,3072]{1,0:T(8,128)(2,1)S(1)}) custom-call(bf16[32,3072]{1,0:T(8,128)(2,1)S(1)} %collective-permute-done.6.near_ref, bf16[32,3072]{1,0:T(8,128)(2,1)S(1)} %collective-permute-done.9.far_ref, bf16[1,3072]{1,0:T(2,128)(2,1)S(1)} %get-tuple-element.32.gain_ref, ...), custom_call_target="tpu_custom_call" | custom-call | flops 226492416 | bytes 3538944 | tf_op jit(solution)/shard_map/pallas_call | solution.py:95
  35.9 0.8 %collective-permute-start.12 = (bf16[32,3072]{1,0:T(8,128)(2,1)S(1)}, bf16[32,3072]{1,0:T(8,128)(2,1)S(1)}, u32[]{:S(2)}, u32[]{:S(2)}) collective-permute-start(bf16[32,3072]{1,0:T(8,128)(2,1)S(1)} %get-tuple-element.53), channel_id=1, source_target_pairs={{0,2},{2,0},{4,6},{6,4},{8,10},{10,8},{12,14},{14,12},{16,18},{18,... | collective-permute-start | bytes 589832 | tf_op jit(solution)/shard_map/ppermute | solution.py:229
  36.7 3.2 %collective-permute-start.11 = (bf16[32,3072]{1,0:T(8,128)(2,1)S(1)}, bf16[32,3072]{1,0:T(8,128)(2,1)S(1)}, u32[]{:S(2)}, u32[]{:S(2)}) collective-permute-start(bf16[32,3072]{1,0:T(8,128)(2,1)S(1)} %add_convert_fusion.2), channel_id=1, source_target_pairs={{0,8},{2,10},{4,12},{6,14},{8,0},{10,2},{12,4},{14,6},{16,24},{18,... | collective-permute-start | bytes 589832 | tf_op jit(solution)/shard_map/ppermute | solution.py:229
  39.9 0.0 collective-permute-done.10.far_ref
  39.9 1.3 %shard_map.79 = (bf16[32,3072]{1,0:T(8,128)(2,1)S(1)}, bf16[32,3072]{1,0:T(8,128)(2,1)S(1)}) custom-call(bf16[32,3072]{1,0:T(8,128)(2,1)S(1)} %collective-permute-done.5.near_ref, bf16[32,3072]{1,0:T(8,128)(2,1)S(1)} %collective-permute-done.10.far_ref, bf16[1,3072]{1,0:T(2,128)(2,1)S(1)} %get-tuple-element.32.gain_ref, ...), custom_call_target="tpu_custom_call" | custom-call | flops 226492416 | bytes 3538944 | tf_op jit(solution)/shard_map/pallas_call | solution.py:95
  41.2 1.6 %collective-permute-start.14 = (bf16[32,3072]{1,0:T(8,128)(2,1)S(1)}, bf16[32,3072]{1,0:T(8,128)(2,1)S(1)}, u32[]{:S(2)}, u32[]{:S(2)}) collective-permute-start(bf16[32,3072]{1,0:T(8,128)(2,1)S(1)} %get-tuple-element.54), channel_id=1, source_target_pairs={{0,2},{2,0},{4,6},{6,4},{8,10},{10,8},{12,14},{14,12},{16,18},{18,... | collective-permute-start | bytes 589832 | tf_op jit(solution)/shard_map/ppermute | solution.py:229
  42.7 0.7 %collective-permute-done.4.refs_1_ = bf16[80,3072]{1,0:T(8,128)(2,1)S(1)} collective-permute-done((bf16[80,3072]{1,0:T(8,128)(2,1)S(1)}, bf16[80,3072]{1,0:T(8,128)(2,1)S(1)}, u32[]{:S(2)}, u32[]{:S(2)}) %collective-permute-start.4) | collective-permute-done | bytes 491552 | tf_op jit(solution)/shard_map/ppermute | solution.py:229
  43.5 0.0 copy-done
  43.5 0.0 copy-done.1
  43.5 1.0 %shard_map.76 = (f32[128,3072]{1,0:T(8,128)S(1)}, bf16[128,160]{1,0:T(8,128)(2,1)S(1)}, bf16[32,3072]{1,0:T(8,128)(2,1)S(1)}) custom-call(bf16[1,3072]{1,0:T(2,128)(2,1)S(1)} %get-tuple-element.32.gain_ref, s32[2,128]{1,0:T(2,128)S(1)} %bitcast.22, f32[2,128]{1,0:T(2,128)S(1)} %bitcast.23, bf16[48,3072]{1,0:T(8,128)(2,1)S(1)} %collective-permute-done.3.refs_0_, ...), custom_call_target="tpu_custom_call" | custom-call | flops 3145728 | bytes 2359296 | tf_op jit(solution)/shard_map/pallas_call | solution.py:150
  44.5 1.3 %shard_map.80 = (bf16[32,3072]{1,0:T(8,128)(2,1)S(1)}, bf16[32,3072]{1,0:T(8,128)(2,1)S(1)}) custom-call(bf16[32,3072]{1,0:T(8,128)(2,1)S(1)} %get-tuple-element.51.near_ref, bf16[32,3072]{1,0:T(8,128)(2,1)S(1)} %collective-permute-done.1.far_ref, bf16[1,3072]{1,0:T(2,128)(2,1)S(1)} %get-tuple-element.32.gain_ref, ...), custom_call_target="tpu_custom_call" | custom-call | flops 226492416 | bytes 3538944 | tf_op jit(solution)/shard_map/pallas_call | solution.py:95
  45.8 0.6 collective-permute-start.16
  46.3 0.0 collective-permute-done.12
  46.4 4.5 %collective-permute-start.13 = (bf16[32,3072]{1,0:T(8,128)(2,1)S(1)}, bf16[32,3072]{1,0:T(8,128)(2,1)S(1)}, u32[]{:S(2)}, u32[]{:S(2)}) collective-permute-start(bf16[32,3072]{1,0:T(8,128)(2,1)S(1)} %add_convert_fusion.1), channel_id=1, source_target_pairs={{0,12},{2,14},{4,8},{6,10},{8,4},{10,6},{12,0},{14,2},{16,28},{18,... | collective-permute-start | bytes 589832 | tf_op jit(solution)/shard_map/ppermute | solution.py:229
  50.9 0.0 collective-permute-done.14
  50.9 0.1 add_convert_fusion
  51.0 0.0 collective-permute-done.11.right_ref
  51.1 0.1 collective-permute-start.15
  51.1 0.4 collective-permute-done.16.refs_3_
  51.5 4.9 %collective-permute-done.13.refs_1_ = bf16[32,3072]{1,0:T(8,128)(2,1)S(1)} collective-permute-done((bf16[32,3072]{1,0:T(8,128)(2,1)S(1)}, bf16[32,3072]{1,0:T(8,128)(2,1)S(1)}, u32[]{:S(2)}, u32[]{:S(2)}) %collective-permute-start.13) | collective-permute-done | bytes 196640 | tf_op jit(solution)/shard_map/ppermute | solution.py:229
  56.4 2.1 %collective-permute-done.15.refs_2_ = bf16[32,3072]{1,0:T(8,128)(2,1)S(1)} collective-permute-done((bf16[32,3072]{1,0:T(8,128)(2,1)S(1)}, bf16[32,3072]{1,0:T(8,128)(2,1)S(1)}, u32[]{:S(2)}, u32[]{:S(2)}) %collective-permute-start.15) | collective-permute-done | bytes 196640 | tf_op jit(solution)/shard_map/ppermute | solution.py:229
  58.5 1.9 %shard_map.82 = bf16[128,3072]{1,0:T(8,128)(2,1)} custom-call(f32[128,3072]{1,0:T(8,128)S(1)} %get-tuple-element.35.base_ref, bf16[128,160]{1,0:T(8,128)(2,1)S(1)} %get-tuple-element.36.table_ref, f32[32,3072]{1,0:T(8,128)S(1)} %shard_map.81.refs_0_, bf16[32,3072]{1,0:T(8,128)(2,1)S(1)} %collective-permute-done.13.refs_1_, ...), custom_call_target="tpu_custom_call" | custom-call | flops 100663296 | bytes 2359296 | tf_op jit(solution)/shard_map/pallas_call | solution.py:182
  (7 shorter events, 0.2 us)
Async XLA Ops:
  0.0 4.7 %collective-permute-start = (s32[1,128,2]{1,2,0:T(2,128)}, s32[1,128,2]{1,2,0:T(2,128)S(1)}, u32[]{:S(2)}, u32[]{:S(2)}) collective-permute-start(s32[1,128,2]{1,2,0:T(2,128)} %param.12), channel_id=1, source_target_pairs={{0,16},{2,18},{4,20},{6,22},{8,24},{10,26},{12,28},{14,30},{16,0},... | collective-permute-start | bytes 3080 | tf_op jit(solution)/shard_map/ppermute | solution.py:229
  5.1 12.2 %collective-permute-start.2 = (bf16[32,3072]{1,0:T(8,128)(2,1)S(1)}, bf16[32,3072]{1,0:T(8,128)(2,1)S(1)}, u32[]{:S(2)}, u32[]{:S(2)}) collective-permute-start(bf16[32,3072]{1,0:T(8,128)(2,1)S(1)} %shard_map.74), channel_id=1, source_target_pairs={{0,24},{2,26},{4,28},{6,30},{8,16},{10,18},{12,20},{14,22},{16,8},... | collective-permute-start | bytes 589832 | tf_op jit(solution)/shard_map/ppermute | solution.py:229
  9.2 12.6 %collective-permute-start.1 = (bf16[32,3072]{1,0:T(8,128)(2,1)S(1)}, bf16[32,3072]{1,0:T(8,128)(2,1)S(1)}, u32[]{:S(2)}, u32[]{:S(2)}) collective-permute-start(bf16[32,3072]{1,0:T(8,128)(2,1)S(1)} %shard_map.74), channel_id=1, source_target_pairs={{0,18},{2,16},{4,22},{6,20},{8,26},{10,24},{12,30},{14,28},{16,2},... | collective-permute-start | bytes 589832 | tf_op jit(solution)/shard_map/ppermute | solution.py:229
  10.7 8.7 %copy-start.2 = (bf16[1,128,3072]{2,1,0:T(8,128)(2,1)S(1)}, bf16[1,128,3072]{2,1,0:T(8,128)(2,1)}, u32[]{:S(2)}) copy-start(bf16[1,128,3072]{2,1,0:T(8,128)(2,1)} %param.7) | copy-start | bytes 2359300
  17.2 9.0 %collective-permute-start.7 = (bf16[32,3072]{1,0:T(8,128)(2,1)S(1)}, bf16[32,3072]{1,0:T(8,128)(2,1)S(1)}, u32[]{:S(2)}, u32[]{:S(2)}) collective-permute-start(bf16[32,3072]{1,0:T(8,128)(2,1)S(1)} %collective-permute-done.2.near_ref), channel_id=1, source_target_pairs={{0,2},{2,0},{4,6},{6,4},{8,10},{10,8},{12,14},{14,12},{16,18},{18,... | collective-permute-start | bytes 589832 | tf_op jit(solution)/shard_map/ppermute | solution.py:229
  18.8 7.5 %collective-permute-start.6 = (bf16[32,3072]{1,0:T(8,128)(2,1)S(1)}, bf16[32,3072]{1,0:T(8,128)(2,1)S(1)}, u32[]{:S(2)}, u32[]{:S(2)}) collective-permute-start(bf16[32,3072]{1,0:T(8,128)(2,1)S(1)} %collective-permute-done.2.near_ref), channel_id=1, source_target_pairs={{0,4},{2,6},{4,0},{6,2},{8,12},{10,14},{12,8},{14,10},{16,20},{18,... | collective-permute-start | bytes 589832 | tf_op jit(solution)/shard_map/ppermute | solution.py:229
  19.4 11.9 %collective-permute-start.5 = (bf16[32,3072]{1,0:T(8,128)(2,1)S(1)}, bf16[32,3072]{1,0:T(8,128)(2,1)S(1)}, u32[]{:S(2)}, u32[]{:S(2)}) collective-permute-start(bf16[32,3072]{1,0:T(8,128)(2,1)S(1)} %shard_map.74), channel_id=1, source_target_pairs={{0,20},{2,22},{4,16},{6,18},{8,28},{10,30},{12,24},{14,26},{16,4},... | collective-permute-start | bytes 589832 | tf_op jit(solution)/shard_map/ppermute | solution.py:229
  21.7 12.9 %collective-permute-start.3 = (bf16[48,3072]{1,0:T(8,128)(2,1)S(1)}, bf16[48,3072]{1,0:T(8,128)(2,1)S(1)}, u32[]{:S(2)}, u32[]{:S(2)}) collective-permute-start(bf16[48,3072]{1,0:T(8,128)(2,1)S(1)} %slice_bitcast_fusion.1), channel_id=1, source_target_pairs={{0,16},{2,18},{4,20},{6,22},{8,24},{10,26},{12,28},{14,30},{16,0},... | collective-permute-start | bytes 884744 | tf_op jit(solution)/shard_map/ppermute | solution.py:229
  27.5 7.1 %collective-permute-start.8 = (bf16[32,3072]{1,0:T(8,128)(2,1)S(1)}, bf16[32,3072]{1,0:T(8,128)(2,1)S(1)}, u32[]{:S(2)}, u32[]{:S(2)}) collective-permute-start(bf16[32,3072]{1,0:T(8,128)(2,1)S(1)} %get-tuple-element.44), channel_id=1, source_target_pairs={{0,2},{2,0},{4,6},{6,4},{8,10},{10,8},{12,14},{14,12},{16,18},{18,... | collective-permute-start | bytes 589832 | tf_op jit(solution)/shard_map/ppermute | solution.py:229
  28.1 6.5 %collective-permute-start.9 = (bf16[32,3072]{1,0:T(8,128)(2,1)S(1)}, bf16[32,3072]{1,0:T(8,128)(2,1)S(1)}, u32[]{:S(2)}, u32[]{:S(2)}) collective-permute-start(bf16[32,3072]{1,0:T(8,128)(2,1)S(1)} %collective-permute-done.7.far_ref), channel_id=1, source_target_pairs={{0,4},{2,6},{4,0},{6,2},{8,12},{10,14},{12,8},{14,10},{16,20},{18,... | collective-permute-start | bytes 589832 | tf_op jit(solution)/shard_map/ppermute | solution.py:229
  29.1 14.4 %collective-permute-start.4 = (bf16[80,3072]{1,0:T(8,128)(2,1)S(1)}, bf16[80,3072]{1,0:T(8,128)(2,1)S(1)}, u32[]{:S(2)}, u32[]{:S(2)}) collective-permute-start(bf16[80,3072]{1,0:T(8,128)(2,1)S(1)} %slice_bitcast_fusion), channel_id=1, source_target_pairs={{0,16},{2,18},{4,20},{6,22},{8,24},{10,26},{12,28},{14,30},{16,0},... | collective-permute-start | bytes 1474568 | tf_op jit(solution)/shard_map/ppermute | solution.py:229
  31.3 8.6 %collective-permute-start.10 = (bf16[32,3072]{1,0:T(8,128)(2,1)S(1)}, bf16[32,3072]{1,0:T(8,128)(2,1)S(1)}, u32[]{:S(2)}, u32[]{:S(2)}) collective-permute-start(bf16[32,3072]{1,0:T(8,128)(2,1)S(1)} %collective-permute-done.5.near_ref), channel_id=1, source_target_pairs={{0,2},{2,0},{4,6},{6,4},{8,10},{10,8},{12,14},{14,12},{16,18},{18,... | collective-permute-start | bytes 589832 | tf_op jit(solution)/shard_map/ppermute | solution.py:229
  35.9 10.5 %collective-permute-start.12 = (bf16[32,3072]{1,0:T(8,128)(2,1)S(1)}, bf16[32,3072]{1,0:T(8,128)(2,1)S(1)}, u32[]{:S(2)}, u32[]{:S(2)}) collective-permute-start(bf16[32,3072]{1,0:T(8,128)(2,1)S(1)} %get-tuple-element.53), channel_id=1, source_target_pairs={{0,2},{2,0},{4,6},{6,4},{8,10},{10,8},{12,14},{14,12},{16,18},{18,... | collective-permute-start | bytes 589832 | tf_op jit(solution)/shard_map/ppermute | solution.py:229
  36.7 14.3 %collective-permute-start.11 = (bf16[32,3072]{1,0:T(8,128)(2,1)S(1)}, bf16[32,3072]{1,0:T(8,128)(2,1)S(1)}, u32[]{:S(2)}, u32[]{:S(2)}) collective-permute-start(bf16[32,3072]{1,0:T(8,128)(2,1)S(1)} %add_convert_fusion.2), channel_id=1, source_target_pairs={{0,8},{2,10},{4,12},{6,14},{8,0},{10,2},{12,4},{14,6},{16,24},{18,... | collective-permute-start | bytes 589832 | tf_op jit(solution)/shard_map/ppermute | solution.py:229
  39.9 3.6 %copy-start = (s32[1,128,2]{1,2,0:T(2,128)S(1)}, s32[1,128,2]{1,2,0:T(2,128)}, u32[]{:S(2)}) copy-start(s32[1,128,2]{1,2,0:T(2,128)} %param.12) | copy-start | bytes 3076
  39.9 3.6 %copy-start.1 = (f32[1,128,2]{1,2,0:T(2,128)S(1)}, f32[1,128,2]{1,2,0:T(2,128)}, u32[]{:S(2)}) copy-start(f32[1,128,2]{1,2,0:T(2,128)} %param.13) | copy-start | bytes 3076
  41.2 9.8 %collective-permute-start.14 = (bf16[32,3072]{1,0:T(8,128)(2,1)S(1)}, bf16[32,3072]{1,0:T(8,128)(2,1)S(1)}, u32[]{:S(2)}, u32[]{:S(2)}) collective-permute-start(bf16[32,3072]{1,0:T(8,128)(2,1)S(1)} %get-tuple-element.54), channel_id=1, source_target_pairs={{0,2},{2,0},{4,6},{6,4},{8,10},{10,8},{12,14},{14,12},{16,18},{18,... | collective-permute-start | bytes 589832 | tf_op jit(solution)/shard_map/ppermute | solution.py:229
  45.8 5.7 %collective-permute-start.16 = (bf16[32,3072]{1,0:T(8,128)(2,1)S(1)}, bf16[32,3072]{1,0:T(8,128)(2,1)S(1)}, u32[]{:S(2)}, u32[]{:S(2)}) collective-permute-start(bf16[32,3072]{1,0:T(8,128)(2,1)S(1)} %get-tuple-element.56), channel_id=1, source_target_pairs={{0,2},{2,0},{4,6},{6,4},{8,10},{10,8},{12,14},{14,12},{16,18},{18,... | collective-permute-start | bytes 589832 | tf_op jit(solution)/shard_map/ppermute | solution.py:229
  46.4 10.0 %collective-permute-start.13 = (bf16[32,3072]{1,0:T(8,128)(2,1)S(1)}, bf16[32,3072]{1,0:T(8,128)(2,1)S(1)}, u32[]{:S(2)}, u32[]{:S(2)}) collective-permute-start(bf16[32,3072]{1,0:T(8,128)(2,1)S(1)} %add_convert_fusion.1), channel_id=1, source_target_pairs={{0,12},{2,14},{4,8},{6,10},{8,4},{10,6},{12,0},{14,2},{16,28},{18,... | collective-permute-start | bytes 589832 | tf_op jit(solution)/shard_map/ppermute | solution.py:229
  51.1 7.4 %collective-permute-start.15 = (bf16[32,3072]{1,0:T(8,128)(2,1)S(1)}, bf16[32,3072]{1,0:T(8,128)(2,1)S(1)}, u32[]{:S(2)}, u32[]{:S(2)}) collective-permute-start(bf16[32,3072]{1,0:T(8,128)(2,1)S(1)} %add_convert_fusion), channel_id=1, source_target_pairs={{0,4},{2,6},{4,0},{6,2},{8,12},{10,14},{12,8},{14,10},{16,20},{18,... | collective-permute-start | bytes 589832 | tf_op jit(solution)/shard_map/ppermute | solution.py:229

commit v8 on v7

--- a/solution.py
+++ b/solution.py
@@ -18,10 +18,61 @@
     return lax.optimization_barrier((value, *others))[0]
 
 
-def load_kernel(count, *refs):
+def parity():
+    return lax.rem(lax.axis_index("expert"), 2)
+
+
+def half_of(ref, which):
+    half = ref.shape[1] // 2
+    return ref.at[:, pl.ds(pl.multiple_of(which * half, half), half)]
+
+
+def part_of(ref, which, parts):
+    rows = ref.shape[0] // parts
+    return ref.at[pl.ds(pl.multiple_of(which * rows, rows), rows)]
+
+
+def load_kernel(kinds, *refs):
+    count = len(kinds)
     sources, targets, sems = refs[:count], refs[count:2 * count], refs[2 * count]
+    copies = []
+    for i, (kind, source, target) in enumerate(zip(kinds, sources, targets)):
+        if kind == "own":
+            source = half_of(source, parity())
+        if kind == "sent":
+            source = half_of(source, 1 - parity())
+            source = part_of(source, lax.axis_index("dp"), source.shape[0] // target.shape[0])
+        copies.append(pltpu.make_async_copy(source, target, sems.at[i]))
+    for copy in copies:
+        copy.start()
+    for copy in copies:
+        copy.wait()
+
+
+def loaded(arrays, kinds):
+    shapes = []
+    for a, kind in zip(arrays, kinds):
+        rows, columns = a.shape
+        rows = rows // lax.axis_size("dp") if kind == "sent" else rows
+        shapes.append((rows, columns if kind == "whole" else columns // 2))
+    return pl.pallas_call(
+        functools.partial(load_kernel, kinds),
+        out_shape=tuple(jax.ShapeDtypeStruct(s, a.dtype) for s, a in zip(shapes, arrays)),
+        in_specs=[HBM] * len(arrays),
+        out_specs=(VMEM,) * len(arrays),
+        scratch_shapes=[pltpu.SemaphoreType.DMA((len(arrays),))],
+        compiler_params=PARAMS,
+        cost_estimate=pl.CostEstimate(
+            flops=0, bytes_accessed=4 * sum(r * c for r, c in shapes), transcendentals=0
+        ),
+    )(*(pltpu.with_memory_space_constraint(a, pltpu.HBM) for a in arrays))
+
+
+def gather_kernel(own_ref, other_ref, out_ref, sems):
+    core = lax.axis_index("dp")
     copies = [
-        pltpu.make_async_copy(a, b, sems.at[i]) for i, (a, b) in enumerate(zip(sources, targets))
+        pltpu.make_async_copy(own_ref, part_of(out_ref, core, 2), sems.at[0]),
+        pltpu.make_async_copy(other_ref, part_of(out_ref, 1 - core, 2), sems.at[1]),
     ]
     for copy in copies:
         copy.start()
@@ -29,16 +80,19 @@
         copy.wait()
 
 
-def loaded(*arrays):
-    return pl.pallas_call(
-        functools.partial(load_kernel, len(arrays)),
-        out_shape=tuple(jax.ShapeDtypeStruct(a.shape, a.dtype) for a in arrays),
-        in_specs=[HBM] * len(arrays),
-        out_specs=(VMEM,) * len(arrays),
-        scratch_shapes=[pltpu.SemaphoreType.DMA((len(arrays),))],
-        compiler_params=PARAMS,
-        cost_estimate=pl.CostEstimate(flops=0, bytes_accessed=6 * 1024 * 1024, transcendentals=0),
-    )(*(pltpu.with_memory_space_constraint(a, pltpu.HBM) for a in arrays))
+def gathered(own, other):
+    rows, columns = own.shape
+    return pl.pallas_call(
+        gather_kernel,
+        out_shape=jax.ShapeDtypeStruct((2 * rows, columns), own.dtype),
+        in_specs=[VMEM, VMEM],
+        out_specs=VMEM,
+        scratch_shapes=[pltpu.SemaphoreType.DMA((2,))],
+        compiler_params=PARAMS,
+        cost_estimate=pl.CostEstimate(
+            flops=0, bytes_accessed=8 * rows * columns, transcendentals=0
+        ),
+    )(own, other)
 
 
 def slot_rows(ids, e):
@@ -73,35 +127,77 @@
     )(ids_t, block)
 
 
-def mlp_kernel(near_ref, far_ref, gain_ref, gate_ref, up_ref, down_ref, near_out, far_out):
-    count = near_ref.shape[0]
+def hidden_kernel(near_ref, far_ref, gain_ref, gate_ref, up_ref, out_ref):
     rows = jnp.concatenate([near_ref[...], far_ref[...]], axis=0).astype(jnp.float32)
     inverse = lax.rsqrt(jnp.mean(rows * rows, axis=-1, keepdims=True) + 1e-06)
     normed = (rows * inverse * gain_ref[...].astype(jnp.float32)).astype(jnp.bfloat16)
     across = (((1,), (1,)), ((), ()))
     gate = lax.dot_general(normed, gate_ref[...], across, preferred_element_type=jnp.float32)
     up = lax.dot_general(normed, up_ref[...], across, preferred_element_type=jnp.float32)
-    hidden = (gate / (1.0 + jnp.exp(-gate)) * up).astype(jnp.bfloat16)
-    partial = jnp.dot(hidden, down_ref[...], preferred_element_type=jnp.float32)
-    partial = partial.astype(jnp.bfloat16)
-    near_out[...] = partial[:count]
-    far_out[...] = partial[count:]
-
-
-def mlp(near, far, gain, gate_t, up_t, down):
-    rows = 2 * near.shape[0]
-    width, hidden = down.shape[1], down.shape[0]
-    out = jax.ShapeDtypeStruct(near.shape, jnp.bfloat16)
-    return pl.pallas_call(
-        mlp_kernel,
-        out_shape=(out, out),
-        in_specs=[VMEM] * 6,
+    out_ref[...] = (gate / (1.0 + jnp.exp(-gate)) * up).astype(jnp.bfloat16)
+
+
+def hidden_of(near, far, gain, gate_t, up_t):
+    rows, (hidden, width) = 2 * near.shape[0], gate_t.shape
+    return pl.pallas_call(
+        hidden_kernel,
+        out_shape=jax.ShapeDtypeStruct((rows, hidden), jnp.bfloat16),
+        in_specs=[VMEM] * 5,
+        out_specs=VMEM,
+        compiler_params=PARAMS,
+        cost_estimate=pl.CostEstimate(
+            flops=4 * rows * width * hidden, bytes_accessed=4 * width * hidden, transcendentals=0
+        ),
+    )(near, far, gain, gate_t, up_t)
+
+
+def down_kernel(own_ref, other_ref, own_down_ref, other_down_ref, out_ref):
+    count = own_ref.shape[0] // 2
+    other = jnp.concatenate([other_ref[count:], other_ref[:count]], axis=0)
+    total = jnp.dot(own_ref[...], own_down_ref[...], preferred_element_type=jnp.float32)
+    total += jnp.dot(other, other_down_ref[...], preferred_element_type=jnp.float32)
+    out_ref[...] = total.astype(jnp.bfloat16)
+
+
+def down_of(own, other, own_down, other_down):
+    rows, (hidden, half) = own.shape[0], own_down.shape
+    return pl.pallas_call(
+        down_kernel,
+        out_shape=jax.ShapeDtypeStruct((rows, half), jnp.bfloat16),
+        in_specs=[VMEM] * 4,
+        out_specs=VMEM,
+        compiler_params=PARAMS,
+        cost_estimate=pl.CostEstimate(
+            flops=4 * rows * half * hidden, bytes_accessed=4 * half * hidden, transcendentals=0
+        ),
+    )(own, other, own_down, other_down)
+
+
+def join_kernel(*refs):
+    back_refs, near_ref, far_ref = refs[:-2], refs[-2], refs[-1]
+    total = back_refs[0][...].astype(jnp.float32)
+    for ref in back_refs[1:]:
+        total = total + ref[...].astype(jnp.float32)
+    count = near_ref.shape[0]
+    near_ref[...] = total[:count]
+    far_ref[...] = total[count:].astype(jnp.bfloat16)
+
+
+def joined(backs):
+    rows, half = backs[0].shape
+    return pl.pallas_call(
+        join_kernel,
+        out_shape=(
+            jax.ShapeDtypeStruct((rows // 2, half), jnp.float32),
+            jax.ShapeDtypeStruct((rows // 2, half), jnp.bfloat16),
+        ),
+        in_specs=[VMEM] * len(backs),
         out_specs=(VMEM, VMEM),
         compiler_params=PARAMS,
         cost_estimate=pl.CostEstimate(
-            flops=6 * rows * width * hidden, bytes_accessed=6 * width * hidden, transcendentals=0
-        ),
-    )(near, far, gain, gate_t, up_t, down)
+            flops=4 * rows * half, bytes_accessed=8 * rows * half, transcendentals=0
+        ),
+    )(*backs)
 
 
 def parts_of(value):
@@ -163,34 +259,37 @@
     )(gain, ids_t, weights_t, *blocks)
 
 
-def end_kernel(columns, base_ref, table_ref, *refs):
-    back_refs, out_ref = refs[:-1], refs[-1]
-    here = pl.ds(pl.multiple_of(pl.program_id(0) * columns, columns), columns)
-    total = back_refs[0][:, here].astype(jnp.float32)
-    for ref in back_refs[1:]:
-        total = total + ref[:, here].astype(jnp.float32)
+def end_kernel(steps, ordered, base_ref, table_ref, near_ref, other_ref, out_ref):
+    step = pl.program_id(0)
+    columns = out_ref.shape[1]
+    here = pl.ds(pl.multiple_of(step * columns, columns), columns)
+    within = pl.ds(pl.multiple_of(lax.rem(step, steps // 2) * columns, columns), columns)
+    first = 0 if ordered else parity()
+    near = near_ref[:, within].astype(jnp.float32)
+    other = other_ref[:, within].astype(jnp.float32)
+    total = jnp.where(lax.div(step, steps // 2) == first, near, other)
     high, low, _ = parts_of(total)
     rows = jnp.concatenate([high, high, high, low, low], axis=0)
     added = jnp.dot(table_ref[...], rows, preferred_element_type=jnp.float32)
     out_ref[...] = (base_ref[:, here] + added).astype(jnp.bfloat16)
 
 
-def ended(base, table, backs):
+def ended(base, table, near, other, ordered):
     count, width = base.shape
-    steps = 3
+    steps = 4
     columns = width // steps
     return pl.pallas_call(
-        functools.partial(end_kernel, columns),
+        functools.partial(end_kernel, steps, ordered),
         out_shape=jax.ShapeDtypeStruct((count, width), jnp.bfloat16),
         grid=(steps,),
-        in_specs=[VMEM] * (2 + len(backs)),
+        in_specs=[VMEM] * 4,
         out_specs=pl.BlockSpec((count, columns), lambda i: (0, i)),
         compiler_params=PARAMS,
         cost_estimate=pl.CostEstimate(
             flops=2 * count * width * table.shape[0], bytes_accessed=6 * count * width,
             transcendentals=0,
         ),
-    )(base, table, *backs)
+    )(base, table, near, other)
 
 
 def early_kernel(left_ref, right_ref, out_ref):
@@ -235,13 +334,20 @@
         ).reshape(experts * CAP, width)
 
     next_ids = moved(route_ids, -1, 0)[0]
-    block, = loaded(blocks[0])
+    block, down_sent = loaded((blocks[0], w_down[0]), ("whole", "sent"))
     picked = picked_rows(experts, jnp.swapaxes(next_ids, 0, 1), block)
     if experts > 1:
         picked = exchanged(picked)
-    gate_t, up_t, down, gain = loaded(
-        after(jnp.swapaxes(w_gate[0], 0, 1), picked), jnp.swapaxes(w_up[0], 0, 1), w_down[0], norm_gain
+    own_down, gate_t, up_t, gain = loaded(
+        (
+            after(w_down[0], picked), jnp.swapaxes(w_gate[0], 0, 1), jnp.swapaxes(w_up[0], 0, 1),
+            norm_gain,
+        ),
+        ("own", "whole", "whole", "whole"),
     )
+    other_down = moved(after(down_sent, picked), 0, 0, 1)
+    if lax.axis_size("dp") == 2:
+        other_down = gathered(other_down, lax.ppermute(other_down, "dp", [(0, 1), (1, 0)]))
 
     near, far = {}, {}
     near[2] = moved(picked, 1, 2)
@@ -249,7 +355,7 @@
     far[2] = moved(after(near[2], gain), 0, 0, 1)
     near[3] = moved(near[2], 0, 1)
     far[3] = moved(far[2], 0, 1)
-    near[1] = moved(after(picked, near[2]), 1, 1)
+    near[1] = moved(after(picked, far[2]), 1, 1)
     cuts = [CAP * 3 // 2]
     arrived = [
         moved(after(piece, far[0], near[2]), 1, 0)
@@ -262,24 +368,26 @@
 
     if experts > 1:
         near[0] = exchanged(near[0])
-    own, other = {}, {}
+    hidden, part, back = {}, {}, {}
     for k in (2, 3, 1, 0):
-        first = {2: (near[3],), 3: (other.get(2), arrived[0]), 1: (own.get(3),), 0: (own.get(1),)}[k]
+        first = {
+            2: (near[3],), 3: (part.get(2), arrived[0]), 1: (hidden.get(3),), 0: (hidden.get(1), back.get(2))
+        }[k]
         if k == 3:
-            far[1] = moved(after(near[1], own[2]), 0, 0, 1)
-        own[k], sent = mlp(after(near[k], *first), far[k], gain, gate_t, up_t, down)
-        other[k] = moved(sent, 0, 0, 1)
-    both = {
-        k: (own[k].astype(jnp.float32) + other[k].astype(jnp.float32)).astype(jnp.bfloat16)
-        for k in (2, 3, 1)
-    }
-    early = summed_early(own[0], moved(both[2], 0, 2))
-    backs = [
-        early, moved(both[3], 0, 3), moved(after(both[1], early), 0, 1), other[0],
-    ]
+            far[1] = moved(after(near[1], part[2]), 0, 0, 1)
+        hidden[k] = hidden_of(after(near[k], *first), far[k], gain, gate_t, up_t)
+        part[k] = down_of(hidden[k], moved(hidden[k], 0, 0, 1), own_down, other_down)
+        back[k] = moved(part[k], 0, k) if k else part[k]
+    early = summed_early(back[0], back[2])
+    own, others = joined([early, back[3], back[1]])
+    others = moved(others, 0, 0, 1)
     if experts > 1:
-        backs = [exchanged(sum(back.astype(jnp.float32) for back in backs).astype(jnp.bfloat16))]
-    return ended(base, table, backs)[None]
+        own = own.astype(jnp.bfloat16)
+        left = parity() == 0
+        summed = [jnp.where(left, own, others), jnp.where(left, others, own)]
+        summed = exchanged(jnp.concatenate(summed, axis=1))
+        own, others = summed[:, :width // 2], summed[:, width // 2:]
+    return ended(base, table, own, others, experts > 1)[None]
 
 
 def solution(mesh):

time: 60.5 us -> 61.9 us (1.023)
  waiting for transfers between devices: 21.4 us -> 23.4 us
  starting transfers between devices: 27.1 us -> 26.3 us
    ppermute x17 -> x19, waiting for transfers between devices: 21.4 us -> 23.4 us  [moved(): return lax.ppermute(value, ('section', 'expert'), pairs)]
    ppermute x17 -> x19, starting transfers between devices: 27.1 us -> 26.3 us  [moved(): return lax.ppermute(value, ('section', 'expert'), pairs)]
    pallas_call x7 -> x13, Pallas kernels: 10.2 us -> 10.5 us  [the longest x4 3.85 us: hidden_of(): pl.pallas_call(hidden_kernel, out_shape=jax.ShapeDtypeStruct((rows, hidde...]
  transfers between devices with their start and end apart: 17 -> 20, of which waited for: 9 -> 12; matrix products, arithmetic and copies ran while one was open for 0% -> 0% of each run, Pallas kernels for 15% -> 15%
where the time goes in v8:
time: 61.9 us; the launch traced here: 61.7 us
  starting transfers between devices  26.3 us (42%)
  waiting for transfers between devices  23.4 us (38%)
  Pallas kernels  11.9 us (19%)
    ppermute x19, starting transfers between devices, moved(): return lax.ppermute(value, ('section', 'expert'), pairs)  26.3 us
    ppermute x19, waiting for transfers between devices, moved(): return lax.ppermute(value, ('section', 'expert'), pairs)  23.4 us
    pallas_call x4, Pallas kernels, hidden_of(): pl.pallas_call(hidden_kernel, out_shape=jax.ShapeDtypeStruct((rows, hidde...  3.85 us
    pallas_call x2, Pallas kernels, loaded(): pl.pallas_call(functools.partial(load_kernel, kinds), out_shape=tuple((ja...  3.13 us
    pallas_call x1, Pallas kernels, ended(): pl.pallas_call(functools.partial(end_kernel, steps, ordered), out_shape=j...  2.02 us
    pallas_call x4, Pallas kernels, down_of(): pl.pallas_call(down_kernel, out_shape=jax.ShapeDtypeStruct((rows, half),...  1.3 us
  transfers between devices with their start and end apart: 20, of which 12 were waited for; matrix products, arithmetic and copies ran while one was open for 0% of the time, Pallas kernels for 15%

profile of v8, /device:TPU:0, one launch (start us, length us, event | category | flops | bytes accessed | tf_op | source)
XLA Modules:
  0.0 61.7 jit_solution(12212787291332106866)
XLA Ops:
  0.0 2.9 %collective-permute-start = (s32[1,128,2]{1,2,0:T(2,128)}, s32[1,128,2]{1,2,0:T(2,128)S(1)}, u32[]{:S(2)}, u32[]{:S(2)}) collective-permute-start(s32[1,128,2]{1,2,0:T(2,128)} %param.12), channel_id=1, source_target_pairs={{0,16},{2,18},{4,20},{6,22},{8,24},{10,26},{12,28},{14,30},{16,0},... | collective-permute-start | bytes 3080 | tf_op jit(solution)/shard_map/ppermute | solution.py:328
  2.9 1.2 %shard_map.73 = (bf16[128,3072]{1,0:T(8,128)(2,1)S(1)}, bf16[96,1536]{1,0:T(8,128)(2,1)S(1)}) custom-call(bf16[128,3072]{1,0:T(8,128)(2,1)} %bitcast.27, bf16[192,3072]{1,0:T(8,128)(2,1)} %bitcast.25), custom_call_target="tpu_custom_call" | custom-call | bytes 2162688 | tf_op jit(solution)/shard_map/pallas_call | solution.py:58
  4.2 0.5 collective-permute-done
  4.7 0.4 shard_map.74
  5.1 4.1 %collective-permute-start.2 = (bf16[32,3072]{1,0:T(8,128)(2,1)S(1)}, bf16[32,3072]{1,0:T(8,128)(2,1)S(1)}, u32[]{:S(2)}, u32[]{:S(2)}) collective-permute-start(bf16[32,3072]{1,0:T(8,128)(2,1)S(1)} %shard_map.74), channel_id=1, source_target_pairs={{0,24},{2,26},{4,28},{6,30},{8,16},{10,18},{12,20},{14,22},{16,8},... | collective-permute-start | bytes 589832 | tf_op jit(solution)/shard_map/ppermute | solution.py:328
  9.2 1.5 %collective-permute-start.1 = (bf16[32,3072]{1,0:T(8,128)(2,1)S(1)}, bf16[32,3072]{1,0:T(8,128)(2,1)S(1)}, u32[]{:S(2)}, u32[]{:S(2)}) collective-permute-start(bf16[32,3072]{1,0:T(8,128)(2,1)S(1)} %shard_map.74), channel_id=1, source_target_pairs={{0,18},{2,16},{4,22},{6,20},{8,26},{10,24},{12,30},{14,28},{16,2},... | collective-permute-start | bytes 589832 | tf_op jit(solution)/shard_map/ppermute | solution.py:328
  10.7 0.5 collective-permute-start.9
  11.2 1.9 %shard_map.75 = (bf16[192,1536]{1,0:T(8,128)(2,1)S(1)}, bf16[192,3072]{1,0:T(8,128)(2,1)S(1)}, bf16[192,3072]{1,0:T(8,128)(2,1)S(1)}, bf16[1,3072]{1,0:T(2,128)(2,1)S(1)}) custom-call(bf16[192,3072]{1,0:T(8,128)(2,1)} %bitcast.26, bf16[192,3072]{1,0:T(8,128)(2,1)} %bitcast.28, bf16[192,3072]{1,0:T(8,128)(2,1)} %bitcast.29, bf16[1,3072]{1,0:T(2,128)(2,1)} %refs_3_.1), custom_call_target="tpu_custom_call" | custom-call | bytes 5910528 | tf_op jit(solution)/shard_map/pallas_call | solution.py:58
  13.1 4.1 %collective-permute-done.2.near_ref = bf16[32,3072]{1,0:T(8,128)(2,1)S(1)} collective-permute-done((bf16[32,3072]{1,0:T(8,128)(2,1)S(1)}, bf16[32,3072]{1,0:T(8,128)(2,1)S(1)}, u32[]{:S(2)}, u32[]{:S(2)}) %collective-permute-start.2) | collective-permute-done | bytes 196640 | tf_op jit(solution)/shard_map/ppermute | solution.py:328
  17.2 1.5 %collective-permute-start.5 = (bf16[32,3072]{1,0:T(8,128)(2,1)S(1)}, bf16[32,3072]{1,0:T(8,128)(2,1)S(1)}, u32[]{:S(2)}, u32[]{:S(2)}) collective-permute-start(bf16[32,3072]{1,0:T(8,128)(2,1)S(1)} %collective-permute-done.2.near_ref), channel_id=1, source_target_pairs={{0,2},{2,0},{4,6},{6,4},{8,10},{10,8},{12,14},{14,12},{16,18},{18,... | collective-permute-start | bytes 589832 | tf_op jit(solution)/shard_map/ppermute | solution.py:328
  18.8 0.1 collective-permute-done.1.far_ref
  18.9 1.4 %collective-permute-start.3 = (bf16[48,3072]{1,0:T(8,128)(2,1)S(1)}, bf16[48,3072]{1,0:T(8,128)(2,1)S(1)}, u32[]{:S(2)}, u32[]{:S(2)}) collective-permute-start(bf16[48,3072]{1,0:T(8,128)(2,1)S(1)} %slice_bitcast_fusion.1), channel_id=1, source_target_pairs={{0,16},{2,18},{4,20},{6,22},{8,24},{10,26},{12,28},{14,30},{16,0},... | collective-permute-start | bytes 884744 | tf_op jit(solution)/shard_map/ppermute | solution.py:328
  20.3 1.1 %collective-permute-start.7 = (bf16[32,3072]{1,0:T(8,128)(2,1)S(1)}, bf16[32,3072]{1,0:T(8,128)(2,1)S(1)}, u32[]{:S(2)}, u32[]{:S(2)}) collective-permute-start(bf16[32,3072]{1,0:T(8,128)(2,1)S(1)} %collective-permute-done.2.near_ref), channel_id=1, source_target_pairs={{0,4},{2,6},{4,0},{6,2},{8,12},{10,14},{12,8},{14,10},{16,20},{18,... | collective-permute-start | bytes 589832 | tf_op jit(solution)/shard_map/ppermute | solution.py:328
  21.4 0.8 %collective-permute-done.9.own_ref = bf16[96,1536]{1,0:T(8,128)(2,1)S(1)} collective-permute-done((bf16[96,1536]{1,0:T(8,128)(2,1)S(1)}, bf16[96,1536]{1,0:T(8,128)(2,1)S(1)}, u32[]{:S(2)}, u32[]{:S(2)}) %collective-permute-start.9) | collective-permute-done | bytes 294944 | tf_op jit(solution)/shard_map/ppermute | solution.py:328
  22.2 3.6 %collective-permute-done.5.far_ref = bf16[32,3072]{1,0:T(8,128)(2,1)S(1)} collective-permute-done((bf16[32,3072]{1,0:T(8,128)(2,1)S(1)}, bf16[32,3072]{1,0:T(8,128)(2,1)S(1)}, u32[]{:S(2)}, u32[]{:S(2)}) %collective-permute-start.5) | collective-permute-done | bytes 196640 | tf_op jit(solution)/shard_map/ppermute | solution.py:328
  25.8 2.7 %collective-permute-start.6 = (bf16[32,3072]{1,0:T(8,128)(2,1)S(1)}, bf16[32,3072]{1,0:T(8,128)(2,1)S(1)}, u32[]{:S(2)}, u32[]{:S(2)}) collective-permute-start(bf16[32,3072]{1,0:T(8,128)(2,1)S(1)} %shard_map.74), channel_id=1, source_target_pairs={{0,20},{2,22},{4,16},{6,18},{8,28},{10,30},{12,24},{14,26},{16,4},... | collective-permute-start | bytes 589832 | tf_op jit(solution)/shard_map/ppermute | solution.py:328
  28.6 0.7 %collective-permute-start.4 = (bf16[80,3072]{1,0:T(8,128)(2,1)S(1)}, bf16[80,3072]{1,0:T(8,128)(2,1)S(1)}, u32[]{:S(2)}, u32[]{:S(2)}) collective-permute-start(bf16[80,3072]{1,0:T(8,128)(2,1)S(1)} %slice_bitcast_fusion), channel_id=1, source_target_pairs={{0,16},{2,18},{4,20},{6,22},{8,24},{10,26},{12,28},{14,30},{16,0},... | collective-permute-start | bytes 1474568 | tf_op jit(solution)/shard_map/ppermute | solution.py:328
  29.2 1.0 %shard_map.77.own_ref = bf16[64,192]{1,0:T(8,128)(2,1)S(1)} custom-call(bf16[32,3072]{1,0:T(8,128)(2,1)S(1)} %collective-permute-done.2.near_ref, bf16[32,3072]{1,0:T(8,128)(2,1)S(1)} %collective-permute-done.5.far_ref, bf16[1,3072]{1,0:T(2,128)(2,1)S(1)} %get-tuple-element.29.gain_ref, bf16[192,3072]{1,0:T(8,128)(2,1)S(1)} %get-tuple-element.38.gate_ref, ...), custom_call_target="tpu_custom_call" | custom-call | flops 150994944 | bytes 2359296 | tf_op jit(solution)/shard_map/pallas_call | solution.py:142
  30.2 0.6 collective-permute-start.8
  30.8 0.4 collective-permute-start.11
  31.3 0.1 shard_map.78.other_down_ref
  31.4 2.8 %collective-permute-done.8.other_ref = bf16[64,192]{1,0:T(8,128)(2,1)S(1)} collective-permute-done((bf16[64,192]{1,0:T(8,128)(2,1)S(1)}, bf16[64,192]{1,0:T(8,128)(2,1)S(1)}, u32[]{:S(2)}, u32[]{:S(2)}) %collective-permute-start.8) | collective-permute-done | bytes 24608 | tf_op jit(solution)/shard_map/ppermute | solution.py:328
  34.2 0.3 shard_map.79
  34.5 0.7 %collective-permute-start.12 = (bf16[32,3072]{1,0:T(8,128)(2,1)S(1)}, bf16[32,3072]{1,0:T(8,128)(2,1)S(1)}, u32[]{:S(2)}, u32[]{:S(2)}) collective-permute-start(bf16[32,3072]{1,0:T(8,128)(2,1)S(1)} %collective-permute-done.6.near_ref), channel_id=1, source_target_pairs={{0,2},{2,0},{4,6},{6,4},{8,10},{10,8},{12,14},{14,12},{16,18},{18,... | collective-permute-start | bytes 589832 | tf_op jit(solution)/shard_map/ppermute | solution.py:328
  35.2 1.2 %collective-permute-start.13 = (bf16[64,1536]{1,0:T(8,128)(2,1)S(1)}, bf16[64,1536]{1,0:T(8,128)(2,1)S(1)}, u32[]{:S(2)}, u32[]{:S(2)}) collective-permute-start(bf16[64,1536]{1,0:T(8,128)(2,1)S(1)} %shard_map.79), channel_id=1, source_target_pairs={{0,8},{2,10},{4,12},{6,14},{8,0},{10,2},{12,4},{14,6},{16,24},{18,... | collective-permute-start | bytes 589832 | tf_op jit(solution)/shard_map/ppermute | solution.py:328
  36.4 3.2 %collective-permute-done.11.far_ref = bf16[32,3072]{1,0:T(8,128)(2,1)S(1)} collective-permute-done((bf16[32,3072]{1,0:T(8,128)(2,1)S(1)}, bf16[32,3072]{1,0:T(8,128)(2,1)S(1)}, u32[]{:S(2)}, u32[]{:S(2)}) %collective-permute-start.11) | collective-permute-done | bytes 196640 | tf_op jit(solution)/shard_map/ppermute | solution.py:328
  39.6 1.0 %shard_map.80.own_ref = bf16[64,192]{1,0:T(8,128)(2,1)S(1)} custom-call(bf16[32,3072]{1,0:T(8,128)(2,1)S(1)} %collective-permute-done.7.near_ref, bf16[32,3072]{1,0:T(8,128)(2,1)S(1)} %collective-permute-done.11.far_ref, bf16[1,3072]{1,0:T(2,128)(2,1)S(1)} %get-tuple-element.29.gain_ref, bf16[192,3072]{1,0:T(8,128)(2,1)S(1)} %get-tuple-element.38.gate_ref, ...), custom_call_target="tpu_custom_call" | custom-call | flops 150994944 | bytes 2359296 | tf_op jit(solution)/shard_map/pallas_call | solution.py:142
  40.6 0.1 collective-permute-start.15
  40.7 1.0 %shard_map.81.own_ref = bf16[64,192]{1,0:T(8,128)(2,1)S(1)} custom-call(bf16[32,3072]{1,0:T(8,128)(2,1)S(1)} %collective-permute-done.6.near_ref, bf16[32,3072]{1,0:T(8,128)(2,1)S(1)} %collective-permute-done.12.far_ref, bf16[1,3072]{1,0:T(2,128)(2,1)S(1)} %get-tuple-element.29.gain_ref, bf16[192,3072]{1,0:T(8,128)(2,1)S(1)} %get-tuple-element.38.gate_ref, ...), custom_call_target="tpu_custom_call" | custom-call | flops 150994944 | bytes 2359296 | tf_op jit(solution)/shard_map/pallas_call | solution.py:142
  41.7 0.0 copy-start
  41.7 0.0 copy-start.1
  41.7 2.1 %collective-permute-start.17 = (bf16[64,192]{1,0:T(8,128)(2,1)S(1)}, bf16[64,192]{1,0:T(8,128)(2,1)S(1)}, u32[]{:S(2)}, u32[]{:S(2)}) collective-permute-start(bf16[64,192]{1,0:T(8,128)(2,1)S(1)} %shard_map.81.own_ref), channel_id=1, source_target_pairs={{0,2},{2,0},{4,6},{6,4},{8,10},{10,8},{12,14},{14,12},{16,18},{18,... | collective-permute-start | bytes 73736 | tf_op jit(solution)/shard_map/ppermute | solution.py:328
  43.7 0.8 %collective-permute-done.15.other_ref = bf16[64,192]{1,0:T(8,128)(2,1)S(1)} collective-permute-done((bf16[64,192]{1,0:T(8,128)(2,1)S(1)}, bf16[64,192]{1,0:T(8,128)(2,1)S(1)}, u32[]{:S(2)}, u32[]{:S(2)}) %collective-permute-start.15) | collective-permute-done | bytes 24608 | tf_op jit(solution)/shard_map/ppermute | solution.py:328
  44.6 0.3 shard_map.85
  44.9 1.0 %collective-permute-start.16 = (bf16[64,1536]{1,0:T(8,128)(2,1)S(1)}, bf16[64,1536]{1,0:T(8,128)(2,1)S(1)}, u32[]{:S(2)}, u32[]{:S(2)}) collective-permute-start(bf16[64,1536]{1,0:T(8,128)(2,1)S(1)} %shard_map.85), channel_id=1, source_target_pairs={{0,12},{2,14},{4,8},{6,10},{8,4},{10,6},{12,0},{14,2},{16,28},{18,... | collective-permute-start | bytes 589832 | tf_op jit(solution)/shard_map/ppermute | solution.py:328
  45.9 0.3 shard_map.86
  46.2 0.6 collective-permute-start.18
  46.8 1.0 %shard_map.76 = (f32[128,3072]{1,0:T(8,128)S(1)}, bf16[128,160]{1,0:T(8,128)(2,1)S(1)}, bf16[32,3072]{1,0:T(8,128)(2,1)S(1)}) custom-call(bf16[1,3072]{1,0:T(2,128)(2,1)S(1)} %get-tuple-element.29.gain_ref, s32[2,128]{1,0:T(2,128)S(1)} %bitcast.22, f32[2,128]{1,0:T(2,128)S(1)} %bitcast.23, bf16[48,3072]{1,0:T(8,128)(2,1)S(1)} %collective-permute-done.3.refs_0_, ...), custom_call_target="tpu_custom_call" | custom-call | flops 3145728 | bytes 2359296 | tf_op jit(solution)/shard_map/pallas_call | solution.py:246
  47.8 1.0 %shard_map.82.own_ref = bf16[64,192]{1,0:T(8,128)(2,1)S(1)} custom-call(bf16[32,3072]{1,0:T(8,128)(2,1)S(1)} %get-tuple-element.46.near_ref, bf16[32,3072]{1,0:T(8,128)(2,1)S(1)} %collective-permute-done.1.far_ref, bf16[1,3072]{1,0:T(2,128)(2,1)S(1)} %get-tuple-element.29.gain_ref, bf16[192,3072]{1,0:T(8,128)(2,1)S(1)} %get-tuple-element.38.gate_ref, ...), custom_call_target="tpu_custom_call" | custom-call | flops 150994944 | bytes 2359296 | tf_op jit(solution)/shard_map/pallas_call | solution.py:142
  48.8 2.1 %collective-permute-start.14 = (bf16[64,192]{1,0:T(8,128)(2,1)S(1)}, bf16[64,192]{1,0:T(8,128)(2,1)S(1)}, u32[]{:S(2)}, u32[]{:S(2)}) collective-permute-start(bf16[64,192]{1,0:T(8,128)(2,1)S(1)} %shard_map.82.own_ref), channel_id=1, source_target_pairs={{0,2},{2,0},{4,6},{6,4},{8,10},{10,8},{12,14},{14,12},{16,18},{18,... | collective-permute-start | bytes 73736 | tf_op jit(solution)/shard_map/ppermute | solution.py:328
  50.9 1.9 %collective-permute-done.14.other_ref = bf16[64,192]{1,0:T(8,128)(2,1)S(1)} collective-permute-done((bf16[64,192]{1,0:T(8,128)(2,1)S(1)}, bf16[64,192]{1,0:T(8,128)(2,1)S(1)}, u32[]{:S(2)}, u32[]{:S(2)}) %collective-permute-start.14) | collective-permute-done | bytes 24608 | tf_op jit(solution)/shard_map/ppermute | solution.py:328
  52.8 0.3 shard_map.83.left_ref
  53.1 0.5 collective-permute-done.16.refs_1_
  53.7 1.3 %collective-permute-done.18.refs_2_ = bf16[64,1536]{1,0:T(8,128)(2,1)S(1)} collective-permute-done((bf16[64,1536]{1,0:T(8,128)(2,1)S(1)}, bf16[64,1536]{1,0:T(8,128)(2,1)S(1)}, u32[]{:S(2)}, u32[]{:S(2)}) %collective-permute-start.18) | collective-permute-done | bytes 196640 | tf_op jit(solution)/shard_map/ppermute | solution.py:328
  55.0 0.1 shard_map.87
  55.0 1.1 %collective-permute-start.19 = (bf16[32,1536]{1,0:T(8,128)(2,1)S(1)}, bf16[32,1536]{1,0:T(8,128)(2,1)S(1)}, u32[]{:S(2)}, u32[]{:S(2)}) collective-permute-start(bf16[32,1536]{1,0:T(8,128)(2,1)S(1)} %get-tuple-element.48), channel_id=1, source_target_pairs={{0,2},{2,0},{4,6},{6,4},{8,10},{10,8},{12,14},{14,12},{16,18},{18,... | collective-permute-start | bytes 294920 | tf_op jit(solution)/shard_map/ppermute | solution.py:328
  56.1 3.6 %collective-permute-done.19.other_ref = bf16[32,1536]{1,0:T(8,128)(2,1)S(1)} collective-permute-done((bf16[32,1536]{1,0:T(8,128)(2,1)S(1)}, bf16[32,1536]{1,0:T(8,128)(2,1)S(1)}, u32[]{:S(2)}, u32[]{:S(2)}) %collective-permute-start.19) | collective-permute-done | bytes 98336 | tf_op jit(solution)/shard_map/ppermute | solution.py:328
  59.7 2.0 %shard_map.88 = bf16[128,3072]{1,0:T(8,128)(2,1)} custom-call(f32[128,3072]{1,0:T(8,128)S(1)} %get-tuple-element.32.base_ref, bf16[128,160]{1,0:T(8,128)(2,1)S(1)} %get-tuple-element.33.table_ref, f32[32,1536]{1,0:T(8,128)S(1)} %get-tuple-element.47.near_ref, bf16[32,1536]{1,0:T(8,128)(2,1)S(1)} %collective-permute-done.19.other_ref), custom_call_target="tpu_custom_call" | custom-call | flops 100663296 | bytes 2359296 | tf_op jit(solution)/shard_map/pallas_call | solution.py:281
  (16 shorter events, 0.1 us)
Async XLA Ops:
  0.0 4.7 %collective-permute-start = (s32[1,128,2]{1,2,0:T(2,128)}, s32[1,128,2]{1,2,0:T(2,128)S(1)}, u32[]{:S(2)}, u32[]{:S(2)}) collective-permute-start(s32[1,128,2]{1,2,0:T(2,128)} %param.12), channel_id=1, source_target_pairs={{0,16},{2,18},{4,20},{6,22},{8,24},{10,26},{12,28},{14,30},{16,0},... | collective-permute-start | bytes 3080 | tf_op jit(solution)/shard_map/ppermute | solution.py:328
  5.1 12.2 %collective-permute-start.2 = (bf16[32,3072]{1,0:T(8,128)(2,1)S(1)}, bf16[32,3072]{1,0:T(8,128)(2,1)S(1)}, u32[]{:S(2)}, u32[]{:S(2)}) collective-permute-start(bf16[32,3072]{1,0:T(8,128)(2,1)S(1)} %shard_map.74), channel_id=1, source_target_pairs={{0,24},{2,26},{4,28},{6,30},{8,16},{10,18},{12,20},{14,22},{16,8},... | collective-permute-start | bytes 589832 | tf_op jit(solution)/shard_map/ppermute | solution.py:328
  9.2 9.7 %collective-permute-start.1 = (bf16[32,3072]{1,0:T(8,128)(2,1)S(1)}, bf16[32,3072]{1,0:T(8,128)(2,1)S(1)}, u32[]{:S(2)}, u32[]{:S(2)}) collective-permute-start(bf16[32,3072]{1,0:T(8,128)(2,1)S(1)} %shard_map.74), channel_id=1, source_target_pairs={{0,18},{2,16},{4,22},{6,20},{8,26},{10,24},{12,30},{14,28},{16,2},... | collective-permute-start | bytes 589832 | tf_op jit(solution)/shard_map/ppermute | solution.py:328
  10.7 11.5 %collective-permute-start.9 = (bf16[96,1536]{1,0:T(8,128)(2,1)S(1)}, bf16[96,1536]{1,0:T(8,128)(2,1)S(1)}, u32[]{:S(2)}, u32[]{:S(2)}) collective-permute-start(bf16[96,1536]{1,0:T(8,128)(2,1)S(1)} %get-tuple-element.42), channel_id=1, source_target_pairs={{0,2},{2,0},{4,6},{6,4},{8,10},{10,8},{12,14},{14,12},{16,18},{18,... | collective-permute-start | bytes 884744 | tf_op jit(solution)/shard_map/ppermute | solution.py:328
  11.2 7.6 %copy-start.2 = (bf16[1,128,3072]{2,1,0:T(8,128)(2,1)S(1)}, bf16[1,128,3072]{2,1,0:T(8,128)(2,1)}, u32[]{:S(2)}) copy-start(bf16[1,128,3072]{2,1,0:T(8,128)(2,1)} %param.7) | copy-start | bytes 2359300
  17.2 8.6 %collective-permute-start.5 = (bf16[32,3072]{1,0:T(8,128)(2,1)S(1)}, bf16[32,3072]{1,0:T(8,128)(2,1)S(1)}, u32[]{:S(2)}, u32[]{:S(2)}) collective-permute-start(bf16[32,3072]{1,0:T(8,128)(2,1)S(1)} %collective-permute-done.2.near_ref), channel_id=1, source_target_pairs={{0,2},{2,0},{4,6},{6,4},{8,10},{10,8},{12,14},{14,12},{16,18},{18,... | collective-permute-start | bytes 589832 | tf_op jit(solution)/shard_map/ppermute | solution.py:328
  18.9 17.5 %collective-permute-start.3 = (bf16[48,3072]{1,0:T(8,128)(2,1)S(1)}, bf16[48,3072]{1,0:T(8,128)(2,1)S(1)}, u32[]{:S(2)}, u32[]{:S(2)}) collective-permute-start(bf16[48,3072]{1,0:T(8,128)(2,1)S(1)} %slice_bitcast_fusion.1), channel_id=1, source_target_pairs={{0,16},{2,18},{4,20},{6,22},{8,24},{10,26},{12,28},{14,30},{16,0},... | collective-permute-start | bytes 884744 | tf_op jit(solution)/shard_map/ppermute | solution.py:328
  20.3 9.0 %collective-permute-start.7 = (bf16[32,3072]{1,0:T(8,128)(2,1)S(1)}, bf16[32,3072]{1,0:T(8,128)(2,1)S(1)}, u32[]{:S(2)}, u32[]{:S(2)}) collective-permute-start(bf16[32,3072]{1,0:T(8,128)(2,1)S(1)} %collective-permute-done.2.near_ref), channel_id=1, source_target_pairs={{0,4},{2,6},{4,0},{6,2},{8,12},{10,14},{12,8},{14,10},{16,20},{18,... | collective-permute-start | bytes 589832 | tf_op jit(solution)/shard_map/ppermute | solution.py:328
  22.2 8.6 %collective-permute-start.10 = (bf16[96,1536]{1,0:T(8,128)(2,1)S(1)}, bf16[96,1536]{1,0:T(8,128)(2,1)S(1)}, u32[]{:S(2)}, u32[]{:S(2)}) collective-permute-start(bf16[96,1536]{1,0:T(8,128)(2,1)S(1)} %collective-permute-done.9.own_ref), channel_id=1, source_target_pairs={{0,1},{1,0},{2,3},{3,2},{4,5},{5,4},{6,7},{7,6},{8,9},{9,8},{10,11... | collective-permute-start | bytes 884744 | tf_op jit(solution)/shard_map/ppermute | solution.py:350
  25.8 8.7 %collective-permute-start.6 = (bf16[32,3072]{1,0:T(8,128)(2,1)S(1)}, bf16[32,3072]{1,0:T(8,128)(2,1)S(1)}, u32[]{:S(2)}, u32[]{:S(2)}) collective-permute-start(bf16[32,3072]{1,0:T(8,128)(2,1)S(1)} %shard_map.74), channel_id=1, source_target_pairs={{0,20},{2,22},{4,16},{6,18},{8,28},{10,30},{12,24},{14,26},{16,4},... | collective-permute-start | bytes 589832 | tf_op jit(solution)/shard_map/ppermute | solution.py:328
  28.6 18.2 %collective-permute-start.4 = (bf16[80,3072]{1,0:T(8,128)(2,1)S(1)}, bf16[80,3072]{1,0:T(8,128)(2,1)S(1)}, u32[]{:S(2)}, u32[]{:S(2)}) collective-permute-start(bf16[80,3072]{1,0:T(8,128)(2,1)S(1)} %slice_bitcast_fusion), channel_id=1, source_target_pairs={{0,16},{2,18},{4,20},{6,22},{8,24},{10,26},{12,28},{14,30},{16,0},... | collective-permute-start | bytes 1474568 | tf_op jit(solution)/shard_map/ppermute | solution.py:328
  30.2 4.0 %collective-permute-start.8 = (bf16[64,192]{1,0:T(8,128)(2,1)S(1)}, bf16[64,192]{1,0:T(8,128)(2,1)S(1)}, u32[]{:S(2)}, u32[]{:S(2)}) collective-permute-start(bf16[64,192]{1,0:T(8,128)(2,1)S(1)} %shard_map.77.own_ref), channel_id=1, source_target_pairs={{0,2},{2,0},{4,6},{6,4},{8,10},{10,8},{12,14},{14,12},{16,18},{18,... | collective-permute-start | bytes 73736 | tf_op jit(solution)/shard_map/ppermute | solution.py:328
  30.8 8.8 %collective-permute-start.11 = (bf16[32,3072]{1,0:T(8,128)(2,1)S(1)}, bf16[32,3072]{1,0:T(8,128)(2,1)S(1)}, u32[]{:S(2)}, u32[]{:S(2)}) collective-permute-start(bf16[32,3072]{1,0:T(8,128)(2,1)S(1)} %collective-permute-done.5.far_ref), channel_id=1, source_target_pairs={{0,4},{2,6},{4,0},{6,2},{8,12},{10,14},{12,8},{14,10},{16,20},{18,... | collective-permute-start | bytes 589832 | tf_op jit(solution)/shard_map/ppermute | solution.py:328
  34.5 6.1 %collective-permute-start.12 = (bf16[32,3072]{1,0:T(8,128)(2,1)S(1)}, bf16[32,3072]{1,0:T(8,128)(2,1)S(1)}, u32[]{:S(2)}, u32[]{:S(2)}) collective-permute-start(bf16[32,3072]{1,0:T(8,128)(2,1)S(1)} %collective-permute-done.6.near_ref), channel_id=1, source_target_pairs={{0,2},{2,0},{4,6},{6,4},{8,10},{10,8},{12,14},{14,12},{16,18},{18,... | collective-permute-start | bytes 589832 | tf_op jit(solution)/shard_map/ppermute | solution.py:328
  35.2 12.6 %collective-permute-start.13 = (bf16[64,1536]{1,0:T(8,128)(2,1)S(1)}, bf16[64,1536]{1,0:T(8,128)(2,1)S(1)}, u32[]{:S(2)}, u32[]{:S(2)}) collective-permute-start(bf16[64,1536]{1,0:T(8,128)(2,1)S(1)} %shard_map.79), channel_id=1, source_target_pairs={{0,8},{2,10},{4,12},{6,14},{8,0},{10,2},{12,4},{14,6},{16,24},{18,... | collective-permute-start | bytes 589832 | tf_op jit(solution)/shard_map/ppermute | solution.py:328
  40.6 4.0 %collective-permute-start.15 = (bf16[64,192]{1,0:T(8,128)(2,1)S(1)}, bf16[64,192]{1,0:T(8,128)(2,1)S(1)}, u32[]{:S(2)}, u32[]{:S(2)}) collective-permute-start(bf16[64,192]{1,0:T(8,128)(2,1)S(1)} %shard_map.80.own_ref), channel_id=1, source_target_pairs={{0,2},{2,0},{4,6},{6,4},{8,10},{10,8},{12,14},{14,12},{16,18},{18,... | collective-permute-start | bytes 73736 | tf_op jit(solution)/shard_map/ppermute | solution.py:328
  41.7 5.2 %copy-start = (s32[1,128,2]{1,2,0:T(2,128)S(1)}, s32[1,128,2]{1,2,0:T(2,128)}, u32[]{:S(2)}) copy-start(s32[1,128,2]{1,2,0:T(2,128)} %param.12) | copy-start | bytes 3076
  41.7 5.2 %copy-start.1 = (f32[1,128,2]{1,2,0:T(2,128)S(1)}, f32[1,128,2]{1,2,0:T(2,128)}, u32[]{:S(2)}) copy-start(f32[1,128,2]{1,2,0:T(2,128)} %param.13) | copy-start | bytes 3076
  41.7 4.2 %collective-permute-start.17 = (bf16[64,192]{1,0:T(8,128)(2,1)S(1)}, bf16[64,192]{1,0:T(8,128)(2,1)S(1)}, u32[]{:S(2)}, u32[]{:S(2)}) collective-permute-start(bf16[64,192]{1,0:T(8,128)(2,1)S(1)} %shard_map.81.own_ref), channel_id=1, source_target_pairs={{0,2},{2,0},{4,6},{6,4},{8,10},{10,8},{12,14},{14,12},{16,18},{18,... | collective-permute-start | bytes 73736 | tf_op jit(solution)/shard_map/ppermute | solution.py:328
  44.9 8.8 %collective-permute-start.16 = (bf16[64,1536]{1,0:T(8,128)(2,1)S(1)}, bf16[64,1536]{1,0:T(8,128)(2,1)S(1)}, u32[]{:S(2)}, u32[]{:S(2)}) collective-permute-start(bf16[64,1536]{1,0:T(8,128)(2,1)S(1)} %shard_map.85), channel_id=1, source_target_pairs={{0,12},{2,14},{4,8},{6,10},{8,4},{10,6},{12,0},{14,2},{16,28},{18,... | collective-permute-start | bytes 589832 | tf_op jit(solution)/shard_map/ppermute | solution.py:328
  46.2 8.7 %collective-permute-start.18 = (bf16[64,1536]{1,0:T(8,128)(2,1)S(1)}, bf16[64,1536]{1,0:T(8,128)(2,1)S(1)}, u32[]{:S(2)}, u32[]{:S(2)}) collective-permute-start(bf16[64,1536]{1,0:T(8,128)(2,1)S(1)} %shard_map.86), channel_id=1, source_target_pairs={{0,4},{2,6},{4,0},{6,2},{8,12},{10,14},{12,8},{14,10},{16,20},{18,... | collective-permute-start | bytes 589832 | tf_op jit(solution)/shard_map/ppermute | solution.py:328
  48.8 4.0 %collective-permute-start.14 = (bf16[64,192]{1,0:T(8,128)(2,1)S(1)}, bf16[64,192]{1,0:T(8,128)(2,1)S(1)}, u32[]{:S(2)}, u32[]{:S(2)}) collective-permute-start(bf16[64,192]{1,0:T(8,128)(2,1)S(1)} %shard_map.82.own_ref), channel_id=1, source_target_pairs={{0,2},{2,0},{4,6},{6,4},{8,10},{10,8},{12,14},{14,12},{16,18},{18,... | collective-permute-start | bytes 73736 | tf_op jit(solution)/shard_map/ppermute | solution.py:328
  55.0 4.7 %collective-permute-start.19 = (bf16[32,1536]{1,0:T(8,128)(2,1)S(1)}, bf16[32,1536]{1,0:T(8,128)(2,1)S(1)}, u32[]{:S(2)}, u32[]{:S(2)}) collective-permute-start(bf16[32,1536]{1,0:T(8,128)(2,1)S(1)} %get-tuple-element.48), channel_id=1, source_target_pairs={{0,2},{2,0},{4,6},{6,4},{8,10},{10,8},{12,14},{14,12},{16,18},{18,... | collective-permute-start | bytes 294920 | tf_op jit(solution)/shard_map/ppermute | solution.py:328

commit v9 on v8

--- a/solution.py
+++ b/solution.py
@@ -355,7 +355,7 @@
     far[2] = moved(after(near[2], gain), 0, 0, 1)
     near[3] = moved(near[2], 0, 1)
     far[3] = moved(far[2], 0, 1)
-    near[1] = moved(after(picked, far[2]), 1, 1)
+    near[1] = moved(after(picked, near[2]), 1, 1)
     cuts = [CAP * 3 // 2]
     arrived = [
         moved(after(piece, far[0], near[2]), 1, 0)
@@ -376,7 +376,10 @@
         if k == 3:
             far[1] = moved(after(near[1], part[2]), 0, 0, 1)
         hidden[k] = hidden_of(after(near[k], *first), far[k], gain, gate_t, up_t)
-        part[k] = down_of(hidden[k], moved(hidden[k], 0, 0, 1), own_down, other_down)
+        crossed = moved(hidden[k], 0, 0, 1)
+        if k == 2:
+            crossed = after(crossed, far[3])
+        part[k] = down_of(hidden[k], crossed, own_down, other_down)
         back[k] = moved(part[k], 0, k) if k else part[k]
     early = summed_early(back[0], back[2])
     own, others = joined([early, back[3], back[1]])

time: 61.9 us -> 60.8 us (0.982)
  waiting for transfers between devices: 23.4 us -> 18.6 us
  starting transfers between devices: 26.3 us -> 29.8 us
    ppermute x19, waiting for transfers between devices: 23.4 us -> 18.6 us  [moved(): return lax.ppermute(value, ('section', 'expert'), pairs)]
    ppermute x19, starting transfers between devices: 26.3 us -> 29.8 us  [moved(): return lax.ppermute(value, ('section', 'expert'), pairs)]
  transfers between devices with their start and end apart: 20 -> 20, of which waited for: 12 -> 10; matrix products, arithmetic and copies ran while one was open for 0% -> 0% of each run, Pallas kernels for 15% -> 16%
where the time goes in v9:
time: 60.8 us; the launch traced here: 60.6 us
  starting transfers between devices  29.8 us (49%)
  waiting for transfers between devices  18.6 us (31%)
  Pallas kernels  11.9 us (20%)
    ppermute x19, starting transfers between devices, moved(): return lax.ppermute(value, ('section', 'expert'), pairs)  29.8 us
    ppermute x19, waiting for transfers between devices, moved(): return lax.ppermute(value, ('section', 'expert'), pairs)  18.6 us
    pallas_call x4, Pallas kernels, hidden_of(): pl.pallas_call(hidden_kernel, out_shape=jax.ShapeDtypeStruct((rows, hidde...  3.85 us
    pallas_call x2, Pallas kernels, loaded(): pl.pallas_call(functools.partial(load_kernel, kinds), out_shape=tuple((ja...  3.13 us
    pallas_call x1, Pallas kernels, ended(): pl.pallas_call(functools.partial(end_kernel, steps, ordered), out_shape=j...  2.02 us
    pallas_call x4, Pallas kernels, down_of(): pl.pallas_call(down_kernel, out_shape=jax.ShapeDtypeStruct((rows, half),...  1.3 us
  transfers between devices with their start and end apart: 20, of which 10 were waited for; matrix products, arithmetic and copies ran while one was open for 0% of the time, Pallas kernels for 16%

profile of v9, /device:TPU:0, one launch (start us, length us, event | category | flops | bytes accessed | tf_op | source)
XLA Modules:
  0.0 60.6 jit_solution(10722446584194495081)
XLA Ops:
  0.0 2.9 %collective-permute-start = (s32[1,128,2]{1,2,0:T(2,128)}, s32[1,128,2]{1,2,0:T(2,128)S(1)}, u32[]{:S(2)}, u32[]{:S(2)}) collective-permute-start(s32[1,128,2]{1,2,0:T(2,128)} %param.12), channel_id=1, source_target_pairs={{0,16},{2,18},{4,20},{6,22},{8,24},{10,26},{12,28},{14,30},{16,0},... | collective-permute-start | bytes 3080 | tf_op jit(solution)/shard_map/ppermute | solution.py:328
  2.9 1.2 %shard_map.73 = (bf16[128,3072]{1,0:T(8,128)(2,1)S(1)}, bf16[96,1536]{1,0:T(8,128)(2,1)S(1)}) custom-call(bf16[128,3072]{1,0:T(8,128)(2,1)} %bitcast.27, bf16[192,3072]{1,0:T(8,128)(2,1)} %bitcast.25), custom_call_target="tpu_custom_call" | custom-call | bytes 2162688 | tf_op jit(solution)/shard_map/pallas_call | solution.py:58
  4.2 0.5 collective-permute-done
  4.7 0.4 shard_map.74
  5.1 4.1 %collective-permute-start.2 = (bf16[32,3072]{1,0:T(8,128)(2,1)S(1)}, bf16[32,3072]{1,0:T(8,128)(2,1)S(1)}, u32[]{:S(2)}, u32[]{:S(2)}) collective-permute-start(bf16[32,3072]{1,0:T(8,128)(2,1)S(1)} %shard_map.74), channel_id=1, source_target_pairs={{0,24},{2,26},{4,28},{6,30},{8,16},{10,18},{12,20},{14,22},{16,8},... | collective-permute-start | bytes 589832 | tf_op jit(solution)/shard_map/ppermute | solution.py:328
  9.2 1.5 %collective-permute-start.1 = (bf16[32,3072]{1,0:T(8,128)(2,1)S(1)}, bf16[32,3072]{1,0:T(8,128)(2,1)S(1)}, u32[]{:S(2)}, u32[]{:S(2)}) collective-permute-start(bf16[32,3072]{1,0:T(8,128)(2,1)S(1)} %shard_map.74), channel_id=1, source_target_pairs={{0,18},{2,16},{4,22},{6,20},{8,26},{10,24},{12,30},{14,28},{16,2},... | collective-permute-start | bytes 589832 | tf_op jit(solution)/shard_map/ppermute | solution.py:328
  10.7 0.5 collective-permute-start.10
  11.2 1.9 %shard_map.75 = (bf16[192,1536]{1,0:T(8,128)(2,1)S(1)}, bf16[192,3072]{1,0:T(8,128)(2,1)S(1)}, bf16[192,3072]{1,0:T(8,128)(2,1)S(1)}, bf16[1,3072]{1,0:T(2,128)(2,1)S(1)}) custom-call(bf16[192,3072]{1,0:T(8,128)(2,1)} %bitcast.26, bf16[192,3072]{1,0:T(8,128)(2,1)} %bitcast.28, bf16[192,3072]{1,0:T(8,128)(2,1)} %bitcast.29, bf16[1,3072]{1,0:T(2,128)(2,1)} %refs_3_.1), custom_call_target="tpu_custom_call" | custom-call | bytes 5910528 | tf_op jit(solution)/shard_map/pallas_call | solution.py:58
  13.1 4.1 %collective-permute-done.2.near_ref = bf16[32,3072]{1,0:T(8,128)(2,1)S(1)} collective-permute-done((bf16[32,3072]{1,0:T(8,128)(2,1)S(1)}, bf16[32,3072]{1,0:T(8,128)(2,1)S(1)}, u32[]{:S(2)}, u32[]{:S(2)}) %collective-permute-start.2) | collective-permute-done | bytes 196640 | tf_op jit(solution)/shard_map/ppermute | solution.py:328
  17.2 1.5 %collective-permute-start.7 = (bf16[32,3072]{1,0:T(8,128)(2,1)S(1)}, bf16[32,3072]{1,0:T(8,128)(2,1)S(1)}, u32[]{:S(2)}, u32[]{:S(2)}) collective-permute-start(bf16[32,3072]{1,0:T(8,128)(2,1)S(1)} %collective-permute-done.2.near_ref), channel_id=1, source_target_pairs={{0,2},{2,0},{4,6},{6,4},{8,10},{10,8},{12,14},{14,12},{16,18},{18,... | collective-permute-start | bytes 589832 | tf_op jit(solution)/shard_map/ppermute | solution.py:328
  18.8 0.6 collective-permute-start.6
  19.4 2.3 %collective-permute-start.5 = (bf16[32,3072]{1,0:T(8,128)(2,1)S(1)}, bf16[32,3072]{1,0:T(8,128)(2,1)S(1)}, u32[]{:S(2)}, u32[]{:S(2)}) collective-permute-start(bf16[32,3072]{1,0:T(8,128)(2,1)S(1)} %shard_map.74), channel_id=1, source_target_pairs={{0,20},{2,22},{4,16},{6,18},{8,28},{10,30},{12,24},{14,26},{16,4},... | collective-permute-start | bytes 589832 | tf_op jit(solution)/shard_map/ppermute | solution.py:328
  21.7 0.0 collective-permute-done.1.far_ref
  21.7 0.6 %collective-permute-start.3 = (bf16[48,3072]{1,0:T(8,128)(2,1)S(1)}, bf16[48,3072]{1,0:T(8,128)(2,1)S(1)}, u32[]{:S(2)}, u32[]{:S(2)}) collective-permute-start(bf16[48,3072]{1,0:T(8,128)(2,1)S(1)} %slice_bitcast_fusion.1), channel_id=1, source_target_pairs={{0,16},{2,18},{4,20},{6,22},{8,24},{10,26},{12,28},{14,30},{16,0},... | collective-permute-start | bytes 884744 | tf_op jit(solution)/shard_map/ppermute | solution.py:328
  22.4 0.0 collective-permute-done.10.own_ref
  22.4 3.9 %collective-permute-done.6.near_ref = bf16[32,3072]{1,0:T(8,128)(2,1)S(1)} collective-permute-done((bf16[32,3072]{1,0:T(8,128)(2,1)S(1)}, bf16[32,3072]{1,0:T(8,128)(2,1)S(1)}, u32[]{:S(2)}, u32[]{:S(2)}) %collective-permute-start.6) | collective-permute-done | bytes 196640 | tf_op jit(solution)/shard_map/ppermute | solution.py:328
  26.2 1.0 %shard_map.77.own_ref = bf16[64,192]{1,0:T(8,128)(2,1)S(1)} custom-call(bf16[32,3072]{1,0:T(8,128)(2,1)S(1)} %collective-permute-done.2.near_ref, bf16[32,3072]{1,0:T(8,128)(2,1)S(1)} %collective-permute-done.7.far_ref, bf16[1,3072]{1,0:T(2,128)(2,1)S(1)} %get-tuple-element.30.gain_ref, bf16[192,3072]{1,0:T(8,128)(2,1)S(1)} %get-tuple-element.39.gate_ref, ...), custom_call_target="tpu_custom_call" | custom-call | flops 150994944 | bytes 2359296 | tf_op jit(solution)/shard_map/pallas_call | solution.py:142
  27.2 0.5 collective-permute-start.8
  27.8 1.5 %collective-permute-start.9 = (bf16[32,3072]{1,0:T(8,128)(2,1)S(1)}, bf16[32,3072]{1,0:T(8,128)(2,1)S(1)}, u32[]{:S(2)}, u32[]{:S(2)}) collective-permute-start(bf16[32,3072]{1,0:T(8,128)(2,1)S(1)} %collective-permute-done.7.far_ref), channel_id=1, source_target_pairs={{0,4},{2,6},{4,0},{6,2},{8,12},{10,14},{12,8},{14,10},{16,20},{18,... | collective-permute-start | bytes 589832 | tf_op jit(solution)/shard_map/ppermute | solution.py:328
  29.3 1.9 %collective-permute-done.8.other_ref = bf16[64,192]{1,0:T(8,128)(2,1)S(1)} collective-permute-done((bf16[64,192]{1,0:T(8,128)(2,1)S(1)}, bf16[64,192]{1,0:T(8,128)(2,1)S(1)}, u32[]{:S(2)}, u32[]{:S(2)}) %collective-permute-start.8) | collective-permute-done | bytes 24608 | tf_op jit(solution)/shard_map/ppermute | solution.py:328
  31.2 1.5 %collective-permute-start.4 = (bf16[80,3072]{1,0:T(8,128)(2,1)S(1)}, bf16[80,3072]{1,0:T(8,128)(2,1)S(1)}, u32[]{:S(2)}, u32[]{:S(2)}) collective-permute-start(bf16[80,3072]{1,0:T(8,128)(2,1)S(1)} %slice_bitcast_fusion), channel_id=1, source_target_pairs={{0,16},{2,18},{4,20},{6,22},{8,24},{10,26},{12,28},{14,30},{16,0},... | collective-permute-start | bytes 1474568 | tf_op jit(solution)/shard_map/ppermute | solution.py:328
  32.7 0.7 %collective-permute-done.9.far_ref = bf16[32,3072]{1,0:T(8,128)(2,1)S(1)} collective-permute-done((bf16[32,3072]{1,0:T(8,128)(2,1)S(1)}, bf16[32,3072]{1,0:T(8,128)(2,1)S(1)}, u32[]{:S(2)}, u32[]{:S(2)}) %collective-permute-start.9) | collective-permute-done | bytes 196640 | tf_op jit(solution)/shard_map/ppermute | solution.py:328
  33.4 0.1 shard_map.78.other_down_ref
  33.6 0.3 shard_map.79
  33.9 1.6 %collective-permute-start.12 = (bf16[32,3072]{1,0:T(8,128)(2,1)S(1)}, bf16[32,3072]{1,0:T(8,128)(2,1)S(1)}, u32[]{:S(2)}, u32[]{:S(2)}) collective-permute-start(bf16[32,3072]{1,0:T(8,128)(2,1)S(1)} %collective-permute-done.5.near_ref), channel_id=1, source_target_pairs={{0,2},{2,0},{4,6},{6,4},{8,10},{10,8},{12,14},{14,12},{16,18},{18,... | collective-permute-start | bytes 589832 | tf_op jit(solution)/shard_map/ppermute | solution.py:328
  35.5 2.3 %collective-permute-start.13 = (bf16[64,1536]{1,0:T(8,128)(2,1)S(1)}, bf16[64,1536]{1,0:T(8,128)(2,1)S(1)}, u32[]{:S(2)}, u32[]{:S(2)}) collective-permute-start(bf16[64,1536]{1,0:T(8,128)(2,1)S(1)} %shard_map.79), channel_id=1, source_target_pairs={{0,8},{2,10},{4,12},{6,14},{8,0},{10,2},{12,4},{14,6},{16,24},{18,... | collective-permute-start | bytes 589832 | tf_op jit(solution)/shard_map/ppermute | solution.py:328
  37.8 1.0 %shard_map.80.own_ref = bf16[64,192]{1,0:T(8,128)(2,1)S(1)} custom-call(bf16[32,3072]{1,0:T(8,128)(2,1)S(1)} %collective-permute-done.6.near_ref, bf16[32,3072]{1,0:T(8,128)(2,1)S(1)} %collective-permute-done.9.far_ref, bf16[1,3072]{1,0:T(2,128)(2,1)S(1)} %get-tuple-element.30.gain_ref, bf16[192,3072]{1,0:T(8,128)(2,1)S(1)} %get-tuple-element.39.gate_ref, ...), custom_call_target="tpu_custom_call" | custom-call | flops 150994944 | bytes 2359296 | tf_op jit(solution)/shard_map/pallas_call | solution.py:142
  38.8 0.8 %collective-permute-start.15 = (bf16[64,192]{1,0:T(8,128)(2,1)S(1)}, bf16[64,192]{1,0:T(8,128)(2,1)S(1)}, u32[]{:S(2)}, u32[]{:S(2)}) collective-permute-start(bf16[64,192]{1,0:T(8,128)(2,1)S(1)} %shard_map.80.own_ref), channel_id=1, source_target_pairs={{0,2},{2,0},{4,6},{6,4},{8,10},{10,8},{12,14},{14,12},{16,18},{18,... | collective-permute-start | bytes 73736 | tf_op jit(solution)/shard_map/ppermute | solution.py:328
  39.5 0.5 collective-permute-done.12.far_ref
  40.0 1.0 %shard_map.81.own_ref = bf16[64,192]{1,0:T(8,128)(2,1)S(1)} custom-call(bf16[32,3072]{1,0:T(8,128)(2,1)S(1)} %collective-permute-done.5.near_ref, bf16[32,3072]{1,0:T(8,128)(2,1)S(1)} %collective-permute-done.12.far_ref, bf16[1,3072]{1,0:T(2,128)(2,1)S(1)} %get-tuple-element.30.gain_ref, bf16[192,3072]{1,0:T(8,128)(2,1)S(1)} %get-tuple-element.39.gate_ref, ...), custom_call_target="tpu_custom_call" | custom-call | flops 150994944 | bytes 2359296 | tf_op jit(solution)/shard_map/pallas_call | solution.py:142
  41.0 0.0 copy-start
  41.0 0.0 copy-start.1
  41.0 1.6 %collective-permute-start.17 = (bf16[64,192]{1,0:T(8,128)(2,1)S(1)}, bf16[64,192]{1,0:T(8,128)(2,1)S(1)}, u32[]{:S(2)}, u32[]{:S(2)}) collective-permute-start(bf16[64,192]{1,0:T(8,128)(2,1)S(1)} %shard_map.81.own_ref), channel_id=1, source_target_pairs={{0,2},{2,0},{4,6},{6,4},{8,10},{10,8},{12,14},{14,12},{16,18},{18,... | collective-permute-start | bytes 73736 | tf_op jit(solution)/shard_map/ppermute | solution.py:328
  42.6 0.1 collective-permute-done.15.other_ref
  42.8 0.3 shard_map.85
  43.1 3.5 %collective-permute-start.16 = (bf16[64,1536]{1,0:T(8,128)(2,1)S(1)}, bf16[64,1536]{1,0:T(8,128)(2,1)S(1)}, u32[]{:S(2)}, u32[]{:S(2)}) collective-permute-start(bf16[64,1536]{1,0:T(8,128)(2,1)S(1)} %shard_map.85), channel_id=1, source_target_pairs={{0,12},{2,14},{4,8},{6,10},{8,4},{10,6},{12,0},{14,2},{16,28},{18,... | collective-permute-start | bytes 589832 | tf_op jit(solution)/shard_map/ppermute | solution.py:328
  46.6 0.3 shard_map.86
  47.0 0.1 collective-permute-start.18
  47.1 1.0 %shard_map.76 = (f32[128,3072]{1,0:T(8,128)S(1)}, bf16[128,160]{1,0:T(8,128)(2,1)S(1)}, bf16[32,3072]{1,0:T(8,128)(2,1)S(1)}) custom-call(bf16[1,3072]{1,0:T(2,128)(2,1)S(1)} %get-tuple-element.30.gain_ref, s32[2,128]{1,0:T(2,128)S(1)} %bitcast.22, f32[2,128]{1,0:T(2,128)S(1)} %bitcast.23, bf16[48,3072]{1,0:T(8,128)(2,1)S(1)} %collective-permute-done.3.refs_0_, ...), custom_call_target="tpu_custom_call" | custom-call | flops 3145728 | bytes 2359296 | tf_op jit(solution)/shard_map/pallas_call | solution.py:246
  48.1 0.4 collective-permute-done.13.right_ref
  48.5 1.0 %shard_map.82.own_ref = bf16[64,192]{1,0:T(8,128)(2,1)S(1)} custom-call(bf16[32,3072]{1,0:T(8,128)(2,1)S(1)} %get-tuple-element.48.near_ref, bf16[32,3072]{1,0:T(8,128)(2,1)S(1)} %collective-permute-done.1.far_ref, bf16[1,3072]{1,0:T(2,128)(2,1)S(1)} %get-tuple-element.30.gain_ref, bf16[192,3072]{1,0:T(8,128)(2,1)S(1)} %get-tuple-element.39.gate_ref, ...), custom_call_target="tpu_custom_call" | custom-call | flops 150994944 | bytes 2359296 | tf_op jit(solution)/shard_map/pallas_call | solution.py:142
  49.5 1.1 %collective-permute-start.14 = (bf16[64,192]{1,0:T(8,128)(2,1)S(1)}, bf16[64,192]{1,0:T(8,128)(2,1)S(1)}, u32[]{:S(2)}, u32[]{:S(2)}) collective-permute-start(bf16[64,192]{1,0:T(8,128)(2,1)S(1)} %shard_map.82.own_ref), channel_id=1, source_target_pairs={{0,2},{2,0},{4,6},{6,4},{8,10},{10,8},{12,14},{14,12},{16,18},{18,... | collective-permute-start | bytes 73736 | tf_op jit(solution)/shard_map/ppermute | solution.py:328
  50.6 2.8 %collective-permute-done.14.other_ref = bf16[64,192]{1,0:T(8,128)(2,1)S(1)} collective-permute-done((bf16[64,192]{1,0:T(8,128)(2,1)S(1)}, bf16[64,192]{1,0:T(8,128)(2,1)S(1)}, u32[]{:S(2)}, u32[]{:S(2)}) %collective-permute-start.14) | collective-permute-done | bytes 24608 | tf_op jit(solution)/shard_map/ppermute | solution.py:328
  53.4 0.3 shard_map.83.left_ref
  53.8 0.1 shard_map.87
  53.9 1.1 %collective-permute-start.19 = (bf16[32,1536]{1,0:T(8,128)(2,1)S(1)}, bf16[32,1536]{1,0:T(8,128)(2,1)S(1)}, u32[]{:S(2)}, u32[]{:S(2)}) collective-permute-start(bf16[32,1536]{1,0:T(8,128)(2,1)S(1)} %get-tuple-element.50), channel_id=1, source_target_pairs={{0,2},{2,0},{4,6},{6,4},{8,10},{10,8},{12,14},{14,12},{16,18},{18,... | collective-permute-start | bytes 294920 | tf_op jit(solution)/shard_map/ppermute | solution.py:328
  55.1 3.5 %collective-permute-done.19.other_ref = bf16[32,1536]{1,0:T(8,128)(2,1)S(1)} collective-permute-done((bf16[32,1536]{1,0:T(8,128)(2,1)S(1)}, bf16[32,1536]{1,0:T(8,128)(2,1)S(1)}, u32[]{:S(2)}, u32[]{:S(2)}) %collective-permute-start.19) | collective-permute-done | bytes 98336 | tf_op jit(solution)/shard_map/ppermute | solution.py:328
  58.6 2.0 %shard_map.88 = bf16[128,3072]{1,0:T(8,128)(2,1)} custom-call(f32[128,3072]{1,0:T(8,128)S(1)} %get-tuple-element.33.base_ref, bf16[128,160]{1,0:T(8,128)(2,1)S(1)} %get-tuple-element.34.table_ref, f32[32,1536]{1,0:T(8,128)S(1)} %get-tuple-element.49.near_ref, bf16[32,1536]{1,0:T(8,128)(2,1)S(1)} %collective-permute-done.19.other_ref), custom_call_target="tpu_custom_call" | custom-call | flops 100663296 | bytes 2359296 | tf_op jit(solution)/shard_map/pallas_call | solution.py:281
  (16 shorter events, 0.1 us)
Async XLA Ops:
  0.0 4.7 %collective-permute-start = (s32[1,128,2]{1,2,0:T(2,128)}, s32[1,128,2]{1,2,0:T(2,128)S(1)}, u32[]{:S(2)}, u32[]{:S(2)}) collective-permute-start(s32[1,128,2]{1,2,0:T(2,128)} %param.12), channel_id=1, source_target_pairs={{0,16},{2,18},{4,20},{6,22},{8,24},{10,26},{12,28},{14,30},{16,0},... | collective-permute-start | bytes 3080 | tf_op jit(solution)/shard_map/ppermute | solution.py:328
  5.1 12.2 %collective-permute-start.2 = (bf16[32,3072]{1,0:T(8,128)(2,1)S(1)}, bf16[32,3072]{1,0:T(8,128)(2,1)S(1)}, u32[]{:S(2)}, u32[]{:S(2)}) collective-permute-start(bf16[32,3072]{1,0:T(8,128)(2,1)S(1)} %shard_map.74), channel_id=1, source_target_pairs={{0,24},{2,26},{4,28},{6,30},{8,16},{10,18},{12,20},{14,22},{16,8},... | collective-permute-start | bytes 589832 | tf_op jit(solution)/shard_map/ppermute | solution.py:328
  9.2 12.6 %collective-permute-start.1 = (bf16[32,3072]{1,0:T(8,128)(2,1)S(1)}, bf16[32,3072]{1,0:T(8,128)(2,1)S(1)}, u32[]{:S(2)}, u32[]{:S(2)}) collective-permute-start(bf16[32,3072]{1,0:T(8,128)(2,1)S(1)} %shard_map.74), channel_id=1, source_target_pairs={{0,18},{2,16},{4,22},{6,20},{8,26},{10,24},{12,30},{14,28},{16,2},... | collective-permute-start | bytes 589832 | tf_op jit(solution)/shard_map/ppermute | solution.py:328
  10.7 11.7 %collective-permute-start.10 = (bf16[96,1536]{1,0:T(8,128)(2,1)S(1)}, bf16[96,1536]{1,0:T(8,128)(2,1)S(1)}, u32[]{:S(2)}, u32[]{:S(2)}) collective-permute-start(bf16[96,1536]{1,0:T(8,128)(2,1)S(1)} %get-tuple-element.44), channel_id=1, source_target_pairs={{0,2},{2,0},{4,6},{6,4},{8,10},{10,8},{12,14},{14,12},{16,18},{18,... | collective-permute-start | bytes 884744 | tf_op jit(solution)/shard_map/ppermute | solution.py:328
  11.2 8.2 %copy-start.2 = (bf16[1,128,3072]{2,1,0:T(8,128)(2,1)S(1)}, bf16[1,128,3072]{2,1,0:T(8,128)(2,1)}, u32[]{:S(2)}) copy-start(bf16[1,128,3072]{2,1,0:T(8,128)(2,1)} %param.7) | copy-start | bytes 2359300
  17.2 9.0 %collective-permute-start.7 = (bf16[32,3072]{1,0:T(8,128)(2,1)S(1)}, bf16[32,3072]{1,0:T(8,128)(2,1)S(1)}, u32[]{:S(2)}, u32[]{:S(2)}) collective-permute-start(bf16[32,3072]{1,0:T(8,128)(2,1)S(1)} %collective-permute-done.2.near_ref), channel_id=1, source_target_pairs={{0,2},{2,0},{4,6},{6,4},{8,10},{10,8},{12,14},{14,12},{16,18},{18,... | collective-permute-start | bytes 589832 | tf_op jit(solution)/shard_map/ppermute | solution.py:328
  18.8 7.5 %collective-permute-start.6 = (bf16[32,3072]{1,0:T(8,128)(2,1)S(1)}, bf16[32,3072]{1,0:T(8,128)(2,1)S(1)}, u32[]{:S(2)}, u32[]{:S(2)}) collective-permute-start(bf16[32,3072]{1,0:T(8,128)(2,1)S(1)} %collective-permute-done.2.near_ref), channel_id=1, source_target_pairs={{0,4},{2,6},{4,0},{6,2},{8,12},{10,14},{12,8},{14,10},{16,20},{18,... | collective-permute-start | bytes 589832 | tf_op jit(solution)/shard_map/ppermute | solution.py:328
  19.4 14.5 %collective-permute-start.5 = (bf16[32,3072]{1,0:T(8,128)(2,1)S(1)}, bf16[32,3072]{1,0:T(8,128)(2,1)S(1)}, u32[]{:S(2)}, u32[]{:S(2)}) collective-permute-start(bf16[32,3072]{1,0:T(8,128)(2,1)S(1)} %shard_map.74), channel_id=1, source_target_pairs={{0,20},{2,22},{4,16},{6,18},{8,28},{10,30},{12,24},{14,26},{16,4},... | collective-permute-start | bytes 589832 | tf_op jit(solution)/shard_map/ppermute | solution.py:328
  21.7 16.1 %collective-permute-start.3 = (bf16[48,3072]{1,0:T(8,128)(2,1)S(1)}, bf16[48,3072]{1,0:T(8,128)(2,1)S(1)}, u32[]{:S(2)}, u32[]{:S(2)}) collective-permute-start(bf16[48,3072]{1,0:T(8,128)(2,1)S(1)} %slice_bitcast_fusion.1), channel_id=1, source_target_pairs={{0,16},{2,18},{4,20},{6,22},{8,24},{10,26},{12,28},{14,30},{16,0},... | collective-permute-start | bytes 884744 | tf_op jit(solution)/shard_map/ppermute | solution.py:328
  22.4 11.1 %collective-permute-start.11 = (bf16[96,1536]{1,0:T(8,128)(2,1)S(1)}, bf16[96,1536]{1,0:T(8,128)(2,1)S(1)}, u32[]{:S(2)}, u32[]{:S(2)}) collective-permute-start(bf16[96,1536]{1,0:T(8,128)(2,1)S(1)} %collective-permute-done.10.own_ref), channel_id=1, source_target_pairs={{0,1},{1,0},{2,3},{3,2},{4,5},{5,4},{6,7},{7,6},{8,9},{9,8},{10,11... | collective-permute-start | bytes 884744 | tf_op jit(solution)/shard_map/ppermute | solution.py:350
  27.2 4.0 %collective-permute-start.8 = (bf16[64,192]{1,0:T(8,128)(2,1)S(1)}, bf16[64,192]{1,0:T(8,128)(2,1)S(1)}, u32[]{:S(2)}, u32[]{:S(2)}) collective-permute-start(bf16[64,192]{1,0:T(8,128)(2,1)S(1)} %shard_map.77.own_ref), channel_id=1, source_target_pairs={{0,2},{2,0},{4,6},{6,4},{8,10},{10,8},{12,14},{14,12},{16,18},{18,... | collective-permute-start | bytes 73736 | tf_op jit(solution)/shard_map/ppermute | solution.py:328
  27.8 5.7 %collective-permute-start.9 = (bf16[32,3072]{1,0:T(8,128)(2,1)S(1)}, bf16[32,3072]{1,0:T(8,128)(2,1)S(1)}, u32[]{:S(2)}, u32[]{:S(2)}) collective-permute-start(bf16[32,3072]{1,0:T(8,128)(2,1)S(1)} %collective-permute-done.7.far_ref), channel_id=1, source_target_pairs={{0,4},{2,6},{4,0},{6,2},{8,12},{10,14},{12,8},{14,10},{16,20},{18,... | collective-permute-start | bytes 589832 | tf_op jit(solution)/shard_map/ppermute | solution.py:328
  31.2 15.8 %collective-permute-start.4 = (bf16[80,3072]{1,0:T(8,128)(2,1)S(1)}, bf16[80,3072]{1,0:T(8,128)(2,1)S(1)}, u32[]{:S(2)}, u32[]{:S(2)}) collective-permute-start(bf16[80,3072]{1,0:T(8,128)(2,1)S(1)} %slice_bitcast_fusion), channel_id=1, source_target_pairs={{0,16},{2,18},{4,20},{6,22},{8,24},{10,26},{12,28},{14,30},{16,0},... | collective-permute-start | bytes 1474568 | tf_op jit(solution)/shard_map/ppermute | solution.py:328
  33.9 6.1 %collective-permute-start.12 = (bf16[32,3072]{1,0:T(8,128)(2,1)S(1)}, bf16[32,3072]{1,0:T(8,128)(2,1)S(1)}, u32[]{:S(2)}, u32[]{:S(2)}) collective-permute-start(bf16[32,3072]{1,0:T(8,128)(2,1)S(1)} %collective-permute-done.5.near_ref), channel_id=1, source_target_pairs={{0,2},{2,0},{4,6},{6,4},{8,10},{10,8},{12,14},{14,12},{16,18},{18,... | collective-permute-start | bytes 589832 | tf_op jit(solution)/shard_map/ppermute | solution.py:328
  35.5 13.0 %collective-permute-start.13 = (bf16[64,1536]{1,0:T(8,128)(2,1)S(1)}, bf16[64,1536]{1,0:T(8,128)(2,1)S(1)}, u32[]{:S(2)}, u32[]{:S(2)}) collective-permute-start(bf16[64,1536]{1,0:T(8,128)(2,1)S(1)} %shard_map.79), channel_id=1, source_target_pairs={{0,8},{2,10},{4,12},{6,14},{8,0},{10,2},{12,4},{14,6},{16,24},{18,... | collective-permute-start | bytes 589832 | tf_op jit(solution)/shard_map/ppermute | solution.py:328
  38.8 4.0 %collective-permute-start.15 = (bf16[64,192]{1,0:T(8,128)(2,1)S(1)}, bf16[64,192]{1,0:T(8,128)(2,1)S(1)}, u32[]{:S(2)}, u32[]{:S(2)}) collective-permute-start(bf16[64,192]{1,0:T(8,128)(2,1)S(1)} %shard_map.80.own_ref), channel_id=1, source_target_pairs={{0,2},{2,0},{4,6},{6,4},{8,10},{10,8},{12,14},{14,12},{16,18},{18,... | collective-permute-start | bytes 73736 | tf_op jit(solution)/shard_map/ppermute | solution.py:328
  41.0 6.1 %copy-start = (s32[1,128,2]{1,2,0:T(2,128)S(1)}, s32[1,128,2]{1,2,0:T(2,128)}, u32[]{:S(2)}) copy-start(s32[1,128,2]{1,2,0:T(2,128)} %param.12) | copy-start | bytes 3076
  41.0 6.1 %copy-start.1 = (f32[1,128,2]{1,2,0:T(2,128)S(1)}, f32[1,128,2]{1,2,0:T(2,128)}, u32[]{:S(2)}) copy-start(f32[1,128,2]{1,2,0:T(2,128)} %param.13) | copy-start | bytes 3076
  41.0 5.6 %collective-permute-start.17 = (bf16[64,192]{1,0:T(8,128)(2,1)S(1)}, bf16[64,192]{1,0:T(8,128)(2,1)S(1)}, u32[]{:S(2)}, u32[]{:S(2)}) collective-permute-start(bf16[64,192]{1,0:T(8,128)(2,1)S(1)} %shard_map.81.own_ref), channel_id=1, source_target_pairs={{0,2},{2,0},{4,6},{6,4},{8,10},{10,8},{12,14},{14,12},{16,18},{18,... | collective-permute-start | bytes 73736 | tf_op jit(solution)/shard_map/ppermute | solution.py:328
  43.1 10.7 %collective-permute-start.16 = (bf16[64,1536]{1,0:T(8,128)(2,1)S(1)}, bf16[64,1536]{1,0:T(8,128)(2,1)S(1)}, u32[]{:S(2)}, u32[]{:S(2)}) collective-permute-start(bf16[64,1536]{1,0:T(8,128)(2,1)S(1)} %shard_map.85), channel_id=1, source_target_pairs={{0,12},{2,14},{4,8},{6,10},{8,4},{10,6},{12,0},{14,2},{16,28},{18,... | collective-permute-start | bytes 589832 | tf_op jit(solution)/shard_map/ppermute | solution.py:328
  47.0 6.9 %collective-permute-start.18 = (bf16[64,1536]{1,0:T(8,128)(2,1)S(1)}, bf16[64,1536]{1,0:T(8,128)(2,1)S(1)}, u32[]{:S(2)}, u32[]{:S(2)}) collective-permute-start(bf16[64,1536]{1,0:T(8,128)(2,1)S(1)} %shard_map.86), channel_id=1, source_target_pairs={{0,4},{2,6},{4,0},{6,2},{8,12},{10,14},{12,8},{14,10},{16,20},{18,... | collective-permute-start | bytes 589832 | tf_op jit(solution)/shard_map/ppermute | solution.py:328
  49.5 4.0 %collective-permute-start.14 = (bf16[64,192]{1,0:T(8,128)(2,1)S(1)}, bf16[64,192]{1,0:T(8,128)(2,1)S(1)}, u32[]{:S(2)}, u32[]{:S(2)}) collective-permute-start(bf16[64,192]{1,0:T(8,128)(2,1)S(1)} %shard_map.82.own_ref), channel_id=1, source_target_pairs={{0,2},{2,0},{4,6},{6,4},{8,10},{10,8},{12,14},{14,12},{16,18},{18,... | collective-permute-start | bytes 73736 | tf_op jit(solution)/shard_map/ppermute | solution.py:328
  53.9 4.7 %collective-permute-start.19 = (bf16[32,1536]{1,0:T(8,128)(2,1)S(1)}, bf16[32,1536]{1,0:T(8,128)(2,1)S(1)}, u32[]{:S(2)}, u32[]{:S(2)}) collective-permute-start(bf16[32,1536]{1,0:T(8,128)(2,1)S(1)} %get-tuple-element.50), channel_id=1, source_target_pairs={{0,2},{2,0},{4,6},{6,4},{8,10},{10,8},{12,14},{14,12},{16,18},{18,... | collective-permute-start | bytes 294920 | tf_op jit(solution)/shard_map/ppermute | solution.py:328

commit v10 on v9

--- a/solution.py
+++ b/solution.py
@@ -259,37 +259,45 @@
     )(gain, ids_t, weights_t, *blocks)
 
 
-def end_kernel(steps, ordered, base_ref, table_ref, near_ref, other_ref, out_ref):
-    step = pl.program_id(0)
-    columns = out_ref.shape[1]
-    here = pl.ds(pl.multiple_of(step * columns, columns), columns)
-    within = pl.ds(pl.multiple_of(lax.rem(step, steps // 2) * columns, columns), columns)
-    first = 0 if ordered else parity()
-    near = near_ref[:, within].astype(jnp.float32)
-    other = other_ref[:, within].astype(jnp.float32)
-    total = jnp.where(lax.div(step, steps // 2) == first, near, other)
-    high, low, _ = parts_of(total)
-    rows = jnp.concatenate([high, high, high, low, low], axis=0)
-    added = jnp.dot(table_ref[...], rows, preferred_element_type=jnp.float32)
-    out_ref[...] = (base_ref[:, here] + added).astype(jnp.bfloat16)
-
-
-def ended(base, table, near, other, ordered):
+def end_kernel(steps, which, base_ref, table_ref, rows_ref, *refs):
+    out_ref, done, sems = refs[-3:]
+    half = rows_ref.shape[1]
+    columns = half // steps
+    if which is None:
+        which = parity()
+    elif which < 0:
+        which = 1 - parity()
+    copies = []
+    for step in range(steps):
+        within = slice(step * columns, (step + 1) * columns)
+        here = pl.ds(pl.multiple_of(which * half + step * columns, columns), columns)
+        high, low, _ = parts_of(rows_ref[:, within].astype(jnp.float32))
+        rows = jnp.concatenate([high, high, high, low, low], axis=0)
+        added = jnp.dot(table_ref[...], rows, preferred_element_type=jnp.float32)
+        done[:, within] = (base_ref[:, here] + added).astype(jnp.bfloat16)
+        copies.append(pltpu.make_async_copy(done.at[:, within], out_ref.at[:, here], sems.at[step]))
+        copies[-1].start()
+    for copy in copies:
+        copy.wait()
+
+
+def ended(base, table, rows, which, out=None):
     count, width = base.shape
-    steps = 4
-    columns = width // steps
-    return pl.pallas_call(
-        functools.partial(end_kernel, steps, ordered),
+    half = rows.shape[1]
+    steps = 3
+    return pl.pallas_call(
+        functools.partial(end_kernel, steps, which),
         out_shape=jax.ShapeDtypeStruct((count, width), jnp.bfloat16),
-        grid=(steps,),
-        in_specs=[VMEM] * 4,
-        out_specs=pl.BlockSpec((count, columns), lambda i: (0, i)),
-        compiler_params=PARAMS,
-        cost_estimate=pl.CostEstimate(
-            flops=2 * count * width * table.shape[0], bytes_accessed=6 * count * width,
+        in_specs=[VMEM] * 3 + ([] if out is None else [HBM]),
+        out_specs=HBM,
+        scratch_shapes=[pltpu.VMEM((count, half), jnp.bfloat16), pltpu.SemaphoreType.DMA((steps,))],
+        input_output_aliases={} if out is None else {3: 0},
+        compiler_params=PARAMS,
+        cost_estimate=pl.CostEstimate(
+            flops=2 * count * half * table.shape[1], bytes_accessed=6 * count * half,
             transcendentals=0,
         ),
-    )(base, table, near, other)
+    )(base, table, rows, *(() if out is None else (out,)))
 
 
 def early_kernel(left_ref, right_ref, out_ref):
@@ -371,7 +379,7 @@
     hidden, part, back = {}, {}, {}
     for k in (2, 3, 1, 0):
         first = {
-            2: (near[3],), 3: (part.get(2), arrived[0]), 1: (hidden.get(3),), 0: (hidden.get(1), back.get(2))
+            2: (near[3],), 3: (part.get(2),), 1: (hidden.get(3),), 0: (hidden.get(1),)
         }[k]
         if k == 3:
             far[1] = moved(after(near[1], part[2]), 0, 0, 1)
@@ -380,7 +388,10 @@
         if k == 2:
             crossed = after(crossed, far[3])
         part[k] = down_of(hidden[k], crossed, own_down, other_down)
-        back[k] = moved(part[k], 0, k) if k else part[k]
+    back[2] = moved(part[2], 0, 2)
+    back[3] = moved(after(part[3], back[2], hidden[0]), 0, 3)
+    back[1] = moved(part[1], 0, 1)
+    back[0] = part[0]
     early = summed_early(back[0], back[2])
     own, others = joined([early, back[3], back[1]])
     others = moved(others, 0, 0, 1)
@@ -389,8 +400,10 @@
         left = parity() == 0
         summed = [jnp.where(left, own, others), jnp.where(left, others, own)]
         summed = exchanged(jnp.concatenate(summed, axis=1))
-        own, others = summed[:, :width // 2], summed[:, width // 2:]
-    return ended(base, table, own, others, experts > 1)[None]
+        out = ended(base, table, summed[:, :width // 2], 0)
+        return ended(base, table, summed[:, width // 2:], 1, out)[None]
+    out = ended(base, table, own, None)
+    return ended(base, table, others, -1, out)[None]
 
 
 def solution(mesh):

time: 60.8 us -> 62.8 us (1.033)
  waiting for transfers between devices: 18.6 us -> 22 us
  starting transfers between devices: 29.8 us -> 28.6 us
    ppermute x19, waiting for transfers between devices: 18.6 us -> 22 us  [moved(): return lax.ppermute(value, ('section', 'expert'), pairs)]
    ppermute x19, starting transfers between devices: 29.8 us -> 28.6 us  [moved(): return lax.ppermute(value, ('section', 'expert'), pairs)]
    pallas_call x1 -> x2, Pallas kernels: 2.02 us -> 1.91 us  [ended(): pl.pallas_call(functools.partial(end_kernel, steps, which), out_shape=jax...]
  transfers between devices with their start and end apart: 20 -> 20, of which waited for: 10 -> 12; matrix products, arithmetic and copies ran while one was open for 0% -> 0% of each run, Pallas kernels for 16% -> 17%
where the time goes in v10:
time: 62.8 us; the launch traced here: 62.6 us
  starting transfers between devices  28.6 us (46%)
  waiting for transfers between devices  22 us (35%)
  Pallas kernels  11.8 us (19%)
    ppermute x19, starting transfers between devices, moved(): return lax.ppermute(value, ('section', 'expert'), pairs)  28.6 us
    ppermute x19, waiting for transfers between devices, moved(): return lax.ppermute(value, ('section', 'expert'), pairs)  22 us
    pallas_call x4, Pallas kernels, hidden_of(): pl.pallas_call(hidden_kernel, out_shape=jax.ShapeDtypeStruct((rows, hidde...  3.86 us
    pallas_call x2, Pallas kernels, loaded(): pl.pallas_call(functools.partial(load_kernel, kinds), out_shape=tuple((ja...  3.13 us
    pallas_call x2, Pallas kernels, ended(): pl.pallas_call(functools.partial(end_kernel, steps, which), out_shape=jax...  1.91 us
    pallas_call x4, Pallas kernels, down_of(): pl.pallas_call(down_kernel, out_shape=jax.ShapeDtypeStruct((rows, half),...  1.3 us
  transfers between devices with their start and end apart: 20, of which 12 were waited for; matrix products, arithmetic and copies ran while one was open for 0% of the time, Pallas kernels for 17%

profile of v10, /device:TPU:0, one launch (start us, length us, event | category | flops | bytes accessed | tf_op | source)
XLA Modules:
  0.0 62.6 jit_solution(8970037283502445793)
XLA Ops:
  0.0 2.9 %collective-permute-start = (s32[1,128,2]{1,2,0:T(2,128)}, s32[1,128,2]{1,2,0:T(2,128)S(1)}, u32[]{:S(2)}, u32[]{:S(2)}) collective-permute-start(s32[1,128,2]{1,2,0:T(2,128)} %param.12), channel_id=1, source_target_pairs={{0,16},{2,18},{4,20},{6,22},{8,24},{10,26},{12,28},{14,30},{16,0},... | collective-permute-start | bytes 3080 | tf_op jit(solution)/shard_map/ppermute | solution.py:336
  2.9 1.2 %shard_map.73 = (bf16[128,3072]{1,0:T(8,128)(2,1)S(1)}, bf16[96,1536]{1,0:T(8,128)(2,1)S(1)}) custom-call(bf16[128,3072]{1,0:T(8,128)(2,1)} %bitcast.27, bf16[192,3072]{1,0:T(8,128)(2,1)} %bitcast.25), custom_call_target="tpu_custom_call" | custom-call | bytes 2162688 | tf_op jit(solution)/shard_map/pallas_call | solution.py:58
  4.2 0.5 collective-permute-done
  4.7 0.4 shard_map.74
  5.1 4.1 %collective-permute-start.2 = (bf16[32,3072]{1,0:T(8,128)(2,1)S(1)}, bf16[32,3072]{1,0:T(8,128)(2,1)S(1)}, u32[]{:S(2)}, u32[]{:S(2)}) collective-permute-start(bf16[32,3072]{1,0:T(8,128)(2,1)S(1)} %shard_map.74), channel_id=1, source_target_pairs={{0,24},{2,26},{4,28},{6,30},{8,16},{10,18},{12,20},{14,22},{16,8},... | collective-permute-start | bytes 589832 | tf_op jit(solution)/shard_map/ppermute | solution.py:336
  9.2 1.5 %collective-permute-start.1 = (bf16[32,3072]{1,0:T(8,128)(2,1)S(1)}, bf16[32,3072]{1,0:T(8,128)(2,1)S(1)}, u32[]{:S(2)}, u32[]{:S(2)}) collective-permute-start(bf16[32,3072]{1,0:T(8,128)(2,1)S(1)} %shard_map.74), channel_id=1, source_target_pairs={{0,18},{2,16},{4,22},{6,20},{8,26},{10,24},{12,30},{14,28},{16,2},... | collective-permute-start | bytes 589832 | tf_op jit(solution)/shard_map/ppermute | solution.py:336
  10.7 0.5 collective-permute-start.10
  11.2 1.9 %shard_map.75 = (bf16[192,1536]{1,0:T(8,128)(2,1)S(1)}, bf16[192,3072]{1,0:T(8,128)(2,1)S(1)}, bf16[192,3072]{1,0:T(8,128)(2,1)S(1)}, bf16[1,3072]{1,0:T(2,128)(2,1)S(1)}) custom-call(bf16[192,3072]{1,0:T(8,128)(2,1)} %bitcast.26, bf16[192,3072]{1,0:T(8,128)(2,1)} %bitcast.28, bf16[192,3072]{1,0:T(8,128)(2,1)} %bitcast.29, bf16[1,3072]{1,0:T(2,128)(2,1)} %refs_3_.1), custom_call_target="tpu_custom_call" | custom-call | bytes 5910528 | tf_op jit(solution)/shard_map/pallas_call | solution.py:58
  13.1 4.1 %collective-permute-done.2.near_ref = bf16[32,3072]{1,0:T(8,128)(2,1)S(1)} collective-permute-done((bf16[32,3072]{1,0:T(8,128)(2,1)S(1)}, bf16[32,3072]{1,0:T(8,128)(2,1)S(1)}, u32[]{:S(2)}, u32[]{:S(2)}) %collective-permute-start.2) | collective-permute-done | bytes 196640 | tf_op jit(solution)/shard_map/ppermute | solution.py:336
  17.2 1.5 %collective-permute-start.7 = (bf16[32,3072]{1,0:T(8,128)(2,1)S(1)}, bf16[32,3072]{1,0:T(8,128)(2,1)S(1)}, u32[]{:S(2)}, u32[]{:S(2)}) collective-permute-start(bf16[32,3072]{1,0:T(8,128)(2,1)S(1)} %collective-permute-done.2.near_ref), channel_id=1, source_target_pairs={{0,2},{2,0},{4,6},{6,4},{8,10},{10,8},{12,14},{14,12},{16,18},{18,... | collective-permute-start | bytes 589832 | tf_op jit(solution)/shard_map/ppermute | solution.py:336
  18.8 0.6 collective-permute-start.6
  19.4 0.9 %collective-permute-start.4 = (bf16[80,3072]{1,0:T(8,128)(2,1)S(1)}, bf16[80,3072]{1,0:T(8,128)(2,1)S(1)}, u32[]{:S(2)}, u32[]{:S(2)}) collective-permute-start(bf16[80,3072]{1,0:T(8,128)(2,1)S(1)} %slice_bitcast_fusion), channel_id=1, source_target_pairs={{0,16},{2,18},{4,20},{6,22},{8,24},{10,26},{12,28},{14,30},{16,0},... | collective-permute-start | bytes 1474568 | tf_op jit(solution)/shard_map/ppermute | solution.py:336
  20.3 2.1 %collective-permute-start.5 = (bf16[32,3072]{1,0:T(8,128)(2,1)S(1)}, bf16[32,3072]{1,0:T(8,128)(2,1)S(1)}, u32[]{:S(2)}, u32[]{:S(2)}) collective-permute-start(bf16[32,3072]{1,0:T(8,128)(2,1)S(1)} %shard_map.74), channel_id=1, source_target_pairs={{0,20},{2,22},{4,16},{6,18},{8,28},{10,30},{12,24},{14,26},{16,4},... | collective-permute-start | bytes 589832 | tf_op jit(solution)/shard_map/ppermute | solution.py:336
  22.4 3.9 %collective-permute-done.6.near_ref = bf16[32,3072]{1,0:T(8,128)(2,1)S(1)} collective-permute-done((bf16[32,3072]{1,0:T(8,128)(2,1)S(1)}, bf16[32,3072]{1,0:T(8,128)(2,1)S(1)}, u32[]{:S(2)}, u32[]{:S(2)}) %collective-permute-start.6) | collective-permute-done | bytes 196640 | tf_op jit(solution)/shard_map/ppermute | solution.py:336
  26.3 1.0 %shard_map.77.own_ref = bf16[64,192]{1,0:T(8,128)(2,1)S(1)} custom-call(bf16[32,3072]{1,0:T(8,128)(2,1)S(1)} %collective-permute-done.2.near_ref, bf16[32,3072]{1,0:T(8,128)(2,1)S(1)} %collective-permute-done.7.far_ref, bf16[1,3072]{1,0:T(2,128)(2,1)S(1)} %get-tuple-element.31.gain_ref, bf16[192,3072]{1,0:T(8,128)(2,1)S(1)} %get-tuple-element.40.gate_ref, ...), custom_call_target="tpu_custom_call" | custom-call | flops 150994944 | bytes 2359296 | tf_op jit(solution)/shard_map/pallas_call | solution.py:142
  27.2 0.5 collective-permute-start.8
  27.8 1.5 %collective-permute-start.9 = (bf16[32,3072]{1,0:T(8,128)(2,1)S(1)}, bf16[32,3072]{1,0:T(8,128)(2,1)S(1)}, u32[]{:S(2)}, u32[]{:S(2)}) collective-permute-start(bf16[32,3072]{1,0:T(8,128)(2,1)S(1)} %collective-permute-done.7.far_ref), channel_id=1, source_target_pairs={{0,4},{2,6},{4,0},{6,2},{8,12},{10,14},{12,8},{14,10},{16,20},{18,... | collective-permute-start | bytes 589832 | tf_op jit(solution)/shard_map/ppermute | solution.py:336
  29.3 1.9 %collective-permute-done.8.other_ref = bf16[64,192]{1,0:T(8,128)(2,1)S(1)} collective-permute-done((bf16[64,192]{1,0:T(8,128)(2,1)S(1)}, bf16[64,192]{1,0:T(8,128)(2,1)S(1)}, u32[]{:S(2)}, u32[]{:S(2)}) %collective-permute-start.8) | collective-permute-done | bytes 24608 | tf_op jit(solution)/shard_map/ppermute | solution.py:336
  31.2 1.5 %collective-permute-start.3 = (bf16[48,3072]{1,0:T(8,128)(2,1)S(1)}, bf16[48,3072]{1,0:T(8,128)(2,1)S(1)}, u32[]{:S(2)}, u32[]{:S(2)}) collective-permute-start(bf16[48,3072]{1,0:T(8,128)(2,1)S(1)} %slice_bitcast_fusion.1), channel_id=1, source_target_pairs={{0,16},{2,18},{4,20},{6,22},{8,24},{10,26},{12,28},{14,30},{16,0},... | collective-permute-start | bytes 884744 | tf_op jit(solution)/shard_map/ppermute | solution.py:336
  32.7 0.7 %collective-permute-done.9.far_ref = bf16[32,3072]{1,0:T(8,128)(2,1)S(1)} collective-permute-done((bf16[32,3072]{1,0:T(8,128)(2,1)S(1)}, bf16[32,3072]{1,0:T(8,128)(2,1)S(1)}, u32[]{:S(2)}, u32[]{:S(2)}) %collective-permute-start.9) | collective-permute-done | bytes 196640 | tf_op jit(solution)/shard_map/ppermute | solution.py:336
  33.4 0.1 shard_map.78.other_down_ref
  33.6 0.3 shard_map.79
  33.9 1.6 %collective-permute-start.12 = (bf16[32,3072]{1,0:T(8,128)(2,1)S(1)}, bf16[32,3072]{1,0:T(8,128)(2,1)S(1)}, u32[]{:S(2)}, u32[]{:S(2)}) collective-permute-start(bf16[32,3072]{1,0:T(8,128)(2,1)S(1)} %collective-permute-done.5.near_ref), channel_id=1, source_target_pairs={{0,2},{2,0},{4,6},{6,4},{8,10},{10,8},{12,14},{14,12},{16,18},{18,... | collective-permute-start | bytes 589832 | tf_op jit(solution)/shard_map/ppermute | solution.py:336
  35.5 2.3 %collective-permute-start.14 = (bf16[64,1536]{1,0:T(8,128)(2,1)S(1)}, bf16[64,1536]{1,0:T(8,128)(2,1)S(1)}, u32[]{:S(2)}, u32[]{:S(2)}) collective-permute-start(bf16[64,1536]{1,0:T(8,128)(2,1)S(1)} %shard_map.79), channel_id=1, source_target_pairs={{0,8},{2,10},{4,12},{6,14},{8,0},{10,2},{12,4},{14,6},{16,24},{18,... | collective-permute-start | bytes 589832 | tf_op jit(solution)/shard_map/ppermute | solution.py:336
  37.8 1.0 %shard_map.80.own_ref = bf16[64,192]{1,0:T(8,128)(2,1)S(1)} custom-call(bf16[32,3072]{1,0:T(8,128)(2,1)S(1)} %collective-permute-done.6.near_ref, bf16[32,3072]{1,0:T(8,128)(2,1)S(1)} %collective-permute-done.9.far_ref, bf16[1,3072]{1,0:T(2,128)(2,1)S(1)} %get-tuple-element.31.gain_ref, bf16[192,3072]{1,0:T(8,128)(2,1)S(1)} %get-tuple-element.40.gate_ref, ...), custom_call_target="tpu_custom_call" | custom-call | flops 150994944 | bytes 2359296 | tf_op jit(solution)/shard_map/pallas_call | solution.py:142
  38.8 0.8 %collective-permute-start.15 = (bf16[64,192]{1,0:T(8,128)(2,1)S(1)}, bf16[64,192]{1,0:T(8,128)(2,1)S(1)}, u32[]{:S(2)}, u32[]{:S(2)}) collective-permute-start(bf16[64,192]{1,0:T(8,128)(2,1)S(1)} %shard_map.80.own_ref), channel_id=1, source_target_pairs={{0,2},{2,0},{4,6},{6,4},{8,10},{10,8},{12,14},{14,12},{16,18},{18,... | collective-permute-start | bytes 73736 | tf_op jit(solution)/shard_map/ppermute | solution.py:336
  39.5 0.5 collective-permute-done.12.far_ref
  40.0 1.0 %shard_map.81.own_ref = bf16[64,192]{1,0:T(8,128)(2,1)S(1)} custom-call(bf16[32,3072]{1,0:T(8,128)(2,1)S(1)} %collective-permute-done.5.near_ref, bf16[32,3072]{1,0:T(8,128)(2,1)S(1)} %collective-permute-done.12.far_ref, bf16[1,3072]{1,0:T(2,128)(2,1)S(1)} %get-tuple-element.31.gain_ref, bf16[192,3072]{1,0:T(8,128)(2,1)S(1)} %get-tuple-element.40.gate_ref, ...), custom_call_target="tpu_custom_call" | custom-call | flops 150994944 | bytes 2359296 | tf_op jit(solution)/shard_map/pallas_call | solution.py:142
  41.0 0.0 copy-start.1
  41.0 1.6 %collective-permute-start.17 = (bf16[64,192]{1,0:T(8,128)(2,1)S(1)}, bf16[64,192]{1,0:T(8,128)(2,1)S(1)}, u32[]{:S(2)}, u32[]{:S(2)}) collective-permute-start(bf16[64,192]{1,0:T(8,128)(2,1)S(1)} %shard_map.81.own_ref), channel_id=1, source_target_pairs={{0,2},{2,0},{4,6},{6,4},{8,10},{10,8},{12,14},{14,12},{16,18},{18,... | collective-permute-start | bytes 73736 | tf_op jit(solution)/shard_map/ppermute | solution.py:336
  42.6 0.1 collective-permute-done.15.other_ref
  42.8 0.3 shard_map.85
  43.1 1.0 %shard_map.76 = (f32[128,3072]{1,0:T(8,128)S(1)}, bf16[128,160]{1,0:T(8,128)(2,1)S(1)}, bf16[32,3072]{1,0:T(8,128)(2,1)S(1)}) custom-call(bf16[1,3072]{1,0:T(2,128)(2,1)S(1)} %get-tuple-element.31.gain_ref, s32[2,128]{1,0:T(2,128)S(1)} %bitcast.22, f32[2,128]{1,0:T(2,128)S(1)} %bitcast.23, bf16[48,3072]{1,0:T(8,128)(2,1)S(1)} %collective-permute-done.3.refs_0_, ...), custom_call_target="tpu_custom_call" | custom-call | flops 3145728 | bytes 2359296 | tf_op jit(solution)/shard_map/pallas_call | solution.py:246
  44.1 1.0 %shard_map.82.own_ref = bf16[64,192]{1,0:T(8,128)(2,1)S(1)} custom-call(bf16[32,3072]{1,0:T(8,128)(2,1)S(1)} %get-tuple-element.49.near_ref, bf16[32,3072]{1,0:T(8,128)(2,1)S(1)} %collective-permute-done.1.far_ref, bf16[1,3072]{1,0:T(2,128)(2,1)S(1)} %get-tuple-element.31.gain_ref, bf16[192,3072]{1,0:T(8,128)(2,1)S(1)} %get-tuple-element.40.gate_ref, ...), custom_call_target="tpu_custom_call" | custom-call | flops 150994944 | bytes 2359296 | tf_op jit(solution)/shard_map/pallas_call | solution.py:142
  45.1 0.1 collective-permute-done.14.right_ref
  45.2 3.5 %collective-permute-start.16 = (bf16[64,1536]{1,0:T(8,128)(2,1)S(1)}, bf16[64,1536]{1,0:T(8,128)(2,1)S(1)}, u32[]{:S(2)}, u32[]{:S(2)}) collective-permute-start(bf16[64,1536]{1,0:T(8,128)(2,1)S(1)} %shard_map.85), channel_id=1, source_target_pairs={{0,12},{2,14},{4,8},{6,10},{8,4},{10,6},{12,0},{14,2},{16,28},{18,... | collective-permute-start | bytes 589832 | tf_op jit(solution)/shard_map/ppermute | solution.py:336
  48.6 0.3 shard_map.86
  49.0 0.1 collective-permute-start.18
  49.0 0.5 collective-permute-start.13
  49.5 3.5 %collective-permute-done.13.other_ref = bf16[64,192]{1,0:T(8,128)(2,1)S(1)} collective-permute-done((bf16[64,192]{1,0:T(8,128)(2,1)S(1)}, bf16[64,192]{1,0:T(8,128)(2,1)S(1)}, u32[]{:S(2)}, u32[]{:S(2)}) %collective-permute-start.13) | collective-permute-done | bytes 24608 | tf_op jit(solution)/shard_map/ppermute | solution.py:336
  53.0 0.3 shard_map.83.left_ref
  53.4 1.4 %collective-permute-done.16.refs_1_ = bf16[64,1536]{1,0:T(8,128)(2,1)S(1)} collective-permute-done((bf16[64,1536]{1,0:T(8,128)(2,1)S(1)}, bf16[64,1536]{1,0:T(8,128)(2,1)S(1)}, u32[]{:S(2)}, u32[]{:S(2)}) %collective-permute-start.16) | collective-permute-done | bytes 196640 | tf_op jit(solution)/shard_map/ppermute | solution.py:336
  54.8 2.2 %collective-permute-done.18.refs_2_ = bf16[64,1536]{1,0:T(8,128)(2,1)S(1)} collective-permute-done((bf16[64,1536]{1,0:T(8,128)(2,1)S(1)}, bf16[64,1536]{1,0:T(8,128)(2,1)S(1)}, u32[]{:S(2)}, u32[]{:S(2)}) %collective-permute-start.18) | collective-permute-done | bytes 196640 | tf_op jit(solution)/shard_map/ppermute | solution.py:336
  56.9 0.1 shard_map.87
  57.0 0.6 collective-permute-start.19
  57.6 1.0 %shard_map.88.refs_0_ = bf16[128,3072]{1,0:T(8,128)(2,1)} custom-call(f32[128,3072]{1,0:T(8,128)S(1)} %get-tuple-element.34.base_ref, bf16[128,160]{1,0:T(8,128)(2,1)S(1)} %get-tuple-element.35.table_ref, f32[32,1536]{1,0:T(8,128)S(1)} %get-tuple-element.52.rows_ref), custom_call_target="tpu_custom_call" | custom-call | flops 62914560 | bytes 1179648 | tf_op jit(solution)/shard_map/pallas_call | solution.py:288
  58.5 3.1 %collective-permute-done.19.rows_ref = bf16[32,1536]{1,0:T(8,128)(2,1)S(1)} collective-permute-done((bf16[32,1536]{1,0:T(8,128)(2,1)S(1)}, bf16[32,1536]{1,0:T(8,128)(2,1)S(1)}, u32[]{:S(2)}, u32[]{:S(2)}) %collective-permute-start.19) | collective-permute-done | bytes 98336 | tf_op jit(solution)/shard_map/ppermute | solution.py:336
  61.7 1.0 %shard_map.89 = bf16[128,3072]{1,0:T(8,128)(2,1)} custom-call(f32[128,3072]{1,0:T(8,128)S(1)} %get-tuple-element.34.base_ref, bf16[128,160]{1,0:T(8,128)(2,1)S(1)} %get-tuple-element.35.table_ref, bf16[32,1536]{1,0:T(8,128)(2,1)S(1)} %collective-permute-done.19.rows_ref, bf16[128,3072]{1,0:T(8,128)(2,1)} %shard_map.88.refs_0_), custom_call_target="tpu_custom_call", output_to_operand_aliasing={{}: (3, {})} | custom-call | flops 62914560 | bytes 1179648 | tf_op jit(solution)/shard_map/pallas_call | solution.py:288
  (17 shorter events, 0.1 us)
Async XLA Ops:
  0.0 4.7 %collective-permute-start = (s32[1,128,2]{1,2,0:T(2,128)}, s32[1,128,2]{1,2,0:T(2,128)S(1)}, u32[]{:S(2)}, u32[]{:S(2)}) collective-permute-start(s32[1,128,2]{1,2,0:T(2,128)} %param.12), channel_id=1, source_target_pairs={{0,16},{2,18},{4,20},{6,22},{8,24},{10,26},{12,28},{14,30},{16,0},... | collective-permute-start | bytes 3080 | tf_op jit(solution)/shard_map/ppermute | solution.py:336
  5.1 12.2 %collective-permute-start.2 = (bf16[32,3072]{1,0:T(8,128)(2,1)S(1)}, bf16[32,3072]{1,0:T(8,128)(2,1)S(1)}, u32[]{:S(2)}, u32[]{:S(2)}) collective-permute-start(bf16[32,3072]{1,0:T(8,128)(2,1)S(1)} %shard_map.74), channel_id=1, source_target_pairs={{0,24},{2,26},{4,28},{6,30},{8,16},{10,18},{12,20},{14,22},{16,8},... | collective-permute-start | bytes 589832 | tf_op jit(solution)/shard_map/ppermute | solution.py:336
  9.2 10.2 %collective-permute-start.1 = (bf16[32,3072]{1,0:T(8,128)(2,1)S(1)}, bf16[32,3072]{1,0:T(8,128)(2,1)S(1)}, u32[]{:S(2)}, u32[]{:S(2)}) collective-permute-start(bf16[32,3072]{1,0:T(8,128)(2,1)S(1)} %shard_map.74), channel_id=1, source_target_pairs={{0,18},{2,16},{4,22},{6,20},{8,26},{10,24},{12,30},{14,28},{16,2},... | collective-permute-start | bytes 589832 | tf_op jit(solution)/shard_map/ppermute | solution.py:336
  10.7 11.7 %collective-permute-start.10 = (bf16[96,1536]{1,0:T(8,128)(2,1)S(1)}, bf16[96,1536]{1,0:T(8,128)(2,1)S(1)}, u32[]{:S(2)}, u32[]{:S(2)}) collective-permute-start(bf16[96,1536]{1,0:T(8,128)(2,1)S(1)} %get-tuple-element.45), channel_id=1, source_target_pairs={{0,2},{2,0},{4,6},{6,4},{8,10},{10,8},{12,14},{14,12},{16,18},{18,... | collective-permute-start | bytes 884744 | tf_op jit(solution)/shard_map/ppermute | solution.py:336
  11.2 8.2 %copy-start.2 = (bf16[1,128,3072]{2,1,0:T(8,128)(2,1)S(1)}, bf16[1,128,3072]{2,1,0:T(8,128)(2,1)}, u32[]{:S(2)}) copy-start(bf16[1,128,3072]{2,1,0:T(8,128)(2,1)} %param.7) | copy-start | bytes 2359300
  17.2 9.0 %collective-permute-start.7 = (bf16[32,3072]{1,0:T(8,128)(2,1)S(1)}, bf16[32,3072]{1,0:T(8,128)(2,1)S(1)}, u32[]{:S(2)}, u32[]{:S(2)}) collective-permute-start(bf16[32,3072]{1,0:T(8,128)(2,1)S(1)} %collective-permute-done.2.near_ref), channel_id=1, source_target_pairs={{0,2},{2,0},{4,6},{6,4},{8,10},{10,8},{12,14},{14,12},{16,18},{18,... | collective-permute-start | bytes 589832 | tf_op jit(solution)/shard_map/ppermute | solution.py:336
  18.8 7.5 %collective-permute-start.6 = (bf16[32,3072]{1,0:T(8,128)(2,1)S(1)}, bf16[32,3072]{1,0:T(8,128)(2,1)S(1)}, u32[]{:S(2)}, u32[]{:S(2)}) collective-permute-start(bf16[32,3072]{1,0:T(8,128)(2,1)S(1)} %collective-permute-done.2.near_ref), channel_id=1, source_target_pairs={{0,4},{2,6},{4,0},{6,2},{8,12},{10,14},{12,8},{14,10},{16,20},{18,... | collective-permute-start | bytes 589832 | tf_op jit(solution)/shard_map/ppermute | solution.py:336
  19.4 23.7 %collective-permute-start.4 = (bf16[80,3072]{1,0:T(8,128)(2,1)S(1)}, bf16[80,3072]{1,0:T(8,128)(2,1)S(1)}, u32[]{:S(2)}, u32[]{:S(2)}) collective-permute-start(bf16[80,3072]{1,0:T(8,128)(2,1)S(1)} %slice_bitcast_fusion), channel_id=1, source_target_pairs={{0,16},{2,18},{4,20},{6,22},{8,24},{10,26},{12,28},{14,30},{16,0},... | collective-permute-start | bytes 1474568 | tf_op jit(solution)/shard_map/ppermute | solution.py:336
  20.3 13.6 %collective-permute-start.5 = (bf16[32,3072]{1,0:T(8,128)(2,1)S(1)}, bf16[32,3072]{1,0:T(8,128)(2,1)S(1)}, u32[]{:S(2)}, u32[]{:S(2)}) collective-permute-start(bf16[32,3072]{1,0:T(8,128)(2,1)S(1)} %shard_map.74), channel_id=1, source_target_pairs={{0,20},{2,22},{4,16},{6,18},{8,28},{10,30},{12,24},{14,26},{16,4},... | collective-permute-start | bytes 589832 | tf_op jit(solution)/shard_map/ppermute | solution.py:336
  22.4 11.0 %collective-permute-start.11 = (bf16[96,1536]{1,0:T(8,128)(2,1)S(1)}, bf16[96,1536]{1,0:T(8,128)(2,1)S(1)}, u32[]{:S(2)}, u32[]{:S(2)}) collective-permute-start(bf16[96,1536]{1,0:T(8,128)(2,1)S(1)} %collective-permute-done.10.own_ref), channel_id=1, source_target_pairs={{0,1},{1,0},{2,3},{3,2},{4,5},{5,4},{6,7},{7,6},{8,9},{9,8},{10,11... | collective-permute-start | bytes 884744 | tf_op jit(solution)/shard_map/ppermute | solution.py:358
  27.2 4.0 %collective-permute-start.8 = (bf16[64,192]{1,0:T(8,128)(2,1)S(1)}, bf16[64,192]{1,0:T(8,128)(2,1)S(1)}, u32[]{:S(2)}, u32[]{:S(2)}) collective-permute-start(bf16[64,192]{1,0:T(8,128)(2,1)S(1)} %shard_map.77.own_ref), channel_id=1, source_target_pairs={{0,2},{2,0},{4,6},{6,4},{8,10},{10,8},{12,14},{14,12},{16,18},{18,... | collective-permute-start | bytes 73736 | tf_op jit(solution)/shard_map/ppermute | solution.py:336
  27.8 5.7 %collective-permute-start.9 = (bf16[32,3072]{1,0:T(8,128)(2,1)S(1)}, bf16[32,3072]{1,0:T(8,128)(2,1)S(1)}, u32[]{:S(2)}, u32[]{:S(2)}) collective-permute-start(bf16[32,3072]{1,0:T(8,128)(2,1)S(1)} %collective-permute-done.7.far_ref), channel_id=1, source_target_pairs={{0,4},{2,6},{4,0},{6,2},{8,12},{10,14},{12,8},{14,10},{16,20},{18,... | collective-permute-start | bytes 589832 | tf_op jit(solution)/shard_map/ppermute | solution.py:336
  31.2 11.9 %collective-permute-start.3 = (bf16[48,3072]{1,0:T(8,128)(2,1)S(1)}, bf16[48,3072]{1,0:T(8,128)(2,1)S(1)}, u32[]{:S(2)}, u32[]{:S(2)}) collective-permute-start(bf16[48,3072]{1,0:T(8,128)(2,1)S(1)} %slice_bitcast_fusion.1), channel_id=1, source_target_pairs={{0,16},{2,18},{4,20},{6,22},{8,24},{10,26},{12,28},{14,30},{16,0},... | collective-permute-start | bytes 884744 | tf_op jit(solution)/shard_map/ppermute | solution.py:336
  33.9 6.1 %collective-permute-start.12 = (bf16[32,3072]{1,0:T(8,128)(2,1)S(1)}, bf16[32,3072]{1,0:T(8,128)(2,1)S(1)}, u32[]{:S(2)}, u32[]{:S(2)}) collective-permute-start(bf16[32,3072]{1,0:T(8,128)(2,1)S(1)} %collective-permute-done.5.near_ref), channel_id=1, source_target_pairs={{0,2},{2,0},{4,6},{6,4},{8,10},{10,8},{12,14},{14,12},{16,18},{18,... | collective-permute-start | bytes 589832 | tf_op jit(solution)/shard_map/ppermute | solution.py:336
  35.5 9.6 %collective-permute-start.14 = (bf16[64,1536]{1,0:T(8,128)(2,1)S(1)}, bf16[64,1536]{1,0:T(8,128)(2,1)S(1)}, u32[]{:S(2)}, u32[]{:S(2)}) collective-permute-start(bf16[64,1536]{1,0:T(8,128)(2,1)S(1)} %shard_map.79), channel_id=1, source_target_pairs={{0,8},{2,10},{4,12},{6,14},{8,0},{10,2},{12,4},{14,6},{16,24},{18,... | collective-permute-start | bytes 589832 | tf_op jit(solution)/shard_map/ppermute | solution.py:336
  38.8 4.0 %collective-permute-start.15 = (bf16[64,192]{1,0:T(8,128)(2,1)S(1)}, bf16[64,192]{1,0:T(8,128)(2,1)S(1)}, u32[]{:S(2)}, u32[]{:S(2)}) collective-permute-start(bf16[64,192]{1,0:T(8,128)(2,1)S(1)} %shard_map.80.own_ref), channel_id=1, source_target_pairs={{0,2},{2,0},{4,6},{6,4},{8,10},{10,8},{12,14},{14,12},{16,18},{18,... | collective-permute-start | bytes 73736 | tf_op jit(solution)/shard_map/ppermute | solution.py:336
  41.0 2.1 %copy-start = (s32[1,128,2]{1,2,0:T(2,128)S(1)}, s32[1,128,2]{1,2,0:T(2,128)}, u32[]{:S(2)}) copy-start(s32[1,128,2]{1,2,0:T(2,128)} %param.12) | copy-start | bytes 3076
  41.0 2.1 %copy-start.1 = (f32[1,128,2]{1,2,0:T(2,128)S(1)}, f32[1,128,2]{1,2,0:T(2,128)}, u32[]{:S(2)}) copy-start(f32[1,128,2]{1,2,0:T(2,128)} %param.13) | copy-start | bytes 3076
  41.0 7.6 %collective-permute-start.17 = (bf16[64,192]{1,0:T(8,128)(2,1)S(1)}, bf16[64,192]{1,0:T(8,128)(2,1)S(1)}, u32[]{:S(2)}, u32[]{:S(2)}) collective-permute-start(bf16[64,192]{1,0:T(8,128)(2,1)S(1)} %shard_map.81.own_ref), channel_id=1, source_target_pairs={{0,2},{2,0},{4,6},{6,4},{8,10},{10,8},{12,14},{14,12},{16,18},{18,... | collective-permute-start | bytes 73736 | tf_op jit(solution)/shard_map/ppermute | solution.py:336
  45.2 9.6 %collective-permute-start.16 = (bf16[64,1536]{1,0:T(8,128)(2,1)S(1)}, bf16[64,1536]{1,0:T(8,128)(2,1)S(1)}, u32[]{:S(2)}, u32[]{:S(2)}) collective-permute-start(bf16[64,1536]{1,0:T(8,128)(2,1)S(1)} %shard_map.85), channel_id=1, source_target_pairs={{0,12},{2,14},{4,8},{6,10},{8,4},{10,6},{12,0},{14,2},{16,28},{18,... | collective-permute-start | bytes 589832 | tf_op jit(solution)/shard_map/ppermute | solution.py:336
  49.0 8.0 %collective-permute-start.18 = (bf16[64,1536]{1,0:T(8,128)(2,1)S(1)}, bf16[64,1536]{1,0:T(8,128)(2,1)S(1)}, u32[]{:S(2)}, u32[]{:S(2)}) collective-permute-start(bf16[64,1536]{1,0:T(8,128)(2,1)S(1)} %shard_map.86), channel_id=1, source_target_pairs={{0,4},{2,6},{4,0},{6,2},{8,12},{10,14},{12,8},{14,10},{16,20},{18,... | collective-permute-start | bytes 589832 | tf_op jit(solution)/shard_map/ppermute | solution.py:336
  49.0 4.0 %collective-permute-start.13 = (bf16[64,192]{1,0:T(8,128)(2,1)S(1)}, bf16[64,192]{1,0:T(8,128)(2,1)S(1)}, u32[]{:S(2)}, u32[]{:S(2)}) collective-permute-start(bf16[64,192]{1,0:T(8,128)(2,1)S(1)} %shard_map.82.own_ref), channel_id=1, source_target_pairs={{0,2},{2,0},{4,6},{6,4},{8,10},{10,8},{12,14},{14,12},{16,18},{18,... | collective-permute-start | bytes 73736 | tf_op jit(solution)/shard_map/ppermute | solution.py:336
  57.0 4.7 %collective-permute-start.19 = (bf16[32,1536]{1,0:T(8,128)(2,1)S(1)}, bf16[32,1536]{1,0:T(8,128)(2,1)S(1)}, u32[]{:S(2)}, u32[]{:S(2)}) collective-permute-start(bf16[32,1536]{1,0:T(8,128)(2,1)S(1)} %get-tuple-element.51), channel_id=1, source_target_pairs={{0,2},{2,0},{4,6},{6,4},{8,10},{10,8},{12,14},{14,12},{16,18},{18,... | collective-permute-start | bytes 294920 | tf_op jit(solution)/shard_map/ppermute | solution.py:336

commit v11 on v10

--- a/solution.py
+++ b/solution.py
@@ -107,24 +107,31 @@
     return jnp.where(rank == slot, hit, 0.0)
 
 
-def pick_kernel(experts, ids_ref, block_ref, out_ref):
+def pick_kernel(experts, ids_ref, *refs):
+    block_refs, out_ref = refs[:-1], refs[-1]
     for e in range(experts):
-        table = slot_rows(ids_ref[...], e).astype(jnp.bfloat16)
-        rows = jnp.dot(table, block_ref[...], preferred_element_type=jnp.float32)
+        table = slot_rows(ids_ref[...], e)
+        start, rows = 0, 0.0
+        for ref in block_refs:
+            end = start + ref.shape[0]
+            part = table[:, start:end].astype(jnp.bfloat16)
+            rows += jnp.dot(part, ref[...], preferred_element_type=jnp.float32)
+            start = end
         out_ref[e * CAP:(e + 1) * CAP, :] = rows.astype(jnp.bfloat16)
 
 
-def picked_rows(experts, ids_t, block):
+def picked_rows(experts, ids_t, *blocks):
+    width, size = blocks[0].shape[1], sum(block.size for block in blocks)
     return pl.pallas_call(
         functools.partial(pick_kernel, experts),
-        out_shape=jax.ShapeDtypeStruct((experts * CAP, block.shape[1]), jnp.bfloat16),
-        in_specs=[VMEM, VMEM],
+        out_shape=jax.ShapeDtypeStruct((experts * CAP, width), jnp.bfloat16),
+        in_specs=[VMEM] * (1 + len(blocks)),
         out_specs=VMEM,
         compiler_params=PARAMS,
         cost_estimate=pl.CostEstimate(
-            flops=2 * experts * CAP * block.size, bytes_accessed=block.size, transcendentals=0
-        ),
-    )(ids_t, block)
+            flops=2 * experts * CAP * size, bytes_accessed=size, transcendentals=0
+        ),
+    )(ids_t, *blocks)
 
 
 def hidden_kernel(near_ref, far_ref, gain_ref, gate_ref, up_ref, out_ref):
@@ -209,7 +216,7 @@
 
 
 def base_kernel(experts, gain_ref, ids_ref, weights_ref, *refs):
-    block_refs, (out_ref, table_ref, pick_ref) = refs[:-3], refs[-3:]
+    block_refs, (out_ref, table_ref) = refs[:-2], refs[-2:]
     ids, weights = ids_ref[...], weights_ref[...]
     count = ids.shape[1]
     zero = jnp.sum(jnp.where(ids >= experts, weights, 0.0), axis=0, keepdims=True)
@@ -228,15 +235,7 @@
     tables = []
     for e in range(experts):
         weight = jnp.sum(jnp.where(ids == e, weights, 0.0), axis=0, keepdims=True)
-        slots = slot_rows(ids, e)
-        tables.append(slots * weight)
-        start, total = 0, 0.0
-        for ref in block_refs:
-            end = start + ref.shape[0]
-            part = slots[:, start:end].astype(jnp.bfloat16)
-            total += jnp.dot(part, ref[...], preferred_element_type=jnp.float32)
-            start = end
-        pick_ref[e * CAP:(e + 1) * CAP, :] = total.astype(jnp.bfloat16)
+        tables.append(slot_rows(ids, e) * weight)
     terms = parts_of(jnp.concatenate(tables, axis=0).T)
     table_ref[...] = jnp.concatenate(terms + terms[:2], axis=1)
 
@@ -248,10 +247,9 @@
         out_shape=(
             jax.ShapeDtypeStruct((count, width), jnp.float32),
             jax.ShapeDtypeStruct((count, 5 * experts * CAP), jnp.bfloat16),
-            jax.ShapeDtypeStruct((experts * CAP, width), jnp.bfloat16),
         ),
         in_specs=[VMEM] * (3 + len(blocks)),
-        out_specs=(VMEM, VMEM, VMEM),
+        out_specs=(VMEM, VMEM),
         compiler_params=PARAMS,
         cost_estimate=pl.CostEstimate(
             flops=8 * count * width, bytes_accessed=6 * count * width, transcendentals=0
@@ -369,17 +367,16 @@
         moved(after(piece, far[0], near[2]), 1, 0)
         for piece in jnp.split(blocks[0], cuts)
     ]
-    base, table, near[0] = based(
-        experts, arrived, gain, jnp.swapaxes(route_ids[0], 0, 1),
-        jnp.swapaxes(route_weights[0], 0, 1),
-    )
+    ids_t = jnp.swapaxes(route_ids[0], 0, 1)
+    near[0] = picked_rows(experts, ids_t, *arrived)
+    base, table = based(experts, arrived, gain, ids_t, jnp.swapaxes(route_weights[0], 0, 1))
 
     if experts > 1:
         near[0] = exchanged(near[0])
     hidden, part, back = {}, {}, {}
     for k in (2, 3, 1, 0):
         first = {
-            2: (near[3],), 3: (part.get(2),), 1: (hidden.get(3),), 0: (hidden.get(1),)
+            2: (near[3],), 3: (part.get(2), arrived[0]), 1: (hidden.get(3),), 0: (hidden.get(1), back.get(2))
         }[k]
         if k == 3:
             far[1] = moved(after(near[1], part[2]), 0, 0, 1)
@@ -388,10 +385,7 @@
         if k == 2:
             crossed = after(crossed, far[3])
         part[k] = down_of(hidden[k], crossed, own_down, other_down)
-    back[2] = moved(part[2], 0, 2)
-    back[3] = moved(after(part[3], back[2], hidden[0]), 0, 3)
-    back[1] = moved(part[1], 0, 1)
-    back[0] = part[0]
+        back[k] = moved(part[k], 0, k) if k else part[k]
     early = summed_early(back[0], back[2])
     own, others = joined([early, back[3], back[1]])
     others = moved(others, 0, 0, 1)

time: 62.8 us -> 59.7 us (0.951)
  waiting for transfers between devices: 22 us -> 18.5 us
    ppermute x19, waiting for transfers between devices: 22 us -> 18.5 us  [moved(): return lax.ppermute(value, ('section', 'expert'), pairs)]
  transfers between devices with their start and end apart: 20 -> 20, of which waited for: 12 -> 10; matrix products, arithmetic and copies ran while one was open for 0% -> 0% of each run, Pallas kernels for 17% -> 18%
where the time goes in v11:
time: 59.7 us; the launch traced here: 59.6 us
  starting transfers between devices  28.8 us (48%)
  waiting for transfers between devices  18.5 us (31%)
  Pallas kernels  11.9 us (20%)
    ppermute x19, starting transfers between devices, moved(): return lax.ppermute(value, ('section', 'expert'), pairs)  28.8 us
    ppermute x19, waiting for transfers between devices, moved(): return lax.ppermute(value, ('section', 'expert'), pairs)  18.5 us
    pallas_call x4, Pallas kernels, hidden_of(): pl.pallas_call(hidden_kernel, out_shape=jax.ShapeDtypeStruct((rows, hidde...  3.85 us
    pallas_call x2, Pallas kernels, loaded(): pl.pallas_call(functools.partial(load_kernel, kinds), out_shape=tuple((ja...  3.13 us
    pallas_call x2, Pallas kernels, ended(): pl.pallas_call(functools.partial(end_kernel, steps, which), out_shape=jax...  1.91 us
    pallas_call x4, Pallas kernels, down_of(): pl.pallas_call(down_kernel, out_shape=jax.ShapeDtypeStruct((rows, half),...  1.3 us
  transfers between devices with their start and end apart: 20, of which 10 were waited for; matrix products, arithmetic and copies ran while one was open for 0% of the time, Pallas kernels for 18%

profile of v11, /device:TPU:0, one launch (start us, length us, event | category | flops | bytes accessed | tf_op | source)
XLA Modules:
  0.0 59.6 jit_solution(8411782731241196427)
XLA Ops:
  0.0 2.9 %collective-permute-start = (s32[1,128,2]{1,2,0:T(2,128)}, s32[1,128,2]{1,2,0:T(2,128)S(1)}, u32[]{:S(2)}, u32[]{:S(2)}) collective-permute-start(s32[1,128,2]{1,2,0:T(2,128)} %param.12), channel_id=1, source_target_pairs={{0,16},{2,18},{4,20},{6,22},{8,24},{10,26},{12,28},{14,30},{16,0},... | collective-permute-start | bytes 3080 | tf_op jit(solution)/shard_map/ppermute | solution.py:334
  2.9 1.2 %shard_map.73 = (bf16[128,3072]{1,0:T(8,128)(2,1)S(1)}, bf16[96,1536]{1,0:T(8,128)(2,1)S(1)}) custom-call(bf16[128,3072]{1,0:T(8,128)(2,1)} %bitcast.28, bf16[192,3072]{1,0:T(8,128)(2,1)} %bitcast.26), custom_call_target="tpu_custom_call" | custom-call | bytes 2162688 | tf_op jit(solution)/shard_map/pallas_call | solution.py:58
  4.2 0.5 collective-permute-done
  4.7 0.4 shard_map.74
  5.1 4.1 %collective-permute-start.2 = (bf16[32,3072]{1,0:T(8,128)(2,1)S(1)}, bf16[32,3072]{1,0:T(8,128)(2,1)S(1)}, u32[]{:S(2)}, u32[]{:S(2)}) collective-permute-start(bf16[32,3072]{1,0:T(8,128)(2,1)S(1)} %shard_map.74), channel_id=1, source_target_pairs={{0,24},{2,26},{4,28},{6,30},{8,16},{10,18},{12,20},{14,22},{16,8},... | collective-permute-start | bytes 589832 | tf_op jit(solution)/shard_map/ppermute | solution.py:334
  9.2 1.5 %collective-permute-start.1 = (bf16[32,3072]{1,0:T(8,128)(2,1)S(1)}, bf16[32,3072]{1,0:T(8,128)(2,1)S(1)}, u32[]{:S(2)}, u32[]{:S(2)}) collective-permute-start(bf16[32,3072]{1,0:T(8,128)(2,1)S(1)} %shard_map.74), channel_id=1, source_target_pairs={{0,18},{2,16},{4,22},{6,20},{8,26},{10,24},{12,30},{14,28},{16,2},... | collective-permute-start | bytes 589832 | tf_op jit(solution)/shard_map/ppermute | solution.py:334
  10.7 0.5 collective-permute-start.10
  11.2 1.9 %shard_map.75 = (bf16[192,1536]{1,0:T(8,128)(2,1)S(1)}, bf16[192,3072]{1,0:T(8,128)(2,1)S(1)}, bf16[192,3072]{1,0:T(8,128)(2,1)S(1)}, bf16[1,3072]{1,0:T(2,128)(2,1)S(1)}) custom-call(bf16[192,3072]{1,0:T(8,128)(2,1)} %bitcast.27, bf16[192,3072]{1,0:T(8,128)(2,1)} %bitcast.29, bf16[192,3072]{1,0:T(8,128)(2,1)} %bitcast.30, bf16[1,3072]{1,0:T(2,128)(2,1)} %refs_3_.1), custom_call_target="tpu_custom_call" | custom-call | bytes 5910528 | tf_op jit(solution)/shard_map/pallas_call | solution.py:58
  13.1 4.1 %collective-permute-done.2.near_ref = bf16[32,3072]{1,0:T(8,128)(2,1)S(1)} collective-permute-done((bf16[32,3072]{1,0:T(8,128)(2,1)S(1)}, bf16[32,3072]{1,0:T(8,128)(2,1)S(1)}, u32[]{:S(2)}, u32[]{:S(2)}) %collective-permute-start.2) | collective-permute-done | bytes 196640 | tf_op jit(solution)/shard_map/ppermute | solution.py:334
  17.2 1.5 %collective-permute-start.7 = (bf16[32,3072]{1,0:T(8,128)(2,1)S(1)}, bf16[32,3072]{1,0:T(8,128)(2,1)S(1)}, u32[]{:S(2)}, u32[]{:S(2)}) collective-permute-start(bf16[32,3072]{1,0:T(8,128)(2,1)S(1)} %collective-permute-done.2.near_ref), channel_id=1, source_target_pairs={{0,2},{2,0},{4,6},{6,4},{8,10},{10,8},{12,14},{14,12},{16,18},{18,... | collective-permute-start | bytes 589832 | tf_op jit(solution)/shard_map/ppermute | solution.py:334
  18.8 0.6 %collective-permute-start.6 = (bf16[32,3072]{1,0:T(8,128)(2,1)S(1)}, bf16[32,3072]{1,0:T(8,128)(2,1)S(1)}, u32[]{:S(2)}, u32[]{:S(2)}) collective-permute-start(bf16[32,3072]{1,0:T(8,128)(2,1)S(1)} %collective-permute-done.2.near_ref), channel_id=1, source_target_pairs={{0,4},{2,6},{4,0},{6,2},{8,12},{10,14},{12,8},{14,10},{16,20},{18,... | collective-permute-start | bytes 589832 | tf_op jit(solution)/shard_map/ppermute | solution.py:334
  19.4 2.3 %collective-permute-start.5 = (bf16[32,3072]{1,0:T(8,128)(2,1)S(1)}, bf16[32,3072]{1,0:T(8,128)(2,1)S(1)}, u32[]{:S(2)}, u32[]{:S(2)}) collective-permute-start(bf16[32,3072]{1,0:T(8,128)(2,1)S(1)} %shard_map.74), channel_id=1, source_target_pairs={{0,20},{2,22},{4,16},{6,18},{8,28},{10,30},{12,24},{14,26},{16,4},... | collective-permute-start | bytes 589832 | tf_op jit(solution)/shard_map/ppermute | solution.py:334
  21.7 0.6 %collective-permute-start.3 = (bf16[48,3072]{1,0:T(8,128)(2,1)S(1)}, bf16[48,3072]{1,0:T(8,128)(2,1)S(1)}, u32[]{:S(2)}, u32[]{:S(2)}) collective-permute-start(bf16[48,3072]{1,0:T(8,128)(2,1)S(1)} %slice_bitcast_fusion.1), channel_id=1, source_target_pairs={{0,16},{2,18},{4,20},{6,22},{8,24},{10,26},{12,28},{14,30},{16,0},... | collective-permute-start | bytes 884744 | tf_op jit(solution)/shard_map/ppermute | solution.py:334
  22.4 3.9 %collective-permute-done.6.near_ref = bf16[32,3072]{1,0:T(8,128)(2,1)S(1)} collective-permute-done((bf16[32,3072]{1,0:T(8,128)(2,1)S(1)}, bf16[32,3072]{1,0:T(8,128)(2,1)S(1)}, u32[]{:S(2)}, u32[]{:S(2)}) %collective-permute-start.6) | collective-permute-done | bytes 196640 | tf_op jit(solution)/shard_map/ppermute | solution.py:334
  26.2 1.0 %shard_map.78.own_ref = bf16[64,192]{1,0:T(8,128)(2,1)S(1)} custom-call(bf16[32,3072]{1,0:T(8,128)(2,1)S(1)} %collective-permute-done.2.near_ref, bf16[32,3072]{1,0:T(8,128)(2,1)S(1)} %collective-permute-done.7.far_ref, bf16[1,3072]{1,0:T(2,128)(2,1)S(1)} %get-tuple-element.29.gain_ref, bf16[192,3072]{1,0:T(8,128)(2,1)S(1)} %get-tuple-element.37.gate_ref, ...), custom_call_target="tpu_custom_call" | custom-call | flops 150994944 | bytes 2359296 | tf_op jit(solution)/shard_map/pallas_call | solution.py:149
  27.2 0.5 collective-permute-start.8
  27.8 1.5 %collective-permute-start.9 = (bf16[32,3072]{1,0:T(8,128)(2,1)S(1)}, bf16[32,3072]{1,0:T(8,128)(2,1)S(1)}, u32[]{:S(2)}, u32[]{:S(2)}) collective-permute-start(bf16[32,3072]{1,0:T(8,128)(2,1)S(1)} %collective-permute-done.7.far_ref), channel_id=1, source_target_pairs={{0,4},{2,6},{4,0},{6,2},{8,12},{10,14},{12,8},{14,10},{16,20},{18,... | collective-permute-start | bytes 589832 | tf_op jit(solution)/shard_map/ppermute | solution.py:334
  29.3 1.9 %collective-permute-done.8.other_ref = bf16[64,192]{1,0:T(8,128)(2,1)S(1)} collective-permute-done((bf16[64,192]{1,0:T(8,128)(2,1)S(1)}, bf16[64,192]{1,0:T(8,128)(2,1)S(1)}, u32[]{:S(2)}, u32[]{:S(2)}) %collective-permute-start.8) | collective-permute-done | bytes 24608 | tf_op jit(solution)/shard_map/ppermute | solution.py:334
  31.2 1.5 %collective-permute-start.4 = (bf16[80,3072]{1,0:T(8,128)(2,1)S(1)}, bf16[80,3072]{1,0:T(8,128)(2,1)S(1)}, u32[]{:S(2)}, u32[]{:S(2)}) collective-permute-start(bf16[80,3072]{1,0:T(8,128)(2,1)S(1)} %slice_bitcast_fusion), channel_id=1, source_target_pairs={{0,16},{2,18},{4,20},{6,22},{8,24},{10,26},{12,28},{14,30},{16,0},... | collective-permute-start | bytes 1474568 | tf_op jit(solution)/shard_map/ppermute | solution.py:334
  32.7 0.7 %collective-permute-done.9.far_ref = bf16[32,3072]{1,0:T(8,128)(2,1)S(1)} collective-permute-done((bf16[32,3072]{1,0:T(8,128)(2,1)S(1)}, bf16[32,3072]{1,0:T(8,128)(2,1)S(1)}, u32[]{:S(2)}, u32[]{:S(2)}) %collective-permute-start.9) | collective-permute-done | bytes 196640 | tf_op jit(solution)/shard_map/ppermute | solution.py:334
  33.4 0.1 shard_map.79.other_down_ref
  33.6 0.3 shard_map.80
  33.9 1.6 %collective-permute-start.12 = (bf16[32,3072]{1,0:T(8,128)(2,1)S(1)}, bf16[32,3072]{1,0:T(8,128)(2,1)S(1)}, u32[]{:S(2)}, u32[]{:S(2)}) collective-permute-start(bf16[32,3072]{1,0:T(8,128)(2,1)S(1)} %collective-permute-done.5.near_ref), channel_id=1, source_target_pairs={{0,2},{2,0},{4,6},{6,4},{8,10},{10,8},{12,14},{14,12},{16,18},{18,... | collective-permute-start | bytes 589832 | tf_op jit(solution)/shard_map/ppermute | solution.py:334
  35.5 2.3 %collective-permute-start.13 = (bf16[64,1536]{1,0:T(8,128)(2,1)S(1)}, bf16[64,1536]{1,0:T(8,128)(2,1)S(1)}, u32[]{:S(2)}, u32[]{:S(2)}) collective-permute-start(bf16[64,1536]{1,0:T(8,128)(2,1)S(1)} %shard_map.80), channel_id=1, source_target_pairs={{0,8},{2,10},{4,12},{6,14},{8,0},{10,2},{12,4},{14,6},{16,24},{18,... | collective-permute-start | bytes 589832 | tf_op jit(solution)/shard_map/ppermute | solution.py:334
  37.8 1.0 %shard_map.81.own_ref = bf16[64,192]{1,0:T(8,128)(2,1)S(1)} custom-call(bf16[32,3072]{1,0:T(8,128)(2,1)S(1)} %collective-permute-done.6.near_ref, bf16[32,3072]{1,0:T(8,128)(2,1)S(1)} %collective-permute-done.9.far_ref, bf16[1,3072]{1,0:T(2,128)(2,1)S(1)} %get-tuple-element.29.gain_ref, bf16[192,3072]{1,0:T(8,128)(2,1)S(1)} %get-tuple-element.37.gate_ref, ...), custom_call_target="tpu_custom_call" | custom-call | flops 150994944 | bytes 2359296 | tf_op jit(solution)/shard_map/pallas_call | solution.py:149
  38.8 0.8 %collective-permute-start.15 = (bf16[64,192]{1,0:T(8,128)(2,1)S(1)}, bf16[64,192]{1,0:T(8,128)(2,1)S(1)}, u32[]{:S(2)}, u32[]{:S(2)}) collective-permute-start(bf16[64,192]{1,0:T(8,128)(2,1)S(1)} %shard_map.81.own_ref), channel_id=1, source_target_pairs={{0,2},{2,0},{4,6},{6,4},{8,10},{10,8},{12,14},{14,12},{16,18},{18,... | collective-permute-start | bytes 73736 | tf_op jit(solution)/shard_map/ppermute | solution.py:334
  39.5 0.5 collective-permute-done.12.far_ref
  40.0 1.0 %shard_map.82.own_ref = bf16[64,192]{1,0:T(8,128)(2,1)S(1)} custom-call(bf16[32,3072]{1,0:T(8,128)(2,1)S(1)} %collective-permute-done.5.near_ref, bf16[32,3072]{1,0:T(8,128)(2,1)S(1)} %collective-permute-done.12.far_ref, bf16[1,3072]{1,0:T(2,128)(2,1)S(1)} %get-tuple-element.29.gain_ref, bf16[192,3072]{1,0:T(8,128)(2,1)S(1)} %get-tuple-element.37.gate_ref, ...), custom_call_target="tpu_custom_call" | custom-call | flops 150994944 | bytes 2359296 | tf_op jit(solution)/shard_map/pallas_call | solution.py:149
  41.0 0.0 copy-start
  41.0 1.6 %collective-permute-start.17 = (bf16[64,192]{1,0:T(8,128)(2,1)S(1)}, bf16[64,192]{1,0:T(8,128)(2,1)S(1)}, u32[]{:S(2)}, u32[]{:S(2)}) collective-permute-start(bf16[64,192]{1,0:T(8,128)(2,1)S(1)} %shard_map.82.own_ref), channel_id=1, source_target_pairs={{0,2},{2,0},{4,6},{6,4},{8,10},{10,8},{12,14},{14,12},{16,18},{18,... | collective-permute-start | bytes 73736 | tf_op jit(solution)/shard_map/ppermute | solution.py:334
  42.6 0.2 collective-permute-done.15.other_ref
  42.8 0.3 shard_map.86
  43.1 3.5 %collective-permute-start.16 = (bf16[64,1536]{1,0:T(8,128)(2,1)S(1)}, bf16[64,1536]{1,0:T(8,128)(2,1)S(1)}, u32[]{:S(2)}, u32[]{:S(2)}) collective-permute-start(bf16[64,1536]{1,0:T(8,128)(2,1)S(1)} %shard_map.86), channel_id=1, source_target_pairs={{0,12},{2,14},{4,8},{6,10},{8,4},{10,6},{12,0},{14,2},{16,28},{18,... | collective-permute-start | bytes 589832 | tf_op jit(solution)/shard_map/ppermute | solution.py:334
  46.7 0.3 shard_map.87
  47.0 0.1 collective-permute-start.18
  47.1 0.5 shard_map.77.near_ref
  47.6 0.9 %collective-permute-done.13.right_ref = bf16[64,1536]{1,0:T(8,128)(2,1)S(1)} collective-permute-done((bf16[64,1536]{1,0:T(8,128)(2,1)S(1)}, bf16[64,1536]{1,0:T(8,128)(2,1)S(1)}, u32[]{:S(2)}, u32[]{:S(2)}) %collective-permute-start.13) | collective-permute-done | bytes 196640 | tf_op jit(solution)/shard_map/ppermute | solution.py:334
  48.5 1.0 %shard_map.83.own_ref = bf16[64,192]{1,0:T(8,128)(2,1)S(1)} custom-call(bf16[32,3072]{1,0:T(8,128)(2,1)S(1)} %shard_map.77.near_ref, bf16[32,3072]{1,0:T(8,128)(2,1)S(1)} %collective-permute-done.1.far_ref, bf16[1,3072]{1,0:T(2,128)(2,1)S(1)} %get-tuple-element.29.gain_ref, bf16[192,3072]{1,0:T(8,128)(2,1)S(1)} %get-tuple-element.37.gate_ref, ...), custom_call_target="tpu_custom_call" | custom-call | flops 150994944 | bytes 2359296 | tf_op jit(solution)/shard_map/pallas_call | solution.py:149
  49.5 0.0 copy-start.1
  49.5 0.6 %collective-permute-start.14 = (bf16[64,192]{1,0:T(8,128)(2,1)S(1)}, bf16[64,192]{1,0:T(8,128)(2,1)S(1)}, u32[]{:S(2)}, u32[]{:S(2)}) collective-permute-start(bf16[64,192]{1,0:T(8,128)(2,1)S(1)} %shard_map.83.own_ref), channel_id=1, source_target_pairs={{0,2},{2,0},{4,6},{6,4},{8,10},{10,8},{12,14},{14,12},{16,18},{18,... | collective-permute-start | bytes 73736 | tf_op jit(solution)/shard_map/ppermute | solution.py:334
  50.1 3.3 %collective-permute-done.14.other_ref = bf16[64,192]{1,0:T(8,128)(2,1)S(1)} collective-permute-done((bf16[64,192]{1,0:T(8,128)(2,1)S(1)}, bf16[64,192]{1,0:T(8,128)(2,1)S(1)}, u32[]{:S(2)}, u32[]{:S(2)}) %collective-permute-start.14) | collective-permute-done | bytes 24608 | tf_op jit(solution)/shard_map/ppermute | solution.py:334
  53.5 0.3 shard_map.84.left_ref
  53.9 0.1 shard_map.88
  53.9 0.6 %collective-permute-start.19 = (bf16[32,1536]{1,0:T(8,128)(2,1)S(1)}, bf16[32,1536]{1,0:T(8,128)(2,1)S(1)}, u32[]{:S(2)}, u32[]{:S(2)}) collective-permute-start(bf16[32,1536]{1,0:T(8,128)(2,1)S(1)} %get-tuple-element.47), channel_id=1, source_target_pairs={{0,2},{2,0},{4,6},{6,4},{8,10},{10,8},{12,14},{14,12},{16,18},{18,... | collective-permute-start | bytes 294920 | tf_op jit(solution)/shard_map/ppermute | solution.py:334
  54.6 0.7 %shard_map.76 = (f32[128,3072]{1,0:T(8,128)S(1)}, bf16[128,160]{1,0:T(8,128)(2,1)S(1)}) custom-call(bf16[1,3072]{1,0:T(2,128)(2,1)S(1)} %get-tuple-element.29.gain_ref, s32[2,128]{1,0:T(2,128)S(1)} %bitcast.23, f32[2,128]{1,0:T(2,128)S(1)} %bitcast.24, bf16[48,3072]{1,0:T(8,128)(2,1)S(1)} %collective-permute-done.3.refs_0_, ...), custom_call_target="tpu_custom_call" | custom-call | flops 3145728 | bytes 2359296 | tf_op jit(solution)/shard_map/pallas_call | solution.py:245
  55.2 1.0 %shard_map.89.refs_0_ = bf16[128,3072]{1,0:T(8,128)(2,1)} custom-call(f32[128,3072]{1,0:T(8,128)S(1)} %get-tuple-element.32.base_ref, bf16[128,160]{1,0:T(8,128)(2,1)S(1)} %get-tuple-element.33.table_ref, f32[32,1536]{1,0:T(8,128)S(1)} %get-tuple-element.48.rows_ref), custom_call_target="tpu_custom_call" | custom-call | flops 62914560 | bytes 1179648 | tf_op jit(solution)/shard_map/pallas_call | solution.py:286
  56.2 2.4 %collective-permute-done.19.rows_ref = bf16[32,1536]{1,0:T(8,128)(2,1)S(1)} collective-permute-done((bf16[32,1536]{1,0:T(8,128)(2,1)S(1)}, bf16[32,1536]{1,0:T(8,128)(2,1)S(1)}, u32[]{:S(2)}, u32[]{:S(2)}) %collective-permute-start.19) | collective-permute-done | bytes 98336 | tf_op jit(solution)/shard_map/ppermute | solution.py:334
  58.6 1.0 %shard_map.90 = bf16[128,3072]{1,0:T(8,128)(2,1)} custom-call(f32[128,3072]{1,0:T(8,128)S(1)} %get-tuple-element.32.base_ref, bf16[128,160]{1,0:T(8,128)(2,1)S(1)} %get-tuple-element.33.table_ref, bf16[32,1536]{1,0:T(8,128)(2,1)S(1)} %collective-permute-done.19.rows_ref, bf16[128,3072]{1,0:T(8,128)(2,1)} %shard_map.89.refs_0_), custom_call_target="tpu_custom_call", output_to_operand_aliasing={{}: (3, {})} | custom-call | flops 62914560 | bytes 1179648 | tf_op jit(solution)/shard_map/pallas_call | solution.py:286
  (18 shorter events, 0.1 us)
Async XLA Ops:
  0.0 4.7 %collective-permute-start = (s32[1,128,2]{1,2,0:T(2,128)}, s32[1,128,2]{1,2,0:T(2,128)S(1)}, u32[]{:S(2)}, u32[]{:S(2)}) collective-permute-start(s32[1,128,2]{1,2,0:T(2,128)} %param.12), channel_id=1, source_target_pairs={{0,16},{2,18},{4,20},{6,22},{8,24},{10,26},{12,28},{14,30},{16,0},... | collective-permute-start | bytes 3080 | tf_op jit(solution)/shard_map/ppermute | solution.py:334
  5.1 12.2 %collective-permute-start.2 = (bf16[32,3072]{1,0:T(8,128)(2,1)S(1)}, bf16[32,3072]{1,0:T(8,128)(2,1)S(1)}, u32[]{:S(2)}, u32[]{:S(2)}) collective-permute-start(bf16[32,3072]{1,0:T(8,128)(2,1)S(1)} %shard_map.74), channel_id=1, source_target_pairs={{0,24},{2,26},{4,28},{6,30},{8,16},{10,18},{12,20},{14,22},{16,8},... | collective-permute-start | bytes 589832 | tf_op jit(solution)/shard_map/ppermute | solution.py:334
  9.2 12.6 %collective-permute-start.1 = (bf16[32,3072]{1,0:T(8,128)(2,1)S(1)}, bf16[32,3072]{1,0:T(8,128)(2,1)S(1)}, u32[]{:S(2)}, u32[]{:S(2)}) collective-permute-start(bf16[32,3072]{1,0:T(8,128)(2,1)S(1)} %shard_map.74), channel_id=1, source_target_pairs={{0,18},{2,16},{4,22},{6,20},{8,26},{10,24},{12,30},{14,28},{16,2},... | collective-permute-start | bytes 589832 | tf_op jit(solution)/shard_map/ppermute | solution.py:334
  10.7 11.7 %collective-permute-start.10 = (bf16[96,1536]{1,0:T(8,128)(2,1)S(1)}, bf16[96,1536]{1,0:T(8,128)(2,1)S(1)}, u32[]{:S(2)}, u32[]{:S(2)}) collective-permute-start(bf16[96,1536]{1,0:T(8,128)(2,1)S(1)} %get-tuple-element.42), channel_id=1, source_target_pairs={{0,2},{2,0},{4,6},{6,4},{8,10},{10,8},{12,14},{14,12},{16,18},{18,... | collective-permute-start | bytes 884744 | tf_op jit(solution)/shard_map/ppermute | solution.py:334
  11.2 8.2 %copy-start.2 = (bf16[1,128,3072]{2,1,0:T(8,128)(2,1)S(1)}, bf16[1,128,3072]{2,1,0:T(8,128)(2,1)}, u32[]{:S(2)}) copy-start(bf16[1,128,3072]{2,1,0:T(8,128)(2,1)} %param.7) | copy-start | bytes 2359300
  17.2 9.0 %collective-permute-start.7 = (bf16[32,3072]{1,0:T(8,128)(2,1)S(1)}, bf16[32,3072]{1,0:T(8,128)(2,1)S(1)}, u32[]{:S(2)}, u32[]{:S(2)}) collective-permute-start(bf16[32,3072]{1,0:T(8,128)(2,1)S(1)} %collective-permute-done.2.near_ref), channel_id=1, source_target_pairs={{0,2},{2,0},{4,6},{6,4},{8,10},{10,8},{12,14},{14,12},{16,18},{18,... | collective-permute-start | bytes 589832 | tf_op jit(solution)/shard_map/ppermute | solution.py:334
  18.8 7.5 %collective-permute-start.6 = (bf16[32,3072]{1,0:T(8,128)(2,1)S(1)}, bf16[32,3072]{1,0:T(8,128)(2,1)S(1)}, u32[]{:S(2)}, u32[]{:S(2)}) collective-permute-start(bf16[32,3072]{1,0:T(8,128)(2,1)S(1)} %collective-permute-done.2.near_ref), channel_id=1, source_target_pairs={{0,4},{2,6},{4,0},{6,2},{8,12},{10,14},{12,8},{14,10},{16,20},{18,... | collective-permute-start | bytes 589832 | tf_op jit(solution)/shard_map/ppermute | solution.py:334
  19.4 14.5 %collective-permute-start.5 = (bf16[32,3072]{1,0:T(8,128)(2,1)S(1)}, bf16[32,3072]{1,0:T(8,128)(2,1)S(1)}, u32[]{:S(2)}, u32[]{:S(2)}) collective-permute-start(bf16[32,3072]{1,0:T(8,128)(2,1)S(1)} %shard_map.74), channel_id=1, source_target_pairs={{0,20},{2,22},{4,16},{6,18},{8,28},{10,30},{12,24},{14,26},{16,4},... | collective-permute-start | bytes 589832 | tf_op jit(solution)/shard_map/ppermute | solution.py:334
  21.7 16.1 %collective-permute-start.3 = (bf16[48,3072]{1,0:T(8,128)(2,1)S(1)}, bf16[48,3072]{1,0:T(8,128)(2,1)S(1)}, u32[]{:S(2)}, u32[]{:S(2)}) collective-permute-start(bf16[48,3072]{1,0:T(8,128)(2,1)S(1)} %slice_bitcast_fusion.1), channel_id=1, source_target_pairs={{0,16},{2,18},{4,20},{6,22},{8,24},{10,26},{12,28},{14,30},{16,0},... | collective-permute-start | bytes 884744 | tf_op jit(solution)/shard_map/ppermute | solution.py:334
  22.4 11.1 %collective-permute-start.11 = (bf16[96,1536]{1,0:T(8,128)(2,1)S(1)}, bf16[96,1536]{1,0:T(8,128)(2,1)S(1)}, u32[]{:S(2)}, u32[]{:S(2)}) collective-permute-start(bf16[96,1536]{1,0:T(8,128)(2,1)S(1)} %collective-permute-done.10.own_ref), channel_id=1, source_target_pairs={{0,1},{1,0},{2,3},{3,2},{4,5},{5,4},{6,7},{7,6},{8,9},{9,8},{10,11... | collective-permute-start | bytes 884744 | tf_op jit(solution)/shard_map/ppermute | solution.py:356
  27.2 4.0 %collective-permute-start.8 = (bf16[64,192]{1,0:T(8,128)(2,1)S(1)}, bf16[64,192]{1,0:T(8,128)(2,1)S(1)}, u32[]{:S(2)}, u32[]{:S(2)}) collective-permute-start(bf16[64,192]{1,0:T(8,128)(2,1)S(1)} %shard_map.78.own_ref), channel_id=1, source_target_pairs={{0,2},{2,0},{4,6},{6,4},{8,10},{10,8},{12,14},{14,12},{16,18},{18,... | collective-permute-start | bytes 73736 | tf_op jit(solution)/shard_map/ppermute | solution.py:334
  27.8 5.7 %collective-permute-start.9 = (bf16[32,3072]{1,0:T(8,128)(2,1)S(1)}, bf16[32,3072]{1,0:T(8,128)(2,1)S(1)}, u32[]{:S(2)}, u32[]{:S(2)}) collective-permute-start(bf16[32,3072]{1,0:T(8,128)(2,1)S(1)} %collective-permute-done.7.far_ref), channel_id=1, source_target_pairs={{0,4},{2,6},{4,0},{6,2},{8,12},{10,14},{12,8},{14,10},{16,20},{18,... | collective-permute-start | bytes 589832 | tf_op jit(solution)/shard_map/ppermute | solution.py:334
  31.2 15.9 %collective-permute-start.4 = (bf16[80,3072]{1,0:T(8,128)(2,1)S(1)}, bf16[80,3072]{1,0:T(8,128)(2,1)S(1)}, u32[]{:S(2)}, u32[]{:S(2)}) collective-permute-start(bf16[80,3072]{1,0:T(8,128)(2,1)S(1)} %slice_bitcast_fusion), channel_id=1, source_target_pairs={{0,16},{2,18},{4,20},{6,22},{8,24},{10,26},{12,28},{14,30},{16,0},... | collective-permute-start | bytes 1474568 | tf_op jit(solution)/shard_map/ppermute | solution.py:334
  33.9 6.1 %collective-permute-start.12 = (bf16[32,3072]{1,0:T(8,128)(2,1)S(1)}, bf16[32,3072]{1,0:T(8,128)(2,1)S(1)}, u32[]{:S(2)}, u32[]{:S(2)}) collective-permute-start(bf16[32,3072]{1,0:T(8,128)(2,1)S(1)} %collective-permute-done.5.near_ref), channel_id=1, source_target_pairs={{0,2},{2,0},{4,6},{6,4},{8,10},{10,8},{12,14},{14,12},{16,18},{18,... | collective-permute-start | bytes 589832 | tf_op jit(solution)/shard_map/ppermute | solution.py:334
  35.5 13.0 %collective-permute-start.13 = (bf16[64,1536]{1,0:T(8,128)(2,1)S(1)}, bf16[64,1536]{1,0:T(8,128)(2,1)S(1)}, u32[]{:S(2)}, u32[]{:S(2)}) collective-permute-start(bf16[64,1536]{1,0:T(8,128)(2,1)S(1)} %shard_map.80), channel_id=1, source_target_pairs={{0,8},{2,10},{4,12},{6,14},{8,0},{10,2},{12,4},{14,6},{16,24},{18,... | collective-permute-start | bytes 589832 | tf_op jit(solution)/shard_map/ppermute | solution.py:334
  38.8 4.0 %collective-permute-start.15 = (bf16[64,192]{1,0:T(8,128)(2,1)S(1)}, bf16[64,192]{1,0:T(8,128)(2,1)S(1)}, u32[]{:S(2)}, u32[]{:S(2)}) collective-permute-start(bf16[64,192]{1,0:T(8,128)(2,1)S(1)} %shard_map.81.own_ref), channel_id=1, source_target_pairs={{0,2},{2,0},{4,6},{6,4},{8,10},{10,8},{12,14},{14,12},{16,18},{18,... | collective-permute-start | bytes 73736 | tf_op jit(solution)/shard_map/ppermute | solution.py:334
  41.0 6.1 %copy-start = (s32[1,128,2]{1,2,0:T(2,128)S(1)}, s32[1,128,2]{1,2,0:T(2,128)}, u32[]{:S(2)}) copy-start(s32[1,128,2]{1,2,0:T(2,128)} %param.12) | copy-start | bytes 3076
  41.0 5.7 %collective-permute-start.17 = (bf16[64,192]{1,0:T(8,128)(2,1)S(1)}, bf16[64,192]{1,0:T(8,128)(2,1)S(1)}, u32[]{:S(2)}, u32[]{:S(2)}) collective-permute-start(bf16[64,192]{1,0:T(8,128)(2,1)S(1)} %shard_map.82.own_ref), channel_id=1, source_target_pairs={{0,2},{2,0},{4,6},{6,4},{8,10},{10,8},{12,14},{14,12},{16,18},{18,... | collective-permute-start | bytes 73736 | tf_op jit(solution)/shard_map/ppermute | solution.py:334
  43.1 10.7 %collective-permute-start.16 = (bf16[64,1536]{1,0:T(8,128)(2,1)S(1)}, bf16[64,1536]{1,0:T(8,128)(2,1)S(1)}, u32[]{:S(2)}, u32[]{:S(2)}) collective-permute-start(bf16[64,1536]{1,0:T(8,128)(2,1)S(1)} %shard_map.86), channel_id=1, source_target_pairs={{0,12},{2,14},{4,8},{6,10},{8,4},{10,6},{12,0},{14,2},{16,28},{18,... | collective-permute-start | bytes 589832 | tf_op jit(solution)/shard_map/ppermute | solution.py:334
  47.0 6.9 %collective-permute-start.18 = (bf16[64,1536]{1,0:T(8,128)(2,1)S(1)}, bf16[64,1536]{1,0:T(8,128)(2,1)S(1)}, u32[]{:S(2)}, u32[]{:S(2)}) collective-permute-start(bf16[64,1536]{1,0:T(8,128)(2,1)S(1)} %shard_map.87), channel_id=1, source_target_pairs={{0,4},{2,6},{4,0},{6,2},{8,12},{10,14},{12,8},{14,10},{16,20},{18,... | collective-permute-start | bytes 589832 | tf_op jit(solution)/shard_map/ppermute | solution.py:334
  49.5 5.1 %copy-start.1 = (f32[1,128,2]{1,2,0:T(2,128)S(1)}, f32[1,128,2]{1,2,0:T(2,128)}, u32[]{:S(2)}) copy-start(f32[1,128,2]{1,2,0:T(2,128)} %param.13) | copy-start | bytes 3076
  49.5 4.0 %collective-permute-start.14 = (bf16[64,192]{1,0:T(8,128)(2,1)S(1)}, bf16[64,192]{1,0:T(8,128)(2,1)S(1)}, u32[]{:S(2)}, u32[]{:S(2)}) collective-permute-start(bf16[64,192]{1,0:T(8,128)(2,1)S(1)} %shard_map.83.own_ref), channel_id=1, source_target_pairs={{0,2},{2,0},{4,6},{6,4},{8,10},{10,8},{12,14},{14,12},{16,18},{18,... | collective-permute-start | bytes 73736 | tf_op jit(solution)/shard_map/ppermute | solution.py:334
  53.9 4.7 %collective-permute-start.19 = (bf16[32,1536]{1,0:T(8,128)(2,1)S(1)}, bf16[32,1536]{1,0:T(8,128)(2,1)S(1)}, u32[]{:S(2)}, u32[]{:S(2)}) collective-permute-start(bf16[32,1536]{1,0:T(8,128)(2,1)S(1)} %get-tuple-element.47), channel_id=1, source_target_pairs={{0,2},{2,0},{4,6},{6,4},{8,10},{10,8},{12,14},{14,12},{16,18},{18,... | collective-permute-start | bytes 294920 | tf_op jit(solution)/shard_map/ppermute | solution.py:334

commit v12 on v7

--- a/solution.py
+++ b/solution.py
@@ -264,7 +264,7 @@
         near[0] = exchanged(near[0])
     own, other = {}, {}
     for k in (2, 3, 1, 0):
-        first = {2: (near[3],), 3: (other.get(2), arrived[0]), 1: (own.get(3),), 0: (own.get(1),)}[k]
+        first = {2: (near[3],), 3: (other.get(2), arrived[0]), 1: (own.get(3),), 0: (own.get(1), other.get(3))}[k]
         if k == 3:
             far[1] = moved(after(near[1], own[2]), 0, 0, 1)
         own[k], sent = mlp(after(near[k], *first), far[k], gain, gate_t, up_t, down)
@@ -275,7 +275,7 @@
     }
     early = summed_early(own[0], moved(both[2], 0, 2))
     backs = [
-        early, moved(both[3], 0, 3), moved(after(both[1], early), 0, 1), other[0],
+        early, moved(both[3], 0, 3), moved(both[1], 0, 1), other[0],
     ]
     if experts > 1:
         backs = [exchanged(sum(back.astype(jnp.float32) for back in backs).astype(jnp.bfloat16))]

time: 60.5 us -> 57.8 us (0.955)
  waiting for transfers between devices: 21.4 us -> 18 us
    ppermute x17, waiting for transfers between devices: 21.4 us -> 18 us  [moved(): return lax.ppermute(value, ('section', 'expert'), pairs)]
  transfers between devices with their start and end apart: 17 -> 17, of which waited for: 9 -> 10; matrix products, arithmetic and copies ran while one was open for 0% -> 0% of each run, Pallas kernels for 15% -> 16%
where the time goes in v12:
time: 57.8 us; the launch traced here: 57.6 us
  starting transfers between devices  27.7 us (48%)
  waiting for transfers between devices  18 us (31%)
  Pallas kernels  11.5 us (20%)
    ppermute x17, starting transfers between devices, moved(): return lax.ppermute(value, ('section', 'expert'), pairs)  27.7 us
    ppermute x17, waiting for transfers between devices, moved(): return lax.ppermute(value, ('section', 'expert'), pairs)  18 us
    pallas_call x4, Pallas kernels, mlp(): pl.pallas_call(mlp_kernel, out_shape=(out, out), in_specs=[VMEM] * 6, out...  5.04 us
    pallas_call x2, Pallas kernels, loaded(): pl.pallas_call(functools.partial(load_kernel, len(arrays)), out_shape=tup...  3.23 us
    pallas_call x1, Pallas kernels, ended(): pl.pallas_call(functools.partial(end_kernel, columns), out_shape=jax.Shap...  1.88 us
  transfers between devices with their start and end apart: 17, of which 10 were waited for; matrix products, arithmetic and copies ran while one was open for 0% of the time, Pallas kernels for 16%

profile of v12, /device:TPU:0, one launch (start us, length us, event | category | flops | bytes accessed | tf_op | source)
XLA Modules:
  0.0 57.6 jit_solution(1326714720117334667)
XLA Ops:
  0.0 2.9 %collective-permute-start = (s32[1,128,2]{1,2,0:T(2,128)}, s32[1,128,2]{1,2,0:T(2,128)S(1)}, u32[]{:S(2)}, u32[]{:S(2)}) collective-permute-start(s32[1,128,2]{1,2,0:T(2,128)} %param.12), channel_id=1, source_target_pairs={{0,16},{2,18},{4,20},{6,22},{8,24},{10,26},{12,28},{14,30},{16,0},... | collective-permute-start | bytes 3080 | tf_op jit(solution)/shard_map/ppermute | solution.py:229
  2.9 1.1 %shard_map.73.block_ref = bf16[128,3072]{1,0:T(8,128)(2,1)S(1)} custom-call(bf16[128,3072]{1,0:T(8,128)(2,1)} %bitcast.25), custom_call_target="tpu_custom_call" | custom-call | bytes 6291456 | tf_op jit(solution)/shard_map/pallas_call | solution.py:33
  4.1 0.6 %collective-permute-done = s32[1,128,2]{1,2,0:T(2,128)S(1)} collective-permute-done((s32[1,128,2]{1,2,0:T(2,128)}, s32[1,128,2]{1,2,0:T(2,128)S(1)}, u32[]{:S(2)}, u32[]{:S(2)}) %collective-permute-start) | collective-permute-done | bytes 1056 | tf_op jit(solution)/shard_map/ppermute | solution.py:229
  4.7 0.4 shard_map.74
  5.1 4.1 %collective-permute-start.2 = (bf16[32,3072]{1,0:T(8,128)(2,1)S(1)}, bf16[32,3072]{1,0:T(8,128)(2,1)S(1)}, u32[]{:S(2)}, u32[]{:S(2)}) collective-permute-start(bf16[32,3072]{1,0:T(8,128)(2,1)S(1)} %shard_map.74), channel_id=1, source_target_pairs={{0,24},{2,26},{4,28},{6,30},{8,16},{10,18},{12,20},{14,22},{16,8},... | collective-permute-start | bytes 589832 | tf_op jit(solution)/shard_map/ppermute | solution.py:229
  9.2 1.5 %collective-permute-start.1 = (bf16[32,3072]{1,0:T(8,128)(2,1)S(1)}, bf16[32,3072]{1,0:T(8,128)(2,1)S(1)}, u32[]{:S(2)}, u32[]{:S(2)}) collective-permute-start(bf16[32,3072]{1,0:T(8,128)(2,1)S(1)} %shard_map.74), channel_id=1, source_target_pairs={{0,18},{2,16},{4,22},{6,20},{8,26},{10,24},{12,30},{14,28},{16,2},... | collective-permute-start | bytes 589832 | tf_op jit(solution)/shard_map/ppermute | solution.py:229
  10.7 2.1 %shard_map.75 = (bf16[192,3072]{1,0:T(8,128)(2,1)S(1)}, bf16[192,3072]{1,0:T(8,128)(2,1)S(1)}, bf16[192,3072]{1,0:T(8,128)(2,1)S(1)}, bf16[1,3072]{1,0:T(2,128)(2,1)S(1)}) custom-call(bf16[192,3072]{1,0:T(8,128)(2,1)} %bitcast.26, bf16[192,3072]{1,0:T(8,128)(2,1)} %bitcast.27, bf16[192,3072]{1,0:T(8,128)(2,1)} %bitcast.28, bf16[1,3072]{1,0:T(2,128)(2,1)} %refs_3_.1), custom_call_target="tpu_custom_call" | custom-call | bytes 6291456 | tf_op jit(solution)/shard_map/pallas_call | solution.py:33
  12.8 4.5 %collective-permute-done.2.near_ref = bf16[32,3072]{1,0:T(8,128)(2,1)S(1)} collective-permute-done((bf16[32,3072]{1,0:T(8,128)(2,1)S(1)}, bf16[32,3072]{1,0:T(8,128)(2,1)S(1)}, u32[]{:S(2)}, u32[]{:S(2)}) %collective-permute-start.2) | collective-permute-done | bytes 196640 | tf_op jit(solution)/shard_map/ppermute | solution.py:229
  17.2 1.5 %collective-permute-start.7 = (bf16[32,3072]{1,0:T(8,128)(2,1)S(1)}, bf16[32,3072]{1,0:T(8,128)(2,1)S(1)}, u32[]{:S(2)}, u32[]{:S(2)}) collective-permute-start(bf16[32,3072]{1,0:T(8,128)(2,1)S(1)} %collective-permute-done.2.near_ref), channel_id=1, source_target_pairs={{0,2},{2,0},{4,6},{6,4},{8,10},{10,8},{12,14},{14,12},{16,18},{18,... | collective-permute-start | bytes 589832 | tf_op jit(solution)/shard_map/ppermute | solution.py:229
  18.8 0.6 %collective-permute-start.6 = (bf16[32,3072]{1,0:T(8,128)(2,1)S(1)}, bf16[32,3072]{1,0:T(8,128)(2,1)S(1)}, u32[]{:S(2)}, u32[]{:S(2)}) collective-permute-start(bf16[32,3072]{1,0:T(8,128)(2,1)S(1)} %collective-permute-done.2.near_ref), channel_id=1, source_target_pairs={{0,4},{2,6},{4,0},{6,2},{8,12},{10,14},{12,8},{14,10},{16,20},{18,... | collective-permute-start | bytes 589832 | tf_op jit(solution)/shard_map/ppermute | solution.py:229
  19.4 0.0 collective-permute-done.1.far_ref
  19.4 0.9 %collective-permute-start.3 = (bf16[48,3072]{1,0:T(8,128)(2,1)S(1)}, bf16[48,3072]{1,0:T(8,128)(2,1)S(1)}, u32[]{:S(2)}, u32[]{:S(2)}) collective-permute-start(bf16[48,3072]{1,0:T(8,128)(2,1)S(1)} %slice_bitcast_fusion.1), channel_id=1, source_target_pairs={{0,16},{2,18},{4,20},{6,22},{8,24},{10,26},{12,28},{14,30},{16,0},... | collective-permute-start | bytes 884744 | tf_op jit(solution)/shard_map/ppermute | solution.py:229
  20.3 2.1 %collective-permute-start.5 = (bf16[32,3072]{1,0:T(8,128)(2,1)S(1)}, bf16[32,3072]{1,0:T(8,128)(2,1)S(1)}, u32[]{:S(2)}, u32[]{:S(2)}) collective-permute-start(bf16[32,3072]{1,0:T(8,128)(2,1)S(1)} %shard_map.74), channel_id=1, source_target_pairs={{0,20},{2,22},{4,16},{6,18},{8,28},{10,30},{12,24},{14,26},{16,4},... | collective-permute-start | bytes 589832 | tf_op jit(solution)/shard_map/ppermute | solution.py:229
  22.4 3.9 %collective-permute-done.6.near_ref = bf16[32,3072]{1,0:T(8,128)(2,1)S(1)} collective-permute-done((bf16[32,3072]{1,0:T(8,128)(2,1)S(1)}, bf16[32,3072]{1,0:T(8,128)(2,1)S(1)}, u32[]{:S(2)}, u32[]{:S(2)}) %collective-permute-start.6) | collective-permute-done | bytes 196640 | tf_op jit(solution)/shard_map/ppermute | solution.py:229
  26.3 0.0 collective-permute-done.7.far_ref
  26.3 1.3 %shard_map.77 = (bf16[32,3072]{1,0:T(8,128)(2,1)S(1)}, bf16[32,3072]{1,0:T(8,128)(2,1)S(1)}) custom-call(bf16[32,3072]{1,0:T(8,128)(2,1)S(1)} %collective-permute-done.2.near_ref, bf16[32,3072]{1,0:T(8,128)(2,1)S(1)} %collective-permute-done.7.far_ref, bf16[1,3072]{1,0:T(2,128)(2,1)S(1)} %get-tuple-element.31.gain_ref, ...), custom_call_target="tpu_custom_call" | custom-call | flops 226492416 | bytes 3538944 | tf_op jit(solution)/shard_map/pallas_call | solution.py:95
  27.5 0.5 collective-permute-start.8
  28.1 1.0 %collective-permute-start.9 = (bf16[32,3072]{1,0:T(8,128)(2,1)S(1)}, bf16[32,3072]{1,0:T(8,128)(2,1)S(1)}, u32[]{:S(2)}, u32[]{:S(2)}) collective-permute-start(bf16[32,3072]{1,0:T(8,128)(2,1)S(1)} %collective-permute-done.7.far_ref), channel_id=1, source_target_pairs={{0,4},{2,6},{4,0},{6,2},{8,12},{10,14},{12,8},{14,10},{16,20},{18,... | collective-permute-start | bytes 589832 | tf_op jit(solution)/shard_map/ppermute | solution.py:229
  29.1 0.6 %collective-permute-start.4 = (bf16[80,3072]{1,0:T(8,128)(2,1)S(1)}, bf16[80,3072]{1,0:T(8,128)(2,1)S(1)}, u32[]{:S(2)}, u32[]{:S(2)}) collective-permute-start(bf16[80,3072]{1,0:T(8,128)(2,1)S(1)} %slice_bitcast_fusion), channel_id=1, source_target_pairs={{0,16},{2,18},{4,20},{6,22},{8,24},{10,26},{12,28},{14,30},{16,0},... | collective-permute-start | bytes 1474568 | tf_op jit(solution)/shard_map/ppermute | solution.py:229
  29.7 1.6 %collective-permute-done.5.near_ref = bf16[32,3072]{1,0:T(8,128)(2,1)S(1)} collective-permute-done((bf16[32,3072]{1,0:T(8,128)(2,1)S(1)}, bf16[32,3072]{1,0:T(8,128)(2,1)S(1)}, u32[]{:S(2)}, u32[]{:S(2)}) %collective-permute-start.5) | collective-permute-done | bytes 196640 | tf_op jit(solution)/shard_map/ppermute | solution.py:229
  31.3 0.0 collective-permute-start.10
  31.3 2.4 %collective-permute-done.3.refs_0_ = bf16[48,3072]{1,0:T(8,128)(2,1)S(1)} collective-permute-done((bf16[48,3072]{1,0:T(8,128)(2,1)S(1)}, bf16[48,3072]{1,0:T(8,128)(2,1)S(1)}, u32[]{:S(2)}, u32[]{:S(2)}) %collective-permute-start.3) | collective-permute-done | bytes 294944 | tf_op jit(solution)/shard_map/ppermute | solution.py:229
  33.6 0.0 collective-permute-done.8
  33.6 0.1 collective-permute-done.9.far_ref
  33.7 1.3 %shard_map.78 = (bf16[32,3072]{1,0:T(8,128)(2,1)S(1)}, bf16[32,3072]{1,0:T(8,128)(2,1)S(1)}) custom-call(bf16[32,3072]{1,0:T(8,128)(2,1)S(1)} %collective-permute-done.6.near_ref, bf16[32,3072]{1,0:T(8,128)(2,1)S(1)} %collective-permute-done.9.far_ref, bf16[1,3072]{1,0:T(2,128)(2,1)S(1)} %get-tuple-element.31.gain_ref, ...), custom_call_target="tpu_custom_call" | custom-call | flops 226492416 | bytes 3538944 | tf_op jit(solution)/shard_map/pallas_call | solution.py:95
  35.0 1.6 %collective-permute-start.11 = (bf16[32,3072]{1,0:T(8,128)(2,1)S(1)}, bf16[32,3072]{1,0:T(8,128)(2,1)S(1)}, u32[]{:S(2)}, u32[]{:S(2)}) collective-permute-start(bf16[32,3072]{1,0:T(8,128)(2,1)S(1)} %get-tuple-element.50), channel_id=1, source_target_pairs={{0,2},{2,0},{4,6},{6,4},{8,10},{10,8},{12,14},{14,12},{16,18},{18,... | collective-permute-start | bytes 589832 | tf_op jit(solution)/shard_map/ppermute | solution.py:229
  36.6 0.1 add_convert_fusion.2
  36.7 0.0 copy-start
  36.7 0.0 copy-start.1
  36.7 2.4 %collective-permute-start.12 = (bf16[32,3072]{1,0:T(8,128)(2,1)S(1)}, bf16[32,3072]{1,0:T(8,128)(2,1)S(1)}, u32[]{:S(2)}, u32[]{:S(2)}) collective-permute-start(bf16[32,3072]{1,0:T(8,128)(2,1)S(1)} %add_convert_fusion.2), channel_id=1, source_target_pairs={{0,8},{2,10},{4,12},{6,14},{8,0},{10,2},{12,4},{14,6},{16,24},{18,... | collective-permute-start | bytes 589832 | tf_op jit(solution)/shard_map/ppermute | solution.py:229
  39.1 0.0 collective-permute-done.10.far_ref
  39.1 1.3 %shard_map.79 = (bf16[32,3072]{1,0:T(8,128)(2,1)S(1)}, bf16[32,3072]{1,0:T(8,128)(2,1)S(1)}) custom-call(bf16[32,3072]{1,0:T(8,128)(2,1)S(1)} %collective-permute-done.5.near_ref, bf16[32,3072]{1,0:T(8,128)(2,1)S(1)} %collective-permute-done.10.far_ref, bf16[1,3072]{1,0:T(2,128)(2,1)S(1)} %get-tuple-element.31.gain_ref, ...), custom_call_target="tpu_custom_call" | custom-call | flops 226492416 | bytes 3538944 | tf_op jit(solution)/shard_map/pallas_call | solution.py:95
  40.4 1.5 %collective-permute-start.14 = (bf16[32,3072]{1,0:T(8,128)(2,1)S(1)}, bf16[32,3072]{1,0:T(8,128)(2,1)S(1)}, u32[]{:S(2)}, u32[]{:S(2)}) collective-permute-start(bf16[32,3072]{1,0:T(8,128)(2,1)S(1)} %get-tuple-element.53), channel_id=1, source_target_pairs={{0,2},{2,0},{4,6},{6,4},{8,10},{10,8},{12,14},{14,12},{16,18},{18,... | collective-permute-start | bytes 589832 | tf_op jit(solution)/shard_map/ppermute | solution.py:229
  41.8 0.7 %collective-permute-done.4.refs_1_ = bf16[80,3072]{1,0:T(8,128)(2,1)S(1)} collective-permute-done((bf16[80,3072]{1,0:T(8,128)(2,1)S(1)}, bf16[80,3072]{1,0:T(8,128)(2,1)S(1)}, u32[]{:S(2)}, u32[]{:S(2)}) %collective-permute-start.4) | collective-permute-done | bytes 491552 | tf_op jit(solution)/shard_map/ppermute | solution.py:229
  42.5 0.0 copy-done.1
  42.5 1.0 %shard_map.76 = (f32[128,3072]{1,0:T(8,128)S(1)}, bf16[128,160]{1,0:T(8,128)(2,1)S(1)}, bf16[32,3072]{1,0:T(8,128)(2,1)S(1)}) custom-call(bf16[1,3072]{1,0:T(2,128)(2,1)S(1)} %get-tuple-element.31.gain_ref, s32[2,128]{1,0:T(2,128)S(1)} %bitcast.22, f32[2,128]{1,0:T(2,128)S(1)} %bitcast.23, bf16[48,3072]{1,0:T(8,128)(2,1)S(1)} %collective-permute-done.3.refs_0_, ...), custom_call_target="tpu_custom_call" | custom-call | flops 3145728 | bytes 2359296 | tf_op jit(solution)/shard_map/pallas_call | solution.py:150
  43.5 0.0 collective-permute-done.11
  43.5 0.1 add_convert_fusion.1
  43.6 4.2 %collective-permute-start.13 = (bf16[32,3072]{1,0:T(8,128)(2,1)S(1)}, bf16[32,3072]{1,0:T(8,128)(2,1)S(1)}, u32[]{:S(2)}, u32[]{:S(2)}) collective-permute-start(bf16[32,3072]{1,0:T(8,128)(2,1)S(1)} %add_convert_fusion.1), channel_id=1, source_target_pairs={{0,12},{2,14},{4,8},{6,10},{8,4},{10,6},{12,0},{14,2},{16,28},{18,... | collective-permute-start | bytes 589832 | tf_op jit(solution)/shard_map/ppermute | solution.py:229
  47.7 0.0 collective-permute-done.14
  47.8 0.9 %collective-permute-start.15 = (bf16[32,3072]{1,0:T(8,128)(2,1)S(1)}, bf16[32,3072]{1,0:T(8,128)(2,1)S(1)}, u32[]{:S(2)}, u32[]{:S(2)}) collective-permute-start(bf16[32,3072]{1,0:T(8,128)(2,1)S(1)} %add_convert_fusion), channel_id=1, source_target_pairs={{0,4},{2,6},{4,0},{6,2},{8,12},{10,14},{12,8},{14,10},{16,20},{18,... | collective-permute-start | bytes 589832 | tf_op jit(solution)/shard_map/ppermute | solution.py:229
  48.7 1.3 %shard_map.80 = (bf16[32,3072]{1,0:T(8,128)(2,1)S(1)}, bf16[32,3072]{1,0:T(8,128)(2,1)S(1)}) custom-call(bf16[32,3072]{1,0:T(8,128)(2,1)S(1)} %get-tuple-element.51.near_ref, bf16[32,3072]{1,0:T(8,128)(2,1)S(1)} %collective-permute-done.1.far_ref, bf16[1,3072]{1,0:T(2,128)(2,1)S(1)} %get-tuple-element.31.gain_ref, ...), custom_call_target="tpu_custom_call" | custom-call | flops 226492416 | bytes 3538944 | tf_op jit(solution)/shard_map/pallas_call | solution.py:95
  50.0 1.4 %collective-permute-start.16 = (bf16[32,3072]{1,0:T(8,128)(2,1)S(1)}, bf16[32,3072]{1,0:T(8,128)(2,1)S(1)}, u32[]{:S(2)}, u32[]{:S(2)}) collective-permute-start(bf16[32,3072]{1,0:T(8,128)(2,1)S(1)} %get-tuple-element.54), channel_id=1, source_target_pairs={{0,2},{2,0},{4,6},{6,4},{8,10},{10,8},{12,14},{14,12},{16,18},{18,... | collective-permute-start | bytes 589832 | tf_op jit(solution)/shard_map/ppermute | solution.py:229
  51.4 0.0 collective-permute-done.12.right_ref
  51.4 1.7 %collective-permute-done.13.refs_1_ = bf16[32,3072]{1,0:T(8,128)(2,1)S(1)} collective-permute-done((bf16[32,3072]{1,0:T(8,128)(2,1)S(1)}, bf16[32,3072]{1,0:T(8,128)(2,1)S(1)}, u32[]{:S(2)}, u32[]{:S(2)}) %collective-permute-start.13) | collective-permute-done | bytes 196640 | tf_op jit(solution)/shard_map/ppermute | solution.py:229
  53.1 2.0 %collective-permute-done.15.refs_2_ = bf16[32,3072]{1,0:T(8,128)(2,1)S(1)} collective-permute-done((bf16[32,3072]{1,0:T(8,128)(2,1)S(1)}, bf16[32,3072]{1,0:T(8,128)(2,1)S(1)}, u32[]{:S(2)}, u32[]{:S(2)}) %collective-permute-start.15) | collective-permute-done | bytes 196640 | tf_op jit(solution)/shard_map/ppermute | solution.py:229
  55.1 0.6 %collective-permute-done.16.refs_3_ = bf16[32,3072]{1,0:T(8,128)(2,1)S(1)} collective-permute-done((bf16[32,3072]{1,0:T(8,128)(2,1)S(1)}, bf16[32,3072]{1,0:T(8,128)(2,1)S(1)}, u32[]{:S(2)}, u32[]{:S(2)}) %collective-permute-start.16) | collective-permute-done | bytes 196640 | tf_op jit(solution)/shard_map/ppermute | solution.py:229
  55.7 1.9 %shard_map.82 = bf16[128,3072]{1,0:T(8,128)(2,1)} custom-call(f32[128,3072]{1,0:T(8,128)S(1)} %get-tuple-element.34.base_ref, bf16[128,160]{1,0:T(8,128)(2,1)S(1)} %get-tuple-element.35.table_ref, f32[32,3072]{1,0:T(8,128)S(1)} %shard_map.81.refs_0_, bf16[32,3072]{1,0:T(8,128)(2,1)S(1)} %collective-permute-done.13.refs_1_, ...), custom_call_target="tpu_custom_call" | custom-call | flops 100663296 | bytes 2359296 | tf_op jit(solution)/shard_map/pallas_call | solution.py:182
  (7 shorter events, 0.1 us)
Async XLA Ops:
  0.0 4.7 %collective-permute-start = (s32[1,128,2]{1,2,0:T(2,128)}, s32[1,128,2]{1,2,0:T(2,128)S(1)}, u32[]{:S(2)}, u32[]{:S(2)}) collective-permute-start(s32[1,128,2]{1,2,0:T(2,128)} %param.12), channel_id=1, source_target_pairs={{0,16},{2,18},{4,20},{6,22},{8,24},{10,26},{12,28},{14,30},{16,0},... | collective-permute-start | bytes 3080 | tf_op jit(solution)/shard_map/ppermute | solution.py:229
  5.1 12.2 %collective-permute-start.2 = (bf16[32,3072]{1,0:T(8,128)(2,1)S(1)}, bf16[32,3072]{1,0:T(8,128)(2,1)S(1)}, u32[]{:S(2)}, u32[]{:S(2)}) collective-permute-start(bf16[32,3072]{1,0:T(8,128)(2,1)S(1)} %shard_map.74), channel_id=1, source_target_pairs={{0,24},{2,26},{4,28},{6,30},{8,16},{10,18},{12,20},{14,22},{16,8},... | collective-permute-start | bytes 589832 | tf_op jit(solution)/shard_map/ppermute | solution.py:229
  9.2 10.2 %collective-permute-start.1 = (bf16[32,3072]{1,0:T(8,128)(2,1)S(1)}, bf16[32,3072]{1,0:T(8,128)(2,1)S(1)}, u32[]{:S(2)}, u32[]{:S(2)}) collective-permute-start(bf16[32,3072]{1,0:T(8,128)(2,1)S(1)} %shard_map.74), channel_id=1, source_target_pairs={{0,18},{2,16},{4,22},{6,20},{8,26},{10,24},{12,30},{14,28},{16,2},... | collective-permute-start | bytes 589832 | tf_op jit(solution)/shard_map/ppermute | solution.py:229
  10.7 8.7 %copy-start.2 = (bf16[1,128,3072]{2,1,0:T(8,128)(2,1)S(1)}, bf16[1,128,3072]{2,1,0:T(8,128)(2,1)}, u32[]{:S(2)}) copy-start(bf16[1,128,3072]{2,1,0:T(8,128)(2,1)} %param.7) | copy-start | bytes 2359300
  17.2 9.0 %collective-permute-start.7 = (bf16[32,3072]{1,0:T(8,128)(2,1)S(1)}, bf16[32,3072]{1,0:T(8,128)(2,1)S(1)}, u32[]{:S(2)}, u32[]{:S(2)}) collective-permute-start(bf16[32,3072]{1,0:T(8,128)(2,1)S(1)} %collective-permute-done.2.near_ref), channel_id=1, source_target_pairs={{0,2},{2,0},{4,6},{6,4},{8,10},{10,8},{12,14},{14,12},{16,18},{18,... | collective-permute-start | bytes 589832 | tf_op jit(solution)/shard_map/ppermute | solution.py:229
  18.8 7.5 %collective-permute-start.6 = (bf16[32,3072]{1,0:T(8,128)(2,1)S(1)}, bf16[32,3072]{1,0:T(8,128)(2,1)S(1)}, u32[]{:S(2)}, u32[]{:S(2)}) collective-permute-start(bf16[32,3072]{1,0:T(8,128)(2,1)S(1)} %collective-permute-done.2.near_ref), channel_id=1, source_target_pairs={{0,4},{2,6},{4,0},{6,2},{8,12},{10,14},{12,8},{14,10},{16,20},{18,... | collective-permute-start | bytes 589832 | tf_op jit(solution)/shard_map/ppermute | solution.py:229
  19.4 14.2 %collective-permute-start.3 = (bf16[48,3072]{1,0:T(8,128)(2,1)S(1)}, bf16[48,3072]{1,0:T(8,128)(2,1)S(1)}, u32[]{:S(2)}, u32[]{:S(2)}) collective-permute-start(bf16[48,3072]{1,0:T(8,128)(2,1)S(1)} %slice_bitcast_fusion.1), channel_id=1, source_target_pairs={{0,16},{2,18},{4,20},{6,22},{8,24},{10,26},{12,28},{14,30},{16,0},... | collective-permute-start | bytes 884744 | tf_op jit(solution)/shard_map/ppermute | solution.py:229
  20.3 11.0 %collective-permute-start.5 = (bf16[32,3072]{1,0:T(8,128)(2,1)S(1)}, bf16[32,3072]{1,0:T(8,128)(2,1)S(1)}, u32[]{:S(2)}, u32[]{:S(2)}) collective-permute-start(bf16[32,3072]{1,0:T(8,128)(2,1)S(1)} %shard_map.74), channel_id=1, source_target_pairs={{0,20},{2,22},{4,16},{6,18},{8,28},{10,30},{12,24},{14,26},{16,4},... | collective-permute-start | bytes 589832 | tf_op jit(solution)/shard_map/ppermute | solution.py:229
  27.5 6.1 %collective-permute-start.8 = (bf16[32,3072]{1,0:T(8,128)(2,1)S(1)}, bf16[32,3072]{1,0:T(8,128)(2,1)S(1)}, u32[]{:S(2)}, u32[]{:S(2)}) collective-permute-start(bf16[32,3072]{1,0:T(8,128)(2,1)S(1)} %get-tuple-element.43), channel_id=1, source_target_pairs={{0,2},{2,0},{4,6},{6,4},{8,10},{10,8},{12,14},{14,12},{16,18},{18,... | collective-permute-start | bytes 589832 | tf_op jit(solution)/shard_map/ppermute | solution.py:229
  28.1 5.7 %collective-permute-start.9 = (bf16[32,3072]{1,0:T(8,128)(2,1)S(1)}, bf16[32,3072]{1,0:T(8,128)(2,1)S(1)}, u32[]{:S(2)}, u32[]{:S(2)}) collective-permute-start(bf16[32,3072]{1,0:T(8,128)(2,1)S(1)} %collective-permute-done.7.far_ref), channel_id=1, source_target_pairs={{0,4},{2,6},{4,0},{6,2},{8,12},{10,14},{12,8},{14,10},{16,20},{18,... | collective-permute-start | bytes 589832 | tf_op jit(solution)/shard_map/ppermute | solution.py:229
  29.1 13.4 %collective-permute-start.4 = (bf16[80,3072]{1,0:T(8,128)(2,1)S(1)}, bf16[80,3072]{1,0:T(8,128)(2,1)S(1)}, u32[]{:S(2)}, u32[]{:S(2)}) collective-permute-start(bf16[80,3072]{1,0:T(8,128)(2,1)S(1)} %slice_bitcast_fusion), channel_id=1, source_target_pairs={{0,16},{2,18},{4,20},{6,22},{8,24},{10,26},{12,28},{14,30},{16,0},... | collective-permute-start | bytes 1474568 | tf_op jit(solution)/shard_map/ppermute | solution.py:229
  31.3 7.8 %collective-permute-start.10 = (bf16[32,3072]{1,0:T(8,128)(2,1)S(1)}, bf16[32,3072]{1,0:T(8,128)(2,1)S(1)}, u32[]{:S(2)}, u32[]{:S(2)}) collective-permute-start(bf16[32,3072]{1,0:T(8,128)(2,1)S(1)} %collective-permute-done.5.near_ref), channel_id=1, source_target_pairs={{0,2},{2,0},{4,6},{6,4},{8,10},{10,8},{12,14},{14,12},{16,18},{18,... | collective-permute-start | bytes 589832 | tf_op jit(solution)/shard_map/ppermute | solution.py:229
  35.0 8.5 %collective-permute-start.11 = (bf16[32,3072]{1,0:T(8,128)(2,1)S(1)}, bf16[32,3072]{1,0:T(8,128)(2,1)S(1)}, u32[]{:S(2)}, u32[]{:S(2)}) collective-permute-start(bf16[32,3072]{1,0:T(8,128)(2,1)S(1)} %get-tuple-element.50), channel_id=1, source_target_pairs={{0,2},{2,0},{4,6},{6,4},{8,10},{10,8},{12,14},{14,12},{16,18},{18,... | collective-permute-start | bytes 589832 | tf_op jit(solution)/shard_map/ppermute | solution.py:229
  36.7 5.8 %copy-start = (s32[1,128,2]{1,2,0:T(2,128)S(1)}, s32[1,128,2]{1,2,0:T(2,128)}, u32[]{:S(2)}) copy-start(s32[1,128,2]{1,2,0:T(2,128)} %param.12) | copy-start | bytes 3076
  36.7 5.8 %copy-start.1 = (f32[1,128,2]{1,2,0:T(2,128)S(1)}, f32[1,128,2]{1,2,0:T(2,128)}, u32[]{:S(2)}) copy-start(f32[1,128,2]{1,2,0:T(2,128)} %param.13) | copy-start | bytes 3076
  36.7 14.6 %collective-permute-start.12 = (bf16[32,3072]{1,0:T(8,128)(2,1)S(1)}, bf16[32,3072]{1,0:T(8,128)(2,1)S(1)}, u32[]{:S(2)}, u32[]{:S(2)}) collective-permute-start(bf16[32,3072]{1,0:T(8,128)(2,1)S(1)} %add_convert_fusion.2), channel_id=1, source_target_pairs={{0,8},{2,10},{4,12},{6,14},{8,0},{10,2},{12,4},{14,6},{16,24},{18,... | collective-permute-start | bytes 589832 | tf_op jit(solution)/shard_map/ppermute | solution.py:229
  40.4 7.4 %collective-permute-start.14 = (bf16[32,3072]{1,0:T(8,128)(2,1)S(1)}, bf16[32,3072]{1,0:T(8,128)(2,1)S(1)}, u32[]{:S(2)}, u32[]{:S(2)}) collective-permute-start(bf16[32,3072]{1,0:T(8,128)(2,1)S(1)} %get-tuple-element.53), channel_id=1, source_target_pairs={{0,2},{2,0},{4,6},{6,4},{8,10},{10,8},{12,14},{14,12},{16,18},{18,... | collective-permute-start | bytes 589832 | tf_op jit(solution)/shard_map/ppermute | solution.py:229
  43.6 9.5 %collective-permute-start.13 = (bf16[32,3072]{1,0:T(8,128)(2,1)S(1)}, bf16[32,3072]{1,0:T(8,128)(2,1)S(1)}, u32[]{:S(2)}, u32[]{:S(2)}) collective-permute-start(bf16[32,3072]{1,0:T(8,128)(2,1)S(1)} %add_convert_fusion.1), channel_id=1, source_target_pairs={{0,12},{2,14},{4,8},{6,10},{8,4},{10,6},{12,0},{14,2},{16,28},{18,... | collective-permute-start | bytes 589832 | tf_op jit(solution)/shard_map/ppermute | solution.py:229
  47.8 7.3 %collective-permute-start.15 = (bf16[32,3072]{1,0:T(8,128)(2,1)S(1)}, bf16[32,3072]{1,0:T(8,128)(2,1)S(1)}, u32[]{:S(2)}, u32[]{:S(2)}) collective-permute-start(bf16[32,3072]{1,0:T(8,128)(2,1)S(1)} %add_convert_fusion), channel_id=1, source_target_pairs={{0,4},{2,6},{4,0},{6,2},{8,12},{10,14},{12,8},{14,10},{16,20},{18,... | collective-permute-start | bytes 589832 | tf_op jit(solution)/shard_map/ppermute | solution.py:229
  50.0 5.7 %collective-permute-start.16 = (bf16[32,3072]{1,0:T(8,128)(2,1)S(1)}, bf16[32,3072]{1,0:T(8,128)(2,1)S(1)}, u32[]{:S(2)}, u32[]{:S(2)}) collective-permute-start(bf16[32,3072]{1,0:T(8,128)(2,1)S(1)} %get-tuple-element.54), channel_id=1, source_target_pairs={{0,2},{2,0},{4,6},{6,4},{8,10},{10,8},{12,14},{14,12},{16,18},{18,... | collective-permute-start | bytes 589832 | tf_op jit(solution)/shard_map/ppermute | solution.py:229

commit v13 on v12

--- a/solution.py
+++ b/solution.py
@@ -18,23 +18,32 @@
     return lax.optimization_barrier((value, *others))[0]
 
 
-def load_kernel(count, *refs):
-    sources, targets, sems = refs[:count], refs[count:2 * count], refs[2 * count]
-    copies = [
-        pltpu.make_async_copy(a, b, sems.at[i]) for i, (a, b) in enumerate(zip(sources, targets))
-    ]
+def load_kernel(groups, *refs):
+    count = sum(groups)
+    sources, targets, sems = refs[:count], refs[count:-1], refs[-1]
+    copies, i = [], 0
+    for group, target in zip(groups, targets):
+        start = 0
+        for source in sources[i:i + group]:
+            rows = target.at[pl.ds(start, source.shape[0])]
+            copies.append(pltpu.make_async_copy(source, rows, sems.at[i]))
+            start, i = start + source.shape[0], i + 1
     for copy in copies:
         copy.start()
     for copy in copies:
         copy.wait()
 
 
-def loaded(*arrays):
-    return pl.pallas_call(
-        functools.partial(load_kernel, len(arrays)),
-        out_shape=tuple(jax.ShapeDtypeStruct(a.shape, a.dtype) for a in arrays),
+def loaded(*groups):
+    arrays = [a for group in groups for a in group]
+    return pl.pallas_call(
+        functools.partial(load_kernel, [len(group) for group in groups]),
+        out_shape=tuple(
+            jax.ShapeDtypeStruct((sum(a.shape[0] for a in group),) + group[0].shape[1:], group[0].dtype)
+            for group in groups
+        ),
         in_specs=[HBM] * len(arrays),
-        out_specs=(VMEM,) * len(arrays),
+        out_specs=(VMEM,) * len(groups),
         scratch_shapes=[pltpu.SemaphoreType.DMA((len(arrays),))],
         compiler_params=PARAMS,
         cost_estimate=pl.CostEstimate(flops=0, bytes_accessed=6 * 1024 * 1024, transcendentals=0),
@@ -73,35 +82,35 @@
     )(ids_t, block)
 
 
-def mlp_kernel(near_ref, far_ref, gain_ref, gate_ref, up_ref, down_ref, near_out, far_out):
-    count = near_ref.shape[0]
+def mlp_kernel(near_ref, far_ref, gain_ref, both_ref, down_ref, near_out, far_out):
+    count, hidden = near_ref.shape[0], down_ref.shape[0]
     rows = jnp.concatenate([near_ref[...], far_ref[...]], axis=0).astype(jnp.float32)
     inverse = lax.rsqrt(jnp.mean(rows * rows, axis=-1, keepdims=True) + 1e-06)
     normed = (rows * inverse * gain_ref[...].astype(jnp.float32)).astype(jnp.bfloat16)
     across = (((1,), (1,)), ((), ()))
-    gate = lax.dot_general(normed, gate_ref[...], across, preferred_element_type=jnp.float32)
-    up = lax.dot_general(normed, up_ref[...], across, preferred_element_type=jnp.float32)
-    hidden = (gate / (1.0 + jnp.exp(-gate)) * up).astype(jnp.bfloat16)
-    partial = jnp.dot(hidden, down_ref[...], preferred_element_type=jnp.float32)
+    both = lax.dot_general(normed, both_ref[...], across, preferred_element_type=jnp.float32)
+    gate, up = both[:, :hidden], both[:, hidden:]
+    inner = (gate / (1.0 + jnp.exp(-gate)) * up).astype(jnp.bfloat16)
+    partial = jnp.dot(inner, down_ref[...], preferred_element_type=jnp.float32)
     partial = partial.astype(jnp.bfloat16)
     near_out[...] = partial[:count]
     far_out[...] = partial[count:]
 
 
-def mlp(near, far, gain, gate_t, up_t, down):
+def mlp(near, far, gain, both_t, down):
     rows = 2 * near.shape[0]
     width, hidden = down.shape[1], down.shape[0]
     out = jax.ShapeDtypeStruct(near.shape, jnp.bfloat16)
     return pl.pallas_call(
         mlp_kernel,
         out_shape=(out, out),
-        in_specs=[VMEM] * 6,
+        in_specs=[VMEM] * 5,
         out_specs=(VMEM, VMEM),
         compiler_params=PARAMS,
         cost_estimate=pl.CostEstimate(
             flops=6 * rows * width * hidden, bytes_accessed=6 * width * hidden, transcendentals=0
         ),
-    )(near, far, gain, gate_t, up_t, down)
+    )(near, far, gain, both_t, down)
 
 
 def parts_of(value):
@@ -163,28 +172,36 @@
     )(gain, ids_t, weights_t, *blocks)
 
 
-def end_kernel(columns, base_ref, table_ref, *refs):
-    back_refs, out_ref = refs[:-1], refs[-1]
-    here = pl.ds(pl.multiple_of(pl.program_id(0) * columns, columns), columns)
-    total = back_refs[0][:, here].astype(jnp.float32)
-    for ref in back_refs[1:]:
-        total = total + ref[:, here].astype(jnp.float32)
-    high, low, _ = parts_of(total)
-    rows = jnp.concatenate([high, high, high, low, low], axis=0)
-    added = jnp.dot(table_ref[...], rows, preferred_element_type=jnp.float32)
-    out_ref[...] = (base_ref[:, here] + added).astype(jnp.bfloat16)
+def end_kernel(steps, base_ref, table_ref, *refs):
+    back_refs, (out_ref, done, sems) = refs[:-3], refs[-3:]
+    columns = base_ref.shape[1] // steps
+    copies = []
+    for step in range(steps):
+        here = slice(step * columns, (step + 1) * columns)
+        total = back_refs[0][:, here].astype(jnp.float32)
+        for ref in back_refs[1:]:
+            total = total + ref[:, here].astype(jnp.float32)
+        high, low, _ = parts_of(total)
+        rows = jnp.concatenate([high, high, high, low, low], axis=0)
+        added = jnp.dot(table_ref[...], rows, preferred_element_type=jnp.float32)
+        done[:, here] = (base_ref[:, here] + added).astype(jnp.bfloat16)
+        copies.append(
+            pltpu.make_async_copy(done.at[:, here], out_ref.at[:, here], sems.at[step])
+        )
+        copies[-1].start()
+    for copy in copies:
+        copy.wait()
 
 
 def ended(base, table, backs):
     count, width = base.shape
-    steps = 3
-    columns = width // steps
-    return pl.pallas_call(
-        functools.partial(end_kernel, columns),
+    steps = 6
+    return pl.pallas_call(
+        functools.partial(end_kernel, steps),
         out_shape=jax.ShapeDtypeStruct((count, width), jnp.bfloat16),
-        grid=(steps,),
         in_specs=[VMEM] * (2 + len(backs)),
-        out_specs=pl.BlockSpec((count, columns), lambda i: (0, i)),
+        out_specs=HBM,
+        scratch_shapes=[pltpu.VMEM((count, width), jnp.bfloat16), pltpu.SemaphoreType.DMA((steps,))],
         compiler_params=PARAMS,
         cost_estimate=pl.CostEstimate(
             flops=2 * count * width * table.shape[0], bytes_accessed=6 * count * width,
@@ -235,12 +252,12 @@
         ).reshape(experts * CAP, width)
 
     next_ids = moved(route_ids, -1, 0)[0]
-    block, = loaded(blocks[0])
+    block, = loaded((blocks[0],))
     picked = picked_rows(experts, jnp.swapaxes(next_ids, 0, 1), block)
     if experts > 1:
         picked = exchanged(picked)
-    gate_t, up_t, down, gain = loaded(
-        after(jnp.swapaxes(w_gate[0], 0, 1), picked), jnp.swapaxes(w_up[0], 0, 1), w_down[0], norm_gain
+    both_t, down, gain = loaded(
+        (after(jnp.swapaxes(w_gate[0], 0, 1), picked), jnp.swapaxes(w_up[0], 0, 1)), (w_down[0],), (norm_gain,)
     )
 
     near, far = {}, {}
@@ -267,7 +284,7 @@
         first = {2: (near[3],), 3: (other.get(2), arrived[0]), 1: (own.get(3),), 0: (own.get(1), other.get(3))}[k]
         if k == 3:
             far[1] = moved(after(near[1], own[2]), 0, 0, 1)
-        own[k], sent = mlp(after(near[k], *first), far[k], gain, gate_t, up_t, down)
+        own[k], sent = mlp(after(near[k], *first), far[k], gain, both_t, down)
         other[k] = moved(sent, 0, 0, 1)
     both = {
         k: (own[k].astype(jnp.float32) + other[k].astype(jnp.float32)).astype(jnp.bfloat16)

time: 57.8 us -> 58.1 us (level)
  starting transfers between devices: 27.7 us -> 28.9 us
  waiting for transfers between devices: 18 us -> 17 us
    ppermute x17, starting transfers between devices: 27.7 us -> 28.9 us  [moved(): return lax.ppermute(value, ('section', 'expert'), pairs)]
    ppermute x17, waiting for transfers between devices: 18 us -> 17 us  [moved(): return lax.ppermute(value, ('section', 'expert'), pairs)]
  transfers between devices with their start and end apart: 17 -> 17, of which waited for: 10 -> 10; matrix products, arithmetic and copies ran while one was open for 0% -> 0% of each run, Pallas kernels for 16% -> 18%
where the time goes in v13:
time: 58.1 us; the launch traced here: 57.9 us
  starting transfers between devices  28.9 us (50%)
  waiting for transfers between devices  17 us (29%)
  Pallas kernels  11.7 us (20%)
    ppermute x17, starting transfers between devices, moved(): return lax.ppermute(value, ('section', 'expert'), pairs)  28.9 us
    ppermute x17, waiting for transfers between devices, moved(): return lax.ppermute(value, ('section', 'expert'), pairs)  17 us
    pallas_call x4, Pallas kernels, mlp(): pl.pallas_call(mlp_kernel, out_shape=(out, out), in_specs=[VMEM] * 5, out...  5.95 us
    pallas_call x2, Pallas kernels, loaded(): pl.pallas_call(functools.partial(load_kernel, [len(group) for group in gr...  3.23 us
  transfers between devices with their start and end apart: 17, of which 10 were waited for; matrix products, arithmetic and copies ran while one was open for 0% of the time, Pallas kernels for 18%

profile of v13, /device:TPU:0, one launch (start us, length us, event | category | flops | bytes accessed | tf_op | source)
XLA Modules:
  0.0 57.9 jit_solution(154070359278087220)
XLA Ops:
  0.0 2.9 %collective-permute-start = (s32[1,128,2]{1,2,0:T(2,128)}, s32[1,128,2]{1,2,0:T(2,128)S(1)}, u32[]{:S(2)}, u32[]{:S(2)}) collective-permute-start(s32[1,128,2]{1,2,0:T(2,128)} %param.12), channel_id=1, source_target_pairs={{0,16},{2,18},{4,20},{6,22},{8,24},{10,26},{12,28},{14,30},{16,0},... | collective-permute-start | bytes 3080 | tf_op jit(solution)/shard_map/ppermute | solution.py:246
  2.9 1.1 %shard_map.73.block_ref = bf16[128,3072]{1,0:T(8,128)(2,1)S(1)} custom-call(bf16[128,3072]{1,0:T(8,128)(2,1)} %bitcast.25), custom_call_target="tpu_custom_call" | custom-call | bytes 6291456 | tf_op jit(solution)/shard_map/pallas_call | solution.py:39
  4.1 0.6 %collective-permute-done = s32[1,128,2]{1,2,0:T(2,128)S(1)} collective-permute-done((s32[1,128,2]{1,2,0:T(2,128)}, s32[1,128,2]{1,2,0:T(2,128)S(1)}, u32[]{:S(2)}, u32[]{:S(2)}) %collective-permute-start) | collective-permute-done | bytes 1056 | tf_op jit(solution)/shard_map/ppermute | solution.py:246
  4.7 0.4 shard_map.74
  5.1 4.1 %collective-permute-start.2 = (bf16[32,3072]{1,0:T(8,128)(2,1)S(1)}, bf16[32,3072]{1,0:T(8,128)(2,1)S(1)}, u32[]{:S(2)}, u32[]{:S(2)}) collective-permute-start(bf16[32,3072]{1,0:T(8,128)(2,1)S(1)} %shard_map.74), channel_id=1, source_target_pairs={{0,24},{2,26},{4,28},{6,30},{8,16},{10,18},{12,20},{14,22},{16,8},... | collective-permute-start | bytes 589832 | tf_op jit(solution)/shard_map/ppermute | solution.py:246
  9.2 1.5 %collective-permute-start.1 = (bf16[32,3072]{1,0:T(8,128)(2,1)S(1)}, bf16[32,3072]{1,0:T(8,128)(2,1)S(1)}, u32[]{:S(2)}, u32[]{:S(2)}) collective-permute-start(bf16[32,3072]{1,0:T(8,128)(2,1)S(1)} %shard_map.74), channel_id=1, source_target_pairs={{0,18},{2,16},{4,22},{6,20},{8,26},{10,24},{12,30},{14,28},{16,2},... | collective-permute-start | bytes 589832 | tf_op jit(solution)/shard_map/ppermute | solution.py:246
  10.7 2.1 %shard_map.75 = (bf16[384,3072]{1,0:T(8,128)(2,1)S(1)}, bf16[192,3072]{1,0:T(8,128)(2,1)S(1)}, bf16[1,3072]{1,0:T(2,128)(2,1)S(1)}) custom-call(bf16[192,3072]{1,0:T(8,128)(2,1)} %bitcast.26, bf16[192,3072]{1,0:T(8,128)(2,1)} %bitcast.27, bf16[192,3072]{1,0:T(8,128)(2,1)} %bitcast.28, bf16[1,3072]{1,0:T(2,128)(2,1)} %refs_3_.1), custom_call_target="tpu_custom_call" | custom-call | bytes 6291456 | tf_op jit(solution)/shard_map/pallas_call | solution.py:39
  12.8 4.5 %collective-permute-done.2.near_ref = bf16[32,3072]{1,0:T(8,128)(2,1)S(1)} collective-permute-done((bf16[32,3072]{1,0:T(8,128)(2,1)S(1)}, bf16[32,3072]{1,0:T(8,128)(2,1)S(1)}, u32[]{:S(2)}, u32[]{:S(2)}) %collective-permute-start.2) | collective-permute-done | bytes 196640 | tf_op jit(solution)/shard_map/ppermute | solution.py:246
  17.2 1.5 %collective-permute-start.7 = (bf16[32,3072]{1,0:T(8,128)(2,1)S(1)}, bf16[32,3072]{1,0:T(8,128)(2,1)S(1)}, u32[]{:S(2)}, u32[]{:S(2)}) collective-permute-start(bf16[32,3072]{1,0:T(8,128)(2,1)S(1)} %collective-permute-done.2.near_ref), channel_id=1, source_target_pairs={{0,2},{2,0},{4,6},{6,4},{8,10},{10,8},{12,14},{14,12},{16,18},{18,... | collective-permute-start | bytes 589832 | tf_op jit(solution)/shard_map/ppermute | solution.py:246
  18.8 0.6 %collective-permute-start.6 = (bf16[32,3072]{1,0:T(8,128)(2,1)S(1)}, bf16[32,3072]{1,0:T(8,128)(2,1)S(1)}, u32[]{:S(2)}, u32[]{:S(2)}) collective-permute-start(bf16[32,3072]{1,0:T(8,128)(2,1)S(1)} %collective-permute-done.2.near_ref), channel_id=1, source_target_pairs={{0,4},{2,6},{4,0},{6,2},{8,12},{10,14},{12,8},{14,10},{16,20},{18,... | collective-permute-start | bytes 589832 | tf_op jit(solution)/shard_map/ppermute | solution.py:246
  19.4 0.0 copy-done.2
  19.4 0.0 collective-permute-done.1.far_ref
  19.4 0.9 %collective-permute-start.3 = (bf16[48,3072]{1,0:T(8,128)(2,1)S(1)}, bf16[48,3072]{1,0:T(8,128)(2,1)S(1)}, u32[]{:S(2)}, u32[]{:S(2)}) collective-permute-start(bf16[48,3072]{1,0:T(8,128)(2,1)S(1)} %slice_bitcast_fusion.1), channel_id=1, source_target_pairs={{0,16},{2,18},{4,20},{6,22},{8,24},{10,26},{12,28},{14,30},{16,0},... | collective-permute-start | bytes 884744 | tf_op jit(solution)/shard_map/ppermute | solution.py:246
  20.3 2.1 %collective-permute-start.5 = (bf16[32,3072]{1,0:T(8,128)(2,1)S(1)}, bf16[32,3072]{1,0:T(8,128)(2,1)S(1)}, u32[]{:S(2)}, u32[]{:S(2)}) collective-permute-start(bf16[32,3072]{1,0:T(8,128)(2,1)S(1)} %shard_map.74), channel_id=1, source_target_pairs={{0,20},{2,22},{4,16},{6,18},{8,28},{10,30},{12,24},{14,26},{16,4},... | collective-permute-start | bytes 589832 | tf_op jit(solution)/shard_map/ppermute | solution.py:246
  22.4 3.9 %collective-permute-done.6.near_ref = bf16[32,3072]{1,0:T(8,128)(2,1)S(1)} collective-permute-done((bf16[32,3072]{1,0:T(8,128)(2,1)S(1)}, bf16[32,3072]{1,0:T(8,128)(2,1)S(1)}, u32[]{:S(2)}, u32[]{:S(2)}) %collective-permute-start.6) | collective-permute-done | bytes 196640 | tf_op jit(solution)/shard_map/ppermute | solution.py:246
  26.3 0.0 collective-permute-done.7.far_ref
  26.3 1.5 %shard_map.77 = (bf16[32,3072]{1,0:T(8,128)(2,1)S(1)}, bf16[32,3072]{1,0:T(8,128)(2,1)S(1)}) custom-call(bf16[32,3072]{1,0:T(8,128)(2,1)S(1)} %collective-permute-done.2.near_ref, bf16[32,3072]{1,0:T(8,128)(2,1)S(1)} %collective-permute-done.7.far_ref, bf16[1,3072]{1,0:T(2,128)(2,1)S(1)} %get-tuple-element.30.gain_ref, ...), custom_call_target="tpu_custom_call" | custom-call | flops 226492416 | bytes 3538944 | tf_op jit(solution)/shard_map/pallas_call | solution.py:104
  27.8 0.5 collective-permute-start.8
  28.3 1.0 %collective-permute-start.9 = (bf16[32,3072]{1,0:T(8,128)(2,1)S(1)}, bf16[32,3072]{1,0:T(8,128)(2,1)S(1)}, u32[]{:S(2)}, u32[]{:S(2)}) collective-permute-start(bf16[32,3072]{1,0:T(8,128)(2,1)S(1)} %collective-permute-done.7.far_ref), channel_id=1, source_target_pairs={{0,4},{2,6},{4,0},{6,2},{8,12},{10,14},{12,8},{14,10},{16,20},{18,... | collective-permute-start | bytes 589832 | tf_op jit(solution)/shard_map/ppermute | solution.py:246
  29.3 0.6 %collective-permute-start.4 = (bf16[80,3072]{1,0:T(8,128)(2,1)S(1)}, bf16[80,3072]{1,0:T(8,128)(2,1)S(1)}, u32[]{:S(2)}, u32[]{:S(2)}) collective-permute-start(bf16[80,3072]{1,0:T(8,128)(2,1)S(1)} %slice_bitcast_fusion), channel_id=1, source_target_pairs={{0,16},{2,18},{4,20},{6,22},{8,24},{10,26},{12,28},{14,30},{16,0},... | collective-permute-start | bytes 1474568 | tf_op jit(solution)/shard_map/ppermute | solution.py:246
  29.9 1.1 %collective-permute-done.5.near_ref = bf16[32,3072]{1,0:T(8,128)(2,1)S(1)} collective-permute-done((bf16[32,3072]{1,0:T(8,128)(2,1)S(1)}, bf16[32,3072]{1,0:T(8,128)(2,1)S(1)}, u32[]{:S(2)}, u32[]{:S(2)}) %collective-permute-start.5) | collective-permute-done | bytes 196640 | tf_op jit(solution)/shard_map/ppermute | solution.py:246
  31.0 0.4 collective-permute-start.10
  31.4 2.2 %collective-permute-done.3.refs_0_ = bf16[48,3072]{1,0:T(8,128)(2,1)S(1)} collective-permute-done((bf16[48,3072]{1,0:T(8,128)(2,1)S(1)}, bf16[48,3072]{1,0:T(8,128)(2,1)S(1)}, u32[]{:S(2)}, u32[]{:S(2)}) %collective-permute-start.3) | collective-permute-done | bytes 294944 | tf_op jit(solution)/shard_map/ppermute | solution.py:246
  33.6 0.0 collective-permute-done.8
  33.6 0.3 collective-permute-done.9.far_ref
  34.0 1.5 %shard_map.78 = (bf16[32,3072]{1,0:T(8,128)(2,1)S(1)}, bf16[32,3072]{1,0:T(8,128)(2,1)S(1)}) custom-call(bf16[32,3072]{1,0:T(8,128)(2,1)S(1)} %collective-permute-done.6.near_ref, bf16[32,3072]{1,0:T(8,128)(2,1)S(1)} %collective-permute-done.9.far_ref, bf16[1,3072]{1,0:T(2,128)(2,1)S(1)} %get-tuple-element.30.gain_ref, ...), custom_call_target="tpu_custom_call" | custom-call | flops 226492416 | bytes 3538944 | tf_op jit(solution)/shard_map/pallas_call | solution.py:104
  35.4 1.6 %collective-permute-start.11 = (bf16[32,3072]{1,0:T(8,128)(2,1)S(1)}, bf16[32,3072]{1,0:T(8,128)(2,1)S(1)}, u32[]{:S(2)}, u32[]{:S(2)}) collective-permute-start(bf16[32,3072]{1,0:T(8,128)(2,1)S(1)} %get-tuple-element.48), channel_id=1, source_target_pairs={{0,2},{2,0},{4,6},{6,4},{8,10},{10,8},{12,14},{14,12},{16,18},{18,... | collective-permute-start | bytes 589832 | tf_op jit(solution)/shard_map/ppermute | solution.py:246
  37.1 0.1 add_convert_fusion.2
  37.1 0.0 copy-start
  37.1 0.0 copy-start.1
  37.2 2.4 %collective-permute-start.12 = (bf16[32,3072]{1,0:T(8,128)(2,1)S(1)}, bf16[32,3072]{1,0:T(8,128)(2,1)S(1)}, u32[]{:S(2)}, u32[]{:S(2)}) collective-permute-start(bf16[32,3072]{1,0:T(8,128)(2,1)S(1)} %add_convert_fusion.2), channel_id=1, source_target_pairs={{0,8},{2,10},{4,12},{6,14},{8,0},{10,2},{12,4},{14,6},{16,24},{18,... | collective-permute-start | bytes 589832 | tf_op jit(solution)/shard_map/ppermute | solution.py:246
  39.5 0.0 collective-permute-done.10.far_ref
  39.5 1.5 %shard_map.79 = (bf16[32,3072]{1,0:T(8,128)(2,1)S(1)}, bf16[32,3072]{1,0:T(8,128)(2,1)S(1)}) custom-call(bf16[32,3072]{1,0:T(8,128)(2,1)S(1)} %collective-permute-done.5.near_ref, bf16[32,3072]{1,0:T(8,128)(2,1)S(1)} %collective-permute-done.10.far_ref, bf16[1,3072]{1,0:T(2,128)(2,1)S(1)} %get-tuple-element.30.gain_ref, ...), custom_call_target="tpu_custom_call" | custom-call | flops 226492416 | bytes 3538944 | tf_op jit(solution)/shard_map/pallas_call | solution.py:104
  41.0 1.4 %collective-permute-start.14 = (bf16[32,3072]{1,0:T(8,128)(2,1)S(1)}, bf16[32,3072]{1,0:T(8,128)(2,1)S(1)}, u32[]{:S(2)}, u32[]{:S(2)}) collective-permute-start(bf16[32,3072]{1,0:T(8,128)(2,1)S(1)} %get-tuple-element.51), channel_id=1, source_target_pairs={{0,2},{2,0},{4,6},{6,4},{8,10},{10,8},{12,14},{14,12},{16,18},{18,... | collective-permute-start | bytes 589832 | tf_op jit(solution)/shard_map/ppermute | solution.py:246
  42.4 0.1 collective-permute-done.4.refs_1_
  42.5 1.0 %shard_map.76 = (f32[128,3072]{1,0:T(8,128)S(1)}, bf16[128,160]{1,0:T(8,128)(2,1)S(1)}, bf16[32,3072]{1,0:T(8,128)(2,1)S(1)}) custom-call(bf16[1,3072]{1,0:T(2,128)(2,1)S(1)} %get-tuple-element.30.gain_ref, s32[2,128]{1,0:T(2,128)S(1)} %bitcast.22, f32[2,128]{1,0:T(2,128)S(1)} %bitcast.23, bf16[48,3072]{1,0:T(8,128)(2,1)S(1)} %collective-permute-done.3.refs_0_, ...), custom_call_target="tpu_custom_call" | custom-call | flops 3145728 | bytes 2359296 | tf_op jit(solution)/shard_map/pallas_call | solution.py:159
  43.5 0.0 collective-permute-done.11
  43.5 0.1 add_convert_fusion.1
  43.6 4.4 %collective-permute-start.13 = (bf16[32,3072]{1,0:T(8,128)(2,1)S(1)}, bf16[32,3072]{1,0:T(8,128)(2,1)S(1)}, u32[]{:S(2)}, u32[]{:S(2)}) collective-permute-start(bf16[32,3072]{1,0:T(8,128)(2,1)S(1)} %add_convert_fusion.1), channel_id=1, source_target_pairs={{0,12},{2,14},{4,8},{6,10},{8,4},{10,6},{12,0},{14,2},{16,28},{18,... | collective-permute-start | bytes 589832 | tf_op jit(solution)/shard_map/ppermute | solution.py:246
  48.0 0.0 collective-permute-done.14
  48.0 1.5 %collective-permute-start.15 = (bf16[32,3072]{1,0:T(8,128)(2,1)S(1)}, bf16[32,3072]{1,0:T(8,128)(2,1)S(1)}, u32[]{:S(2)}, u32[]{:S(2)}) collective-permute-start(bf16[32,3072]{1,0:T(8,128)(2,1)S(1)} %add_convert_fusion), channel_id=1, source_target_pairs={{0,4},{2,6},{4,0},{6,2},{8,12},{10,14},{12,8},{14,10},{16,20},{18,... | collective-permute-start | bytes 589832 | tf_op jit(solution)/shard_map/ppermute | solution.py:246
  49.5 1.5 %shard_map.80 = (bf16[32,3072]{1,0:T(8,128)(2,1)S(1)}, bf16[32,3072]{1,0:T(8,128)(2,1)S(1)}) custom-call(bf16[32,3072]{1,0:T(8,128)(2,1)S(1)} %get-tuple-element.49.near_ref, bf16[32,3072]{1,0:T(8,128)(2,1)S(1)} %collective-permute-done.1.far_ref, bf16[1,3072]{1,0:T(2,128)(2,1)S(1)} %get-tuple-element.30.gain_ref, ...), custom_call_target="tpu_custom_call" | custom-call | flops 226492416 | bytes 3538944 | tf_op jit(solution)/shard_map/pallas_call | solution.py:104
  51.0 1.4 %collective-permute-start.16 = (bf16[32,3072]{1,0:T(8,128)(2,1)S(1)}, bf16[32,3072]{1,0:T(8,128)(2,1)S(1)}, u32[]{:S(2)}, u32[]{:S(2)}) collective-permute-start(bf16[32,3072]{1,0:T(8,128)(2,1)S(1)} %get-tuple-element.52), channel_id=1, source_target_pairs={{0,2},{2,0},{4,6},{6,4},{8,10},{10,8},{12,14},{14,12},{16,18},{18,... | collective-permute-start | bytes 589832 | tf_op jit(solution)/shard_map/ppermute | solution.py:246
  52.4 0.0 collective-permute-done.12.right_ref
  52.5 0.6 %collective-permute-done.13.refs_1_ = bf16[32,3072]{1,0:T(8,128)(2,1)S(1)} collective-permute-done((bf16[32,3072]{1,0:T(8,128)(2,1)S(1)}, bf16[32,3072]{1,0:T(8,128)(2,1)S(1)}, u32[]{:S(2)}, u32[]{:S(2)}) %collective-permute-start.13) | collective-permute-done | bytes 196640 | tf_op jit(solution)/shard_map/ppermute | solution.py:246
  53.1 2.0 %collective-permute-done.15.refs_2_ = bf16[32,3072]{1,0:T(8,128)(2,1)S(1)} collective-permute-done((bf16[32,3072]{1,0:T(8,128)(2,1)S(1)}, bf16[32,3072]{1,0:T(8,128)(2,1)S(1)}, u32[]{:S(2)}, u32[]{:S(2)}) %collective-permute-start.15) | collective-permute-done | bytes 196640 | tf_op jit(solution)/shard_map/ppermute | solution.py:246
  55.1 1.7 %collective-permute-done.16.refs_3_ = bf16[32,3072]{1,0:T(8,128)(2,1)S(1)} collective-permute-done((bf16[32,3072]{1,0:T(8,128)(2,1)S(1)}, bf16[32,3072]{1,0:T(8,128)(2,1)S(1)}, u32[]{:S(2)}, u32[]{:S(2)}) %collective-permute-start.16) | collective-permute-done | bytes 196640 | tf_op jit(solution)/shard_map/ppermute | solution.py:246
  56.8 1.1 %shard_map.82 = bf16[128,3072]{1,0:T(8,128)(2,1)} custom-call(f32[128,3072]{1,0:T(8,128)S(1)} %get-tuple-element.33.base_ref, bf16[128,160]{1,0:T(8,128)(2,1)S(1)} %get-tuple-element.34.table_ref, f32[32,3072]{1,0:T(8,128)S(1)} %shard_map.81.refs_0_, bf16[32,3072]{1,0:T(8,128)(2,1)S(1)} %collective-permute-done.13.refs_1_, ...), custom_call_target="tpu_custom_call" | custom-call | flops 100663296 | bytes 2359296 | tf_op jit(solution)/shard_map/pallas_call | solution.py:199
  (7 shorter events, 0.1 us)
Async XLA Ops:
  0.0 4.7 %collective-permute-start = (s32[1,128,2]{1,2,0:T(2,128)}, s32[1,128,2]{1,2,0:T(2,128)S(1)}, u32[]{:S(2)}, u32[]{:S(2)}) collective-permute-start(s32[1,128,2]{1,2,0:T(2,128)} %param.12), channel_id=1, source_target_pairs={{0,16},{2,18},{4,20},{6,22},{8,24},{10,26},{12,28},{14,30},{16,0},... | collective-permute-start | bytes 3080 | tf_op jit(solution)/shard_map/ppermute | solution.py:246
  5.1 12.2 %collective-permute-start.2 = (bf16[32,3072]{1,0:T(8,128)(2,1)S(1)}, bf16[32,3072]{1,0:T(8,128)(2,1)S(1)}, u32[]{:S(2)}, u32[]{:S(2)}) collective-permute-start(bf16[32,3072]{1,0:T(8,128)(2,1)S(1)} %shard_map.74), channel_id=1, source_target_pairs={{0,24},{2,26},{4,28},{6,30},{8,16},{10,18},{12,20},{14,22},{16,8},... | collective-permute-start | bytes 589832 | tf_op jit(solution)/shard_map/ppermute | solution.py:246
  9.2 10.2 %collective-permute-start.1 = (bf16[32,3072]{1,0:T(8,128)(2,1)S(1)}, bf16[32,3072]{1,0:T(8,128)(2,1)S(1)}, u32[]{:S(2)}, u32[]{:S(2)}) collective-permute-start(bf16[32,3072]{1,0:T(8,128)(2,1)S(1)} %shard_map.74), channel_id=1, source_target_pairs={{0,18},{2,16},{4,22},{6,20},{8,26},{10,24},{12,30},{14,28},{16,2},... | collective-permute-start | bytes 589832 | tf_op jit(solution)/shard_map/ppermute | solution.py:246
  10.7 8.7 %copy-start.2 = (bf16[1,128,3072]{2,1,0:T(8,128)(2,1)S(1)}, bf16[1,128,3072]{2,1,0:T(8,128)(2,1)}, u32[]{:S(2)}) copy-start(bf16[1,128,3072]{2,1,0:T(8,128)(2,1)} %param.7) | copy-start | bytes 2359300
  17.2 9.0 %collective-permute-start.7 = (bf16[32,3072]{1,0:T(8,128)(2,1)S(1)}, bf16[32,3072]{1,0:T(8,128)(2,1)S(1)}, u32[]{:S(2)}, u32[]{:S(2)}) collective-permute-start(bf16[32,3072]{1,0:T(8,128)(2,1)S(1)} %collective-permute-done.2.near_ref), channel_id=1, source_target_pairs={{0,2},{2,0},{4,6},{6,4},{8,10},{10,8},{12,14},{14,12},{16,18},{18,... | collective-permute-start | bytes 589832 | tf_op jit(solution)/shard_map/ppermute | solution.py:246
  18.8 7.5 %collective-permute-start.6 = (bf16[32,3072]{1,0:T(8,128)(2,1)S(1)}, bf16[32,3072]{1,0:T(8,128)(2,1)S(1)}, u32[]{:S(2)}, u32[]{:S(2)}) collective-permute-start(bf16[32,3072]{1,0:T(8,128)(2,1)S(1)} %collective-permute-done.2.near_ref), channel_id=1, source_target_pairs={{0,4},{2,6},{4,0},{6,2},{8,12},{10,14},{12,8},{14,10},{16,20},{18,... | collective-permute-start | bytes 589832 | tf_op jit(solution)/shard_map/ppermute | solution.py:246
  19.4 14.2 %collective-permute-start.3 = (bf16[48,3072]{1,0:T(8,128)(2,1)S(1)}, bf16[48,3072]{1,0:T(8,128)(2,1)S(1)}, u32[]{:S(2)}, u32[]{:S(2)}) collective-permute-start(bf16[48,3072]{1,0:T(8,128)(2,1)S(1)} %slice_bitcast_fusion.1), channel_id=1, source_target_pairs={{0,16},{2,18},{4,20},{6,22},{8,24},{10,26},{12,28},{14,30},{16,0},... | collective-permute-start | bytes 884744 | tf_op jit(solution)/shard_map/ppermute | solution.py:246
  20.3 10.8 %collective-permute-start.5 = (bf16[32,3072]{1,0:T(8,128)(2,1)S(1)}, bf16[32,3072]{1,0:T(8,128)(2,1)S(1)}, u32[]{:S(2)}, u32[]{:S(2)}) collective-permute-start(bf16[32,3072]{1,0:T(8,128)(2,1)S(1)} %shard_map.74), channel_id=1, source_target_pairs={{0,20},{2,22},{4,16},{6,18},{8,28},{10,30},{12,24},{14,26},{16,4},... | collective-permute-start | bytes 589832 | tf_op jit(solution)/shard_map/ppermute | solution.py:246
  27.8 5.9 %collective-permute-start.8 = (bf16[32,3072]{1,0:T(8,128)(2,1)S(1)}, bf16[32,3072]{1,0:T(8,128)(2,1)S(1)}, u32[]{:S(2)}, u32[]{:S(2)}) collective-permute-start(bf16[32,3072]{1,0:T(8,128)(2,1)S(1)} %get-tuple-element.41), channel_id=1, source_target_pairs={{0,2},{2,0},{4,6},{6,4},{8,10},{10,8},{12,14},{14,12},{16,18},{18,... | collective-permute-start | bytes 589832 | tf_op jit(solution)/shard_map/ppermute | solution.py:246
  28.3 5.7 %collective-permute-start.9 = (bf16[32,3072]{1,0:T(8,128)(2,1)S(1)}, bf16[32,3072]{1,0:T(8,128)(2,1)S(1)}, u32[]{:S(2)}, u32[]{:S(2)}) collective-permute-start(bf16[32,3072]{1,0:T(8,128)(2,1)S(1)} %collective-permute-done.7.far_ref), channel_id=1, source_target_pairs={{0,4},{2,6},{4,0},{6,2},{8,12},{10,14},{12,8},{14,10},{16,20},{18,... | collective-permute-start | bytes 589832 | tf_op jit(solution)/shard_map/ppermute | solution.py:246
  29.3 13.2 %collective-permute-start.4 = (bf16[80,3072]{1,0:T(8,128)(2,1)S(1)}, bf16[80,3072]{1,0:T(8,128)(2,1)S(1)}, u32[]{:S(2)}, u32[]{:S(2)}) collective-permute-start(bf16[80,3072]{1,0:T(8,128)(2,1)S(1)} %slice_bitcast_fusion), channel_id=1, source_target_pairs={{0,16},{2,18},{4,20},{6,22},{8,24},{10,26},{12,28},{14,30},{16,0},... | collective-permute-start | bytes 1474568 | tf_op jit(solution)/shard_map/ppermute | solution.py:246
  31.0 8.5 %collective-permute-start.10 = (bf16[32,3072]{1,0:T(8,128)(2,1)S(1)}, bf16[32,3072]{1,0:T(8,128)(2,1)S(1)}, u32[]{:S(2)}, u32[]{:S(2)}) collective-permute-start(bf16[32,3072]{1,0:T(8,128)(2,1)S(1)} %collective-permute-done.5.near_ref), channel_id=1, source_target_pairs={{0,2},{2,0},{4,6},{6,4},{8,10},{10,8},{12,14},{14,12},{16,18},{18,... | collective-permute-start | bytes 589832 | tf_op jit(solution)/shard_map/ppermute | solution.py:246
  35.4 8.1 %collective-permute-start.11 = (bf16[32,3072]{1,0:T(8,128)(2,1)S(1)}, bf16[32,3072]{1,0:T(8,128)(2,1)S(1)}, u32[]{:S(2)}, u32[]{:S(2)}) collective-permute-start(bf16[32,3072]{1,0:T(8,128)(2,1)S(1)} %get-tuple-element.48), channel_id=1, source_target_pairs={{0,2},{2,0},{4,6},{6,4},{8,10},{10,8},{12,14},{14,12},{16,18},{18,... | collective-permute-start | bytes 589832 | tf_op jit(solution)/shard_map/ppermute | solution.py:246
  37.1 5.4 %copy-start = (s32[1,128,2]{1,2,0:T(2,128)S(1)}, s32[1,128,2]{1,2,0:T(2,128)}, u32[]{:S(2)}) copy-start(s32[1,128,2]{1,2,0:T(2,128)} %param.12) | copy-start | bytes 3076
  37.1 5.4 %copy-start.1 = (f32[1,128,2]{1,2,0:T(2,128)S(1)}, f32[1,128,2]{1,2,0:T(2,128)}, u32[]{:S(2)}) copy-start(f32[1,128,2]{1,2,0:T(2,128)} %param.13) | copy-start | bytes 3076
  37.2 15.3 %collective-permute-start.12 = (bf16[32,3072]{1,0:T(8,128)(2,1)S(1)}, bf16[32,3072]{1,0:T(8,128)(2,1)S(1)}, u32[]{:S(2)}, u32[]{:S(2)}) collective-permute-start(bf16[32,3072]{1,0:T(8,128)(2,1)S(1)} %add_convert_fusion.2), channel_id=1, source_target_pairs={{0,8},{2,10},{4,12},{6,14},{8,0},{10,2},{12,4},{14,6},{16,24},{18,... | collective-permute-start | bytes 589832 | tf_op jit(solution)/shard_map/ppermute | solution.py:246
  41.0 7.0 %collective-permute-start.14 = (bf16[32,3072]{1,0:T(8,128)(2,1)S(1)}, bf16[32,3072]{1,0:T(8,128)(2,1)S(1)}, u32[]{:S(2)}, u32[]{:S(2)}) collective-permute-start(bf16[32,3072]{1,0:T(8,128)(2,1)S(1)} %get-tuple-element.51), channel_id=1, source_target_pairs={{0,2},{2,0},{4,6},{6,4},{8,10},{10,8},{12,14},{14,12},{16,18},{18,... | collective-permute-start | bytes 589832 | tf_op jit(solution)/shard_map/ppermute | solution.py:246
  43.6 9.5 %collective-permute-start.13 = (bf16[32,3072]{1,0:T(8,128)(2,1)S(1)}, bf16[32,3072]{1,0:T(8,128)(2,1)S(1)}, u32[]{:S(2)}, u32[]{:S(2)}) collective-permute-start(bf16[32,3072]{1,0:T(8,128)(2,1)S(1)} %add_convert_fusion.1), channel_id=1, source_target_pairs={{0,12},{2,14},{4,8},{6,10},{8,4},{10,6},{12,0},{14,2},{16,28},{18,... | collective-permute-start | bytes 589832 | tf_op jit(solution)/shard_map/ppermute | solution.py:246
  48.0 7.1 %collective-permute-start.15 = (bf16[32,3072]{1,0:T(8,128)(2,1)S(1)}, bf16[32,3072]{1,0:T(8,128)(2,1)S(1)}, u32[]{:S(2)}, u32[]{:S(2)}) collective-permute-start(bf16[32,3072]{1,0:T(8,128)(2,1)S(1)} %add_convert_fusion), channel_id=1, source_target_pairs={{0,4},{2,6},{4,0},{6,2},{8,12},{10,14},{12,8},{14,10},{16,20},{18,... | collective-permute-start | bytes 589832 | tf_op jit(solution)/shard_map/ppermute | solution.py:246
  51.0 5.7 %collective-permute-start.16 = (bf16[32,3072]{1,0:T(8,128)(2,1)S(1)}, bf16[32,3072]{1,0:T(8,128)(2,1)S(1)}, u32[]{:S(2)}, u32[]{:S(2)}) collective-permute-start(bf16[32,3072]{1,0:T(8,128)(2,1)S(1)} %get-tuple-element.52), channel_id=1, source_target_pairs={{0,2},{2,0},{4,6},{6,4},{8,10},{10,8},{12,14},{14,12},{16,18},{18,... | collective-permute-start | bytes 589832 | tf_op jit(solution)/shard_map/ppermute | solution.py:246

commit v14 on v12

--- a/solution.py
+++ b/solution.py
@@ -163,28 +163,36 @@
     )(gain, ids_t, weights_t, *blocks)
 
 
-def end_kernel(columns, base_ref, table_ref, *refs):
-    back_refs, out_ref = refs[:-1], refs[-1]
-    here = pl.ds(pl.multiple_of(pl.program_id(0) * columns, columns), columns)
-    total = back_refs[0][:, here].astype(jnp.float32)
-    for ref in back_refs[1:]:
-        total = total + ref[:, here].astype(jnp.float32)
-    high, low, _ = parts_of(total)
-    rows = jnp.concatenate([high, high, high, low, low], axis=0)
-    added = jnp.dot(table_ref[...], rows, preferred_element_type=jnp.float32)
-    out_ref[...] = (base_ref[:, here] + added).astype(jnp.bfloat16)
+def end_kernel(steps, base_ref, table_ref, *refs):
+    back_refs, (out_ref, done, sems) = refs[:-3], refs[-3:]
+    columns = base_ref.shape[1] // steps
+    copies = []
+    for step in range(steps):
+        here = slice(step * columns, (step + 1) * columns)
+        total = back_refs[0][:, here].astype(jnp.float32)
+        for ref in back_refs[1:]:
+            total = total + ref[:, here].astype(jnp.float32)
+        high, low, _ = parts_of(total)
+        rows = jnp.concatenate([high, high, high, low, low], axis=0)
+        added = jnp.dot(table_ref[...], rows, preferred_element_type=jnp.float32)
+        done[:, here] = (base_ref[:, here] + added).astype(jnp.bfloat16)
+        copies.append(
+            pltpu.make_async_copy(done.at[:, here], out_ref.at[:, here], sems.at[step])
+        )
+        copies[-1].start()
+    for copy in copies:
+        copy.wait()
 
 
 def ended(base, table, backs):
     count, width = base.shape
-    steps = 3
-    columns = width // steps
-    return pl.pallas_call(
-        functools.partial(end_kernel, columns),
+    steps = 6
+    return pl.pallas_call(
+        functools.partial(end_kernel, steps),
         out_shape=jax.ShapeDtypeStruct((count, width), jnp.bfloat16),
-        grid=(steps,),
         in_specs=[VMEM] * (2 + len(backs)),
-        out_specs=pl.BlockSpec((count, columns), lambda i: (0, i)),
+        out_specs=HBM,
+        scratch_shapes=[pltpu.VMEM((count, width), jnp.bfloat16), pltpu.SemaphoreType.DMA((steps,))],
         compiler_params=PARAMS,
         cost_estimate=pl.CostEstimate(
             flops=2 * count * width * table.shape[0], bytes_accessed=6 * count * width,

time: 57.8 us -> 57 us (0.986)
  Pallas kernels: 11.5 us -> 10.8 us
    pallas_call x1, Pallas kernels: 1.88 us -> 1.14 us  [ended(): pl.pallas_call(functools.partial(end_kernel, steps), out_shape=jax.ShapeD...]
where the time goes in v14:
time: 57 us; the launch traced here: 56.9 us
  starting transfers between devices  27.7 us (49%)
  waiting for transfers between devices  18 us (32%)
  Pallas kernels  10.8 us (19%)
    ppermute x17, starting transfers between devices, moved(): return lax.ppermute(value, ('section', 'expert'), pairs)  27.7 us
    ppermute x17, waiting for transfers between devices, moved(): return lax.ppermute(value, ('section', 'expert'), pairs)  18 us
    pallas_call x4, Pallas kernels, mlp(): pl.pallas_call(mlp_kernel, out_shape=(out, out), in_specs=[VMEM] * 6, out...  5.04 us
    pallas_call x2, Pallas kernels, loaded(): pl.pallas_call(functools.partial(load_kernel, len(arrays)), out_shape=tup...  3.23 us
    pallas_call x1, Pallas kernels, ended(): pl.pallas_call(functools.partial(end_kernel, steps), out_shape=jax.ShapeD...  1.14 us
  transfers between devices with their start and end apart: 17, of which 10 were waited for; matrix products, arithmetic and copies ran while one was open for 0% of the time, Pallas kernels for 16%

profile of v14, /device:TPU:0, one launch (start us, length us, event | category | flops | bytes accessed | tf_op | source)
XLA Modules:
  0.0 56.9 jit_solution(16983381379574318983)
XLA Ops:
  0.0 2.9 %collective-permute-start = (s32[1,128,2]{1,2,0:T(2,128)}, s32[1,128,2]{1,2,0:T(2,128)S(1)}, u32[]{:S(2)}, u32[]{:S(2)}) collective-permute-start(s32[1,128,2]{1,2,0:T(2,128)} %param.12), channel_id=1, source_target_pairs={{0,16},{2,18},{4,20},{6,22},{8,24},{10,26},{12,28},{14,30},{16,0},... | collective-permute-start | bytes 3080 | tf_op jit(solution)/shard_map/ppermute | solution.py:237
  2.9 1.1 %shard_map.73.block_ref = bf16[128,3072]{1,0:T(8,128)(2,1)S(1)} custom-call(bf16[128,3072]{1,0:T(8,128)(2,1)} %bitcast.25), custom_call_target="tpu_custom_call" | custom-call | bytes 6291456 | tf_op jit(solution)/shard_map/pallas_call | solution.py:33
  4.1 0.6 %collective-permute-done = s32[1,128,2]{1,2,0:T(2,128)S(1)} collective-permute-done((s32[1,128,2]{1,2,0:T(2,128)}, s32[1,128,2]{1,2,0:T(2,128)S(1)}, u32[]{:S(2)}, u32[]{:S(2)}) %collective-permute-start) | collective-permute-done | bytes 1056 | tf_op jit(solution)/shard_map/ppermute | solution.py:237
  4.7 0.4 shard_map.74
  5.1 4.1 %collective-permute-start.2 = (bf16[32,3072]{1,0:T(8,128)(2,1)S(1)}, bf16[32,3072]{1,0:T(8,128)(2,1)S(1)}, u32[]{:S(2)}, u32[]{:S(2)}) collective-permute-start(bf16[32,3072]{1,0:T(8,128)(2,1)S(1)} %shard_map.74), channel_id=1, source_target_pairs={{0,24},{2,26},{4,28},{6,30},{8,16},{10,18},{12,20},{14,22},{16,8},... | collective-permute-start | bytes 589832 | tf_op jit(solution)/shard_map/ppermute | solution.py:237
  9.2 1.5 %collective-permute-start.1 = (bf16[32,3072]{1,0:T(8,128)(2,1)S(1)}, bf16[32,3072]{1,0:T(8,128)(2,1)S(1)}, u32[]{:S(2)}, u32[]{:S(2)}) collective-permute-start(bf16[32,3072]{1,0:T(8,128)(2,1)S(1)} %shard_map.74), channel_id=1, source_target_pairs={{0,18},{2,16},{4,22},{6,20},{8,26},{10,24},{12,30},{14,28},{16,2},... | collective-permute-start | bytes 589832 | tf_op jit(solution)/shard_map/ppermute | solution.py:237
  10.7 2.1 %shard_map.75 = (bf16[192,3072]{1,0:T(8,128)(2,1)S(1)}, bf16[192,3072]{1,0:T(8,128)(2,1)S(1)}, bf16[192,3072]{1,0:T(8,128)(2,1)S(1)}, bf16[1,3072]{1,0:T(2,128)(2,1)S(1)}) custom-call(bf16[192,3072]{1,0:T(8,128)(2,1)} %bitcast.26, bf16[192,3072]{1,0:T(8,128)(2,1)} %bitcast.27, bf16[192,3072]{1,0:T(8,128)(2,1)} %bitcast.28, bf16[1,3072]{1,0:T(2,128)(2,1)} %refs_3_.1), custom_call_target="tpu_custom_call" | custom-call | bytes 6291456 | tf_op jit(solution)/shard_map/pallas_call | solution.py:33
  12.8 4.5 %collective-permute-done.2.near_ref = bf16[32,3072]{1,0:T(8,128)(2,1)S(1)} collective-permute-done((bf16[32,3072]{1,0:T(8,128)(2,1)S(1)}, bf16[32,3072]{1,0:T(8,128)(2,1)S(1)}, u32[]{:S(2)}, u32[]{:S(2)}) %collective-permute-start.2) | collective-permute-done | bytes 196640 | tf_op jit(solution)/shard_map/ppermute | solution.py:237
  17.2 1.5 %collective-permute-start.7 = (bf16[32,3072]{1,0:T(8,128)(2,1)S(1)}, bf16[32,3072]{1,0:T(8,128)(2,1)S(1)}, u32[]{:S(2)}, u32[]{:S(2)}) collective-permute-start(bf16[32,3072]{1,0:T(8,128)(2,1)S(1)} %collective-permute-done.2.near_ref), channel_id=1, source_target_pairs={{0,2},{2,0},{4,6},{6,4},{8,10},{10,8},{12,14},{14,12},{16,18},{18,... | collective-permute-start | bytes 589832 | tf_op jit(solution)/shard_map/ppermute | solution.py:237
  18.8 0.6 %collective-permute-start.6 = (bf16[32,3072]{1,0:T(8,128)(2,1)S(1)}, bf16[32,3072]{1,0:T(8,128)(2,1)S(1)}, u32[]{:S(2)}, u32[]{:S(2)}) collective-permute-start(bf16[32,3072]{1,0:T(8,128)(2,1)S(1)} %collective-permute-done.2.near_ref), channel_id=1, source_target_pairs={{0,4},{2,6},{4,0},{6,2},{8,12},{10,14},{12,8},{14,10},{16,20},{18,... | collective-permute-start | bytes 589832 | tf_op jit(solution)/shard_map/ppermute | solution.py:237
  19.4 0.0 copy-done.2
  19.4 0.0 collective-permute-done.1.far_ref
  19.4 0.9 %collective-permute-start.3 = (bf16[48,3072]{1,0:T(8,128)(2,1)S(1)}, bf16[48,3072]{1,0:T(8,128)(2,1)S(1)}, u32[]{:S(2)}, u32[]{:S(2)}) collective-permute-start(bf16[48,3072]{1,0:T(8,128)(2,1)S(1)} %slice_bitcast_fusion.1), channel_id=1, source_target_pairs={{0,16},{2,18},{4,20},{6,22},{8,24},{10,26},{12,28},{14,30},{16,0},... | collective-permute-start | bytes 884744 | tf_op jit(solution)/shard_map/ppermute | solution.py:237
  20.3 2.1 %collective-permute-start.5 = (bf16[32,3072]{1,0:T(8,128)(2,1)S(1)}, bf16[32,3072]{1,0:T(8,128)(2,1)S(1)}, u32[]{:S(2)}, u32[]{:S(2)}) collective-permute-start(bf16[32,3072]{1,0:T(8,128)(2,1)S(1)} %shard_map.74), channel_id=1, source_target_pairs={{0,20},{2,22},{4,16},{6,18},{8,28},{10,30},{12,24},{14,26},{16,4},... | collective-permute-start | bytes 589832 | tf_op jit(solution)/shard_map/ppermute | solution.py:237
  22.4 3.9 %collective-permute-done.6.near_ref = bf16[32,3072]{1,0:T(8,128)(2,1)S(1)} collective-permute-done((bf16[32,3072]{1,0:T(8,128)(2,1)S(1)}, bf16[32,3072]{1,0:T(8,128)(2,1)S(1)}, u32[]{:S(2)}, u32[]{:S(2)}) %collective-permute-start.6) | collective-permute-done | bytes 196640 | tf_op jit(solution)/shard_map/ppermute | solution.py:237
  26.3 0.0 collective-permute-done.7.far_ref
  26.3 1.3 %shard_map.77 = (bf16[32,3072]{1,0:T(8,128)(2,1)S(1)}, bf16[32,3072]{1,0:T(8,128)(2,1)S(1)}) custom-call(bf16[32,3072]{1,0:T(8,128)(2,1)S(1)} %collective-permute-done.2.near_ref, bf16[32,3072]{1,0:T(8,128)(2,1)S(1)} %collective-permute-done.7.far_ref, bf16[1,3072]{1,0:T(2,128)(2,1)S(1)} %get-tuple-element.31.gain_ref, ...), custom_call_target="tpu_custom_call" | custom-call | flops 226492416 | bytes 3538944 | tf_op jit(solution)/shard_map/pallas_call | solution.py:95
  27.5 0.5 collective-permute-start.8
  28.1 1.0 %collective-permute-start.9 = (bf16[32,3072]{1,0:T(8,128)(2,1)S(1)}, bf16[32,3072]{1,0:T(8,128)(2,1)S(1)}, u32[]{:S(2)}, u32[]{:S(2)}) collective-permute-start(bf16[32,3072]{1,0:T(8,128)(2,1)S(1)} %collective-permute-done.7.far_ref), channel_id=1, source_target_pairs={{0,4},{2,6},{4,0},{6,2},{8,12},{10,14},{12,8},{14,10},{16,20},{18,... | collective-permute-start | bytes 589832 | tf_op jit(solution)/shard_map/ppermute | solution.py:237
  29.1 0.6 %collective-permute-start.4 = (bf16[80,3072]{1,0:T(8,128)(2,1)S(1)}, bf16[80,3072]{1,0:T(8,128)(2,1)S(1)}, u32[]{:S(2)}, u32[]{:S(2)}) collective-permute-start(bf16[80,3072]{1,0:T(8,128)(2,1)S(1)} %slice_bitcast_fusion), channel_id=1, source_target_pairs={{0,16},{2,18},{4,20},{6,22},{8,24},{10,26},{12,28},{14,30},{16,0},... | collective-permute-start | bytes 1474568 | tf_op jit(solution)/shard_map/ppermute | solution.py:237
  29.7 1.6 %collective-permute-done.5.near_ref = bf16[32,3072]{1,0:T(8,128)(2,1)S(1)} collective-permute-done((bf16[32,3072]{1,0:T(8,128)(2,1)S(1)}, bf16[32,3072]{1,0:T(8,128)(2,1)S(1)}, u32[]{:S(2)}, u32[]{:S(2)}) %collective-permute-start.5) | collective-permute-done | bytes 196640 | tf_op jit(solution)/shard_map/ppermute | solution.py:237
  31.3 0.0 collective-permute-start.10
  31.3 2.4 %collective-permute-done.3.refs_0_ = bf16[48,3072]{1,0:T(8,128)(2,1)S(1)} collective-permute-done((bf16[48,3072]{1,0:T(8,128)(2,1)S(1)}, bf16[48,3072]{1,0:T(8,128)(2,1)S(1)}, u32[]{:S(2)}, u32[]{:S(2)}) %collective-permute-start.3) | collective-permute-done | bytes 294944 | tf_op jit(solution)/shard_map/ppermute | solution.py:237
  33.6 0.0 collective-permute-done.8
  33.6 0.1 collective-permute-done.9.far_ref
  33.7 1.3 %shard_map.78 = (bf16[32,3072]{1,0:T(8,128)(2,1)S(1)}, bf16[32,3072]{1,0:T(8,128)(2,1)S(1)}) custom-call(bf16[32,3072]{1,0:T(8,128)(2,1)S(1)} %collective-permute-done.6.near_ref, bf16[32,3072]{1,0:T(8,128)(2,1)S(1)} %collective-permute-done.9.far_ref, bf16[1,3072]{1,0:T(2,128)(2,1)S(1)} %get-tuple-element.31.gain_ref, ...), custom_call_target="tpu_custom_call" | custom-call | flops 226492416 | bytes 3538944 | tf_op jit(solution)/shard_map/pallas_call | solution.py:95
  35.0 1.6 %collective-permute-start.11 = (bf16[32,3072]{1,0:T(8,128)(2,1)S(1)}, bf16[32,3072]{1,0:T(8,128)(2,1)S(1)}, u32[]{:S(2)}, u32[]{:S(2)}) collective-permute-start(bf16[32,3072]{1,0:T(8,128)(2,1)S(1)} %get-tuple-element.50), channel_id=1, source_target_pairs={{0,2},{2,0},{4,6},{6,4},{8,10},{10,8},{12,14},{14,12},{16,18},{18,... | collective-permute-start | bytes 589832 | tf_op jit(solution)/shard_map/ppermute | solution.py:237
  36.6 0.1 add_convert_fusion.2
  36.7 0.0 copy-start
  36.7 0.0 copy-start.1
  36.7 2.4 %collective-permute-start.12 = (bf16[32,3072]{1,0:T(8,128)(2,1)S(1)}, bf16[32,3072]{1,0:T(8,128)(2,1)S(1)}, u32[]{:S(2)}, u32[]{:S(2)}) collective-permute-start(bf16[32,3072]{1,0:T(8,128)(2,1)S(1)} %add_convert_fusion.2), channel_id=1, source_target_pairs={{0,8},{2,10},{4,12},{6,14},{8,0},{10,2},{12,4},{14,6},{16,24},{18,... | collective-permute-start | bytes 589832 | tf_op jit(solution)/shard_map/ppermute | solution.py:237
  39.1 0.0 collective-permute-done.10.far_ref
  39.1 1.3 %shard_map.79 = (bf16[32,3072]{1,0:T(8,128)(2,1)S(1)}, bf16[32,3072]{1,0:T(8,128)(2,1)S(1)}) custom-call(bf16[32,3072]{1,0:T(8,128)(2,1)S(1)} %collective-permute-done.5.near_ref, bf16[32,3072]{1,0:T(8,128)(2,1)S(1)} %collective-permute-done.10.far_ref, bf16[1,3072]{1,0:T(2,128)(2,1)S(1)} %get-tuple-element.31.gain_ref, ...), custom_call_target="tpu_custom_call" | custom-call | flops 226492416 | bytes 3538944 | tf_op jit(solution)/shard_map/pallas_call | solution.py:95
  40.4 1.5 %collective-permute-start.14 = (bf16[32,3072]{1,0:T(8,128)(2,1)S(1)}, bf16[32,3072]{1,0:T(8,128)(2,1)S(1)}, u32[]{:S(2)}, u32[]{:S(2)}) collective-permute-start(bf16[32,3072]{1,0:T(8,128)(2,1)S(1)} %get-tuple-element.53), channel_id=1, source_target_pairs={{0,2},{2,0},{4,6},{6,4},{8,10},{10,8},{12,14},{14,12},{16,18},{18,... | collective-permute-start | bytes 589832 | tf_op jit(solution)/shard_map/ppermute | solution.py:237
  41.8 0.7 %collective-permute-done.4.refs_1_ = bf16[80,3072]{1,0:T(8,128)(2,1)S(1)} collective-permute-done((bf16[80,3072]{1,0:T(8,128)(2,1)S(1)}, bf16[80,3072]{1,0:T(8,128)(2,1)S(1)}, u32[]{:S(2)}, u32[]{:S(2)}) %collective-permute-start.4) | collective-permute-done | bytes 491552 | tf_op jit(solution)/shard_map/ppermute | solution.py:237
  42.5 1.0 %shard_map.76 = (f32[128,3072]{1,0:T(8,128)S(1)}, bf16[128,160]{1,0:T(8,128)(2,1)S(1)}, bf16[32,3072]{1,0:T(8,128)(2,1)S(1)}) custom-call(bf16[1,3072]{1,0:T(2,128)(2,1)S(1)} %get-tuple-element.31.gain_ref, s32[2,128]{1,0:T(2,128)S(1)} %bitcast.22, f32[2,128]{1,0:T(2,128)S(1)} %bitcast.23, bf16[48,3072]{1,0:T(8,128)(2,1)S(1)} %collective-permute-done.3.refs_0_, ...), custom_call_target="tpu_custom_call" | custom-call | flops 3145728 | bytes 2359296 | tf_op jit(solution)/shard_map/pallas_call | solution.py:150
  43.5 0.0 collective-permute-done.11
  43.5 0.1 add_convert_fusion.1
  43.6 4.2 %collective-permute-start.13 = (bf16[32,3072]{1,0:T(8,128)(2,1)S(1)}, bf16[32,3072]{1,0:T(8,128)(2,1)S(1)}, u32[]{:S(2)}, u32[]{:S(2)}) collective-permute-start(bf16[32,3072]{1,0:T(8,128)(2,1)S(1)} %add_convert_fusion.1), channel_id=1, source_target_pairs={{0,12},{2,14},{4,8},{6,10},{8,4},{10,6},{12,0},{14,2},{16,28},{18,... | collective-permute-start | bytes 589832 | tf_op jit(solution)/shard_map/ppermute | solution.py:237
  47.7 0.0 collective-permute-done.14
  47.8 0.9 %collective-permute-start.15 = (bf16[32,3072]{1,0:T(8,128)(2,1)S(1)}, bf16[32,3072]{1,0:T(8,128)(2,1)S(1)}, u32[]{:S(2)}, u32[]{:S(2)}) collective-permute-start(bf16[32,3072]{1,0:T(8,128)(2,1)S(1)} %add_convert_fusion), channel_id=1, source_target_pairs={{0,4},{2,6},{4,0},{6,2},{8,12},{10,14},{12,8},{14,10},{16,20},{18,... | collective-permute-start | bytes 589832 | tf_op jit(solution)/shard_map/ppermute | solution.py:237
  48.7 1.3 %shard_map.80 = (bf16[32,3072]{1,0:T(8,128)(2,1)S(1)}, bf16[32,3072]{1,0:T(8,128)(2,1)S(1)}) custom-call(bf16[32,3072]{1,0:T(8,128)(2,1)S(1)} %get-tuple-element.51.near_ref, bf16[32,3072]{1,0:T(8,128)(2,1)S(1)} %collective-permute-done.1.far_ref, bf16[1,3072]{1,0:T(2,128)(2,1)S(1)} %get-tuple-element.31.gain_ref, ...), custom_call_target="tpu_custom_call" | custom-call | flops 226492416 | bytes 3538944 | tf_op jit(solution)/shard_map/pallas_call | solution.py:95
  50.0 1.4 %collective-permute-start.16 = (bf16[32,3072]{1,0:T(8,128)(2,1)S(1)}, bf16[32,3072]{1,0:T(8,128)(2,1)S(1)}, u32[]{:S(2)}, u32[]{:S(2)}) collective-permute-start(bf16[32,3072]{1,0:T(8,128)(2,1)S(1)} %get-tuple-element.54), channel_id=1, source_target_pairs={{0,2},{2,0},{4,6},{6,4},{8,10},{10,8},{12,14},{14,12},{16,18},{18,... | collective-permute-start | bytes 589832 | tf_op jit(solution)/shard_map/ppermute | solution.py:237
  51.4 0.0 collective-permute-done.12.right_ref
  51.4 1.7 %collective-permute-done.13.refs_1_ = bf16[32,3072]{1,0:T(8,128)(2,1)S(1)} collective-permute-done((bf16[32,3072]{1,0:T(8,128)(2,1)S(1)}, bf16[32,3072]{1,0:T(8,128)(2,1)S(1)}, u32[]{:S(2)}, u32[]{:S(2)}) %collective-permute-start.13) | collective-permute-done | bytes 196640 | tf_op jit(solution)/shard_map/ppermute | solution.py:237
  53.1 2.0 %collective-permute-done.15.refs_2_ = bf16[32,3072]{1,0:T(8,128)(2,1)S(1)} collective-permute-done((bf16[32,3072]{1,0:T(8,128)(2,1)S(1)}, bf16[32,3072]{1,0:T(8,128)(2,1)S(1)}, u32[]{:S(2)}, u32[]{:S(2)}) %collective-permute-start.15) | collective-permute-done | bytes 196640 | tf_op jit(solution)/shard_map/ppermute | solution.py:237
  55.1 0.6 %collective-permute-done.16.refs_3_ = bf16[32,3072]{1,0:T(8,128)(2,1)S(1)} collective-permute-done((bf16[32,3072]{1,0:T(8,128)(2,1)S(1)}, bf16[32,3072]{1,0:T(8,128)(2,1)S(1)}, u32[]{:S(2)}, u32[]{:S(2)}) %collective-permute-start.16) | collective-permute-done | bytes 196640 | tf_op jit(solution)/shard_map/ppermute | solution.py:237
  55.7 1.1 %shard_map.82 = bf16[128,3072]{1,0:T(8,128)(2,1)} custom-call(f32[128,3072]{1,0:T(8,128)S(1)} %get-tuple-element.34.base_ref, bf16[128,160]{1,0:T(8,128)(2,1)S(1)} %get-tuple-element.35.table_ref, f32[32,3072]{1,0:T(8,128)S(1)} %shard_map.81.refs_0_, bf16[32,3072]{1,0:T(8,128)(2,1)S(1)} %collective-permute-done.13.refs_1_, ...), custom_call_target="tpu_custom_call" | custom-call | flops 100663296 | bytes 2359296 | tf_op jit(solution)/shard_map/pallas_call | solution.py:190
  (7 shorter events, 0.1 us)
Async XLA Ops:
  0.0 4.7 %collective-permute-start = (s32[1,128,2]{1,2,0:T(2,128)}, s32[1,128,2]{1,2,0:T(2,128)S(1)}, u32[]{:S(2)}, u32[]{:S(2)}) collective-permute-start(s32[1,128,2]{1,2,0:T(2,128)} %param.12), channel_id=1, source_target_pairs={{0,16},{2,18},{4,20},{6,22},{8,24},{10,26},{12,28},{14,30},{16,0},... | collective-permute-start | bytes 3080 | tf_op jit(solution)/shard_map/ppermute | solution.py:237
  5.1 12.2 %collective-permute-start.2 = (bf16[32,3072]{1,0:T(8,128)(2,1)S(1)}, bf16[32,3072]{1,0:T(8,128)(2,1)S(1)}, u32[]{:S(2)}, u32[]{:S(2)}) collective-permute-start(bf16[32,3072]{1,0:T(8,128)(2,1)S(1)} %shard_map.74), channel_id=1, source_target_pairs={{0,24},{2,26},{4,28},{6,30},{8,16},{10,18},{12,20},{14,22},{16,8},... | collective-permute-start | bytes 589832 | tf_op jit(solution)/shard_map/ppermute | solution.py:237
  9.2 10.2 %collective-permute-start.1 = (bf16[32,3072]{1,0:T(8,128)(2,1)S(1)}, bf16[32,3072]{1,0:T(8,128)(2,1)S(1)}, u32[]{:S(2)}, u32[]{:S(2)}) collective-permute-start(bf16[32,3072]{1,0:T(8,128)(2,1)S(1)} %shard_map.74), channel_id=1, source_target_pairs={{0,18},{2,16},{4,22},{6,20},{8,26},{10,24},{12,30},{14,28},{16,2},... | collective-permute-start | bytes 589832 | tf_op jit(solution)/shard_map/ppermute | solution.py:237
  10.7 8.7 %copy-start.2 = (bf16[1,128,3072]{2,1,0:T(8,128)(2,1)S(1)}, bf16[1,128,3072]{2,1,0:T(8,128)(2,1)}, u32[]{:S(2)}) copy-start(bf16[1,128,3072]{2,1,0:T(8,128)(2,1)} %param.7) | copy-start | bytes 2359300
  17.2 9.0 %collective-permute-start.7 = (bf16[32,3072]{1,0:T(8,128)(2,1)S(1)}, bf16[32,3072]{1,0:T(8,128)(2,1)S(1)}, u32[]{:S(2)}, u32[]{:S(2)}) collective-permute-start(bf16[32,3072]{1,0:T(8,128)(2,1)S(1)} %collective-permute-done.2.near_ref), channel_id=1, source_target_pairs={{0,2},{2,0},{4,6},{6,4},{8,10},{10,8},{12,14},{14,12},{16,18},{18,... | collective-permute-start | bytes 589832 | tf_op jit(solution)/shard_map/ppermute | solution.py:237
  18.8 7.5 %collective-permute-start.6 = (bf16[32,3072]{1,0:T(8,128)(2,1)S(1)}, bf16[32,3072]{1,0:T(8,128)(2,1)S(1)}, u32[]{:S(2)}, u32[]{:S(2)}) collective-permute-start(bf16[32,3072]{1,0:T(8,128)(2,1)S(1)} %collective-permute-done.2.near_ref), channel_id=1, source_target_pairs={{0,4},{2,6},{4,0},{6,2},{8,12},{10,14},{12,8},{14,10},{16,20},{18,... | collective-permute-start | bytes 589832 | tf_op jit(solution)/shard_map/ppermute | solution.py:237
  19.4 14.2 %collective-permute-start.3 = (bf16[48,3072]{1,0:T(8,128)(2,1)S(1)}, bf16[48,3072]{1,0:T(8,128)(2,1)S(1)}, u32[]{:S(2)}, u32[]{:S(2)}) collective-permute-start(bf16[48,3072]{1,0:T(8,128)(2,1)S(1)} %slice_bitcast_fusion.1), channel_id=1, source_target_pairs={{0,16},{2,18},{4,20},{6,22},{8,24},{10,26},{12,28},{14,30},{16,0},... | collective-permute-start | bytes 884744 | tf_op jit(solution)/shard_map/ppermute | solution.py:237
  20.3 11.0 %collective-permute-start.5 = (bf16[32,3072]{1,0:T(8,128)(2,1)S(1)}, bf16[32,3072]{1,0:T(8,128)(2,1)S(1)}, u32[]{:S(2)}, u32[]{:S(2)}) collective-permute-start(bf16[32,3072]{1,0:T(8,128)(2,1)S(1)} %shard_map.74), channel_id=1, source_target_pairs={{0,20},{2,22},{4,16},{6,18},{8,28},{10,30},{12,24},{14,26},{16,4},... | collective-permute-start | bytes 589832 | tf_op jit(solution)/shard_map/ppermute | solution.py:237
  27.5 6.1 %collective-permute-start.8 = (bf16[32,3072]{1,0:T(8,128)(2,1)S(1)}, bf16[32,3072]{1,0:T(8,128)(2,1)S(1)}, u32[]{:S(2)}, u32[]{:S(2)}) collective-permute-start(bf16[32,3072]{1,0:T(8,128)(2,1)S(1)} %get-tuple-element.43), channel_id=1, source_target_pairs={{0,2},{2,0},{4,6},{6,4},{8,10},{10,8},{12,14},{14,12},{16,18},{18,... | collective-permute-start | bytes 589832 | tf_op jit(solution)/shard_map/ppermute | solution.py:237
  28.1 5.7 %collective-permute-start.9 = (bf16[32,3072]{1,0:T(8,128)(2,1)S(1)}, bf16[32,3072]{1,0:T(8,128)(2,1)S(1)}, u32[]{:S(2)}, u32[]{:S(2)}) collective-permute-start(bf16[32,3072]{1,0:T(8,128)(2,1)S(1)} %collective-permute-done.7.far_ref), channel_id=1, source_target_pairs={{0,4},{2,6},{4,0},{6,2},{8,12},{10,14},{12,8},{14,10},{16,20},{18,... | collective-permute-start | bytes 589832 | tf_op jit(solution)/shard_map/ppermute | solution.py:237
  29.1 13.4 %collective-permute-start.4 = (bf16[80,3072]{1,0:T(8,128)(2,1)S(1)}, bf16[80,3072]{1,0:T(8,128)(2,1)S(1)}, u32[]{:S(2)}, u32[]{:S(2)}) collective-permute-start(bf16[80,3072]{1,0:T(8,128)(2,1)S(1)} %slice_bitcast_fusion), channel_id=1, source_target_pairs={{0,16},{2,18},{4,20},{6,22},{8,24},{10,26},{12,28},{14,30},{16,0},... | collective-permute-start | bytes 1474568 | tf_op jit(solution)/shard_map/ppermute | solution.py:237
  31.3 7.8 %collective-permute-start.10 = (bf16[32,3072]{1,0:T(8,128)(2,1)S(1)}, bf16[32,3072]{1,0:T(8,128)(2,1)S(1)}, u32[]{:S(2)}, u32[]{:S(2)}) collective-permute-start(bf16[32,3072]{1,0:T(8,128)(2,1)S(1)} %collective-permute-done.5.near_ref), channel_id=1, source_target_pairs={{0,2},{2,0},{4,6},{6,4},{8,10},{10,8},{12,14},{14,12},{16,18},{18,... | collective-permute-start | bytes 589832 | tf_op jit(solution)/shard_map/ppermute | solution.py:237
  35.0 8.5 %collective-permute-start.11 = (bf16[32,3072]{1,0:T(8,128)(2,1)S(1)}, bf16[32,3072]{1,0:T(8,128)(2,1)S(1)}, u32[]{:S(2)}, u32[]{:S(2)}) collective-permute-start(bf16[32,3072]{1,0:T(8,128)(2,1)S(1)} %get-tuple-element.50), channel_id=1, source_target_pairs={{0,2},{2,0},{4,6},{6,4},{8,10},{10,8},{12,14},{14,12},{16,18},{18,... | collective-permute-start | bytes 589832 | tf_op jit(solution)/shard_map/ppermute | solution.py:237
  36.7 5.8 %copy-start = (s32[1,128,2]{1,2,0:T(2,128)S(1)}, s32[1,128,2]{1,2,0:T(2,128)}, u32[]{:S(2)}) copy-start(s32[1,128,2]{1,2,0:T(2,128)} %param.12) | copy-start | bytes 3076
  36.7 5.8 %copy-start.1 = (f32[1,128,2]{1,2,0:T(2,128)S(1)}, f32[1,128,2]{1,2,0:T(2,128)}, u32[]{:S(2)}) copy-start(f32[1,128,2]{1,2,0:T(2,128)} %param.13) | copy-start | bytes 3076
  36.7 14.6 %collective-permute-start.12 = (bf16[32,3072]{1,0:T(8,128)(2,1)S(1)}, bf16[32,3072]{1,0:T(8,128)(2,1)S(1)}, u32[]{:S(2)}, u32[]{:S(2)}) collective-permute-start(bf16[32,3072]{1,0:T(8,128)(2,1)S(1)} %add_convert_fusion.2), channel_id=1, source_target_pairs={{0,8},{2,10},{4,12},{6,14},{8,0},{10,2},{12,4},{14,6},{16,24},{18,... | collective-permute-start | bytes 589832 | tf_op jit(solution)/shard_map/ppermute | solution.py:237
  40.4 7.4 %collective-permute-start.14 = (bf16[32,3072]{1,0:T(8,128)(2,1)S(1)}, bf16[32,3072]{1,0:T(8,128)(2,1)S(1)}, u32[]{:S(2)}, u32[]{:S(2)}) collective-permute-start(bf16[32,3072]{1,0:T(8,128)(2,1)S(1)} %get-tuple-element.53), channel_id=1, source_target_pairs={{0,2},{2,0},{4,6},{6,4},{8,10},{10,8},{12,14},{14,12},{16,18},{18,... | collective-permute-start | bytes 589832 | tf_op jit(solution)/shard_map/ppermute | solution.py:237
  43.6 9.5 %collective-permute-start.13 = (bf16[32,3072]{1,0:T(8,128)(2,1)S(1)}, bf16[32,3072]{1,0:T(8,128)(2,1)S(1)}, u32[]{:S(2)}, u32[]{:S(2)}) collective-permute-start(bf16[32,3072]{1,0:T(8,128)(2,1)S(1)} %add_convert_fusion.1), channel_id=1, source_target_pairs={{0,12},{2,14},{4,8},{6,10},{8,4},{10,6},{12,0},{14,2},{16,28},{18,... | collective-permute-start | bytes 589832 | tf_op jit(solution)/shard_map/ppermute | solution.py:237
  47.8 7.3 %collective-permute-start.15 = (bf16[32,3072]{1,0:T(8,128)(2,1)S(1)}, bf16[32,3072]{1,0:T(8,128)(2,1)S(1)}, u32[]{:S(2)}, u32[]{:S(2)}) collective-permute-start(bf16[32,3072]{1,0:T(8,128)(2,1)S(1)} %add_convert_fusion), channel_id=1, source_target_pairs={{0,4},{2,6},{4,0},{6,2},{8,12},{10,14},{12,8},{14,10},{16,20},{18,... | collective-permute-start | bytes 589832 | tf_op jit(solution)/shard_map/ppermute | solution.py:237
  50.0 5.7 %collective-permute-start.16 = (bf16[32,3072]{1,0:T(8,128)(2,1)S(1)}, bf16[32,3072]{1,0:T(8,128)(2,1)S(1)}, u32[]{:S(2)}, u32[]{:S(2)}) collective-permute-start(bf16[32,3072]{1,0:T(8,128)(2,1)S(1)} %get-tuple-element.54), channel_id=1, source_target_pairs={{0,2},{2,0},{4,6},{6,4},{8,10},{10,8},{12,14},{14,12},{16,18},{18,... | collective-permute-start | bytes 589832 | tf_op jit(solution)/shard_map/ppermute | solution.py:237

commit v15 on v14

--- a/solution.py
+++ b/solution.py
@@ -79,10 +79,11 @@
     inverse = lax.rsqrt(jnp.mean(rows * rows, axis=-1, keepdims=True) + 1e-06)
     normed = (rows * inverse * gain_ref[...].astype(jnp.float32)).astype(jnp.bfloat16)
     across = (((1,), (1,)), ((), ()))
-    gate = lax.dot_general(normed, gate_ref[...], across, preferred_element_type=jnp.float32)
-    up = lax.dot_general(normed, up_ref[...], across, preferred_element_type=jnp.float32)
+    gate = lax.dot_general(gate_ref[...], normed, across, preferred_element_type=jnp.float32)
+    up = lax.dot_general(up_ref[...], normed, across, preferred_element_type=jnp.float32)
     hidden = (gate / (1.0 + jnp.exp(-gate)) * up).astype(jnp.bfloat16)
-    partial = jnp.dot(hidden, down_ref[...], preferred_element_type=jnp.float32)
+    first = (((0,), (0,)), ((), ()))
+    partial = lax.dot_general(hidden, down_ref[...], first, preferred_element_type=jnp.float32)
     partial = partial.astype(jnp.bfloat16)
     near_out[...] = partial[:count]
     far_out[...] = partial[count:]

time: 57 us -> 57 us (level)
  no operation moved by 1% of the time
where the time goes in v15:
time: 57 us; the launch traced here: 56.8 us
  starting transfers between devices  27.7 us (49%)
  waiting for transfers between devices  18 us (32%)
  Pallas kernels  10.8 us (19%)
    ppermute x17, starting transfers between devices, moved(): return lax.ppermute(value, ('section', 'expert'), pairs)  27.7 us
    ppermute x17, waiting for transfers between devices, moved(): return lax.ppermute(value, ('section', 'expert'), pairs)  18 us
    pallas_call x4, Pallas kernels, mlp(): pl.pallas_call(mlp_kernel, out_shape=(out, out), in_specs=[VMEM] * 6, out...  5.02 us
    pallas_call x2, Pallas kernels, loaded(): pl.pallas_call(functools.partial(load_kernel, len(arrays)), out_shape=tup...  3.23 us
    pallas_call x1, Pallas kernels, ended(): pl.pallas_call(functools.partial(end_kernel, steps), out_shape=jax.ShapeD...  1.14 us
  transfers between devices with their start and end apart: 17, of which 10 were waited for; matrix products, arithmetic and copies ran while one was open for 0% of the time, Pallas kernels for 16%

profile of v15, /device:TPU:0, one launch (start us, length us, event | category | flops | bytes accessed | tf_op | source)
XLA Modules:
  0.0 56.8 jit_solution(3154964748074883817)
XLA Ops:
  0.0 2.9 %collective-permute-start = (s32[1,128,2]{1,2,0:T(2,128)}, s32[1,128,2]{1,2,0:T(2,128)S(1)}, u32[]{:S(2)}, u32[]{:S(2)}) collective-permute-start(s32[1,128,2]{1,2,0:T(2,128)} %param.12), channel_id=1, source_target_pairs={{0,16},{2,18},{4,20},{6,22},{8,24},{10,26},{12,28},{14,30},{16,0},... | collective-permute-start | bytes 3080 | tf_op jit(solution)/shard_map/ppermute | solution.py:238
  2.9 1.1 %shard_map.73.block_ref = bf16[128,3072]{1,0:T(8,128)(2,1)S(1)} custom-call(bf16[128,3072]{1,0:T(8,128)(2,1)} %bitcast.25), custom_call_target="tpu_custom_call" | custom-call | bytes 6291456 | tf_op jit(solution)/shard_map/pallas_call | solution.py:33
  4.1 0.6 %collective-permute-done = s32[1,128,2]{1,2,0:T(2,128)S(1)} collective-permute-done((s32[1,128,2]{1,2,0:T(2,128)}, s32[1,128,2]{1,2,0:T(2,128)S(1)}, u32[]{:S(2)}, u32[]{:S(2)}) %collective-permute-start) | collective-permute-done | bytes 1056 | tf_op jit(solution)/shard_map/ppermute | solution.py:238
  4.7 0.4 shard_map.74
  5.1 4.1 %collective-permute-start.2 = (bf16[32,3072]{1,0:T(8,128)(2,1)S(1)}, bf16[32,3072]{1,0:T(8,128)(2,1)S(1)}, u32[]{:S(2)}, u32[]{:S(2)}) collective-permute-start(bf16[32,3072]{1,0:T(8,128)(2,1)S(1)} %shard_map.74), channel_id=1, source_target_pairs={{0,24},{2,26},{4,28},{6,30},{8,16},{10,18},{12,20},{14,22},{16,8},... | collective-permute-start | bytes 589832 | tf_op jit(solution)/shard_map/ppermute | solution.py:238
  9.2 1.5 %collective-permute-start.1 = (bf16[32,3072]{1,0:T(8,128)(2,1)S(1)}, bf16[32,3072]{1,0:T(8,128)(2,1)S(1)}, u32[]{:S(2)}, u32[]{:S(2)}) collective-permute-start(bf16[32,3072]{1,0:T(8,128)(2,1)S(1)} %shard_map.74), channel_id=1, source_target_pairs={{0,18},{2,16},{4,22},{6,20},{8,26},{10,24},{12,30},{14,28},{16,2},... | collective-permute-start | bytes 589832 | tf_op jit(solution)/shard_map/ppermute | solution.py:238
  10.7 2.1 %shard_map.75 = (bf16[192,3072]{1,0:T(8,128)(2,1)S(1)}, bf16[192,3072]{1,0:T(8,128)(2,1)S(1)}, bf16[192,3072]{1,0:T(8,128)(2,1)S(1)}, bf16[1,3072]{1,0:T(2,128)(2,1)S(1)}) custom-call(bf16[192,3072]{1,0:T(8,128)(2,1)} %bitcast.26, bf16[192,3072]{1,0:T(8,128)(2,1)} %bitcast.27, bf16[192,3072]{1,0:T(8,128)(2,1)} %bitcast.28, bf16[1,3072]{1,0:T(2,128)(2,1)} %refs_3_.1), custom_call_target="tpu_custom_call" | custom-call | bytes 6291456 | tf_op jit(solution)/shard_map/pallas_call | solution.py:33
  12.8 4.5 %collective-permute-done.2.near_ref = bf16[32,3072]{1,0:T(8,128)(2,1)S(1)} collective-permute-done((bf16[32,3072]{1,0:T(8,128)(2,1)S(1)}, bf16[32,3072]{1,0:T(8,128)(2,1)S(1)}, u32[]{:S(2)}, u32[]{:S(2)}) %collective-permute-start.2) | collective-permute-done | bytes 196640 | tf_op jit(solution)/shard_map/ppermute | solution.py:238
  17.2 1.5 %collective-permute-start.7 = (bf16[32,3072]{1,0:T(8,128)(2,1)S(1)}, bf16[32,3072]{1,0:T(8,128)(2,1)S(1)}, u32[]{:S(2)}, u32[]{:S(2)}) collective-permute-start(bf16[32,3072]{1,0:T(8,128)(2,1)S(1)} %collective-permute-done.2.near_ref), channel_id=1, source_target_pairs={{0,2},{2,0},{4,6},{6,4},{8,10},{10,8},{12,14},{14,12},{16,18},{18,... | collective-permute-start | bytes 589832 | tf_op jit(solution)/shard_map/ppermute | solution.py:238
  18.8 0.6 %collective-permute-start.6 = (bf16[32,3072]{1,0:T(8,128)(2,1)S(1)}, bf16[32,3072]{1,0:T(8,128)(2,1)S(1)}, u32[]{:S(2)}, u32[]{:S(2)}) collective-permute-start(bf16[32,3072]{1,0:T(8,128)(2,1)S(1)} %collective-permute-done.2.near_ref), channel_id=1, source_target_pairs={{0,4},{2,6},{4,0},{6,2},{8,12},{10,14},{12,8},{14,10},{16,20},{18,... | collective-permute-start | bytes 589832 | tf_op jit(solution)/shard_map/ppermute | solution.py:238
  19.4 0.0 copy-done.2
  19.4 0.0 collective-permute-done.1.far_ref
  19.4 0.9 %collective-permute-start.3 = (bf16[48,3072]{1,0:T(8,128)(2,1)S(1)}, bf16[48,3072]{1,0:T(8,128)(2,1)S(1)}, u32[]{:S(2)}, u32[]{:S(2)}) collective-permute-start(bf16[48,3072]{1,0:T(8,128)(2,1)S(1)} %slice_bitcast_fusion.1), channel_id=1, source_target_pairs={{0,16},{2,18},{4,20},{6,22},{8,24},{10,26},{12,28},{14,30},{16,0},... | collective-permute-start | bytes 884744 | tf_op jit(solution)/shard_map/ppermute | solution.py:238
  20.3 2.1 %collective-permute-start.5 = (bf16[32,3072]{1,0:T(8,128)(2,1)S(1)}, bf16[32,3072]{1,0:T(8,128)(2,1)S(1)}, u32[]{:S(2)}, u32[]{:S(2)}) collective-permute-start(bf16[32,3072]{1,0:T(8,128)(2,1)S(1)} %shard_map.74), channel_id=1, source_target_pairs={{0,20},{2,22},{4,16},{6,18},{8,28},{10,30},{12,24},{14,26},{16,4},... | collective-permute-start | bytes 589832 | tf_op jit(solution)/shard_map/ppermute | solution.py:238
  22.4 3.9 %collective-permute-done.6.near_ref = bf16[32,3072]{1,0:T(8,128)(2,1)S(1)} collective-permute-done((bf16[32,3072]{1,0:T(8,128)(2,1)S(1)}, bf16[32,3072]{1,0:T(8,128)(2,1)S(1)}, u32[]{:S(2)}, u32[]{:S(2)}) %collective-permute-start.6) | collective-permute-done | bytes 196640 | tf_op jit(solution)/shard_map/ppermute | solution.py:238
  26.3 0.0 collective-permute-done.7.far_ref
  26.3 1.3 %shard_map.77 = (bf16[32,3072]{1,0:T(8,128)(2,1)S(1)}, bf16[32,3072]{1,0:T(8,128)(2,1)S(1)}) custom-call(bf16[32,3072]{1,0:T(8,128)(2,1)S(1)} %collective-permute-done.2.near_ref, bf16[32,3072]{1,0:T(8,128)(2,1)S(1)} %collective-permute-done.7.far_ref, bf16[1,3072]{1,0:T(2,128)(2,1)S(1)} %get-tuple-element.31.gain_ref, ...), custom_call_target="tpu_custom_call" | custom-call | flops 226492416 | bytes 3538944 | tf_op jit(solution)/shard_map/pallas_call | solution.py:96
  27.5 0.5 collective-permute-start.8
  28.1 1.0 %collective-permute-start.9 = (bf16[32,3072]{1,0:T(8,128)(2,1)S(1)}, bf16[32,3072]{1,0:T(8,128)(2,1)S(1)}, u32[]{:S(2)}, u32[]{:S(2)}) collective-permute-start(bf16[32,3072]{1,0:T(8,128)(2,1)S(1)} %collective-permute-done.7.far_ref), channel_id=1, source_target_pairs={{0,4},{2,6},{4,0},{6,2},{8,12},{10,14},{12,8},{14,10},{16,20},{18,... | collective-permute-start | bytes 589832 | tf_op jit(solution)/shard_map/ppermute | solution.py:238
  29.1 0.6 %collective-permute-start.4 = (bf16[80,3072]{1,0:T(8,128)(2,1)S(1)}, bf16[80,3072]{1,0:T(8,128)(2,1)S(1)}, u32[]{:S(2)}, u32[]{:S(2)}) collective-permute-start(bf16[80,3072]{1,0:T(8,128)(2,1)S(1)} %slice_bitcast_fusion), channel_id=1, source_target_pairs={{0,16},{2,18},{4,20},{6,22},{8,24},{10,26},{12,28},{14,30},{16,0},... | collective-permute-start | bytes 1474568 | tf_op jit(solution)/shard_map/ppermute | solution.py:238
  29.7 1.6 %collective-permute-done.5.near_ref = bf16[32,3072]{1,0:T(8,128)(2,1)S(1)} collective-permute-done((bf16[32,3072]{1,0:T(8,128)(2,1)S(1)}, bf16[32,3072]{1,0:T(8,128)(2,1)S(1)}, u32[]{:S(2)}, u32[]{:S(2)}) %collective-permute-start.5) | collective-permute-done | bytes 196640 | tf_op jit(solution)/shard_map/ppermute | solution.py:238
  31.3 0.0 collective-permute-start.10
  31.3 2.4 %collective-permute-done.3.refs_0_ = bf16[48,3072]{1,0:T(8,128)(2,1)S(1)} collective-permute-done((bf16[48,3072]{1,0:T(8,128)(2,1)S(1)}, bf16[48,3072]{1,0:T(8,128)(2,1)S(1)}, u32[]{:S(2)}, u32[]{:S(2)}) %collective-permute-start.3) | collective-permute-done | bytes 294944 | tf_op jit(solution)/shard_map/ppermute | solution.py:238
  33.6 0.0 collective-permute-done.8
  33.6 0.1 collective-permute-done.9.far_ref
  33.7 1.3 %shard_map.78 = (bf16[32,3072]{1,0:T(8,128)(2,1)S(1)}, bf16[32,3072]{1,0:T(8,128)(2,1)S(1)}) custom-call(bf16[32,3072]{1,0:T(8,128)(2,1)S(1)} %collective-permute-done.6.near_ref, bf16[32,3072]{1,0:T(8,128)(2,1)S(1)} %collective-permute-done.9.far_ref, bf16[1,3072]{1,0:T(2,128)(2,1)S(1)} %get-tuple-element.31.gain_ref, ...), custom_call_target="tpu_custom_call" | custom-call | flops 226492416 | bytes 3538944 | tf_op jit(solution)/shard_map/pallas_call | solution.py:96
  35.0 1.6 %collective-permute-start.11 = (bf16[32,3072]{1,0:T(8,128)(2,1)S(1)}, bf16[32,3072]{1,0:T(8,128)(2,1)S(1)}, u32[]{:S(2)}, u32[]{:S(2)}) collective-permute-start(bf16[32,3072]{1,0:T(8,128)(2,1)S(1)} %get-tuple-element.50), channel_id=1, source_target_pairs={{0,2},{2,0},{4,6},{6,4},{8,10},{10,8},{12,14},{14,12},{16,18},{18,... | collective-permute-start | bytes 589832 | tf_op jit(solution)/shard_map/ppermute | solution.py:238
  36.6 0.1 add_convert_fusion.2
  36.7 0.0 copy-start
  36.7 0.0 copy-start.1
  36.7 2.4 %collective-permute-start.12 = (bf16[32,3072]{1,0:T(8,128)(2,1)S(1)}, bf16[32,3072]{1,0:T(8,128)(2,1)S(1)}, u32[]{:S(2)}, u32[]{:S(2)}) collective-permute-start(bf16[32,3072]{1,0:T(8,128)(2,1)S(1)} %add_convert_fusion.2), channel_id=1, source_target_pairs={{0,8},{2,10},{4,12},{6,14},{8,0},{10,2},{12,4},{14,6},{16,24},{18,... | collective-permute-start | bytes 589832 | tf_op jit(solution)/shard_map/ppermute | solution.py:238
  39.1 0.0 collective-permute-done.10.far_ref
  39.1 1.3 %shard_map.79 = (bf16[32,3072]{1,0:T(8,128)(2,1)S(1)}, bf16[32,3072]{1,0:T(8,128)(2,1)S(1)}) custom-call(bf16[32,3072]{1,0:T(8,128)(2,1)S(1)} %collective-permute-done.5.near_ref, bf16[32,3072]{1,0:T(8,128)(2,1)S(1)} %collective-permute-done.10.far_ref, bf16[1,3072]{1,0:T(2,128)(2,1)S(1)} %get-tuple-element.31.gain_ref, ...), custom_call_target="tpu_custom_call" | custom-call | flops 226492416 | bytes 3538944 | tf_op jit(solution)/shard_map/pallas_call | solution.py:96
  40.3 1.5 %collective-permute-start.14 = (bf16[32,3072]{1,0:T(8,128)(2,1)S(1)}, bf16[32,3072]{1,0:T(8,128)(2,1)S(1)}, u32[]{:S(2)}, u32[]{:S(2)}) collective-permute-start(bf16[32,3072]{1,0:T(8,128)(2,1)S(1)} %get-tuple-element.53), channel_id=1, source_target_pairs={{0,2},{2,0},{4,6},{6,4},{8,10},{10,8},{12,14},{14,12},{16,18},{18,... | collective-permute-start | bytes 589832 | tf_op jit(solution)/shard_map/ppermute | solution.py:238
  41.8 0.7 %collective-permute-done.4.refs_1_ = bf16[80,3072]{1,0:T(8,128)(2,1)S(1)} collective-permute-done((bf16[80,3072]{1,0:T(8,128)(2,1)S(1)}, bf16[80,3072]{1,0:T(8,128)(2,1)S(1)}, u32[]{:S(2)}, u32[]{:S(2)}) %collective-permute-start.4) | collective-permute-done | bytes 491552 | tf_op jit(solution)/shard_map/ppermute | solution.py:238
  42.5 1.0 %shard_map.76 = (f32[128,3072]{1,0:T(8,128)S(1)}, bf16[128,160]{1,0:T(8,128)(2,1)S(1)}, bf16[32,3072]{1,0:T(8,128)(2,1)S(1)}) custom-call(bf16[1,3072]{1,0:T(2,128)(2,1)S(1)} %get-tuple-element.31.gain_ref, s32[2,128]{1,0:T(2,128)S(1)} %bitcast.22, f32[2,128]{1,0:T(2,128)S(1)} %bitcast.23, bf16[48,3072]{1,0:T(8,128)(2,1)S(1)} %collective-permute-done.3.refs_0_, ...), custom_call_target="tpu_custom_call" | custom-call | flops 3145728 | bytes 2359296 | tf_op jit(solution)/shard_map/pallas_call | solution.py:151
  43.5 0.0 collective-permute-done.11
  43.5 0.1 add_convert_fusion.1
  43.6 4.2 %collective-permute-start.13 = (bf16[32,3072]{1,0:T(8,128)(2,1)S(1)}, bf16[32,3072]{1,0:T(8,128)(2,1)S(1)}, u32[]{:S(2)}, u32[]{:S(2)}) collective-permute-start(bf16[32,3072]{1,0:T(8,128)(2,1)S(1)} %add_convert_fusion.1), channel_id=1, source_target_pairs={{0,12},{2,14},{4,8},{6,10},{8,4},{10,6},{12,0},{14,2},{16,28},{18,... | collective-permute-start | bytes 589832 | tf_op jit(solution)/shard_map/ppermute | solution.py:238
  47.7 0.0 collective-permute-done.14
  47.8 0.9 %collective-permute-start.15 = (bf16[32,3072]{1,0:T(8,128)(2,1)S(1)}, bf16[32,3072]{1,0:T(8,128)(2,1)S(1)}, u32[]{:S(2)}, u32[]{:S(2)}) collective-permute-start(bf16[32,3072]{1,0:T(8,128)(2,1)S(1)} %add_convert_fusion), channel_id=1, source_target_pairs={{0,4},{2,6},{4,0},{6,2},{8,12},{10,14},{12,8},{14,10},{16,20},{18,... | collective-permute-start | bytes 589832 | tf_op jit(solution)/shard_map/ppermute | solution.py:238
  48.7 1.3 %shard_map.80 = (bf16[32,3072]{1,0:T(8,128)(2,1)S(1)}, bf16[32,3072]{1,0:T(8,128)(2,1)S(1)}) custom-call(bf16[32,3072]{1,0:T(8,128)(2,1)S(1)} %get-tuple-element.51.near_ref, bf16[32,3072]{1,0:T(8,128)(2,1)S(1)} %collective-permute-done.1.far_ref, bf16[1,3072]{1,0:T(2,128)(2,1)S(1)} %get-tuple-element.31.gain_ref, ...), custom_call_target="tpu_custom_call" | custom-call | flops 226492416 | bytes 3538944 | tf_op jit(solution)/shard_map/pallas_call | solution.py:96
  50.0 1.4 %collective-permute-start.16 = (bf16[32,3072]{1,0:T(8,128)(2,1)S(1)}, bf16[32,3072]{1,0:T(8,128)(2,1)S(1)}, u32[]{:S(2)}, u32[]{:S(2)}) collective-permute-start(bf16[32,3072]{1,0:T(8,128)(2,1)S(1)} %get-tuple-element.54), channel_id=1, source_target_pairs={{0,2},{2,0},{4,6},{6,4},{8,10},{10,8},{12,14},{14,12},{16,18},{18,... | collective-permute-start | bytes 589832 | tf_op jit(solution)/shard_map/ppermute | solution.py:238
  51.3 0.0 collective-permute-done.12.right_ref
  51.4 1.7 %collective-permute-done.13.refs_1_ = bf16[32,3072]{1,0:T(8,128)(2,1)S(1)} collective-permute-done((bf16[32,3072]{1,0:T(8,128)(2,1)S(1)}, bf16[32,3072]{1,0:T(8,128)(2,1)S(1)}, u32[]{:S(2)}, u32[]{:S(2)}) %collective-permute-start.13) | collective-permute-done | bytes 196640 | tf_op jit(solution)/shard_map/ppermute | solution.py:238
  53.1 2.0 %collective-permute-done.15.refs_2_ = bf16[32,3072]{1,0:T(8,128)(2,1)S(1)} collective-permute-done((bf16[32,3072]{1,0:T(8,128)(2,1)S(1)}, bf16[32,3072]{1,0:T(8,128)(2,1)S(1)}, u32[]{:S(2)}, u32[]{:S(2)}) %collective-permute-start.15) | collective-permute-done | bytes 196640 | tf_op jit(solution)/shard_map/ppermute | solution.py:238
  55.1 0.6 %collective-permute-done.16.refs_3_ = bf16[32,3072]{1,0:T(8,128)(2,1)S(1)} collective-permute-done((bf16[32,3072]{1,0:T(8,128)(2,1)S(1)}, bf16[32,3072]{1,0:T(8,128)(2,1)S(1)}, u32[]{:S(2)}, u32[]{:S(2)}) %collective-permute-start.16) | collective-permute-done | bytes 196640 | tf_op jit(solution)/shard_map/ppermute | solution.py:238
  55.7 1.1 %shard_map.82 = bf16[128,3072]{1,0:T(8,128)(2,1)} custom-call(f32[128,3072]{1,0:T(8,128)S(1)} %get-tuple-element.34.base_ref, bf16[128,160]{1,0:T(8,128)(2,1)S(1)} %get-tuple-element.35.table_ref, f32[32,3072]{1,0:T(8,128)S(1)} %shard_map.81.refs_0_, bf16[32,3072]{1,0:T(8,128)(2,1)S(1)} %collective-permute-done.13.refs_1_, ...), custom_call_target="tpu_custom_call" | custom-call | flops 100663296 | bytes 2359296 | tf_op jit(solution)/shard_map/pallas_call | solution.py:191
  (7 shorter events, 0.1 us)
Async XLA Ops:
  0.0 4.7 %collective-permute-start = (s32[1,128,2]{1,2,0:T(2,128)}, s32[1,128,2]{1,2,0:T(2,128)S(1)}, u32[]{:S(2)}, u32[]{:S(2)}) collective-permute-start(s32[1,128,2]{1,2,0:T(2,128)} %param.12), channel_id=1, source_target_pairs={{0,16},{2,18},{4,20},{6,22},{8,24},{10,26},{12,28},{14,30},{16,0},... | collective-permute-start | bytes 3080 | tf_op jit(solution)/shard_map/ppermute | solution.py:238
  5.1 12.2 %collective-permute-start.2 = (bf16[32,3072]{1,0:T(8,128)(2,1)S(1)}, bf16[32,3072]{1,0:T(8,128)(2,1)S(1)}, u32[]{:S(2)}, u32[]{:S(2)}) collective-permute-start(bf16[32,3072]{1,0:T(8,128)(2,1)S(1)} %shard_map.74), channel_id=1, source_target_pairs={{0,24},{2,26},{4,28},{6,30},{8,16},{10,18},{12,20},{14,22},{16,8},... | collective-permute-start | bytes 589832 | tf_op jit(solution)/shard_map/ppermute | solution.py:238
  9.2 10.2 %collective-permute-start.1 = (bf16[32,3072]{1,0:T(8,128)(2,1)S(1)}, bf16[32,3072]{1,0:T(8,128)(2,1)S(1)}, u32[]{:S(2)}, u32[]{:S(2)}) collective-permute-start(bf16[32,3072]{1,0:T(8,128)(2,1)S(1)} %shard_map.74), channel_id=1, source_target_pairs={{0,18},{2,16},{4,22},{6,20},{8,26},{10,24},{12,30},{14,28},{16,2},... | collective-permute-start | bytes 589832 | tf_op jit(solution)/shard_map/ppermute | solution.py:238
  10.7 8.7 %copy-start.2 = (bf16[1,128,3072]{2,1,0:T(8,128)(2,1)S(1)}, bf16[1,128,3072]{2,1,0:T(8,128)(2,1)}, u32[]{:S(2)}) copy-start(bf16[1,128,3072]{2,1,0:T(8,128)(2,1)} %param.7) | copy-start | bytes 2359300
  17.2 9.0 %collective-permute-start.7 = (bf16[32,3072]{1,0:T(8,128)(2,1)S(1)}, bf16[32,3072]{1,0:T(8,128)(2,1)S(1)}, u32[]{:S(2)}, u32[]{:S(2)}) collective-permute-start(bf16[32,3072]{1,0:T(8,128)(2,1)S(1)} %collective-permute-done.2.near_ref), channel_id=1, source_target_pairs={{0,2},{2,0},{4,6},{6,4},{8,10},{10,8},{12,14},{14,12},{16,18},{18,... | collective-permute-start | bytes 589832 | tf_op jit(solution)/shard_map/ppermute | solution.py:238
  18.8 7.5 %collective-permute-start.6 = (bf16[32,3072]{1,0:T(8,128)(2,1)S(1)}, bf16[32,3072]{1,0:T(8,128)(2,1)S(1)}, u32[]{:S(2)}, u32[]{:S(2)}) collective-permute-start(bf16[32,3072]{1,0:T(8,128)(2,1)S(1)} %collective-permute-done.2.near_ref), channel_id=1, source_target_pairs={{0,4},{2,6},{4,0},{6,2},{8,12},{10,14},{12,8},{14,10},{16,20},{18,... | collective-permute-start | bytes 589832 | tf_op jit(solution)/shard_map/ppermute | solution.py:238
  19.4 14.2 %collective-permute-start.3 = (bf16[48,3072]{1,0:T(8,128)(2,1)S(1)}, bf16[48,3072]{1,0:T(8,128)(2,1)S(1)}, u32[]{:S(2)}, u32[]{:S(2)}) collective-permute-start(bf16[48,3072]{1,0:T(8,128)(2,1)S(1)} %slice_bitcast_fusion.1), channel_id=1, source_target_pairs={{0,16},{2,18},{4,20},{6,22},{8,24},{10,26},{12,28},{14,30},{16,0},... | collective-permute-start | bytes 884744 | tf_op jit(solution)/shard_map/ppermute | solution.py:238
  20.3 11.0 %collective-permute-start.5 = (bf16[32,3072]{1,0:T(8,128)(2,1)S(1)}, bf16[32,3072]{1,0:T(8,128)(2,1)S(1)}, u32[]{:S(2)}, u32[]{:S(2)}) collective-permute-start(bf16[32,3072]{1,0:T(8,128)(2,1)S(1)} %shard_map.74), channel_id=1, source_target_pairs={{0,20},{2,22},{4,16},{6,18},{8,28},{10,30},{12,24},{14,26},{16,4},... | collective-permute-start | bytes 589832 | tf_op jit(solution)/shard_map/ppermute | solution.py:238
  27.5 6.1 %collective-permute-start.8 = (bf16[32,3072]{1,0:T(8,128)(2,1)S(1)}, bf16[32,3072]{1,0:T(8,128)(2,1)S(1)}, u32[]{:S(2)}, u32[]{:S(2)}) collective-permute-start(bf16[32,3072]{1,0:T(8,128)(2,1)S(1)} %get-tuple-element.43), channel_id=1, source_target_pairs={{0,2},{2,0},{4,6},{6,4},{8,10},{10,8},{12,14},{14,12},{16,18},{18,... | collective-permute-start | bytes 589832 | tf_op jit(solution)/shard_map/ppermute | solution.py:238
  28.1 5.7 %collective-permute-start.9 = (bf16[32,3072]{1,0:T(8,128)(2,1)S(1)}, bf16[32,3072]{1,0:T(8,128)(2,1)S(1)}, u32[]{:S(2)}, u32[]{:S(2)}) collective-permute-start(bf16[32,3072]{1,0:T(8,128)(2,1)S(1)} %collective-permute-done.7.far_ref), channel_id=1, source_target_pairs={{0,4},{2,6},{4,0},{6,2},{8,12},{10,14},{12,8},{14,10},{16,20},{18,... | collective-permute-start | bytes 589832 | tf_op jit(solution)/shard_map/ppermute | solution.py:238
  29.1 13.4 %collective-permute-start.4 = (bf16[80,3072]{1,0:T(8,128)(2,1)S(1)}, bf16[80,3072]{1,0:T(8,128)(2,1)S(1)}, u32[]{:S(2)}, u32[]{:S(2)}) collective-permute-start(bf16[80,3072]{1,0:T(8,128)(2,1)S(1)} %slice_bitcast_fusion), channel_id=1, source_target_pairs={{0,16},{2,18},{4,20},{6,22},{8,24},{10,26},{12,28},{14,30},{16,0},... | collective-permute-start | bytes 1474568 | tf_op jit(solution)/shard_map/ppermute | solution.py:238
  31.3 7.8 %collective-permute-start.10 = (bf16[32,3072]{1,0:T(8,128)(2,1)S(1)}, bf16[32,3072]{1,0:T(8,128)(2,1)S(1)}, u32[]{:S(2)}, u32[]{:S(2)}) collective-permute-start(bf16[32,3072]{1,0:T(8,128)(2,1)S(1)} %collective-permute-done.5.near_ref), channel_id=1, source_target_pairs={{0,2},{2,0},{4,6},{6,4},{8,10},{10,8},{12,14},{14,12},{16,18},{18,... | collective-permute-start | bytes 589832 | tf_op jit(solution)/shard_map/ppermute | solution.py:238
  35.0 8.5 %collective-permute-start.11 = (bf16[32,3072]{1,0:T(8,128)(2,1)S(1)}, bf16[32,3072]{1,0:T(8,128)(2,1)S(1)}, u32[]{:S(2)}, u32[]{:S(2)}) collective-permute-start(bf16[32,3072]{1,0:T(8,128)(2,1)S(1)} %get-tuple-element.50), channel_id=1, source_target_pairs={{0,2},{2,0},{4,6},{6,4},{8,10},{10,8},{12,14},{14,12},{16,18},{18,... | collective-permute-start | bytes 589832 | tf_op jit(solution)/shard_map/ppermute | solution.py:238
  36.7 5.8 %copy-start = (s32[1,128,2]{1,2,0:T(2,128)S(1)}, s32[1,128,2]{1,2,0:T(2,128)}, u32[]{:S(2)}) copy-start(s32[1,128,2]{1,2,0:T(2,128)} %param.12) | copy-start | bytes 3076
  36.7 5.8 %copy-start.1 = (f32[1,128,2]{1,2,0:T(2,128)S(1)}, f32[1,128,2]{1,2,0:T(2,128)}, u32[]{:S(2)}) copy-start(f32[1,128,2]{1,2,0:T(2,128)} %param.13) | copy-start | bytes 3076
  36.7 14.6 %collective-permute-start.12 = (bf16[32,3072]{1,0:T(8,128)(2,1)S(1)}, bf16[32,3072]{1,0:T(8,128)(2,1)S(1)}, u32[]{:S(2)}, u32[]{:S(2)}) collective-permute-start(bf16[32,3072]{1,0:T(8,128)(2,1)S(1)} %add_convert_fusion.2), channel_id=1, source_target_pairs={{0,8},{2,10},{4,12},{6,14},{8,0},{10,2},{12,4},{14,6},{16,24},{18,... | collective-permute-start | bytes 589832 | tf_op jit(solution)/shard_map/ppermute | solution.py:238
  40.3 7.4 %collective-permute-start.14 = (bf16[32,3072]{1,0:T(8,128)(2,1)S(1)}, bf16[32,3072]{1,0:T(8,128)(2,1)S(1)}, u32[]{:S(2)}, u32[]{:S(2)}) collective-permute-start(bf16[32,3072]{1,0:T(8,128)(2,1)S(1)} %get-tuple-element.53), channel_id=1, source_target_pairs={{0,2},{2,0},{4,6},{6,4},{8,10},{10,8},{12,14},{14,12},{16,18},{18,... | collective-permute-start | bytes 589832 | tf_op jit(solution)/shard_map/ppermute | solution.py:238
  43.6 9.5 %collective-permute-start.13 = (bf16[32,3072]{1,0:T(8,128)(2,1)S(1)}, bf16[32,3072]{1,0:T(8,128)(2,1)S(1)}, u32[]{:S(2)}, u32[]{:S(2)}) collective-permute-start(bf16[32,3072]{1,0:T(8,128)(2,1)S(1)} %add_convert_fusion.1), channel_id=1, source_target_pairs={{0,12},{2,14},{4,8},{6,10},{8,4},{10,6},{12,0},{14,2},{16,28},{18,... | collective-permute-start | bytes 589832 | tf_op jit(solution)/shard_map/ppermute | solution.py:238
  47.8 7.3 %collective-permute-start.15 = (bf16[32,3072]{1,0:T(8,128)(2,1)S(1)}, bf16[32,3072]{1,0:T(8,128)(2,1)S(1)}, u32[]{:S(2)}, u32[]{:S(2)}) collective-permute-start(bf16[32,3072]{1,0:T(8,128)(2,1)S(1)} %add_convert_fusion), channel_id=1, source_target_pairs={{0,4},{2,6},{4,0},{6,2},{8,12},{10,14},{12,8},{14,10},{16,20},{18,... | collective-permute-start | bytes 589832 | tf_op jit(solution)/shard_map/ppermute | solution.py:238
  50.0 5.7 %collective-permute-start.16 = (bf16[32,3072]{1,0:T(8,128)(2,1)S(1)}, bf16[32,3072]{1,0:T(8,128)(2,1)S(1)}, u32[]{:S(2)}, u32[]{:S(2)}) collective-permute-start(bf16[32,3072]{1,0:T(8,128)(2,1)S(1)} %get-tuple-element.54), channel_id=1, source_target_pairs={{0,2},{2,0},{4,6},{6,4},{8,10},{10,8},{12,14},{14,12},{16,18},{18,... | collective-permute-start | bytes 589832 | tf_op jit(solution)/shard_map/ppermute | solution.py:238

commit v16 on v14

--- a/solution.py
+++ b/solution.py
@@ -75,12 +75,14 @@
 
 def mlp_kernel(near_ref, far_ref, gain_ref, gate_ref, up_ref, down_ref, near_out, far_out):
     count = near_ref.shape[0]
-    rows = jnp.concatenate([near_ref[...], far_ref[...]], axis=0).astype(jnp.float32)
-    inverse = lax.rsqrt(jnp.mean(rows * rows, axis=-1, keepdims=True) + 1e-06)
-    normed = (rows * inverse * gain_ref[...].astype(jnp.float32)).astype(jnp.bfloat16)
+    rows = jnp.concatenate([near_ref[...], far_ref[...]], axis=0)
+    scaled = rows * gain_ref[...]
     across = (((1,), (1,)), ((), ()))
-    gate = lax.dot_general(normed, gate_ref[...], across, preferred_element_type=jnp.float32)
-    up = lax.dot_general(normed, up_ref[...], across, preferred_element_type=jnp.float32)
+    gate = lax.dot_general(scaled, gate_ref[...], across, preferred_element_type=jnp.float32)
+    up = lax.dot_general(scaled, up_ref[...], across, preferred_element_type=jnp.float32)
+    wide = rows.astype(jnp.float32)
+    inverse = lax.rsqrt(jnp.mean(wide * wide, axis=-1, keepdims=True) + 1e-06)
+    gate, up = gate * inverse, up * inverse
     hidden = (gate / (1.0 + jnp.exp(-gate)) * up).astype(jnp.bfloat16)
     partial = jnp.dot(hidden, down_ref[...], preferred_element_type=jnp.float32)
     partial = partial.astype(jnp.bfloat16)

time: 57 us -> 56.6 us (level)
  transfers between devices with their start and end apart: 17 -> 17, of which waited for: 10 -> 9; matrix products, arithmetic and copies ran while one was open for 0% -> 0% of each run, Pallas kernels for 16% -> 16%
where the time goes in v16:
time: 56.6 us; the launch traced here: 56.4 us
  starting transfers between devices  27.5 us (49%)
  waiting for transfers between devices  18.1 us (32%)
  Pallas kernels  10.5 us (19%)
    ppermute x17, starting transfers between devices, moved(): return lax.ppermute(value, ('section', 'expert'), pairs)  27.5 us
    ppermute x17, waiting for transfers between devices, moved(): return lax.ppermute(value, ('section', 'expert'), pairs)  18.1 us
    pallas_call x4, Pallas kernels, mlp(): pl.pallas_call(mlp_kernel, out_shape=(out, out), in_specs=[VMEM] * 6, out...  4.69 us
    pallas_call x2, Pallas kernels, loaded(): pl.pallas_call(functools.partial(load_kernel, len(arrays)), out_shape=tup...  3.23 us
    pallas_call x1, Pallas kernels, ended(): pl.pallas_call(functools.partial(end_kernel, steps), out_shape=jax.ShapeD...  1.14 us
  transfers between devices with their start and end apart: 17, of which 9 were waited for; matrix products, arithmetic and copies ran while one was open for 0% of the time, Pallas kernels for 16%

profile of v16, /device:TPU:0, one launch (start us, length us, event | category | flops | bytes accessed | tf_op | source)
XLA Modules:
  0.0 56.4 jit_solution(15258464387616881396)
XLA Ops:
  0.0 2.9 %collective-permute-start = (s32[1,128,2]{1,2,0:T(2,128)}, s32[1,128,2]{1,2,0:T(2,128)S(1)}, u32[]{:S(2)}, u32[]{:S(2)}) collective-permute-start(s32[1,128,2]{1,2,0:T(2,128)} %param.12), channel_id=1, source_target_pairs={{0,16},{2,18},{4,20},{6,22},{8,24},{10,26},{12,28},{14,30},{16,0},... | collective-permute-start | bytes 3080 | tf_op jit(solution)/shard_map/ppermute | solution.py:239
  2.9 1.1 %shard_map.73.block_ref = bf16[128,3072]{1,0:T(8,128)(2,1)S(1)} custom-call(bf16[128,3072]{1,0:T(8,128)(2,1)} %bitcast.25), custom_call_target="tpu_custom_call" | custom-call | bytes 6291456 | tf_op jit(solution)/shard_map/pallas_call | solution.py:33
  4.1 0.6 %collective-permute-done = s32[1,128,2]{1,2,0:T(2,128)S(1)} collective-permute-done((s32[1,128,2]{1,2,0:T(2,128)}, s32[1,128,2]{1,2,0:T(2,128)S(1)}, u32[]{:S(2)}, u32[]{:S(2)}) %collective-permute-start) | collective-permute-done | bytes 1056 | tf_op jit(solution)/shard_map/ppermute | solution.py:239
  4.7 0.4 shard_map.74
  5.1 4.1 %collective-permute-start.2 = (bf16[32,3072]{1,0:T(8,128)(2,1)S(1)}, bf16[32,3072]{1,0:T(8,128)(2,1)S(1)}, u32[]{:S(2)}, u32[]{:S(2)}) collective-permute-start(bf16[32,3072]{1,0:T(8,128)(2,1)S(1)} %shard_map.74), channel_id=1, source_target_pairs={{0,24},{2,26},{4,28},{6,30},{8,16},{10,18},{12,20},{14,22},{16,8},... | collective-permute-start | bytes 589832 | tf_op jit(solution)/shard_map/ppermute | solution.py:239
  9.2 1.5 %collective-permute-start.1 = (bf16[32,3072]{1,0:T(8,128)(2,1)S(1)}, bf16[32,3072]{1,0:T(8,128)(2,1)S(1)}, u32[]{:S(2)}, u32[]{:S(2)}) collective-permute-start(bf16[32,3072]{1,0:T(8,128)(2,1)S(1)} %shard_map.74), channel_id=1, source_target_pairs={{0,18},{2,16},{4,22},{6,20},{8,26},{10,24},{12,30},{14,28},{16,2},... | collective-permute-start | bytes 589832 | tf_op jit(solution)/shard_map/ppermute | solution.py:239
  10.7 2.1 %shard_map.75 = (bf16[192,3072]{1,0:T(8,128)(2,1)S(1)}, bf16[192,3072]{1,0:T(8,128)(2,1)S(1)}, bf16[192,3072]{1,0:T(8,128)(2,1)S(1)}, bf16[1,3072]{1,0:T(2,128)(2,1)S(1)}) custom-call(bf16[192,3072]{1,0:T(8,128)(2,1)} %bitcast.26, bf16[192,3072]{1,0:T(8,128)(2,1)} %bitcast.27, bf16[192,3072]{1,0:T(8,128)(2,1)} %bitcast.28, bf16[1,3072]{1,0:T(2,128)(2,1)} %refs_3_.1), custom_call_target="tpu_custom_call" | custom-call | bytes 6291456 | tf_op jit(solution)/shard_map/pallas_call | solution.py:33
  12.8 4.5 %collective-permute-done.2.near_ref = bf16[32,3072]{1,0:T(8,128)(2,1)S(1)} collective-permute-done((bf16[32,3072]{1,0:T(8,128)(2,1)S(1)}, bf16[32,3072]{1,0:T(8,128)(2,1)S(1)}, u32[]{:S(2)}, u32[]{:S(2)}) %collective-permute-start.2) | collective-permute-done | bytes 196640 | tf_op jit(solution)/shard_map/ppermute | solution.py:239
  17.2 1.5 %collective-permute-start.7 = (bf16[32,3072]{1,0:T(8,128)(2,1)S(1)}, bf16[32,3072]{1,0:T(8,128)(2,1)S(1)}, u32[]{:S(2)}, u32[]{:S(2)}) collective-permute-start(bf16[32,3072]{1,0:T(8,128)(2,1)S(1)} %collective-permute-done.2.near_ref), channel_id=1, source_target_pairs={{0,2},{2,0},{4,6},{6,4},{8,10},{10,8},{12,14},{14,12},{16,18},{18,... | collective-permute-start | bytes 589832 | tf_op jit(solution)/shard_map/ppermute | solution.py:239
  18.8 0.6 %collective-permute-start.6 = (bf16[32,3072]{1,0:T(8,128)(2,1)S(1)}, bf16[32,3072]{1,0:T(8,128)(2,1)S(1)}, u32[]{:S(2)}, u32[]{:S(2)}) collective-permute-start(bf16[32,3072]{1,0:T(8,128)(2,1)S(1)} %collective-permute-done.2.near_ref), channel_id=1, source_target_pairs={{0,4},{2,6},{4,0},{6,2},{8,12},{10,14},{12,8},{14,10},{16,20},{18,... | collective-permute-start | bytes 589832 | tf_op jit(solution)/shard_map/ppermute | solution.py:239
  19.4 0.0 collective-permute-done.1.far_ref
  19.4 0.9 %collective-permute-start.3 = (bf16[48,3072]{1,0:T(8,128)(2,1)S(1)}, bf16[48,3072]{1,0:T(8,128)(2,1)S(1)}, u32[]{:S(2)}, u32[]{:S(2)}) collective-permute-start(bf16[48,3072]{1,0:T(8,128)(2,1)S(1)} %slice_bitcast_fusion.1), channel_id=1, source_target_pairs={{0,16},{2,18},{4,20},{6,22},{8,24},{10,26},{12,28},{14,30},{16,0},... | collective-permute-start | bytes 884744 | tf_op jit(solution)/shard_map/ppermute | solution.py:239
  20.3 2.1 %collective-permute-start.5 = (bf16[32,3072]{1,0:T(8,128)(2,1)S(1)}, bf16[32,3072]{1,0:T(8,128)(2,1)S(1)}, u32[]{:S(2)}, u32[]{:S(2)}) collective-permute-start(bf16[32,3072]{1,0:T(8,128)(2,1)S(1)} %shard_map.74), channel_id=1, source_target_pairs={{0,20},{2,22},{4,16},{6,18},{8,28},{10,30},{12,24},{14,26},{16,4},... | collective-permute-start | bytes 589832 | tf_op jit(solution)/shard_map/ppermute | solution.py:239
  22.4 3.9 %collective-permute-done.6.near_ref = bf16[32,3072]{1,0:T(8,128)(2,1)S(1)} collective-permute-done((bf16[32,3072]{1,0:T(8,128)(2,1)S(1)}, bf16[32,3072]{1,0:T(8,128)(2,1)S(1)}, u32[]{:S(2)}, u32[]{:S(2)}) %collective-permute-start.6) | collective-permute-done | bytes 196640 | tf_op jit(solution)/shard_map/ppermute | solution.py:239
  26.3 0.0 collective-permute-done.7.far_ref
  26.3 1.2 %shard_map.77 = (bf16[32,3072]{1,0:T(8,128)(2,1)S(1)}, bf16[32,3072]{1,0:T(8,128)(2,1)S(1)}) custom-call(bf16[32,3072]{1,0:T(8,128)(2,1)S(1)} %collective-permute-done.2.near_ref, bf16[32,3072]{1,0:T(8,128)(2,1)S(1)} %collective-permute-done.7.far_ref, bf16[1,3072]{1,0:T(2,128)(2,1)S(1)} %get-tuple-element.31.gain_ref, ...), custom_call_target="tpu_custom_call" | custom-call | flops 226492416 | bytes 3538944 | tf_op jit(solution)/shard_map/pallas_call | solution.py:97
  27.5 0.5 collective-permute-start.8
  28.0 1.0 %collective-permute-start.9 = (bf16[32,3072]{1,0:T(8,128)(2,1)S(1)}, bf16[32,3072]{1,0:T(8,128)(2,1)S(1)}, u32[]{:S(2)}, u32[]{:S(2)}) collective-permute-start(bf16[32,3072]{1,0:T(8,128)(2,1)S(1)} %collective-permute-done.7.far_ref), channel_id=1, source_target_pairs={{0,4},{2,6},{4,0},{6,2},{8,12},{10,14},{12,8},{14,10},{16,20},{18,... | collective-permute-start | bytes 589832 | tf_op jit(solution)/shard_map/ppermute | solution.py:239
  29.0 0.6 %collective-permute-start.4 = (bf16[80,3072]{1,0:T(8,128)(2,1)S(1)}, bf16[80,3072]{1,0:T(8,128)(2,1)S(1)}, u32[]{:S(2)}, u32[]{:S(2)}) collective-permute-start(bf16[80,3072]{1,0:T(8,128)(2,1)S(1)} %slice_bitcast_fusion), channel_id=1, source_target_pairs={{0,16},{2,18},{4,20},{6,22},{8,24},{10,26},{12,28},{14,30},{16,0},... | collective-permute-start | bytes 1474568 | tf_op jit(solution)/shard_map/ppermute | solution.py:239
  29.6 1.7 %collective-permute-done.5.near_ref = bf16[32,3072]{1,0:T(8,128)(2,1)S(1)} collective-permute-done((bf16[32,3072]{1,0:T(8,128)(2,1)S(1)}, bf16[32,3072]{1,0:T(8,128)(2,1)S(1)}, u32[]{:S(2)}, u32[]{:S(2)}) %collective-permute-start.5) | collective-permute-done | bytes 196640 | tf_op jit(solution)/shard_map/ppermute | solution.py:239
  31.3 0.0 collective-permute-start.10
  31.3 2.3 %collective-permute-done.3.refs_0_ = bf16[48,3072]{1,0:T(8,128)(2,1)S(1)} collective-permute-done((bf16[48,3072]{1,0:T(8,128)(2,1)S(1)}, bf16[48,3072]{1,0:T(8,128)(2,1)S(1)}, u32[]{:S(2)}, u32[]{:S(2)}) %collective-permute-start.3) | collective-permute-done | bytes 294944 | tf_op jit(solution)/shard_map/ppermute | solution.py:239
  33.6 0.0 collective-permute-done.8
  33.6 0.0 collective-permute-done.9.far_ref
  33.6 1.2 %shard_map.78 = (bf16[32,3072]{1,0:T(8,128)(2,1)S(1)}, bf16[32,3072]{1,0:T(8,128)(2,1)S(1)}) custom-call(bf16[32,3072]{1,0:T(8,128)(2,1)S(1)} %collective-permute-done.6.near_ref, bf16[32,3072]{1,0:T(8,128)(2,1)S(1)} %collective-permute-done.9.far_ref, bf16[1,3072]{1,0:T(2,128)(2,1)S(1)} %get-tuple-element.31.gain_ref, ...), custom_call_target="tpu_custom_call" | custom-call | flops 226492416 | bytes 3538944 | tf_op jit(solution)/shard_map/pallas_call | solution.py:97
  34.8 1.6 %collective-permute-start.11 = (bf16[32,3072]{1,0:T(8,128)(2,1)S(1)}, bf16[32,3072]{1,0:T(8,128)(2,1)S(1)}, u32[]{:S(2)}, u32[]{:S(2)}) collective-permute-start(bf16[32,3072]{1,0:T(8,128)(2,1)S(1)} %get-tuple-element.50), channel_id=1, source_target_pairs={{0,2},{2,0},{4,6},{6,4},{8,10},{10,8},{12,14},{14,12},{16,18},{18,... | collective-permute-start | bytes 589832 | tf_op jit(solution)/shard_map/ppermute | solution.py:239
  36.5 0.1 add_convert_fusion.2
  36.5 0.0 copy-start
  36.5 0.0 copy-start.1
  36.5 2.5 %collective-permute-start.12 = (bf16[32,3072]{1,0:T(8,128)(2,1)S(1)}, bf16[32,3072]{1,0:T(8,128)(2,1)S(1)}, u32[]{:S(2)}, u32[]{:S(2)}) collective-permute-start(bf16[32,3072]{1,0:T(8,128)(2,1)S(1)} %add_convert_fusion.2), channel_id=1, source_target_pairs={{0,8},{2,10},{4,12},{6,14},{8,0},{10,2},{12,4},{14,6},{16,24},{18,... | collective-permute-start | bytes 589832 | tf_op jit(solution)/shard_map/ppermute | solution.py:239
  39.0 0.0 collective-permute-done.10.far_ref
  39.0 1.2 %shard_map.79 = (bf16[32,3072]{1,0:T(8,128)(2,1)S(1)}, bf16[32,3072]{1,0:T(8,128)(2,1)S(1)}) custom-call(bf16[32,3072]{1,0:T(8,128)(2,1)S(1)} %collective-permute-done.5.near_ref, bf16[32,3072]{1,0:T(8,128)(2,1)S(1)} %collective-permute-done.10.far_ref, bf16[1,3072]{1,0:T(2,128)(2,1)S(1)} %get-tuple-element.31.gain_ref, ...), custom_call_target="tpu_custom_call" | custom-call | flops 226492416 | bytes 3538944 | tf_op jit(solution)/shard_map/pallas_call | solution.py:97
  40.2 1.5 %collective-permute-start.14 = (bf16[32,3072]{1,0:T(8,128)(2,1)S(1)}, bf16[32,3072]{1,0:T(8,128)(2,1)S(1)}, u32[]{:S(2)}, u32[]{:S(2)}) collective-permute-start(bf16[32,3072]{1,0:T(8,128)(2,1)S(1)} %get-tuple-element.53), channel_id=1, source_target_pairs={{0,2},{2,0},{4,6},{6,4},{8,10},{10,8},{12,14},{14,12},{16,18},{18,... | collective-permute-start | bytes 589832 | tf_op jit(solution)/shard_map/ppermute | solution.py:239
  41.7 0.8 %collective-permute-done.4.refs_1_ = bf16[80,3072]{1,0:T(8,128)(2,1)S(1)} collective-permute-done((bf16[80,3072]{1,0:T(8,128)(2,1)S(1)}, bf16[80,3072]{1,0:T(8,128)(2,1)S(1)}, u32[]{:S(2)}, u32[]{:S(2)}) %collective-permute-start.4) | collective-permute-done | bytes 491552 | tf_op jit(solution)/shard_map/ppermute | solution.py:239
  42.5 0.0 copy-done
  42.5 1.0 %shard_map.76 = (f32[128,3072]{1,0:T(8,128)S(1)}, bf16[128,160]{1,0:T(8,128)(2,1)S(1)}, bf16[32,3072]{1,0:T(8,128)(2,1)S(1)}) custom-call(bf16[1,3072]{1,0:T(2,128)(2,1)S(1)} %get-tuple-element.31.gain_ref, s32[2,128]{1,0:T(2,128)S(1)} %bitcast.22, f32[2,128]{1,0:T(2,128)S(1)} %bitcast.23, bf16[48,3072]{1,0:T(8,128)(2,1)S(1)} %collective-permute-done.3.refs_0_, ...), custom_call_target="tpu_custom_call" | custom-call | flops 3145728 | bytes 2359296 | tf_op jit(solution)/shard_map/pallas_call | solution.py:152
  43.5 0.0 collective-permute-done.11
  43.5 0.1 add_convert_fusion.1
  43.6 4.0 %collective-permute-start.13 = (bf16[32,3072]{1,0:T(8,128)(2,1)S(1)}, bf16[32,3072]{1,0:T(8,128)(2,1)S(1)}, u32[]{:S(2)}, u32[]{:S(2)}) collective-permute-start(bf16[32,3072]{1,0:T(8,128)(2,1)S(1)} %add_convert_fusion.1), channel_id=1, source_target_pairs={{0,12},{2,14},{4,8},{6,10},{8,4},{10,6},{12,0},{14,2},{16,28},{18,... | collective-permute-start | bytes 589832 | tf_op jit(solution)/shard_map/ppermute | solution.py:239
  47.6 0.0 collective-permute-done.14
  47.6 0.8 %collective-permute-start.15 = (bf16[32,3072]{1,0:T(8,128)(2,1)S(1)}, bf16[32,3072]{1,0:T(8,128)(2,1)S(1)}, u32[]{:S(2)}, u32[]{:S(2)}) collective-permute-start(bf16[32,3072]{1,0:T(8,128)(2,1)S(1)} %add_convert_fusion), channel_id=1, source_target_pairs={{0,4},{2,6},{4,0},{6,2},{8,12},{10,14},{12,8},{14,10},{16,20},{18,... | collective-permute-start | bytes 589832 | tf_op jit(solution)/shard_map/ppermute | solution.py:239
  48.4 1.2 %shard_map.80 = (bf16[32,3072]{1,0:T(8,128)(2,1)S(1)}, bf16[32,3072]{1,0:T(8,128)(2,1)S(1)}) custom-call(bf16[32,3072]{1,0:T(8,128)(2,1)S(1)} %get-tuple-element.51.near_ref, bf16[32,3072]{1,0:T(8,128)(2,1)S(1)} %collective-permute-done.1.far_ref, bf16[1,3072]{1,0:T(2,128)(2,1)S(1)} %get-tuple-element.31.gain_ref, ...), custom_call_target="tpu_custom_call" | custom-call | flops 226492416 | bytes 3538944 | tf_op jit(solution)/shard_map/pallas_call | solution.py:97
  49.6 1.4 %collective-permute-start.16 = (bf16[32,3072]{1,0:T(8,128)(2,1)S(1)}, bf16[32,3072]{1,0:T(8,128)(2,1)S(1)}, u32[]{:S(2)}, u32[]{:S(2)}) collective-permute-start(bf16[32,3072]{1,0:T(8,128)(2,1)S(1)} %get-tuple-element.54), channel_id=1, source_target_pairs={{0,2},{2,0},{4,6},{6,4},{8,10},{10,8},{12,14},{14,12},{16,18},{18,... | collective-permute-start | bytes 589832 | tf_op jit(solution)/shard_map/ppermute | solution.py:239
  51.0 0.0 collective-permute-done.12.right_ref
  51.1 1.9 %collective-permute-done.13.refs_1_ = bf16[32,3072]{1,0:T(8,128)(2,1)S(1)} collective-permute-done((bf16[32,3072]{1,0:T(8,128)(2,1)S(1)}, bf16[32,3072]{1,0:T(8,128)(2,1)S(1)}, u32[]{:S(2)}, u32[]{:S(2)}) %collective-permute-start.13) | collective-permute-done | bytes 196640 | tf_op jit(solution)/shard_map/ppermute | solution.py:239
  53.0 2.1 %collective-permute-done.15.refs_2_ = bf16[32,3072]{1,0:T(8,128)(2,1)S(1)} collective-permute-done((bf16[32,3072]{1,0:T(8,128)(2,1)S(1)}, bf16[32,3072]{1,0:T(8,128)(2,1)S(1)}, u32[]{:S(2)}, u32[]{:S(2)}) %collective-permute-start.15) | collective-permute-done | bytes 196640 | tf_op jit(solution)/shard_map/ppermute | solution.py:239
  55.1 0.2 collective-permute-done.16.refs_3_
  55.3 1.1 %shard_map.82 = bf16[128,3072]{1,0:T(8,128)(2,1)} custom-call(f32[128,3072]{1,0:T(8,128)S(1)} %get-tuple-element.34.base_ref, bf16[128,160]{1,0:T(8,128)(2,1)S(1)} %get-tuple-element.35.table_ref, f32[32,3072]{1,0:T(8,128)S(1)} %shard_map.81.refs_0_, bf16[32,3072]{1,0:T(8,128)(2,1)S(1)} %collective-permute-done.13.refs_1_, ...), custom_call_target="tpu_custom_call" | custom-call | flops 100663296 | bytes 2359296 | tf_op jit(solution)/shard_map/pallas_call | solution.py:192
  (7 shorter events, 0.1 us)
Async XLA Ops:
  0.0 4.7 %collective-permute-start = (s32[1,128,2]{1,2,0:T(2,128)}, s32[1,128,2]{1,2,0:T(2,128)S(1)}, u32[]{:S(2)}, u32[]{:S(2)}) collective-permute-start(s32[1,128,2]{1,2,0:T(2,128)} %param.12), channel_id=1, source_target_pairs={{0,16},{2,18},{4,20},{6,22},{8,24},{10,26},{12,28},{14,30},{16,0},... | collective-permute-start | bytes 3080 | tf_op jit(solution)/shard_map/ppermute | solution.py:239
  5.1 12.2 %collective-permute-start.2 = (bf16[32,3072]{1,0:T(8,128)(2,1)S(1)}, bf16[32,3072]{1,0:T(8,128)(2,1)S(1)}, u32[]{:S(2)}, u32[]{:S(2)}) collective-permute-start(bf16[32,3072]{1,0:T(8,128)(2,1)S(1)} %shard_map.74), channel_id=1, source_target_pairs={{0,24},{2,26},{4,28},{6,30},{8,16},{10,18},{12,20},{14,22},{16,8},... | collective-permute-start | bytes 589832 | tf_op jit(solution)/shard_map/ppermute | solution.py:239
  9.2 10.2 %collective-permute-start.1 = (bf16[32,3072]{1,0:T(8,128)(2,1)S(1)}, bf16[32,3072]{1,0:T(8,128)(2,1)S(1)}, u32[]{:S(2)}, u32[]{:S(2)}) collective-permute-start(bf16[32,3072]{1,0:T(8,128)(2,1)S(1)} %shard_map.74), channel_id=1, source_target_pairs={{0,18},{2,16},{4,22},{6,20},{8,26},{10,24},{12,30},{14,28},{16,2},... | collective-permute-start | bytes 589832 | tf_op jit(solution)/shard_map/ppermute | solution.py:239
  10.7 8.7 %copy-start.2 = (bf16[1,128,3072]{2,1,0:T(8,128)(2,1)S(1)}, bf16[1,128,3072]{2,1,0:T(8,128)(2,1)}, u32[]{:S(2)}) copy-start(bf16[1,128,3072]{2,1,0:T(8,128)(2,1)} %param.7) | copy-start | bytes 2359300
  17.2 9.0 %collective-permute-start.7 = (bf16[32,3072]{1,0:T(8,128)(2,1)S(1)}, bf16[32,3072]{1,0:T(8,128)(2,1)S(1)}, u32[]{:S(2)}, u32[]{:S(2)}) collective-permute-start(bf16[32,3072]{1,0:T(8,128)(2,1)S(1)} %collective-permute-done.2.near_ref), channel_id=1, source_target_pairs={{0,2},{2,0},{4,6},{6,4},{8,10},{10,8},{12,14},{14,12},{16,18},{18,... | collective-permute-start | bytes 589832 | tf_op jit(solution)/shard_map/ppermute | solution.py:239
  18.8 7.5 %collective-permute-start.6 = (bf16[32,3072]{1,0:T(8,128)(2,1)S(1)}, bf16[32,3072]{1,0:T(8,128)(2,1)S(1)}, u32[]{:S(2)}, u32[]{:S(2)}) collective-permute-start(bf16[32,3072]{1,0:T(8,128)(2,1)S(1)} %collective-permute-done.2.near_ref), channel_id=1, source_target_pairs={{0,4},{2,6},{4,0},{6,2},{8,12},{10,14},{12,8},{14,10},{16,20},{18,... | collective-permute-start | bytes 589832 | tf_op jit(solution)/shard_map/ppermute | solution.py:239
  19.4 14.2 %collective-permute-start.3 = (bf16[48,3072]{1,0:T(8,128)(2,1)S(1)}, bf16[48,3072]{1,0:T(8,128)(2,1)S(1)}, u32[]{:S(2)}, u32[]{:S(2)}) collective-permute-start(bf16[48,3072]{1,0:T(8,128)(2,1)S(1)} %slice_bitcast_fusion.1), channel_id=1, source_target_pairs={{0,16},{2,18},{4,20},{6,22},{8,24},{10,26},{12,28},{14,30},{16,0},... | collective-permute-start | bytes 884744 | tf_op jit(solution)/shard_map/ppermute | solution.py:239
  20.3 11.1 %collective-permute-start.5 = (bf16[32,3072]{1,0:T(8,128)(2,1)S(1)}, bf16[32,3072]{1,0:T(8,128)(2,1)S(1)}, u32[]{:S(2)}, u32[]{:S(2)}) collective-permute-start(bf16[32,3072]{1,0:T(8,128)(2,1)S(1)} %shard_map.74), channel_id=1, source_target_pairs={{0,20},{2,22},{4,16},{6,18},{8,28},{10,30},{12,24},{14,26},{16,4},... | collective-permute-start | bytes 589832 | tf_op jit(solution)/shard_map/ppermute | solution.py:239
  27.5 6.2 %collective-permute-start.8 = (bf16[32,3072]{1,0:T(8,128)(2,1)S(1)}, bf16[32,3072]{1,0:T(8,128)(2,1)S(1)}, u32[]{:S(2)}, u32[]{:S(2)}) collective-permute-start(bf16[32,3072]{1,0:T(8,128)(2,1)S(1)} %get-tuple-element.43), channel_id=1, source_target_pairs={{0,2},{2,0},{4,6},{6,4},{8,10},{10,8},{12,14},{14,12},{16,18},{18,... | collective-permute-start | bytes 589832 | tf_op jit(solution)/shard_map/ppermute | solution.py:239
  28.0 5.7 %collective-permute-start.9 = (bf16[32,3072]{1,0:T(8,128)(2,1)S(1)}, bf16[32,3072]{1,0:T(8,128)(2,1)S(1)}, u32[]{:S(2)}, u32[]{:S(2)}) collective-permute-start(bf16[32,3072]{1,0:T(8,128)(2,1)S(1)} %collective-permute-done.7.far_ref), channel_id=1, source_target_pairs={{0,4},{2,6},{4,0},{6,2},{8,12},{10,14},{12,8},{14,10},{16,20},{18,... | collective-permute-start | bytes 589832 | tf_op jit(solution)/shard_map/ppermute | solution.py:239
  29.0 13.5 %collective-permute-start.4 = (bf16[80,3072]{1,0:T(8,128)(2,1)S(1)}, bf16[80,3072]{1,0:T(8,128)(2,1)S(1)}, u32[]{:S(2)}, u32[]{:S(2)}) collective-permute-start(bf16[80,3072]{1,0:T(8,128)(2,1)S(1)} %slice_bitcast_fusion), channel_id=1, source_target_pairs={{0,16},{2,18},{4,20},{6,22},{8,24},{10,26},{12,28},{14,30},{16,0},... | collective-permute-start | bytes 1474568 | tf_op jit(solution)/shard_map/ppermute | solution.py:239
  31.3 7.7 %collective-permute-start.10 = (bf16[32,3072]{1,0:T(8,128)(2,1)S(1)}, bf16[32,3072]{1,0:T(8,128)(2,1)S(1)}, u32[]{:S(2)}, u32[]{:S(2)}) collective-permute-start(bf16[32,3072]{1,0:T(8,128)(2,1)S(1)} %collective-permute-done.5.near_ref), channel_id=1, source_target_pairs={{0,2},{2,0},{4,6},{6,4},{8,10},{10,8},{12,14},{14,12},{16,18},{18,... | collective-permute-start | bytes 589832 | tf_op jit(solution)/shard_map/ppermute | solution.py:239
  34.8 8.7 %collective-permute-start.11 = (bf16[32,3072]{1,0:T(8,128)(2,1)S(1)}, bf16[32,3072]{1,0:T(8,128)(2,1)S(1)}, u32[]{:S(2)}, u32[]{:S(2)}) collective-permute-start(bf16[32,3072]{1,0:T(8,128)(2,1)S(1)} %get-tuple-element.50), channel_id=1, source_target_pairs={{0,2},{2,0},{4,6},{6,4},{8,10},{10,8},{12,14},{14,12},{16,18},{18,... | collective-permute-start | bytes 589832 | tf_op jit(solution)/shard_map/ppermute | solution.py:239
  36.5 6.0 %copy-start = (s32[1,128,2]{1,2,0:T(2,128)S(1)}, s32[1,128,2]{1,2,0:T(2,128)}, u32[]{:S(2)}) copy-start(s32[1,128,2]{1,2,0:T(2,128)} %param.12) | copy-start | bytes 3076
  36.5 6.0 %copy-start.1 = (f32[1,128,2]{1,2,0:T(2,128)S(1)}, f32[1,128,2]{1,2,0:T(2,128)}, u32[]{:S(2)}) copy-start(f32[1,128,2]{1,2,0:T(2,128)} %param.13) | copy-start | bytes 3076
  36.5 14.5 %collective-permute-start.12 = (bf16[32,3072]{1,0:T(8,128)(2,1)S(1)}, bf16[32,3072]{1,0:T(8,128)(2,1)S(1)}, u32[]{:S(2)}, u32[]{:S(2)}) collective-permute-start(bf16[32,3072]{1,0:T(8,128)(2,1)S(1)} %add_convert_fusion.2), channel_id=1, source_target_pairs={{0,8},{2,10},{4,12},{6,14},{8,0},{10,2},{12,4},{14,6},{16,24},{18,... | collective-permute-start | bytes 589832 | tf_op jit(solution)/shard_map/ppermute | solution.py:239
  40.2 7.4 %collective-permute-start.14 = (bf16[32,3072]{1,0:T(8,128)(2,1)S(1)}, bf16[32,3072]{1,0:T(8,128)(2,1)S(1)}, u32[]{:S(2)}, u32[]{:S(2)}) collective-permute-start(bf16[32,3072]{1,0:T(8,128)(2,1)S(1)} %get-tuple-element.53), channel_id=1, source_target_pairs={{0,2},{2,0},{4,6},{6,4},{8,10},{10,8},{12,14},{14,12},{16,18},{18,... | collective-permute-start | bytes 589832 | tf_op jit(solution)/shard_map/ppermute | solution.py:239
  43.6 9.4 %collective-permute-start.13 = (bf16[32,3072]{1,0:T(8,128)(2,1)S(1)}, bf16[32,3072]{1,0:T(8,128)(2,1)S(1)}, u32[]{:S(2)}, u32[]{:S(2)}) collective-permute-start(bf16[32,3072]{1,0:T(8,128)(2,1)S(1)} %add_convert_fusion.1), channel_id=1, source_target_pairs={{0,12},{2,14},{4,8},{6,10},{8,4},{10,6},{12,0},{14,2},{16,28},{18,... | collective-permute-start | bytes 589832 | tf_op jit(solution)/shard_map/ppermute | solution.py:239
  47.6 7.5 %collective-permute-start.15 = (bf16[32,3072]{1,0:T(8,128)(2,1)S(1)}, bf16[32,3072]{1,0:T(8,128)(2,1)S(1)}, u32[]{:S(2)}, u32[]{:S(2)}) collective-permute-start(bf16[32,3072]{1,0:T(8,128)(2,1)S(1)} %add_convert_fusion), channel_id=1, source_target_pairs={{0,4},{2,6},{4,0},{6,2},{8,12},{10,14},{12,8},{14,10},{16,20},{18,... | collective-permute-start | bytes 589832 | tf_op jit(solution)/shard_map/ppermute | solution.py:239
  49.6 5.7 %collective-permute-start.16 = (bf16[32,3072]{1,0:T(8,128)(2,1)S(1)}, bf16[32,3072]{1,0:T(8,128)(2,1)S(1)}, u32[]{:S(2)}, u32[]{:S(2)}) collective-permute-start(bf16[32,3072]{1,0:T(8,128)(2,1)S(1)} %get-tuple-element.54), channel_id=1, source_target_pairs={{0,2},{2,0},{4,6},{6,4},{8,10},{10,8},{12,14},{14,12},{16,18},{18,... | collective-permute-start | bytes 589832 | tf_op jit(solution)/shard_map/ppermute | solution.py:239

commit v17 on v16

--- a/solution.py
+++ b/solution.py
@@ -136,12 +136,8 @@
         weight = jnp.sum(jnp.where(ids == e, weights, 0.0), axis=0, keepdims=True)
         slots = slot_rows(ids, e)
         tables.append(slots * weight)
-        start, total = 0, 0.0
-        for ref in block_refs:
-            end = start + ref.shape[0]
-            part = slots[:, start:end].astype(jnp.bfloat16)
-            total += jnp.dot(part, ref[...], preferred_element_type=jnp.float32)
-            start = end
+        whole = jnp.concatenate([ref[...] for ref in block_refs], axis=0)
+        total = jnp.dot(slots.astype(jnp.bfloat16), whole, preferred_element_type=jnp.float32)
         pick_ref[e * CAP:(e + 1) * CAP, :] = total.astype(jnp.bfloat16)
     terms = parts_of(jnp.concatenate(tables, axis=0).T)
     table_ref[...] = jnp.concatenate(terms + terms[:2], axis=1)

time: 56.6 us -> 56.6 us (level)
  transfers between devices with their start and end apart: 17 -> 17, of which waited for: 9 -> 9; matrix products, arithmetic and copies ran while one was open for 0% -> 0% of each run, Pallas kernels for 16% -> 15%
where the time goes in v17:
time: 56.6 us; the launch traced here: 56.4 us
  starting transfers between devices  27.8 us (49%)
  waiting for transfers between devices  18.1 us (32%)
  Pallas kernels  10.2 us (18%)
    ppermute x17, starting transfers between devices, moved(): return lax.ppermute(value, ('section', 'expert'), pairs)  27.8 us
    ppermute x17, waiting for transfers between devices, moved(): return lax.ppermute(value, ('section', 'expert'), pairs)  18.1 us
    pallas_call x4, Pallas kernels, mlp(): pl.pallas_call(mlp_kernel, out_shape=(out, out), in_specs=[VMEM] * 6, out...  4.69 us
    pallas_call x2, Pallas kernels, loaded(): pl.pallas_call(functools.partial(load_kernel, len(arrays)), out_shape=tup...  3.23 us
    pallas_call x1, Pallas kernels, ended(): pl.pallas_call(functools.partial(end_kernel, steps), out_shape=jax.ShapeD...  1.14 us
  transfers between devices with their start and end apart: 17, of which 9 were waited for; matrix products, arithmetic and copies ran while one was open for 0% of the time, Pallas kernels for 15%

profile of v17, /device:TPU:0, one launch (start us, length us, event | category | flops | bytes accessed | tf_op | source)
XLA Modules:
  0.0 56.4 jit_solution(14096617125548335496)
XLA Ops:
  0.0 2.9 %collective-permute-start = (s32[1,128,2]{1,2,0:T(2,128)}, s32[1,128,2]{1,2,0:T(2,128)S(1)}, u32[]{:S(2)}, u32[]{:S(2)}) collective-permute-start(s32[1,128,2]{1,2,0:T(2,128)} %param.12), channel_id=1, source_target_pairs={{0,16},{2,18},{4,20},{6,22},{8,24},{10,26},{12,28},{14,30},{16,0},... | collective-permute-start | bytes 3080 | tf_op jit(solution)/shard_map/ppermute | solution.py:235
  2.9 1.1 %shard_map.73.block_ref = bf16[128,3072]{1,0:T(8,128)(2,1)S(1)} custom-call(bf16[128,3072]{1,0:T(8,128)(2,1)} %bitcast.25), custom_call_target="tpu_custom_call" | custom-call | bytes 6291456 | tf_op jit(solution)/shard_map/pallas_call | solution.py:33
  4.1 0.6 %collective-permute-done = s32[1,128,2]{1,2,0:T(2,128)S(1)} collective-permute-done((s32[1,128,2]{1,2,0:T(2,128)}, s32[1,128,2]{1,2,0:T(2,128)S(1)}, u32[]{:S(2)}, u32[]{:S(2)}) %collective-permute-start) | collective-permute-done | bytes 1056 | tf_op jit(solution)/shard_map/ppermute | solution.py:235
  4.7 0.4 shard_map.74
  5.1 4.1 %collective-permute-start.2 = (bf16[32,3072]{1,0:T(8,128)(2,1)S(1)}, bf16[32,3072]{1,0:T(8,128)(2,1)S(1)}, u32[]{:S(2)}, u32[]{:S(2)}) collective-permute-start(bf16[32,3072]{1,0:T(8,128)(2,1)S(1)} %shard_map.74), channel_id=1, source_target_pairs={{0,24},{2,26},{4,28},{6,30},{8,16},{10,18},{12,20},{14,22},{16,8},... | collective-permute-start | bytes 589832 | tf_op jit(solution)/shard_map/ppermute | solution.py:235
  9.2 1.5 %collective-permute-start.1 = (bf16[32,3072]{1,0:T(8,128)(2,1)S(1)}, bf16[32,3072]{1,0:T(8,128)(2,1)S(1)}, u32[]{:S(2)}, u32[]{:S(2)}) collective-permute-start(bf16[32,3072]{1,0:T(8,128)(2,1)S(1)} %shard_map.74), channel_id=1, source_target_pairs={{0,18},{2,16},{4,22},{6,20},{8,26},{10,24},{12,30},{14,28},{16,2},... | collective-permute-start | bytes 589832 | tf_op jit(solution)/shard_map/ppermute | solution.py:235
  10.7 2.1 %shard_map.75 = (bf16[192,3072]{1,0:T(8,128)(2,1)S(1)}, bf16[192,3072]{1,0:T(8,128)(2,1)S(1)}, bf16[192,3072]{1,0:T(8,128)(2,1)S(1)}, bf16[1,3072]{1,0:T(2,128)(2,1)S(1)}) custom-call(bf16[192,3072]{1,0:T(8,128)(2,1)} %bitcast.26, bf16[192,3072]{1,0:T(8,128)(2,1)} %bitcast.27, bf16[192,3072]{1,0:T(8,128)(2,1)} %bitcast.28, bf16[1,3072]{1,0:T(2,128)(2,1)} %refs_3_.1), custom_call_target="tpu_custom_call" | custom-call | bytes 6291456 | tf_op jit(solution)/shard_map/pallas_call | solution.py:33
  12.8 4.5 %collective-permute-done.2.near_ref = bf16[32,3072]{1,0:T(8,128)(2,1)S(1)} collective-permute-done((bf16[32,3072]{1,0:T(8,128)(2,1)S(1)}, bf16[32,3072]{1,0:T(8,128)(2,1)S(1)}, u32[]{:S(2)}, u32[]{:S(2)}) %collective-permute-start.2) | collective-permute-done | bytes 196640 | tf_op jit(solution)/shard_map/ppermute | solution.py:235
  17.2 1.5 %collective-permute-start.7 = (bf16[32,3072]{1,0:T(8,128)(2,1)S(1)}, bf16[32,3072]{1,0:T(8,128)(2,1)S(1)}, u32[]{:S(2)}, u32[]{:S(2)}) collective-permute-start(bf16[32,3072]{1,0:T(8,128)(2,1)S(1)} %collective-permute-done.2.near_ref), channel_id=1, source_target_pairs={{0,2},{2,0},{4,6},{6,4},{8,10},{10,8},{12,14},{14,12},{16,18},{18,... | collective-permute-start | bytes 589832 | tf_op jit(solution)/shard_map/ppermute | solution.py:235
  18.8 0.6 %collective-permute-start.6 = (bf16[32,3072]{1,0:T(8,128)(2,1)S(1)}, bf16[32,3072]{1,0:T(8,128)(2,1)S(1)}, u32[]{:S(2)}, u32[]{:S(2)}) collective-permute-start(bf16[32,3072]{1,0:T(8,128)(2,1)S(1)} %collective-permute-done.2.near_ref), channel_id=1, source_target_pairs={{0,4},{2,6},{4,0},{6,2},{8,12},{10,14},{12,8},{14,10},{16,20},{18,... | collective-permute-start | bytes 589832 | tf_op jit(solution)/shard_map/ppermute | solution.py:235
  19.4 0.0 copy-done.2
  19.4 0.0 collective-permute-done.1.far_ref
  19.4 0.9 %collective-permute-start.3 = (bf16[48,3072]{1,0:T(8,128)(2,1)S(1)}, bf16[48,3072]{1,0:T(8,128)(2,1)S(1)}, u32[]{:S(2)}, u32[]{:S(2)}) collective-permute-start(bf16[48,3072]{1,0:T(8,128)(2,1)S(1)} %slice_bitcast_fusion.1), channel_id=1, source_target_pairs={{0,16},{2,18},{4,20},{6,22},{8,24},{10,26},{12,28},{14,30},{16,0},... | collective-permute-start | bytes 884744 | tf_op jit(solution)/shard_map/ppermute | solution.py:235
  20.3 2.1 %collective-permute-start.5 = (bf16[32,3072]{1,0:T(8,128)(2,1)S(1)}, bf16[32,3072]{1,0:T(8,128)(2,1)S(1)}, u32[]{:S(2)}, u32[]{:S(2)}) collective-permute-start(bf16[32,3072]{1,0:T(8,128)(2,1)S(1)} %shard_map.74), channel_id=1, source_target_pairs={{0,20},{2,22},{4,16},{6,18},{8,28},{10,30},{12,24},{14,26},{16,4},... | collective-permute-start | bytes 589832 | tf_op jit(solution)/shard_map/ppermute | solution.py:235
  22.4 3.9 %collective-permute-done.6.near_ref = bf16[32,3072]{1,0:T(8,128)(2,1)S(1)} collective-permute-done((bf16[32,3072]{1,0:T(8,128)(2,1)S(1)}, bf16[32,3072]{1,0:T(8,128)(2,1)S(1)}, u32[]{:S(2)}, u32[]{:S(2)}) %collective-permute-start.6) | collective-permute-done | bytes 196640 | tf_op jit(solution)/shard_map/ppermute | solution.py:235
  26.3 0.0 collective-permute-done.7.far_ref
  26.3 1.2 %shard_map.77 = (bf16[32,3072]{1,0:T(8,128)(2,1)S(1)}, bf16[32,3072]{1,0:T(8,128)(2,1)S(1)}) custom-call(bf16[32,3072]{1,0:T(8,128)(2,1)S(1)} %collective-permute-done.2.near_ref, bf16[32,3072]{1,0:T(8,128)(2,1)S(1)} %collective-permute-done.7.far_ref, bf16[1,3072]{1,0:T(2,128)(2,1)S(1)} %get-tuple-element.31.gain_ref, ...), custom_call_target="tpu_custom_call" | custom-call | flops 226492416 | bytes 3538944 | tf_op jit(solution)/shard_map/pallas_call | solution.py:97
  27.5 0.5 collective-permute-start.8
  28.0 1.0 %collective-permute-start.9 = (bf16[32,3072]{1,0:T(8,128)(2,1)S(1)}, bf16[32,3072]{1,0:T(8,128)(2,1)S(1)}, u32[]{:S(2)}, u32[]{:S(2)}) collective-permute-start(bf16[32,3072]{1,0:T(8,128)(2,1)S(1)} %collective-permute-done.7.far_ref), channel_id=1, source_target_pairs={{0,4},{2,6},{4,0},{6,2},{8,12},{10,14},{12,8},{14,10},{16,20},{18,... | collective-permute-start | bytes 589832 | tf_op jit(solution)/shard_map/ppermute | solution.py:235
  29.0 0.6 %collective-permute-start.4 = (bf16[80,3072]{1,0:T(8,128)(2,1)S(1)}, bf16[80,3072]{1,0:T(8,128)(2,1)S(1)}, u32[]{:S(2)}, u32[]{:S(2)}) collective-permute-start(bf16[80,3072]{1,0:T(8,128)(2,1)S(1)} %slice_bitcast_fusion), channel_id=1, source_target_pairs={{0,16},{2,18},{4,20},{6,22},{8,24},{10,26},{12,28},{14,30},{16,0},... | collective-permute-start | bytes 1474568 | tf_op jit(solution)/shard_map/ppermute | solution.py:235
  29.6 1.7 %collective-permute-done.5.near_ref = bf16[32,3072]{1,0:T(8,128)(2,1)S(1)} collective-permute-done((bf16[32,3072]{1,0:T(8,128)(2,1)S(1)}, bf16[32,3072]{1,0:T(8,128)(2,1)S(1)}, u32[]{:S(2)}, u32[]{:S(2)}) %collective-permute-start.5) | collective-permute-done | bytes 196640 | tf_op jit(solution)/shard_map/ppermute | solution.py:235
  31.3 0.0 collective-permute-start.10
  31.3 2.3 %collective-permute-done.3.refs_0_ = bf16[48,3072]{1,0:T(8,128)(2,1)S(1)} collective-permute-done((bf16[48,3072]{1,0:T(8,128)(2,1)S(1)}, bf16[48,3072]{1,0:T(8,128)(2,1)S(1)}, u32[]{:S(2)}, u32[]{:S(2)}) %collective-permute-start.3) | collective-permute-done | bytes 294944 | tf_op jit(solution)/shard_map/ppermute | solution.py:235
  33.6 0.0 collective-permute-done.8
  33.6 0.0 collective-permute-done.9.far_ref
  33.6 1.2 %shard_map.78 = (bf16[32,3072]{1,0:T(8,128)(2,1)S(1)}, bf16[32,3072]{1,0:T(8,128)(2,1)S(1)}) custom-call(bf16[32,3072]{1,0:T(8,128)(2,1)S(1)} %collective-permute-done.6.near_ref, bf16[32,3072]{1,0:T(8,128)(2,1)S(1)} %collective-permute-done.9.far_ref, bf16[1,3072]{1,0:T(2,128)(2,1)S(1)} %get-tuple-element.31.gain_ref, ...), custom_call_target="tpu_custom_call" | custom-call | flops 226492416 | bytes 3538944 | tf_op jit(solution)/shard_map/pallas_call | solution.py:97
  34.8 1.6 %collective-permute-start.11 = (bf16[32,3072]{1,0:T(8,128)(2,1)S(1)}, bf16[32,3072]{1,0:T(8,128)(2,1)S(1)}, u32[]{:S(2)}, u32[]{:S(2)}) collective-permute-start(bf16[32,3072]{1,0:T(8,128)(2,1)S(1)} %get-tuple-element.50), channel_id=1, source_target_pairs={{0,2},{2,0},{4,6},{6,4},{8,10},{10,8},{12,14},{14,12},{16,18},{18,... | collective-permute-start | bytes 589832 | tf_op jit(solution)/shard_map/ppermute | solution.py:235
  36.5 0.1 add_convert_fusion.2
  36.5 0.0 copy-start
  36.5 0.0 copy-start.1
  36.5 2.5 %collective-permute-start.12 = (bf16[32,3072]{1,0:T(8,128)(2,1)S(1)}, bf16[32,3072]{1,0:T(8,128)(2,1)S(1)}, u32[]{:S(2)}, u32[]{:S(2)}) collective-permute-start(bf16[32,3072]{1,0:T(8,128)(2,1)S(1)} %add_convert_fusion.2), channel_id=1, source_target_pairs={{0,8},{2,10},{4,12},{6,14},{8,0},{10,2},{12,4},{14,6},{16,24},{18,... | collective-permute-start | bytes 589832 | tf_op jit(solution)/shard_map/ppermute | solution.py:235
  39.0 0.0 collective-permute-done.10.far_ref
  39.0 1.2 %shard_map.79 = (bf16[32,3072]{1,0:T(8,128)(2,1)S(1)}, bf16[32,3072]{1,0:T(8,128)(2,1)S(1)}) custom-call(bf16[32,3072]{1,0:T(8,128)(2,1)S(1)} %collective-permute-done.5.near_ref, bf16[32,3072]{1,0:T(8,128)(2,1)S(1)} %collective-permute-done.10.far_ref, bf16[1,3072]{1,0:T(2,128)(2,1)S(1)} %get-tuple-element.31.gain_ref, ...), custom_call_target="tpu_custom_call" | custom-call | flops 226492416 | bytes 3538944 | tf_op jit(solution)/shard_map/pallas_call | solution.py:97
  40.2 1.5 %collective-permute-start.14 = (bf16[32,3072]{1,0:T(8,128)(2,1)S(1)}, bf16[32,3072]{1,0:T(8,128)(2,1)S(1)}, u32[]{:S(2)}, u32[]{:S(2)}) collective-permute-start(bf16[32,3072]{1,0:T(8,128)(2,1)S(1)} %get-tuple-element.53), channel_id=1, source_target_pairs={{0,2},{2,0},{4,6},{6,4},{8,10},{10,8},{12,14},{14,12},{16,18},{18,... | collective-permute-start | bytes 589832 | tf_op jit(solution)/shard_map/ppermute | solution.py:235
  41.7 0.8 %collective-permute-done.4.refs_1_ = bf16[80,3072]{1,0:T(8,128)(2,1)S(1)} collective-permute-done((bf16[80,3072]{1,0:T(8,128)(2,1)S(1)}, bf16[80,3072]{1,0:T(8,128)(2,1)S(1)}, u32[]{:S(2)}, u32[]{:S(2)}) %collective-permute-start.4) | collective-permute-done | bytes 491552 | tf_op jit(solution)/shard_map/ppermute | solution.py:235
  42.5 0.0 copy-done.1
  42.5 0.8 %shard_map.76 = (f32[128,3072]{1,0:T(8,128)S(1)}, bf16[128,160]{1,0:T(8,128)(2,1)S(1)}, bf16[32,3072]{1,0:T(8,128)(2,1)S(1)}) custom-call(bf16[1,3072]{1,0:T(2,128)(2,1)S(1)} %get-tuple-element.31.gain_ref, s32[2,128]{1,0:T(2,128)S(1)} %bitcast.22, f32[2,128]{1,0:T(2,128)S(1)} %bitcast.23, bf16[48,3072]{1,0:T(8,128)(2,1)S(1)} %collective-permute-done.3.refs_0_, ...), custom_call_target="tpu_custom_call" | custom-call | flops 3145728 | bytes 2359296 | tf_op jit(solution)/shard_map/pallas_call | solution.py:148
  43.3 0.0 collective-permute-done.11
  43.3 4.2 %collective-permute-start.13 = (bf16[32,3072]{1,0:T(8,128)(2,1)S(1)}, bf16[32,3072]{1,0:T(8,128)(2,1)S(1)}, u32[]{:S(2)}, u32[]{:S(2)}) collective-permute-start(bf16[32,3072]{1,0:T(8,128)(2,1)S(1)} %add_convert_fusion.1), channel_id=1, source_target_pairs={{0,12},{2,14},{4,8},{6,10},{8,4},{10,6},{12,0},{14,2},{16,28},{18,... | collective-permute-start | bytes 589832 | tf_op jit(solution)/shard_map/ppermute | solution.py:235
  47.6 0.0 collective-permute-done.14
  47.6 0.8 %collective-permute-start.15 = (bf16[32,3072]{1,0:T(8,128)(2,1)S(1)}, bf16[32,3072]{1,0:T(8,128)(2,1)S(1)}, u32[]{:S(2)}, u32[]{:S(2)}) collective-permute-start(bf16[32,3072]{1,0:T(8,128)(2,1)S(1)} %add_convert_fusion), channel_id=1, source_target_pairs={{0,4},{2,6},{4,0},{6,2},{8,12},{10,14},{12,8},{14,10},{16,20},{18,... | collective-permute-start | bytes 589832 | tf_op jit(solution)/shard_map/ppermute | solution.py:235
  48.4 1.2 %shard_map.80 = (bf16[32,3072]{1,0:T(8,128)(2,1)S(1)}, bf16[32,3072]{1,0:T(8,128)(2,1)S(1)}) custom-call(bf16[32,3072]{1,0:T(8,128)(2,1)S(1)} %get-tuple-element.51.near_ref, bf16[32,3072]{1,0:T(8,128)(2,1)S(1)} %collective-permute-done.1.far_ref, bf16[1,3072]{1,0:T(2,128)(2,1)S(1)} %get-tuple-element.31.gain_ref, ...), custom_call_target="tpu_custom_call" | custom-call | flops 226492416 | bytes 3538944 | tf_op jit(solution)/shard_map/pallas_call | solution.py:97
  49.6 1.4 %collective-permute-start.16 = (bf16[32,3072]{1,0:T(8,128)(2,1)S(1)}, bf16[32,3072]{1,0:T(8,128)(2,1)S(1)}, u32[]{:S(2)}, u32[]{:S(2)}) collective-permute-start(bf16[32,3072]{1,0:T(8,128)(2,1)S(1)} %get-tuple-element.54), channel_id=1, source_target_pairs={{0,2},{2,0},{4,6},{6,4},{8,10},{10,8},{12,14},{14,12},{16,18},{18,... | collective-permute-start | bytes 589832 | tf_op jit(solution)/shard_map/ppermute | solution.py:235
  51.0 0.0 collective-permute-done.12.right_ref
  51.1 1.8 %collective-permute-done.13.refs_1_ = bf16[32,3072]{1,0:T(8,128)(2,1)S(1)} collective-permute-done((bf16[32,3072]{1,0:T(8,128)(2,1)S(1)}, bf16[32,3072]{1,0:T(8,128)(2,1)S(1)}, u32[]{:S(2)}, u32[]{:S(2)}) %collective-permute-start.13) | collective-permute-done | bytes 196640 | tf_op jit(solution)/shard_map/ppermute | solution.py:235
  52.8 2.0 %collective-permute-done.15.refs_2_ = bf16[32,3072]{1,0:T(8,128)(2,1)S(1)} collective-permute-done((bf16[32,3072]{1,0:T(8,128)(2,1)S(1)}, bf16[32,3072]{1,0:T(8,128)(2,1)S(1)}, u32[]{:S(2)}, u32[]{:S(2)}) %collective-permute-start.15) | collective-permute-done | bytes 196640 | tf_op jit(solution)/shard_map/ppermute | solution.py:235
  54.9 0.4 collective-permute-done.16.refs_3_
  55.3 1.1 %shard_map.82 = bf16[128,3072]{1,0:T(8,128)(2,1)} custom-call(f32[128,3072]{1,0:T(8,128)S(1)} %get-tuple-element.34.base_ref, bf16[128,160]{1,0:T(8,128)(2,1)S(1)} %get-tuple-element.35.table_ref, f32[32,3072]{1,0:T(8,128)S(1)} %shard_map.81.refs_0_, bf16[32,3072]{1,0:T(8,128)(2,1)S(1)} %collective-permute-done.13.refs_1_, ...), custom_call_target="tpu_custom_call" | custom-call | flops 100663296 | bytes 2359296 | tf_op jit(solution)/shard_map/pallas_call | solution.py:188
  (7 shorter events, 0.2 us)
Async XLA Ops:
  0.0 4.7 %collective-permute-start = (s32[1,128,2]{1,2,0:T(2,128)}, s32[1,128,2]{1,2,0:T(2,128)S(1)}, u32[]{:S(2)}, u32[]{:S(2)}) collective-permute-start(s32[1,128,2]{1,2,0:T(2,128)} %param.12), channel_id=1, source_target_pairs={{0,16},{2,18},{4,20},{6,22},{8,24},{10,26},{12,28},{14,30},{16,0},... | collective-permute-start | bytes 3080 | tf_op jit(solution)/shard_map/ppermute | solution.py:235
  5.1 12.2 %collective-permute-start.2 = (bf16[32,3072]{1,0:T(8,128)(2,1)S(1)}, bf16[32,3072]{1,0:T(8,128)(2,1)S(1)}, u32[]{:S(2)}, u32[]{:S(2)}) collective-permute-start(bf16[32,3072]{1,0:T(8,128)(2,1)S(1)} %shard_map.74), channel_id=1, source_target_pairs={{0,24},{2,26},{4,28},{6,30},{8,16},{10,18},{12,20},{14,22},{16,8},... | collective-permute-start | bytes 589832 | tf_op jit(solution)/shard_map/ppermute | solution.py:235
  9.2 10.2 %collective-permute-start.1 = (bf16[32,3072]{1,0:T(8,128)(2,1)S(1)}, bf16[32,3072]{1,0:T(8,128)(2,1)S(1)}, u32[]{:S(2)}, u32[]{:S(2)}) collective-permute-start(bf16[32,3072]{1,0:T(8,128)(2,1)S(1)} %shard_map.74), channel_id=1, source_target_pairs={{0,18},{2,16},{4,22},{6,20},{8,26},{10,24},{12,30},{14,28},{16,2},... | collective-permute-start | bytes 589832 | tf_op jit(solution)/shard_map/ppermute | solution.py:235
  10.7 8.7 %copy-start.2 = (bf16[1,128,3072]{2,1,0:T(8,128)(2,1)S(1)}, bf16[1,128,3072]{2,1,0:T(8,128)(2,1)}, u32[]{:S(2)}) copy-start(bf16[1,128,3072]{2,1,0:T(8,128)(2,1)} %param.7) | copy-start | bytes 2359300
  17.2 9.0 %collective-permute-start.7 = (bf16[32,3072]{1,0:T(8,128)(2,1)S(1)}, bf16[32,3072]{1,0:T(8,128)(2,1)S(1)}, u32[]{:S(2)}, u32[]{:S(2)}) collective-permute-start(bf16[32,3072]{1,0:T(8,128)(2,1)S(1)} %collective-permute-done.2.near_ref), channel_id=1, source_target_pairs={{0,2},{2,0},{4,6},{6,4},{8,10},{10,8},{12,14},{14,12},{16,18},{18,... | collective-permute-start | bytes 589832 | tf_op jit(solution)/shard_map/ppermute | solution.py:235
  18.8 7.5 %collective-permute-start.6 = (bf16[32,3072]{1,0:T(8,128)(2,1)S(1)}, bf16[32,3072]{1,0:T(8,128)(2,1)S(1)}, u32[]{:S(2)}, u32[]{:S(2)}) collective-permute-start(bf16[32,3072]{1,0:T(8,128)(2,1)S(1)} %collective-permute-done.2.near_ref), channel_id=1, source_target_pairs={{0,4},{2,6},{4,0},{6,2},{8,12},{10,14},{12,8},{14,10},{16,20},{18,... | collective-permute-start | bytes 589832 | tf_op jit(solution)/shard_map/ppermute | solution.py:235
  19.4 14.2 %collective-permute-start.3 = (bf16[48,3072]{1,0:T(8,128)(2,1)S(1)}, bf16[48,3072]{1,0:T(8,128)(2,1)S(1)}, u32[]{:S(2)}, u32[]{:S(2)}) collective-permute-start(bf16[48,3072]{1,0:T(8,128)(2,1)S(1)} %slice_bitcast_fusion.1), channel_id=1, source_target_pairs={{0,16},{2,18},{4,20},{6,22},{8,24},{10,26},{12,28},{14,30},{16,0},... | collective-permute-start | bytes 884744 | tf_op jit(solution)/shard_map/ppermute | solution.py:235
  20.3 11.1 %collective-permute-start.5 = (bf16[32,3072]{1,0:T(8,128)(2,1)S(1)}, bf16[32,3072]{1,0:T(8,128)(2,1)S(1)}, u32[]{:S(2)}, u32[]{:S(2)}) collective-permute-start(bf16[32,3072]{1,0:T(8,128)(2,1)S(1)} %shard_map.74), channel_id=1, source_target_pairs={{0,20},{2,22},{4,16},{6,18},{8,28},{10,30},{12,24},{14,26},{16,4},... | collective-permute-start | bytes 589832 | tf_op jit(solution)/shard_map/ppermute | solution.py:235
  27.5 6.2 %collective-permute-start.8 = (bf16[32,3072]{1,0:T(8,128)(2,1)S(1)}, bf16[32,3072]{1,0:T(8,128)(2,1)S(1)}, u32[]{:S(2)}, u32[]{:S(2)}) collective-permute-start(bf16[32,3072]{1,0:T(8,128)(2,1)S(1)} %get-tuple-element.43), channel_id=1, source_target_pairs={{0,2},{2,0},{4,6},{6,4},{8,10},{10,8},{12,14},{14,12},{16,18},{18,... | collective-permute-start | bytes 589832 | tf_op jit(solution)/shard_map/ppermute | solution.py:235
  28.0 5.7 %collective-permute-start.9 = (bf16[32,3072]{1,0:T(8,128)(2,1)S(1)}, bf16[32,3072]{1,0:T(8,128)(2,1)S(1)}, u32[]{:S(2)}, u32[]{:S(2)}) collective-permute-start(bf16[32,3072]{1,0:T(8,128)(2,1)S(1)} %collective-permute-done.7.far_ref), channel_id=1, source_target_pairs={{0,4},{2,6},{4,0},{6,2},{8,12},{10,14},{12,8},{14,10},{16,20},{18,... | collective-permute-start | bytes 589832 | tf_op jit(solution)/shard_map/ppermute | solution.py:235
  29.0 13.5 %collective-permute-start.4 = (bf16[80,3072]{1,0:T(8,128)(2,1)S(1)}, bf16[80,3072]{1,0:T(8,128)(2,1)S(1)}, u32[]{:S(2)}, u32[]{:S(2)}) collective-permute-start(bf16[80,3072]{1,0:T(8,128)(2,1)S(1)} %slice_bitcast_fusion), channel_id=1, source_target_pairs={{0,16},{2,18},{4,20},{6,22},{8,24},{10,26},{12,28},{14,30},{16,0},... | collective-permute-start | bytes 1474568 | tf_op jit(solution)/shard_map/ppermute | solution.py:235
  31.3 7.7 %collective-permute-start.10 = (bf16[32,3072]{1,0:T(8,128)(2,1)S(1)}, bf16[32,3072]{1,0:T(8,128)(2,1)S(1)}, u32[]{:S(2)}, u32[]{:S(2)}) collective-permute-start(bf16[32,3072]{1,0:T(8,128)(2,1)S(1)} %collective-permute-done.5.near_ref), channel_id=1, source_target_pairs={{0,2},{2,0},{4,6},{6,4},{8,10},{10,8},{12,14},{14,12},{16,18},{18,... | collective-permute-start | bytes 589832 | tf_op jit(solution)/shard_map/ppermute | solution.py:235
  34.8 8.5 %collective-permute-start.11 = (bf16[32,3072]{1,0:T(8,128)(2,1)S(1)}, bf16[32,3072]{1,0:T(8,128)(2,1)S(1)}, u32[]{:S(2)}, u32[]{:S(2)}) collective-permute-start(bf16[32,3072]{1,0:T(8,128)(2,1)S(1)} %get-tuple-element.50), channel_id=1, source_target_pairs={{0,2},{2,0},{4,6},{6,4},{8,10},{10,8},{12,14},{14,12},{16,18},{18,... | collective-permute-start | bytes 589832 | tf_op jit(solution)/shard_map/ppermute | solution.py:235
  36.5 6.0 %copy-start = (s32[1,128,2]{1,2,0:T(2,128)S(1)}, s32[1,128,2]{1,2,0:T(2,128)}, u32[]{:S(2)}) copy-start(s32[1,128,2]{1,2,0:T(2,128)} %param.12) | copy-start | bytes 3076
  36.5 6.0 %copy-start.1 = (f32[1,128,2]{1,2,0:T(2,128)S(1)}, f32[1,128,2]{1,2,0:T(2,128)}, u32[]{:S(2)}) copy-start(f32[1,128,2]{1,2,0:T(2,128)} %param.13) | copy-start | bytes 3076
  36.5 14.5 %collective-permute-start.12 = (bf16[32,3072]{1,0:T(8,128)(2,1)S(1)}, bf16[32,3072]{1,0:T(8,128)(2,1)S(1)}, u32[]{:S(2)}, u32[]{:S(2)}) collective-permute-start(bf16[32,3072]{1,0:T(8,128)(2,1)S(1)} %add_convert_fusion.2), channel_id=1, source_target_pairs={{0,8},{2,10},{4,12},{6,14},{8,0},{10,2},{12,4},{14,6},{16,24},{18,... | collective-permute-start | bytes 589832 | tf_op jit(solution)/shard_map/ppermute | solution.py:235
  40.2 7.4 %collective-permute-start.14 = (bf16[32,3072]{1,0:T(8,128)(2,1)S(1)}, bf16[32,3072]{1,0:T(8,128)(2,1)S(1)}, u32[]{:S(2)}, u32[]{:S(2)}) collective-permute-start(bf16[32,3072]{1,0:T(8,128)(2,1)S(1)} %get-tuple-element.53), channel_id=1, source_target_pairs={{0,2},{2,0},{4,6},{6,4},{8,10},{10,8},{12,14},{14,12},{16,18},{18,... | collective-permute-start | bytes 589832 | tf_op jit(solution)/shard_map/ppermute | solution.py:235
  43.3 9.5 %collective-permute-start.13 = (bf16[32,3072]{1,0:T(8,128)(2,1)S(1)}, bf16[32,3072]{1,0:T(8,128)(2,1)S(1)}, u32[]{:S(2)}, u32[]{:S(2)}) collective-permute-start(bf16[32,3072]{1,0:T(8,128)(2,1)S(1)} %add_convert_fusion.1), channel_id=1, source_target_pairs={{0,12},{2,14},{4,8},{6,10},{8,4},{10,6},{12,0},{14,2},{16,28},{18,... | collective-permute-start | bytes 589832 | tf_op jit(solution)/shard_map/ppermute | solution.py:235
  47.6 7.2 %collective-permute-start.15 = (bf16[32,3072]{1,0:T(8,128)(2,1)S(1)}, bf16[32,3072]{1,0:T(8,128)(2,1)S(1)}, u32[]{:S(2)}, u32[]{:S(2)}) collective-permute-start(bf16[32,3072]{1,0:T(8,128)(2,1)S(1)} %add_convert_fusion), channel_id=1, source_target_pairs={{0,4},{2,6},{4,0},{6,2},{8,12},{10,14},{12,8},{14,10},{16,20},{18,... | collective-permute-start | bytes 589832 | tf_op jit(solution)/shard_map/ppermute | solution.py:235
  49.6 5.7 %collective-permute-start.16 = (bf16[32,3072]{1,0:T(8,128)(2,1)S(1)}, bf16[32,3072]{1,0:T(8,128)(2,1)S(1)}, u32[]{:S(2)}, u32[]{:S(2)}) collective-permute-start(bf16[32,3072]{1,0:T(8,128)(2,1)S(1)} %get-tuple-element.54), channel_id=1, source_target_pairs={{0,2},{2,0},{4,6},{6,4},{8,10},{10,8},{12,14},{14,12},{16,18},{18,... | collective-permute-start | bytes 589832 | tf_op jit(solution)/shard_map/ppermute | solution.py:235

commit v18 on v17

--- a/solution.py
+++ b/solution.py
@@ -270,7 +270,7 @@
         near[0] = exchanged(near[0])
     own, other = {}, {}
     for k in (2, 3, 1, 0):
-        first = {2: (near[3],), 3: (other.get(2), arrived[0]), 1: (own.get(3),), 0: (own.get(1), other.get(3))}[k]
+        first = {2: (gain,), 3: (other.get(2), arrived[0]), 1: (own.get(3),), 0: (own.get(1), other.get(3))}[k]
         if k == 3:
             far[1] = moved(after(near[1], own[2]), 0, 0, 1)
         own[k], sent = mlp(after(near[k], *first), far[k], gain, gate_t, up_t, down)

time: 56.6 us -> 56.9 us (level)
  starting transfers between devices: 27.8 us -> 28.5 us
    ppermute x17, starting transfers between devices: 27.8 us -> 28.5 us  [moved(): return lax.ppermute(value, ('section', 'expert'), pairs)]
  transfers between devices with their start and end apart: 17 -> 17, of which waited for: 9 -> 11; matrix products, arithmetic and copies ran while one was open for 0% -> 0% of each run, Pallas kernels for 15% -> 15%
where the time goes in v18:
time: 56.9 us; the launch traced here: 56.7 us
  starting transfers between devices  28.5 us (50%)
  waiting for transfers between devices  17.7 us (31%)
  Pallas kernels  10.2 us (18%)
    ppermute x17, starting transfers between devices, moved(): return lax.ppermute(value, ('section', 'expert'), pairs)  28.5 us
    ppermute x17, waiting for transfers between devices, moved(): return lax.ppermute(value, ('section', 'expert'), pairs)  17.7 us
    pallas_call x4, Pallas kernels, mlp(): pl.pallas_call(mlp_kernel, out_shape=(out, out), in_specs=[VMEM] * 6, out...  4.69 us
    pallas_call x2, Pallas kernels, loaded(): pl.pallas_call(functools.partial(load_kernel, len(arrays)), out_shape=tup...  3.23 us
    pallas_call x1, Pallas kernels, ended(): pl.pallas_call(functools.partial(end_kernel, steps), out_shape=jax.ShapeD...  1.14 us
  transfers between devices with their start and end apart: 17, of which 11 were waited for; matrix products, arithmetic and copies ran while one was open for 0% of the time, Pallas kernels for 15%

profile of v18, /device:TPU:0, one launch (start us, length us, event | category | flops | bytes accessed | tf_op | source)
XLA Modules:
  0.0 56.7 jit_solution(3794307092933820830)
XLA Ops:
  0.0 2.9 %collective-permute-start = (s32[1,128,2]{1,2,0:T(2,128)}, s32[1,128,2]{1,2,0:T(2,128)S(1)}, u32[]{:S(2)}, u32[]{:S(2)}) collective-permute-start(s32[1,128,2]{1,2,0:T(2,128)} %param.12), channel_id=1, source_target_pairs={{0,16},{2,18},{4,20},{6,22},{8,24},{10,26},{12,28},{14,30},{16,0},... | collective-permute-start | bytes 3080 | tf_op jit(solution)/shard_map/ppermute | solution.py:235
  2.9 1.1 %shard_map.73.block_ref = bf16[128,3072]{1,0:T(8,128)(2,1)S(1)} custom-call(bf16[128,3072]{1,0:T(8,128)(2,1)} %bitcast.25), custom_call_target="tpu_custom_call" | custom-call | bytes 6291456 | tf_op jit(solution)/shard_map/pallas_call | solution.py:33
  4.1 0.6 %collective-permute-done = s32[1,128,2]{1,2,0:T(2,128)S(1)} collective-permute-done((s32[1,128,2]{1,2,0:T(2,128)}, s32[1,128,2]{1,2,0:T(2,128)S(1)}, u32[]{:S(2)}, u32[]{:S(2)}) %collective-permute-start) | collective-permute-done | bytes 1056 | tf_op jit(solution)/shard_map/ppermute | solution.py:235
  4.7 0.4 shard_map.74
  5.1 4.1 %collective-permute-start.2 = (bf16[32,3072]{1,0:T(8,128)(2,1)S(1)}, bf16[32,3072]{1,0:T(8,128)(2,1)S(1)}, u32[]{:S(2)}, u32[]{:S(2)}) collective-permute-start(bf16[32,3072]{1,0:T(8,128)(2,1)S(1)} %shard_map.74), channel_id=1, source_target_pairs={{0,24},{2,26},{4,28},{6,30},{8,16},{10,18},{12,20},{14,22},{16,8},... | collective-permute-start | bytes 589832 | tf_op jit(solution)/shard_map/ppermute | solution.py:235
  9.2 1.5 %collective-permute-start.1 = (bf16[32,3072]{1,0:T(8,128)(2,1)S(1)}, bf16[32,3072]{1,0:T(8,128)(2,1)S(1)}, u32[]{:S(2)}, u32[]{:S(2)}) collective-permute-start(bf16[32,3072]{1,0:T(8,128)(2,1)S(1)} %shard_map.74), channel_id=1, source_target_pairs={{0,18},{2,16},{4,22},{6,20},{8,26},{10,24},{12,30},{14,28},{16,2},... | collective-permute-start | bytes 589832 | tf_op jit(solution)/shard_map/ppermute | solution.py:235
  10.7 2.1 %shard_map.75 = (bf16[192,3072]{1,0:T(8,128)(2,1)S(1)}, bf16[192,3072]{1,0:T(8,128)(2,1)S(1)}, bf16[192,3072]{1,0:T(8,128)(2,1)S(1)}, bf16[1,3072]{1,0:T(2,128)(2,1)S(1)}) custom-call(bf16[192,3072]{1,0:T(8,128)(2,1)} %bitcast.26, bf16[192,3072]{1,0:T(8,128)(2,1)} %bitcast.27, bf16[192,3072]{1,0:T(8,128)(2,1)} %bitcast.28, bf16[1,3072]{1,0:T(2,128)(2,1)} %refs_3_.1), custom_call_target="tpu_custom_call" | custom-call | bytes 6291456 | tf_op jit(solution)/shard_map/pallas_call | solution.py:33
  12.8 4.5 %collective-permute-done.2.near_ref = bf16[32,3072]{1,0:T(8,128)(2,1)S(1)} collective-permute-done((bf16[32,3072]{1,0:T(8,128)(2,1)S(1)}, bf16[32,3072]{1,0:T(8,128)(2,1)S(1)}, u32[]{:S(2)}, u32[]{:S(2)}) %collective-permute-start.2) | collective-permute-done | bytes 196640 | tf_op jit(solution)/shard_map/ppermute | solution.py:235
  17.2 1.5 %collective-permute-start.7 = (bf16[32,3072]{1,0:T(8,128)(2,1)S(1)}, bf16[32,3072]{1,0:T(8,128)(2,1)S(1)}, u32[]{:S(2)}, u32[]{:S(2)}) collective-permute-start(bf16[32,3072]{1,0:T(8,128)(2,1)S(1)} %collective-permute-done.2.near_ref), channel_id=1, source_target_pairs={{0,2},{2,0},{4,6},{6,4},{8,10},{10,8},{12,14},{14,12},{16,18},{18,... | collective-permute-start | bytes 589832 | tf_op jit(solution)/shard_map/ppermute | solution.py:235
  18.8 0.0 copy-done.2
  18.8 0.0 collective-permute-done.1.far_ref
  18.8 1.5 %collective-permute-start.3 = (bf16[48,3072]{1,0:T(8,128)(2,1)S(1)}, bf16[48,3072]{1,0:T(8,128)(2,1)S(1)}, u32[]{:S(2)}, u32[]{:S(2)}) collective-permute-start(bf16[48,3072]{1,0:T(8,128)(2,1)S(1)} %slice_bitcast_fusion.1), channel_id=1, source_target_pairs={{0,16},{2,18},{4,20},{6,22},{8,24},{10,26},{12,28},{14,30},{16,0},... | collective-permute-start | bytes 884744 | tf_op jit(solution)/shard_map/ppermute | solution.py:235
  20.3 1.0 %collective-permute-start.5 = (bf16[32,3072]{1,0:T(8,128)(2,1)S(1)}, bf16[32,3072]{1,0:T(8,128)(2,1)S(1)}, u32[]{:S(2)}, u32[]{:S(2)}) collective-permute-start(bf16[32,3072]{1,0:T(8,128)(2,1)S(1)} %shard_map.74), channel_id=1, source_target_pairs={{0,20},{2,22},{4,16},{6,18},{8,28},{10,30},{12,24},{14,26},{16,4},... | collective-permute-start | bytes 589832 | tf_op jit(solution)/shard_map/ppermute | solution.py:235
  21.3 1.1 %collective-permute-start.6 = (bf16[32,3072]{1,0:T(8,128)(2,1)S(1)}, bf16[32,3072]{1,0:T(8,128)(2,1)S(1)}, u32[]{:S(2)}, u32[]{:S(2)}) collective-permute-start(bf16[32,3072]{1,0:T(8,128)(2,1)S(1)} %collective-permute-done.2.near_ref), channel_id=1, source_target_pairs={{0,4},{2,6},{4,0},{6,2},{8,12},{10,14},{12,8},{14,10},{16,20},{18,... | collective-permute-start | bytes 589832 | tf_op jit(solution)/shard_map/ppermute | solution.py:235
  22.4 0.6 %collective-permute-done.7.far_ref = bf16[32,3072]{1,0:T(8,128)(2,1)S(1)} collective-permute-done((bf16[32,3072]{1,0:T(8,128)(2,1)S(1)}, bf16[32,3072]{1,0:T(8,128)(2,1)S(1)}, u32[]{:S(2)}, u32[]{:S(2)}) %collective-permute-start.7) | collective-permute-done | bytes 196640 | tf_op jit(solution)/shard_map/ppermute | solution.py:235
  23.0 1.2 %shard_map.77 = (bf16[32,3072]{1,0:T(8,128)(2,1)S(1)}, bf16[32,3072]{1,0:T(8,128)(2,1)S(1)}) custom-call(bf16[32,3072]{1,0:T(8,128)(2,1)S(1)} %collective-permute-done.2.near_ref, bf16[32,3072]{1,0:T(8,128)(2,1)S(1)} %collective-permute-done.7.far_ref, bf16[1,3072]{1,0:T(2,128)(2,1)S(1)} %get-tuple-element.30.gain_ref, ...), custom_call_target="tpu_custom_call" | custom-call | flops 226492416 | bytes 3538944 | tf_op jit(solution)/shard_map/pallas_call | solution.py:97
  24.2 1.6 %collective-permute-start.8 = (bf16[32,3072]{1,0:T(8,128)(2,1)S(1)}, bf16[32,3072]{1,0:T(8,128)(2,1)S(1)}, u32[]{:S(2)}, u32[]{:S(2)}) collective-permute-start(bf16[32,3072]{1,0:T(8,128)(2,1)S(1)} %get-tuple-element.41), channel_id=1, source_target_pairs={{0,2},{2,0},{4,6},{6,4},{8,10},{10,8},{12,14},{14,12},{16,18},{18,... | collective-permute-start | bytes 589832 | tf_op jit(solution)/shard_map/ppermute | solution.py:235
  25.7 1.7 %collective-permute-start.9 = (bf16[32,3072]{1,0:T(8,128)(2,1)S(1)}, bf16[32,3072]{1,0:T(8,128)(2,1)S(1)}, u32[]{:S(2)}, u32[]{:S(2)}) collective-permute-start(bf16[32,3072]{1,0:T(8,128)(2,1)S(1)} %collective-permute-done.7.far_ref), channel_id=1, source_target_pairs={{0,4},{2,6},{4,0},{6,2},{8,12},{10,14},{12,8},{14,10},{16,20},{18,... | collective-permute-start | bytes 589832 | tf_op jit(solution)/shard_map/ppermute | solution.py:235
  27.4 1.6 %collective-permute-done.5.near_ref = bf16[32,3072]{1,0:T(8,128)(2,1)S(1)} collective-permute-done((bf16[32,3072]{1,0:T(8,128)(2,1)S(1)}, bf16[32,3072]{1,0:T(8,128)(2,1)S(1)}, u32[]{:S(2)}, u32[]{:S(2)}) %collective-permute-start.5) | collective-permute-done | bytes 196640 | tf_op jit(solution)/shard_map/ppermute | solution.py:235
  29.0 0.6 %collective-permute-start.4 = (bf16[80,3072]{1,0:T(8,128)(2,1)S(1)}, bf16[80,3072]{1,0:T(8,128)(2,1)S(1)}, u32[]{:S(2)}, u32[]{:S(2)}) collective-permute-start(bf16[80,3072]{1,0:T(8,128)(2,1)S(1)} %slice_bitcast_fusion), channel_id=1, source_target_pairs={{0,16},{2,18},{4,20},{6,22},{8,24},{10,26},{12,28},{14,30},{16,0},... | collective-permute-start | bytes 1474568 | tf_op jit(solution)/shard_map/ppermute | solution.py:235
  29.6 2.7 %collective-permute-done.6.near_ref = bf16[32,3072]{1,0:T(8,128)(2,1)S(1)} collective-permute-done((bf16[32,3072]{1,0:T(8,128)(2,1)S(1)}, bf16[32,3072]{1,0:T(8,128)(2,1)S(1)}, u32[]{:S(2)}, u32[]{:S(2)}) %collective-permute-start.6) | collective-permute-done | bytes 196640 | tf_op jit(solution)/shard_map/ppermute | solution.py:235
  32.4 0.6 collective-permute-start.10
  33.0 0.0 collective-permute-done.3.refs_0_
  33.0 0.0 collective-permute-done.8
  33.0 1.6 %collective-permute-done.9.far_ref = bf16[32,3072]{1,0:T(8,128)(2,1)S(1)} collective-permute-done((bf16[32,3072]{1,0:T(8,128)(2,1)S(1)}, bf16[32,3072]{1,0:T(8,128)(2,1)S(1)}, u32[]{:S(2)}, u32[]{:S(2)}) %collective-permute-start.9) | collective-permute-done | bytes 196640 | tf_op jit(solution)/shard_map/ppermute | solution.py:235
  34.6 1.2 %shard_map.78 = (bf16[32,3072]{1,0:T(8,128)(2,1)S(1)}, bf16[32,3072]{1,0:T(8,128)(2,1)S(1)}) custom-call(bf16[32,3072]{1,0:T(8,128)(2,1)S(1)} %collective-permute-done.6.near_ref, bf16[32,3072]{1,0:T(8,128)(2,1)S(1)} %collective-permute-done.9.far_ref, bf16[1,3072]{1,0:T(2,128)(2,1)S(1)} %get-tuple-element.30.gain_ref, ...), custom_call_target="tpu_custom_call" | custom-call | flops 226492416 | bytes 3538944 | tf_op jit(solution)/shard_map/pallas_call | solution.py:97
  35.7 0.6 %collective-permute-start.11 = (bf16[32,3072]{1,0:T(8,128)(2,1)S(1)}, bf16[32,3072]{1,0:T(8,128)(2,1)S(1)}, u32[]{:S(2)}, u32[]{:S(2)}) collective-permute-start(bf16[32,3072]{1,0:T(8,128)(2,1)S(1)} %get-tuple-element.48), channel_id=1, source_target_pairs={{0,2},{2,0},{4,6},{6,4},{8,10},{10,8},{12,14},{14,12},{16,18},{18,... | collective-permute-start | bytes 589832 | tf_op jit(solution)/shard_map/ppermute | solution.py:235
  36.4 0.0 copy-start
  36.4 0.0 copy-start.1
  36.4 2.7 %collective-permute-start.12 = (bf16[32,3072]{1,0:T(8,128)(2,1)S(1)}, bf16[32,3072]{1,0:T(8,128)(2,1)S(1)}, u32[]{:S(2)}, u32[]{:S(2)}) collective-permute-start(bf16[32,3072]{1,0:T(8,128)(2,1)S(1)} %add_convert_fusion.2), channel_id=1, source_target_pairs={{0,8},{2,10},{4,12},{6,14},{8,0},{10,2},{12,4},{14,6},{16,24},{18,... | collective-permute-start | bytes 589832 | tf_op jit(solution)/shard_map/ppermute | solution.py:235
  39.1 0.5 collective-permute-done.10.far_ref
  39.7 1.2 %shard_map.79 = (bf16[32,3072]{1,0:T(8,128)(2,1)S(1)}, bf16[32,3072]{1,0:T(8,128)(2,1)S(1)}) custom-call(bf16[32,3072]{1,0:T(8,128)(2,1)S(1)} %collective-permute-done.5.near_ref, bf16[32,3072]{1,0:T(8,128)(2,1)S(1)} %collective-permute-done.10.far_ref, bf16[1,3072]{1,0:T(2,128)(2,1)S(1)} %get-tuple-element.30.gain_ref, ...), custom_call_target="tpu_custom_call" | custom-call | flops 226492416 | bytes 3538944 | tf_op jit(solution)/shard_map/pallas_call | solution.py:97
  40.9 1.0 %collective-permute-start.14 = (bf16[32,3072]{1,0:T(8,128)(2,1)S(1)}, bf16[32,3072]{1,0:T(8,128)(2,1)S(1)}, u32[]{:S(2)}, u32[]{:S(2)}) collective-permute-start(bf16[32,3072]{1,0:T(8,128)(2,1)S(1)} %get-tuple-element.51), channel_id=1, source_target_pairs={{0,2},{2,0},{4,6},{6,4},{8,10},{10,8},{12,14},{14,12},{16,18},{18,... | collective-permute-start | bytes 589832 | tf_op jit(solution)/shard_map/ppermute | solution.py:235
  41.9 0.0 collective-permute-done.4.refs_1_
  41.9 0.0 copy-done
  41.9 0.0 copy-done.1
  41.9 0.8 %shard_map.76 = (f32[128,3072]{1,0:T(8,128)S(1)}, bf16[128,160]{1,0:T(8,128)(2,1)S(1)}, bf16[32,3072]{1,0:T(8,128)(2,1)S(1)}) custom-call(bf16[1,3072]{1,0:T(2,128)(2,1)S(1)} %get-tuple-element.30.gain_ref, s32[2,128]{1,0:T(2,128)S(1)} %bitcast.22, f32[2,128]{1,0:T(2,128)S(1)} %bitcast.23, bf16[48,3072]{1,0:T(8,128)(2,1)S(1)} %collective-permute-done.3.refs_0_, ...), custom_call_target="tpu_custom_call" | custom-call | flops 3145728 | bytes 2359296 | tf_op jit(solution)/shard_map/pallas_call | solution.py:148
  42.7 0.6 %collective-permute-done.11 = bf16[32,3072]{1,0:T(8,128)(2,1)S(1)} collective-permute-done((bf16[32,3072]{1,0:T(8,128)(2,1)S(1)}, bf16[32,3072]{1,0:T(8,128)(2,1)S(1)}, u32[]{:S(2)}, u32[]{:S(2)}) %collective-permute-start.11) | collective-permute-done | bytes 196640 | tf_op jit(solution)/shard_map/ppermute | solution.py:235
  43.3 4.3 %collective-permute-start.13 = (bf16[32,3072]{1,0:T(8,128)(2,1)S(1)}, bf16[32,3072]{1,0:T(8,128)(2,1)S(1)}, u32[]{:S(2)}, u32[]{:S(2)}) collective-permute-start(bf16[32,3072]{1,0:T(8,128)(2,1)S(1)} %add_convert_fusion.1), channel_id=1, source_target_pairs={{0,12},{2,14},{4,8},{6,10},{8,4},{10,6},{12,0},{14,2},{16,28},{18,... | collective-permute-start | bytes 589832 | tf_op jit(solution)/shard_map/ppermute | solution.py:235
  47.6 0.0 collective-permute-done.14
  47.6 0.2 collective-permute-start.15
  47.9 1.2 %shard_map.80 = (bf16[32,3072]{1,0:T(8,128)(2,1)S(1)}, bf16[32,3072]{1,0:T(8,128)(2,1)S(1)}) custom-call(bf16[32,3072]{1,0:T(8,128)(2,1)S(1)} %get-tuple-element.49.near_ref, bf16[32,3072]{1,0:T(8,128)(2,1)S(1)} %collective-permute-done.1.far_ref, bf16[1,3072]{1,0:T(2,128)(2,1)S(1)} %get-tuple-element.30.gain_ref, ...), custom_call_target="tpu_custom_call" | custom-call | flops 226492416 | bytes 3538944 | tf_op jit(solution)/shard_map/pallas_call | solution.py:97
  49.1 1.6 %collective-permute-start.16 = (bf16[32,3072]{1,0:T(8,128)(2,1)S(1)}, bf16[32,3072]{1,0:T(8,128)(2,1)S(1)}, u32[]{:S(2)}, u32[]{:S(2)}) collective-permute-start(bf16[32,3072]{1,0:T(8,128)(2,1)S(1)} %get-tuple-element.52), channel_id=1, source_target_pairs={{0,2},{2,0},{4,6},{6,4},{8,10},{10,8},{12,14},{14,12},{16,18},{18,... | collective-permute-start | bytes 589832 | tf_op jit(solution)/shard_map/ppermute | solution.py:235
  50.7 0.6 %collective-permute-done.12.right_ref = bf16[32,3072]{1,0:T(8,128)(2,1)S(1)} collective-permute-done((bf16[32,3072]{1,0:T(8,128)(2,1)S(1)}, bf16[32,3072]{1,0:T(8,128)(2,1)S(1)}, u32[]{:S(2)}, u32[]{:S(2)}) %collective-permute-start.12) | collective-permute-done | bytes 196640 | tf_op jit(solution)/shard_map/ppermute | solution.py:235
  51.3 2.0 %collective-permute-done.13.refs_1_ = bf16[32,3072]{1,0:T(8,128)(2,1)S(1)} collective-permute-done((bf16[32,3072]{1,0:T(8,128)(2,1)S(1)}, bf16[32,3072]{1,0:T(8,128)(2,1)S(1)}, u32[]{:S(2)}, u32[]{:S(2)}) %collective-permute-start.13) | collective-permute-done | bytes 196640 | tf_op jit(solution)/shard_map/ppermute | solution.py:235
  53.3 2.3 %collective-permute-done.15.refs_2_ = bf16[32,3072]{1,0:T(8,128)(2,1)S(1)} collective-permute-done((bf16[32,3072]{1,0:T(8,128)(2,1)S(1)}, bf16[32,3072]{1,0:T(8,128)(2,1)S(1)}, u32[]{:S(2)}, u32[]{:S(2)}) %collective-permute-start.15) | collective-permute-done | bytes 196640 | tf_op jit(solution)/shard_map/ppermute | solution.py:235
  55.6 0.0 collective-permute-done.16.refs_3_
  55.6 1.1 %shard_map.82 = bf16[128,3072]{1,0:T(8,128)(2,1)} custom-call(f32[128,3072]{1,0:T(8,128)S(1)} %get-tuple-element.33.base_ref, bf16[128,160]{1,0:T(8,128)(2,1)S(1)} %get-tuple-element.34.table_ref, f32[32,3072]{1,0:T(8,128)S(1)} %shard_map.81.refs_0_, bf16[32,3072]{1,0:T(8,128)(2,1)S(1)} %collective-permute-done.13.refs_1_, ...), custom_call_target="tpu_custom_call" | custom-call | flops 100663296 | bytes 2359296 | tf_op jit(solution)/shard_map/pallas_call | solution.py:188
  (7 shorter events, 0.2 us)
Async XLA Ops:
  0.0 4.7 %collective-permute-start = (s32[1,128,2]{1,2,0:T(2,128)}, s32[1,128,2]{1,2,0:T(2,128)S(1)}, u32[]{:S(2)}, u32[]{:S(2)}) collective-permute-start(s32[1,128,2]{1,2,0:T(2,128)} %param.12), channel_id=1, source_target_pairs={{0,16},{2,18},{4,20},{6,22},{8,24},{10,26},{12,28},{14,30},{16,0},... | collective-permute-start | bytes 3080 | tf_op jit(solution)/shard_map/ppermute | solution.py:235
  5.1 12.2 %collective-permute-start.2 = (bf16[32,3072]{1,0:T(8,128)(2,1)S(1)}, bf16[32,3072]{1,0:T(8,128)(2,1)S(1)}, u32[]{:S(2)}, u32[]{:S(2)}) collective-permute-start(bf16[32,3072]{1,0:T(8,128)(2,1)S(1)} %shard_map.74), channel_id=1, source_target_pairs={{0,24},{2,26},{4,28},{6,30},{8,16},{10,18},{12,20},{14,22},{16,8},... | collective-permute-start | bytes 589832 | tf_op jit(solution)/shard_map/ppermute | solution.py:235
  9.2 9.6 %collective-permute-start.1 = (bf16[32,3072]{1,0:T(8,128)(2,1)S(1)}, bf16[32,3072]{1,0:T(8,128)(2,1)S(1)}, u32[]{:S(2)}, u32[]{:S(2)}) collective-permute-start(bf16[32,3072]{1,0:T(8,128)(2,1)S(1)} %shard_map.74), channel_id=1, source_target_pairs={{0,18},{2,16},{4,22},{6,20},{8,26},{10,24},{12,30},{14,28},{16,2},... | collective-permute-start | bytes 589832 | tf_op jit(solution)/shard_map/ppermute | solution.py:235
  10.7 8.1 %copy-start.2 = (bf16[1,128,3072]{2,1,0:T(8,128)(2,1)S(1)}, bf16[1,128,3072]{2,1,0:T(8,128)(2,1)}, u32[]{:S(2)}) copy-start(bf16[1,128,3072]{2,1,0:T(8,128)(2,1)} %param.7) | copy-start | bytes 2359300
  17.2 5.7 %collective-permute-start.7 = (bf16[32,3072]{1,0:T(8,128)(2,1)S(1)}, bf16[32,3072]{1,0:T(8,128)(2,1)S(1)}, u32[]{:S(2)}, u32[]{:S(2)}) collective-permute-start(bf16[32,3072]{1,0:T(8,128)(2,1)S(1)} %collective-permute-done.2.near_ref), channel_id=1, source_target_pairs={{0,2},{2,0},{4,6},{6,4},{8,10},{10,8},{12,14},{14,12},{16,18},{18,... | collective-permute-start | bytes 589832 | tf_op jit(solution)/shard_map/ppermute | solution.py:235
  18.8 14.1 %collective-permute-start.3 = (bf16[48,3072]{1,0:T(8,128)(2,1)S(1)}, bf16[48,3072]{1,0:T(8,128)(2,1)S(1)}, u32[]{:S(2)}, u32[]{:S(2)}) collective-permute-start(bf16[48,3072]{1,0:T(8,128)(2,1)S(1)} %slice_bitcast_fusion.1), channel_id=1, source_target_pairs={{0,16},{2,18},{4,20},{6,22},{8,24},{10,26},{12,28},{14,30},{16,0},... | collective-permute-start | bytes 884744 | tf_op jit(solution)/shard_map/ppermute | solution.py:235
  20.3 8.7 %collective-permute-start.5 = (bf16[32,3072]{1,0:T(8,128)(2,1)S(1)}, bf16[32,3072]{1,0:T(8,128)(2,1)S(1)}, u32[]{:S(2)}, u32[]{:S(2)}) collective-permute-start(bf16[32,3072]{1,0:T(8,128)(2,1)S(1)} %shard_map.74), channel_id=1, source_target_pairs={{0,20},{2,22},{4,16},{6,18},{8,28},{10,30},{12,24},{14,26},{16,4},... | collective-permute-start | bytes 589832 | tf_op jit(solution)/shard_map/ppermute | solution.py:235
  21.3 11.1 %collective-permute-start.6 = (bf16[32,3072]{1,0:T(8,128)(2,1)S(1)}, bf16[32,3072]{1,0:T(8,128)(2,1)S(1)}, u32[]{:S(2)}, u32[]{:S(2)}) collective-permute-start(bf16[32,3072]{1,0:T(8,128)(2,1)S(1)} %collective-permute-done.2.near_ref), channel_id=1, source_target_pairs={{0,4},{2,6},{4,0},{6,2},{8,12},{10,14},{12,8},{14,10},{16,20},{18,... | collective-permute-start | bytes 589832 | tf_op jit(solution)/shard_map/ppermute | solution.py:235
  24.2 8.8 %collective-permute-start.8 = (bf16[32,3072]{1,0:T(8,128)(2,1)S(1)}, bf16[32,3072]{1,0:T(8,128)(2,1)S(1)}, u32[]{:S(2)}, u32[]{:S(2)}) collective-permute-start(bf16[32,3072]{1,0:T(8,128)(2,1)S(1)} %get-tuple-element.41), channel_id=1, source_target_pairs={{0,2},{2,0},{4,6},{6,4},{8,10},{10,8},{12,14},{14,12},{16,18},{18,... | collective-permute-start | bytes 589832 | tf_op jit(solution)/shard_map/ppermute | solution.py:235
  25.7 8.8 %collective-permute-start.9 = (bf16[32,3072]{1,0:T(8,128)(2,1)S(1)}, bf16[32,3072]{1,0:T(8,128)(2,1)S(1)}, u32[]{:S(2)}, u32[]{:S(2)}) collective-permute-start(bf16[32,3072]{1,0:T(8,128)(2,1)S(1)} %collective-permute-done.7.far_ref), channel_id=1, source_target_pairs={{0,4},{2,6},{4,0},{6,2},{8,12},{10,14},{12,8},{14,10},{16,20},{18,... | collective-permute-start | bytes 589832 | tf_op jit(solution)/shard_map/ppermute | solution.py:235
  29.0 12.9 %collective-permute-start.4 = (bf16[80,3072]{1,0:T(8,128)(2,1)S(1)}, bf16[80,3072]{1,0:T(8,128)(2,1)S(1)}, u32[]{:S(2)}, u32[]{:S(2)}) collective-permute-start(bf16[80,3072]{1,0:T(8,128)(2,1)S(1)} %slice_bitcast_fusion), channel_id=1, source_target_pairs={{0,16},{2,18},{4,20},{6,22},{8,24},{10,26},{12,28},{14,30},{16,0},... | collective-permute-start | bytes 1474568 | tf_op jit(solution)/shard_map/ppermute | solution.py:235
  32.4 7.3 %collective-permute-start.10 = (bf16[32,3072]{1,0:T(8,128)(2,1)S(1)}, bf16[32,3072]{1,0:T(8,128)(2,1)S(1)}, u32[]{:S(2)}, u32[]{:S(2)}) collective-permute-start(bf16[32,3072]{1,0:T(8,128)(2,1)S(1)} %collective-permute-done.5.near_ref), channel_id=1, source_target_pairs={{0,2},{2,0},{4,6},{6,4},{8,10},{10,8},{12,14},{14,12},{16,18},{18,... | collective-permute-start | bytes 589832 | tf_op jit(solution)/shard_map/ppermute | solution.py:235
  35.7 7.5 %collective-permute-start.11 = (bf16[32,3072]{1,0:T(8,128)(2,1)S(1)}, bf16[32,3072]{1,0:T(8,128)(2,1)S(1)}, u32[]{:S(2)}, u32[]{:S(2)}) collective-permute-start(bf16[32,3072]{1,0:T(8,128)(2,1)S(1)} %get-tuple-element.48), channel_id=1, source_target_pairs={{0,2},{2,0},{4,6},{6,4},{8,10},{10,8},{12,14},{14,12},{16,18},{18,... | collective-permute-start | bytes 589832 | tf_op jit(solution)/shard_map/ppermute | solution.py:235
  36.4 5.5 %copy-start = (s32[1,128,2]{1,2,0:T(2,128)S(1)}, s32[1,128,2]{1,2,0:T(2,128)}, u32[]{:S(2)}) copy-start(s32[1,128,2]{1,2,0:T(2,128)} %param.12) | copy-start | bytes 3076
  36.4 5.5 %copy-start.1 = (f32[1,128,2]{1,2,0:T(2,128)S(1)}, f32[1,128,2]{1,2,0:T(2,128)}, u32[]{:S(2)}) copy-start(f32[1,128,2]{1,2,0:T(2,128)} %param.13) | copy-start | bytes 3076
  36.4 14.9 %collective-permute-start.12 = (bf16[32,3072]{1,0:T(8,128)(2,1)S(1)}, bf16[32,3072]{1,0:T(8,128)(2,1)S(1)}, u32[]{:S(2)}, u32[]{:S(2)}) collective-permute-start(bf16[32,3072]{1,0:T(8,128)(2,1)S(1)} %add_convert_fusion.2), channel_id=1, source_target_pairs={{0,8},{2,10},{4,12},{6,14},{8,0},{10,2},{12,4},{14,6},{16,24},{18,... | collective-permute-start | bytes 589832 | tf_op jit(solution)/shard_map/ppermute | solution.py:235
  40.9 6.7 %collective-permute-start.14 = (bf16[32,3072]{1,0:T(8,128)(2,1)S(1)}, bf16[32,3072]{1,0:T(8,128)(2,1)S(1)}, u32[]{:S(2)}, u32[]{:S(2)}) collective-permute-start(bf16[32,3072]{1,0:T(8,128)(2,1)S(1)} %get-tuple-element.51), channel_id=1, source_target_pairs={{0,2},{2,0},{4,6},{6,4},{8,10},{10,8},{12,14},{14,12},{16,18},{18,... | collective-permute-start | bytes 589832 | tf_op jit(solution)/shard_map/ppermute | solution.py:235
  43.3 10.0 %collective-permute-start.13 = (bf16[32,3072]{1,0:T(8,128)(2,1)S(1)}, bf16[32,3072]{1,0:T(8,128)(2,1)S(1)}, u32[]{:S(2)}, u32[]{:S(2)}) collective-permute-start(bf16[32,3072]{1,0:T(8,128)(2,1)S(1)} %add_convert_fusion.1), channel_id=1, source_target_pairs={{0,12},{2,14},{4,8},{6,10},{8,4},{10,6},{12,0},{14,2},{16,28},{18,... | collective-permute-start | bytes 589832 | tf_op jit(solution)/shard_map/ppermute | solution.py:235
  47.6 7.9 %collective-permute-start.15 = (bf16[32,3072]{1,0:T(8,128)(2,1)S(1)}, bf16[32,3072]{1,0:T(8,128)(2,1)S(1)}, u32[]{:S(2)}, u32[]{:S(2)}) collective-permute-start(bf16[32,3072]{1,0:T(8,128)(2,1)S(1)} %add_convert_fusion), channel_id=1, source_target_pairs={{0,4},{2,6},{4,0},{6,2},{8,12},{10,14},{12,8},{14,10},{16,20},{18,... | collective-permute-start | bytes 589832 | tf_op jit(solution)/shard_map/ppermute | solution.py:235
  49.1 6.5 %collective-permute-start.16 = (bf16[32,3072]{1,0:T(8,128)(2,1)S(1)}, bf16[32,3072]{1,0:T(8,128)(2,1)S(1)}, u32[]{:S(2)}, u32[]{:S(2)}) collective-permute-start(bf16[32,3072]{1,0:T(8,128)(2,1)S(1)} %get-tuple-element.52), channel_id=1, source_target_pairs={{0,2},{2,0},{4,6},{6,4},{8,10},{10,8},{12,14},{14,12},{16,18},{18,... | collective-permute-start | bytes 589832 | tf_op jit(solution)/shard_map/ppermute | solution.py:235

commit v19 on v18

--- a/solution.py
+++ b/solution.py
@@ -256,7 +256,7 @@
     near[3] = moved(near[2], 0, 1)
     far[3] = moved(far[2], 0, 1)
     near[1] = moved(after(picked, near[2]), 1, 1)
-    cuts = [CAP * 3 // 2]
+    cuts = [CAP]
     arrived = [
         moved(after(piece, far[0], near[2]), 1, 0)
         for piece in jnp.split(blocks[0], cuts)

time: 56.9 us -> 56.6 us (level)
  waiting for transfers between devices: 17.7 us -> 15.5 us
  starting transfers between devices: 28.5 us -> 30.4 us
    ppermute x17, waiting for transfers between devices: 17.7 us -> 15.5 us  [moved(): return lax.ppermute(value, ('section', 'expert'), pairs)]
    ppermute x17, starting transfers between devices: 28.5 us -> 30.4 us  [moved(): return lax.ppermute(value, ('section', 'expert'), pairs)]
  transfers between devices with their start and end apart: 17 -> 17, of which waited for: 11 -> 9; matrix products, arithmetic and copies ran while one was open for 0% -> 0% of each run, Pallas kernels for 15% -> 15%
where the time goes in v19:
time: 56.6 us; the launch traced here: 56.5 us
  starting transfers between devices  30.4 us (54%)
  waiting for transfers between devices  15.5 us (27%)
  Pallas kernels  10.2 us (18%)
    ppermute x17, starting transfers between devices, moved(): return lax.ppermute(value, ('section', 'expert'), pairs)  30.4 us
    ppermute x17, waiting for transfers between devices, moved(): return lax.ppermute(value, ('section', 'expert'), pairs)  15.5 us
    pallas_call x4, Pallas kernels, mlp(): pl.pallas_call(mlp_kernel, out_shape=(out, out), in_specs=[VMEM] * 6, out...  4.71 us
    pallas_call x2, Pallas kernels, loaded(): pl.pallas_call(functools.partial(load_kernel, len(arrays)), out_shape=tup...  3.23 us
    pallas_call x1, Pallas kernels, ended(): pl.pallas_call(functools.partial(end_kernel, steps), out_shape=jax.ShapeD...  1.14 us
  transfers between devices with their start and end apart: 17, of which 9 were waited for; matrix products, arithmetic and copies ran while one was open for 0% of the time, Pallas kernels for 15%

profile of v19, /device:TPU:0, one launch (start us, length us, event | category | flops | bytes accessed | tf_op | source)
XLA Modules:
  0.0 56.5 jit_solution(2807625641349666102)
XLA Ops:
  0.0 2.9 %collective-permute-start = (s32[1,128,2]{1,2,0:T(2,128)}, s32[1,128,2]{1,2,0:T(2,128)S(1)}, u32[]{:S(2)}, u32[]{:S(2)}) collective-permute-start(s32[1,128,2]{1,2,0:T(2,128)} %param.12), channel_id=1, source_target_pairs={{0,16},{2,18},{4,20},{6,22},{8,24},{10,26},{12,28},{14,30},{16,0},... | collective-permute-start | bytes 3080 | tf_op jit(solution)/shard_map/ppermute | solution.py:235
  2.9 1.1 %shard_map.73.block_ref = bf16[128,3072]{1,0:T(8,128)(2,1)S(1)} custom-call(bf16[128,3072]{1,0:T(8,128)(2,1)} %bitcast.25), custom_call_target="tpu_custom_call" | custom-call | bytes 6291456 | tf_op jit(solution)/shard_map/pallas_call | solution.py:33
  4.1 0.6 %collective-permute-done = s32[1,128,2]{1,2,0:T(2,128)S(1)} collective-permute-done((s32[1,128,2]{1,2,0:T(2,128)}, s32[1,128,2]{1,2,0:T(2,128)S(1)}, u32[]{:S(2)}, u32[]{:S(2)}) %collective-permute-start) | collective-permute-done | bytes 1056 | tf_op jit(solution)/shard_map/ppermute | solution.py:235
  4.7 0.4 shard_map.74
  5.1 4.1 %collective-permute-start.2 = (bf16[32,3072]{1,0:T(8,128)(2,1)S(1)}, bf16[32,3072]{1,0:T(8,128)(2,1)S(1)}, u32[]{:S(2)}, u32[]{:S(2)}) collective-permute-start(bf16[32,3072]{1,0:T(8,128)(2,1)S(1)} %shard_map.74), channel_id=1, source_target_pairs={{0,24},{2,26},{4,28},{6,30},{8,16},{10,18},{12,20},{14,22},{16,8},... | collective-permute-start | bytes 589832 | tf_op jit(solution)/shard_map/ppermute | solution.py:235
  9.2 1.5 %collective-permute-start.1 = (bf16[32,3072]{1,0:T(8,128)(2,1)S(1)}, bf16[32,3072]{1,0:T(8,128)(2,1)S(1)}, u32[]{:S(2)}, u32[]{:S(2)}) collective-permute-start(bf16[32,3072]{1,0:T(8,128)(2,1)S(1)} %shard_map.74), channel_id=1, source_target_pairs={{0,18},{2,16},{4,22},{6,20},{8,26},{10,24},{12,30},{14,28},{16,2},... | collective-permute-start | bytes 589832 | tf_op jit(solution)/shard_map/ppermute | solution.py:235
  10.7 2.1 %shard_map.75 = (bf16[192,3072]{1,0:T(8,128)(2,1)S(1)}, bf16[192,3072]{1,0:T(8,128)(2,1)S(1)}, bf16[192,3072]{1,0:T(8,128)(2,1)S(1)}, bf16[1,3072]{1,0:T(2,128)(2,1)S(1)}) custom-call(bf16[192,3072]{1,0:T(8,128)(2,1)} %bitcast.26, bf16[192,3072]{1,0:T(8,128)(2,1)} %bitcast.27, bf16[192,3072]{1,0:T(8,128)(2,1)} %bitcast.28, bf16[1,3072]{1,0:T(2,128)(2,1)} %refs_3_.1), custom_call_target="tpu_custom_call" | custom-call | bytes 6291456 | tf_op jit(solution)/shard_map/pallas_call | solution.py:33
  12.8 4.5 %collective-permute-done.2.near_ref = bf16[32,3072]{1,0:T(8,128)(2,1)S(1)} collective-permute-done((bf16[32,3072]{1,0:T(8,128)(2,1)S(1)}, bf16[32,3072]{1,0:T(8,128)(2,1)S(1)}, u32[]{:S(2)}, u32[]{:S(2)}) %collective-permute-start.2) | collective-permute-done | bytes 196640 | tf_op jit(solution)/shard_map/ppermute | solution.py:235
  17.2 1.5 %collective-permute-start.7 = (bf16[32,3072]{1,0:T(8,128)(2,1)S(1)}, bf16[32,3072]{1,0:T(8,128)(2,1)S(1)}, u32[]{:S(2)}, u32[]{:S(2)}) collective-permute-start(bf16[32,3072]{1,0:T(8,128)(2,1)S(1)} %collective-permute-done.2.near_ref), channel_id=1, source_target_pairs={{0,2},{2,0},{4,6},{6,4},{8,10},{10,8},{12,14},{14,12},{16,18},{18,... | collective-permute-start | bytes 589832 | tf_op jit(solution)/shard_map/ppermute | solution.py:235
  18.8 0.0 copy-done.2
  18.8 0.0 collective-permute-done.1.far_ref
  18.8 1.5 %collective-permute-start.3 = (bf16[32,3072]{1,0:T(8,128)(2,1)S(1)}, bf16[32,3072]{1,0:T(8,128)(2,1)S(1)}, u32[]{:S(2)}, u32[]{:S(2)}) collective-permute-start(bf16[32,3072]{1,0:T(8,128)(2,1)S(1)} %slice_bitcast_fusion.1), channel_id=1, source_target_pairs={{0,16},{2,18},{4,20},{6,22},{8,24},{10,26},{12,28},{14,30},{16,0},... | collective-permute-start | bytes 589832 | tf_op jit(solution)/shard_map/ppermute | solution.py:235
  20.3 1.0 %collective-permute-start.5 = (bf16[32,3072]{1,0:T(8,128)(2,1)S(1)}, bf16[32,3072]{1,0:T(8,128)(2,1)S(1)}, u32[]{:S(2)}, u32[]{:S(2)}) collective-permute-start(bf16[32,3072]{1,0:T(8,128)(2,1)S(1)} %shard_map.74), channel_id=1, source_target_pairs={{0,20},{2,22},{4,16},{6,18},{8,28},{10,30},{12,24},{14,26},{16,4},... | collective-permute-start | bytes 589832 | tf_op jit(solution)/shard_map/ppermute | solution.py:235
  21.3 1.1 %collective-permute-start.6 = (bf16[32,3072]{1,0:T(8,128)(2,1)S(1)}, bf16[32,3072]{1,0:T(8,128)(2,1)S(1)}, u32[]{:S(2)}, u32[]{:S(2)}) collective-permute-start(bf16[32,3072]{1,0:T(8,128)(2,1)S(1)} %collective-permute-done.2.near_ref), channel_id=1, source_target_pairs={{0,4},{2,6},{4,0},{6,2},{8,12},{10,14},{12,8},{14,10},{16,20},{18,... | collective-permute-start | bytes 589832 | tf_op jit(solution)/shard_map/ppermute | solution.py:235
  22.4 0.6 %collective-permute-done.7.far_ref = bf16[32,3072]{1,0:T(8,128)(2,1)S(1)} collective-permute-done((bf16[32,3072]{1,0:T(8,128)(2,1)S(1)}, bf16[32,3072]{1,0:T(8,128)(2,1)S(1)}, u32[]{:S(2)}, u32[]{:S(2)}) %collective-permute-start.7) | collective-permute-done | bytes 196640 | tf_op jit(solution)/shard_map/ppermute | solution.py:235
  23.0 1.2 %shard_map.77 = (bf16[32,3072]{1,0:T(8,128)(2,1)S(1)}, bf16[32,3072]{1,0:T(8,128)(2,1)S(1)}) custom-call(bf16[32,3072]{1,0:T(8,128)(2,1)S(1)} %collective-permute-done.2.near_ref, bf16[32,3072]{1,0:T(8,128)(2,1)S(1)} %collective-permute-done.7.far_ref, bf16[1,3072]{1,0:T(2,128)(2,1)S(1)} %get-tuple-element.30.gain_ref, ...), custom_call_target="tpu_custom_call" | custom-call | flops 226492416 | bytes 3538944 | tf_op jit(solution)/shard_map/pallas_call | solution.py:97
  24.2 1.6 %collective-permute-start.8 = (bf16[32,3072]{1,0:T(8,128)(2,1)S(1)}, bf16[32,3072]{1,0:T(8,128)(2,1)S(1)}, u32[]{:S(2)}, u32[]{:S(2)}) collective-permute-start(bf16[32,3072]{1,0:T(8,128)(2,1)S(1)} %get-tuple-element.41), channel_id=1, source_target_pairs={{0,2},{2,0},{4,6},{6,4},{8,10},{10,8},{12,14},{14,12},{16,18},{18,... | collective-permute-start | bytes 589832 | tf_op jit(solution)/shard_map/ppermute | solution.py:235
  25.7 1.7 %collective-permute-start.9 = (bf16[32,3072]{1,0:T(8,128)(2,1)S(1)}, bf16[32,3072]{1,0:T(8,128)(2,1)S(1)}, u32[]{:S(2)}, u32[]{:S(2)}) collective-permute-start(bf16[32,3072]{1,0:T(8,128)(2,1)S(1)} %collective-permute-done.7.far_ref), channel_id=1, source_target_pairs={{0,4},{2,6},{4,0},{6,2},{8,12},{10,14},{12,8},{14,10},{16,20},{18,... | collective-permute-start | bytes 589832 | tf_op jit(solution)/shard_map/ppermute | solution.py:235
  27.4 1.6 %collective-permute-done.5.near_ref = bf16[32,3072]{1,0:T(8,128)(2,1)S(1)} collective-permute-done((bf16[32,3072]{1,0:T(8,128)(2,1)S(1)}, bf16[32,3072]{1,0:T(8,128)(2,1)S(1)}, u32[]{:S(2)}, u32[]{:S(2)}) %collective-permute-start.5) | collective-permute-done | bytes 196640 | tf_op jit(solution)/shard_map/ppermute | solution.py:235
  29.0 0.6 %collective-permute-start.4 = (bf16[96,3072]{1,0:T(8,128)(2,1)S(1)}, bf16[96,3072]{1,0:T(8,128)(2,1)S(1)}, u32[]{:S(2)}, u32[]{:S(2)}) collective-permute-start(bf16[96,3072]{1,0:T(8,128)(2,1)S(1)} %slice_bitcast_fusion), channel_id=1, source_target_pairs={{0,16},{2,18},{4,20},{6,22},{8,24},{10,26},{12,28},{14,30},{16,0},... | collective-permute-start | bytes 1769480 | tf_op jit(solution)/shard_map/ppermute | solution.py:235
  29.6 0.0 collective-permute-done.3.refs_0_
  29.6 1.4 %collective-permute-start.10 = (bf16[32,3072]{1,0:T(8,128)(2,1)S(1)}, bf16[32,3072]{1,0:T(8,128)(2,1)S(1)}, u32[]{:S(2)}, u32[]{:S(2)}) collective-permute-start(bf16[32,3072]{1,0:T(8,128)(2,1)S(1)} %collective-permute-done.5.near_ref), channel_id=1, source_target_pairs={{0,2},{2,0},{4,6},{6,4},{8,10},{10,8},{12,14},{14,12},{16,18},{18,... | collective-permute-start | bytes 589832 | tf_op jit(solution)/shard_map/ppermute | solution.py:235
  31.0 1.4 %collective-permute-done.6.near_ref = bf16[32,3072]{1,0:T(8,128)(2,1)S(1)} collective-permute-done((bf16[32,3072]{1,0:T(8,128)(2,1)S(1)}, bf16[32,3072]{1,0:T(8,128)(2,1)S(1)}, u32[]{:S(2)}, u32[]{:S(2)}) %collective-permute-start.6) | collective-permute-done | bytes 196640 | tf_op jit(solution)/shard_map/ppermute | solution.py:235
  32.4 0.0 collective-permute-done.8
  32.4 2.2 %collective-permute-done.9.far_ref = bf16[32,3072]{1,0:T(8,128)(2,1)S(1)} collective-permute-done((bf16[32,3072]{1,0:T(8,128)(2,1)S(1)}, bf16[32,3072]{1,0:T(8,128)(2,1)S(1)}, u32[]{:S(2)}, u32[]{:S(2)}) %collective-permute-start.9) | collective-permute-done | bytes 196640 | tf_op jit(solution)/shard_map/ppermute | solution.py:235
  34.6 1.2 %shard_map.78 = (bf16[32,3072]{1,0:T(8,128)(2,1)S(1)}, bf16[32,3072]{1,0:T(8,128)(2,1)S(1)}) custom-call(bf16[32,3072]{1,0:T(8,128)(2,1)S(1)} %collective-permute-done.6.near_ref, bf16[32,3072]{1,0:T(8,128)(2,1)S(1)} %collective-permute-done.9.far_ref, bf16[1,3072]{1,0:T(2,128)(2,1)S(1)} %get-tuple-element.30.gain_ref, ...), custom_call_target="tpu_custom_call" | custom-call | flops 226492416 | bytes 3538944 | tf_op jit(solution)/shard_map/pallas_call | solution.py:97
  35.7 0.6 %collective-permute-start.11 = (bf16[32,3072]{1,0:T(8,128)(2,1)S(1)}, bf16[32,3072]{1,0:T(8,128)(2,1)S(1)}, u32[]{:S(2)}, u32[]{:S(2)}) collective-permute-start(bf16[32,3072]{1,0:T(8,128)(2,1)S(1)} %get-tuple-element.48), channel_id=1, source_target_pairs={{0,2},{2,0},{4,6},{6,4},{8,10},{10,8},{12,14},{14,12},{16,18},{18,... | collective-permute-start | bytes 589832 | tf_op jit(solution)/shard_map/ppermute | solution.py:235
  36.4 0.0 copy-start
  36.4 0.0 copy-start.1
  36.4 2.7 %collective-permute-start.12 = (bf16[32,3072]{1,0:T(8,128)(2,1)S(1)}, bf16[32,3072]{1,0:T(8,128)(2,1)S(1)}, u32[]{:S(2)}, u32[]{:S(2)}) collective-permute-start(bf16[32,3072]{1,0:T(8,128)(2,1)S(1)} %add_convert_fusion.2), channel_id=1, source_target_pairs={{0,8},{2,10},{4,12},{6,14},{8,0},{10,2},{12,4},{14,6},{16,24},{18,... | collective-permute-start | bytes 589832 | tf_op jit(solution)/shard_map/ppermute | solution.py:235
  39.1 0.0 collective-permute-done.10.far_ref
  39.1 1.2 %shard_map.79 = (bf16[32,3072]{1,0:T(8,128)(2,1)S(1)}, bf16[32,3072]{1,0:T(8,128)(2,1)S(1)}) custom-call(bf16[32,3072]{1,0:T(8,128)(2,1)S(1)} %collective-permute-done.5.near_ref, bf16[32,3072]{1,0:T(8,128)(2,1)S(1)} %collective-permute-done.10.far_ref, bf16[1,3072]{1,0:T(2,128)(2,1)S(1)} %get-tuple-element.30.gain_ref, ...), custom_call_target="tpu_custom_call" | custom-call | flops 226492416 | bytes 3538944 | tf_op jit(solution)/shard_map/pallas_call | solution.py:97
  40.3 1.6 %collective-permute-start.14 = (bf16[32,3072]{1,0:T(8,128)(2,1)S(1)}, bf16[32,3072]{1,0:T(8,128)(2,1)S(1)}, u32[]{:S(2)}, u32[]{:S(2)}) collective-permute-start(bf16[32,3072]{1,0:T(8,128)(2,1)S(1)} %get-tuple-element.51), channel_id=1, source_target_pairs={{0,2},{2,0},{4,6},{6,4},{8,10},{10,8},{12,14},{14,12},{16,18},{18,... | collective-permute-start | bytes 589832 | tf_op jit(solution)/shard_map/ppermute | solution.py:235
  41.9 0.0 collective-permute-done.11
  41.9 0.0 collective-permute-done.4.refs_1_
  42.0 0.0 copy-done
  42.0 0.0 copy-done.1
  42.0 0.8 %shard_map.76 = (f32[128,3072]{1,0:T(8,128)S(1)}, bf16[128,160]{1,0:T(8,128)(2,1)S(1)}, bf16[32,3072]{1,0:T(8,128)(2,1)S(1)}) custom-call(bf16[1,3072]{1,0:T(2,128)(2,1)S(1)} %get-tuple-element.30.gain_ref, s32[2,128]{1,0:T(2,128)S(1)} %bitcast.22, f32[2,128]{1,0:T(2,128)S(1)} %bitcast.23, bf16[32,3072]{1,0:T(8,128)(2,1)S(1)} %collective-permute-done.3.refs_0_, ...), custom_call_target="tpu_custom_call" | custom-call | flops 3145728 | bytes 2359296 | tf_op jit(solution)/shard_map/pallas_call | solution.py:148
  42.7 5.2 %collective-permute-start.13 = (bf16[32,3072]{1,0:T(8,128)(2,1)S(1)}, bf16[32,3072]{1,0:T(8,128)(2,1)S(1)}, u32[]{:S(2)}, u32[]{:S(2)}) collective-permute-start(bf16[32,3072]{1,0:T(8,128)(2,1)S(1)} %add_convert_fusion.1), channel_id=1, source_target_pairs={{0,12},{2,14},{4,8},{6,10},{8,4},{10,6},{12,0},{14,2},{16,28},{18,... | collective-permute-start | bytes 589832 | tf_op jit(solution)/shard_map/ppermute | solution.py:235
  47.9 0.0 collective-permute-done.14
  48.0 0.1 collective-permute-start.15
  48.1 1.2 %shard_map.80 = (bf16[32,3072]{1,0:T(8,128)(2,1)S(1)}, bf16[32,3072]{1,0:T(8,128)(2,1)S(1)}) custom-call(bf16[32,3072]{1,0:T(8,128)(2,1)S(1)} %get-tuple-element.49.near_ref, bf16[32,3072]{1,0:T(8,128)(2,1)S(1)} %collective-permute-done.1.far_ref, bf16[1,3072]{1,0:T(2,128)(2,1)S(1)} %get-tuple-element.30.gain_ref, ...), custom_call_target="tpu_custom_call" | custom-call | flops 226492416 | bytes 3538944 | tf_op jit(solution)/shard_map/pallas_call | solution.py:97
  49.3 1.4 %collective-permute-start.16 = (bf16[32,3072]{1,0:T(8,128)(2,1)S(1)}, bf16[32,3072]{1,0:T(8,128)(2,1)S(1)}, u32[]{:S(2)}, u32[]{:S(2)}) collective-permute-start(bf16[32,3072]{1,0:T(8,128)(2,1)S(1)} %get-tuple-element.52), channel_id=1, source_target_pairs={{0,2},{2,0},{4,6},{6,4},{8,10},{10,8},{12,14},{14,12},{16,18},{18,... | collective-permute-start | bytes 589832 | tf_op jit(solution)/shard_map/ppermute | solution.py:235
  50.6 0.2 collective-permute-done.12.right_ref
  50.9 1.8 %collective-permute-done.13.refs_1_ = bf16[32,3072]{1,0:T(8,128)(2,1)S(1)} collective-permute-done((bf16[32,3072]{1,0:T(8,128)(2,1)S(1)}, bf16[32,3072]{1,0:T(8,128)(2,1)S(1)}, u32[]{:S(2)}, u32[]{:S(2)}) %collective-permute-start.13) | collective-permute-done | bytes 196640 | tf_op jit(solution)/shard_map/ppermute | solution.py:235
  52.7 2.7 %collective-permute-done.15.refs_2_ = bf16[32,3072]{1,0:T(8,128)(2,1)S(1)} collective-permute-done((bf16[32,3072]{1,0:T(8,128)(2,1)S(1)}, bf16[32,3072]{1,0:T(8,128)(2,1)S(1)}, u32[]{:S(2)}, u32[]{:S(2)}) %collective-permute-start.15) | collective-permute-done | bytes 196640 | tf_op jit(solution)/shard_map/ppermute | solution.py:235
  55.4 0.0 collective-permute-done.16.refs_3_
  55.4 1.1 %shard_map.82 = bf16[128,3072]{1,0:T(8,128)(2,1)} custom-call(f32[128,3072]{1,0:T(8,128)S(1)} %get-tuple-element.33.base_ref, bf16[128,160]{1,0:T(8,128)(2,1)S(1)} %get-tuple-element.34.table_ref, f32[32,3072]{1,0:T(8,128)S(1)} %shard_map.81.refs_0_, bf16[32,3072]{1,0:T(8,128)(2,1)S(1)} %collective-permute-done.13.refs_1_, ...), custom_call_target="tpu_custom_call" | custom-call | flops 100663296 | bytes 2359296 | tf_op jit(solution)/shard_map/pallas_call | solution.py:188
  (7 shorter events, 0.2 us)
Async XLA Ops:
  0.0 4.7 %collective-permute-start = (s32[1,128,2]{1,2,0:T(2,128)}, s32[1,128,2]{1,2,0:T(2,128)S(1)}, u32[]{:S(2)}, u32[]{:S(2)}) collective-permute-start(s32[1,128,2]{1,2,0:T(2,128)} %param.12), channel_id=1, source_target_pairs={{0,16},{2,18},{4,20},{6,22},{8,24},{10,26},{12,28},{14,30},{16,0},... | collective-permute-start | bytes 3080 | tf_op jit(solution)/shard_map/ppermute | solution.py:235
  5.1 12.2 %collective-permute-start.2 = (bf16[32,3072]{1,0:T(8,128)(2,1)S(1)}, bf16[32,3072]{1,0:T(8,128)(2,1)S(1)}, u32[]{:S(2)}, u32[]{:S(2)}) collective-permute-start(bf16[32,3072]{1,0:T(8,128)(2,1)S(1)} %shard_map.74), channel_id=1, source_target_pairs={{0,24},{2,26},{4,28},{6,30},{8,16},{10,18},{12,20},{14,22},{16,8},... | collective-permute-start | bytes 589832 | tf_op jit(solution)/shard_map/ppermute | solution.py:235
  9.2 9.6 %collective-permute-start.1 = (bf16[32,3072]{1,0:T(8,128)(2,1)S(1)}, bf16[32,3072]{1,0:T(8,128)(2,1)S(1)}, u32[]{:S(2)}, u32[]{:S(2)}) collective-permute-start(bf16[32,3072]{1,0:T(8,128)(2,1)S(1)} %shard_map.74), channel_id=1, source_target_pairs={{0,18},{2,16},{4,22},{6,20},{8,26},{10,24},{12,30},{14,28},{16,2},... | collective-permute-start | bytes 589832 | tf_op jit(solution)/shard_map/ppermute | solution.py:235
  10.7 8.1 %copy-start.2 = (bf16[1,128,3072]{2,1,0:T(8,128)(2,1)S(1)}, bf16[1,128,3072]{2,1,0:T(8,128)(2,1)}, u32[]{:S(2)}) copy-start(bf16[1,128,3072]{2,1,0:T(8,128)(2,1)} %param.7) | copy-start | bytes 2359300
  17.2 5.7 %collective-permute-start.7 = (bf16[32,3072]{1,0:T(8,128)(2,1)S(1)}, bf16[32,3072]{1,0:T(8,128)(2,1)S(1)}, u32[]{:S(2)}, u32[]{:S(2)}) collective-permute-start(bf16[32,3072]{1,0:T(8,128)(2,1)S(1)} %collective-permute-done.2.near_ref), channel_id=1, source_target_pairs={{0,2},{2,0},{4,6},{6,4},{8,10},{10,8},{12,14},{14,12},{16,18},{18,... | collective-permute-start | bytes 589832 | tf_op jit(solution)/shard_map/ppermute | solution.py:235
  18.8 10.8 %collective-permute-start.3 = (bf16[32,3072]{1,0:T(8,128)(2,1)S(1)}, bf16[32,3072]{1,0:T(8,128)(2,1)S(1)}, u32[]{:S(2)}, u32[]{:S(2)}) collective-permute-start(bf16[32,3072]{1,0:T(8,128)(2,1)S(1)} %slice_bitcast_fusion.1), channel_id=1, source_target_pairs={{0,16},{2,18},{4,20},{6,22},{8,24},{10,26},{12,28},{14,30},{16,0},... | collective-permute-start | bytes 589832 | tf_op jit(solution)/shard_map/ppermute | solution.py:235
  20.3 8.7 %collective-permute-start.5 = (bf16[32,3072]{1,0:T(8,128)(2,1)S(1)}, bf16[32,3072]{1,0:T(8,128)(2,1)S(1)}, u32[]{:S(2)}, u32[]{:S(2)}) collective-permute-start(bf16[32,3072]{1,0:T(8,128)(2,1)S(1)} %shard_map.74), channel_id=1, source_target_pairs={{0,20},{2,22},{4,16},{6,18},{8,28},{10,30},{12,24},{14,26},{16,4},... | collective-permute-start | bytes 589832 | tf_op jit(solution)/shard_map/ppermute | solution.py:235
  21.3 11.1 %collective-permute-start.6 = (bf16[32,3072]{1,0:T(8,128)(2,1)S(1)}, bf16[32,3072]{1,0:T(8,128)(2,1)S(1)}, u32[]{:S(2)}, u32[]{:S(2)}) collective-permute-start(bf16[32,3072]{1,0:T(8,128)(2,1)S(1)} %collective-permute-done.2.near_ref), channel_id=1, source_target_pairs={{0,4},{2,6},{4,0},{6,2},{8,12},{10,14},{12,8},{14,10},{16,20},{18,... | collective-permute-start | bytes 589832 | tf_op jit(solution)/shard_map/ppermute | solution.py:235
  24.2 8.2 %collective-permute-start.8 = (bf16[32,3072]{1,0:T(8,128)(2,1)S(1)}, bf16[32,3072]{1,0:T(8,128)(2,1)S(1)}, u32[]{:S(2)}, u32[]{:S(2)}) collective-permute-start(bf16[32,3072]{1,0:T(8,128)(2,1)S(1)} %get-tuple-element.41), channel_id=1, source_target_pairs={{0,2},{2,0},{4,6},{6,4},{8,10},{10,8},{12,14},{14,12},{16,18},{18,... | collective-permute-start | bytes 589832 | tf_op jit(solution)/shard_map/ppermute | solution.py:235
  25.7 8.8 %collective-permute-start.9 = (bf16[32,3072]{1,0:T(8,128)(2,1)S(1)}, bf16[32,3072]{1,0:T(8,128)(2,1)S(1)}, u32[]{:S(2)}, u32[]{:S(2)}) collective-permute-start(bf16[32,3072]{1,0:T(8,128)(2,1)S(1)} %collective-permute-done.7.far_ref), channel_id=1, source_target_pairs={{0,4},{2,6},{4,0},{6,2},{8,12},{10,14},{12,8},{14,10},{16,20},{18,... | collective-permute-start | bytes 589832 | tf_op jit(solution)/shard_map/ppermute | solution.py:235
  29.0 12.9 %collective-permute-start.4 = (bf16[96,3072]{1,0:T(8,128)(2,1)S(1)}, bf16[96,3072]{1,0:T(8,128)(2,1)S(1)}, u32[]{:S(2)}, u32[]{:S(2)}) collective-permute-start(bf16[96,3072]{1,0:T(8,128)(2,1)S(1)} %slice_bitcast_fusion), channel_id=1, source_target_pairs={{0,16},{2,18},{4,20},{6,22},{8,24},{10,26},{12,28},{14,30},{16,0},... | collective-permute-start | bytes 1769480 | tf_op jit(solution)/shard_map/ppermute | solution.py:235
  29.6 9.5 %collective-permute-start.10 = (bf16[32,3072]{1,0:T(8,128)(2,1)S(1)}, bf16[32,3072]{1,0:T(8,128)(2,1)S(1)}, u32[]{:S(2)}, u32[]{:S(2)}) collective-permute-start(bf16[32,3072]{1,0:T(8,128)(2,1)S(1)} %collective-permute-done.5.near_ref), channel_id=1, source_target_pairs={{0,2},{2,0},{4,6},{6,4},{8,10},{10,8},{12,14},{14,12},{16,18},{18,... | collective-permute-start | bytes 589832 | tf_op jit(solution)/shard_map/ppermute | solution.py:235
  35.7 6.2 %collective-permute-start.11 = (bf16[32,3072]{1,0:T(8,128)(2,1)S(1)}, bf16[32,3072]{1,0:T(8,128)(2,1)S(1)}, u32[]{:S(2)}, u32[]{:S(2)}) collective-permute-start(bf16[32,3072]{1,0:T(8,128)(2,1)S(1)} %get-tuple-element.48), channel_id=1, source_target_pairs={{0,2},{2,0},{4,6},{6,4},{8,10},{10,8},{12,14},{14,12},{16,18},{18,... | collective-permute-start | bytes 589832 | tf_op jit(solution)/shard_map/ppermute | solution.py:235
  36.4 5.6 %copy-start = (s32[1,128,2]{1,2,0:T(2,128)S(1)}, s32[1,128,2]{1,2,0:T(2,128)}, u32[]{:S(2)}) copy-start(s32[1,128,2]{1,2,0:T(2,128)} %param.12) | copy-start | bytes 3076
  36.4 5.6 %copy-start.1 = (f32[1,128,2]{1,2,0:T(2,128)S(1)}, f32[1,128,2]{1,2,0:T(2,128)}, u32[]{:S(2)}) copy-start(f32[1,128,2]{1,2,0:T(2,128)} %param.13) | copy-start | bytes 3076
  36.4 14.5 %collective-permute-start.12 = (bf16[32,3072]{1,0:T(8,128)(2,1)S(1)}, bf16[32,3072]{1,0:T(8,128)(2,1)S(1)}, u32[]{:S(2)}, u32[]{:S(2)}) collective-permute-start(bf16[32,3072]{1,0:T(8,128)(2,1)S(1)} %add_convert_fusion.2), channel_id=1, source_target_pairs={{0,8},{2,10},{4,12},{6,14},{8,0},{10,2},{12,4},{14,6},{16,24},{18,... | collective-permute-start | bytes 589832 | tf_op jit(solution)/shard_map/ppermute | solution.py:235
  40.3 7.6 %collective-permute-start.14 = (bf16[32,3072]{1,0:T(8,128)(2,1)S(1)}, bf16[32,3072]{1,0:T(8,128)(2,1)S(1)}, u32[]{:S(2)}, u32[]{:S(2)}) collective-permute-start(bf16[32,3072]{1,0:T(8,128)(2,1)S(1)} %get-tuple-element.51), channel_id=1, source_target_pairs={{0,2},{2,0},{4,6},{6,4},{8,10},{10,8},{12,14},{14,12},{16,18},{18,... | collective-permute-start | bytes 589832 | tf_op jit(solution)/shard_map/ppermute | solution.py:235
  42.7 9.9 %collective-permute-start.13 = (bf16[32,3072]{1,0:T(8,128)(2,1)S(1)}, bf16[32,3072]{1,0:T(8,128)(2,1)S(1)}, u32[]{:S(2)}, u32[]{:S(2)}) collective-permute-start(bf16[32,3072]{1,0:T(8,128)(2,1)S(1)} %add_convert_fusion.1), channel_id=1, source_target_pairs={{0,12},{2,14},{4,8},{6,10},{8,4},{10,6},{12,0},{14,2},{16,28},{18,... | collective-permute-start | bytes 589832 | tf_op jit(solution)/shard_map/ppermute | solution.py:235
  48.0 7.4 %collective-permute-start.15 = (bf16[32,3072]{1,0:T(8,128)(2,1)S(1)}, bf16[32,3072]{1,0:T(8,128)(2,1)S(1)}, u32[]{:S(2)}, u32[]{:S(2)}) collective-permute-start(bf16[32,3072]{1,0:T(8,128)(2,1)S(1)} %add_convert_fusion), channel_id=1, source_target_pairs={{0,4},{2,6},{4,0},{6,2},{8,12},{10,14},{12,8},{14,10},{16,20},{18,... | collective-permute-start | bytes 589832 | tf_op jit(solution)/shard_map/ppermute | solution.py:235
  49.3 6.1 %collective-permute-start.16 = (bf16[32,3072]{1,0:T(8,128)(2,1)S(1)}, bf16[32,3072]{1,0:T(8,128)(2,1)S(1)}, u32[]{:S(2)}, u32[]{:S(2)}) collective-permute-start(bf16[32,3072]{1,0:T(8,128)(2,1)S(1)} %get-tuple-element.52), channel_id=1, source_target_pairs={{0,2},{2,0},{4,6},{6,4},{8,10},{10,8},{12,14},{14,12},{16,18},{18,... | collective-permute-start | bytes 589832 | tf_op jit(solution)/shard_map/ppermute | solution.py:235
